TPU v7x, 32 devices: a whole 2x2x4 slice. The times are simulated.
32 devices in a mesh: tier: 4 (over y, x), tile: 8 (over z, core).
Axes of the slice: x: 2, y: 2, z: 4, core: 2. Of those that a mesh axis runs over, the one named last changes fastest.
Arguments:
- warming_above_ambient: float32 [4, 16, 256, 2048], P('tier', None, 'tile'), may hold values from -6 to 6
- substance_label: int32 [4, 16, 256, 2048], P('tier', None, 'tile'), may hold values from 0 to 15
- glue_zone_label: int32 [256, 2048], P('tile'), may hold values from 0 to 7
- patch_label_per_cell: int32 [4, 256, 2048], P('tier', 'tile'), may hold values from 0 to 127
- heat_conductance_per_substance: float32 [16], replicated, may hold values from 0.3 to 4
- dissipation_per_patch: float32 [4, 128], P('tier'), may hold values from 0.5 to 5
- glue_sheet_reciprocal_operators: float32 [8, 8, 8], replicated, may hold values from -0.3 to 1.3, as said below
Outputs:
- final_state: float32 [4, 16, 256, 2048], P('tier', None, 'tile')
Inputs may be any that keep to these rules, and one draw needn't show every extreme that they name: `glue_sheet_reciprocal_operators`: each matrix has diagonal entries of 0.6 to 1.0 plus a perturbation, and perturbed entries elsewhere.
All inputs are finite; a program needn't handle non-finite values.
Results may differ from a plain program's by a relative error of at most 0.0001.
Values sent between devices are 32-bit elements; how exact they have to be, the bound alone decides.
No kernel may reach another device: no remote copies, remote signals or barrier semaphores. Data moves between devices by JAX's collectives and lax.ppermute only.
A program may use at most 128 MiB of HBM per device.

v0:
```python
import jax
import jax.numpy as jnp
from jax import lax
from jax.sharding import PartitionSpec as P

MATERIALS = 16
REGIONS = 8
POWER_TILES = 128
STEPS = 2


step_dt = 0.04


def padded(cells, sides, width):
    for axis, dim in sides:
        count = lax.axis_size(axis)
        ends = count - 1
        head = lax.slice_in_dim(cells, 0, width, axis=dim)
        tail = lax.slice_in_dim(cells, cells.shape[dim] - width, cells.shape[dim], axis=dim)
        cells = jnp.concatenate(
            [
                lax.ppermute(tail, axis, [(i, (i + 1) % count) for i in range(ends)]),
                cells,
                lax.ppermute(head, axis, [((i + 1) % count, i) for i in range(ends)]),
            ],
            axis=dim,
        )
    return cells


def pad_axis(field, axis, low, high):
    widths = [(0, 0)] * field.ndim
    widths[axis] = (low, high)
    return jnp.pad(field, widths)


def conduct(padded_t, padded_k):
    centre = padded_t[..., 1:-1, :]
    kcell = padded_k[..., 1:-1, :]
    flux = 0.5 * (kcell + padded_k[..., 2:, :]) * (padded_t[..., 2:, :] - centre)
    flux = flux + 0.5 * (kcell + padded_k[..., :-2, :]) * (padded_t[..., :-2, :] - centre)
    side_t = pad_axis(centre, centre.ndim - 1, 1, 1)
    side_k = pad_axis(kcell, kcell.ndim - 1, 1, 1)
    flux = flux + 0.5 * (kcell + side_k[..., 2:]) * (side_t[..., 2:] - centre)
    flux = flux + 0.5 * (kcell + side_k[..., :-2]) * (side_t[..., :-2] - centre)
    face = (
        0.5
        * (kcell[..., 1:, :, :] + kcell[..., :-1, :, :])
        * (centre[..., 1:, :, :] - centre[..., :-1, :, :])
    )
    axis = centre.ndim - 3
    return flux + pad_axis(face, axis, 0, 1) - pad_axis(face, axis, 1, 0)


def select_solve(matrices, planes, regions):
    solved = jnp.zeros((matrices.shape[1],) + planes.shape[1:], jnp.float32)
    for which in range(REGIONS):
        mapped = jnp.einsum("ij,jxc->ixc", matrices[which], planes, precision=lax.Precision.HIGHEST)
        solved = solved + jnp.where(regions == which, mapped, 0.0)
    return solved


def local(
    warming_above_ambient,
    substance_label,
    glue_zone_label,
    patch_label_per_cell,
    heat_conductance_per_substance,
    dissipation_per_patch,
    glue_sheet_reciprocal_operators,
):
    kappa = jnp.zeros(substance_label.shape, jnp.float32)
    for which in range(MATERIALS):
        kappa = jnp.where(substance_label == which, heat_conductance_per_substance[which], kappa)
    onehot = (patch_label_per_cell[0][..., None] == lax.iota(jnp.int32, POWER_TILES)).astype(
        jnp.float32
    )
    source = jnp.dot(
        onehot.reshape(-1, POWER_TILES), dissipation_per_patch[0], precision=lax.Precision.HIGHEST
    )
    source = source.reshape(patch_label_per_cell.shape[1:])
    tier_index = lax.axis_index("tier")
    heating_snapshot = warming_above_ambient
    for step in range(STEPS):
        joined = padded(jnp.stack([heating_snapshot, kappa]), (("tile", 3),), 1)
        padded_t = joined[0]
        padded_k = joined[1]
        heating_snapshot = heating_snapshot + step_dt * conduct(padded_t, padded_k)
        heating_snapshot = heating_snapshot.at[:, 0].add(step_dt * source)
        planes = jnp.stack([heating_snapshot[0, 0], heating_snapshot[0, -1]])
        gathered = lax.all_gather(planes, "tier", axis=0, tiled=True)
        own_rows = lax.dynamic_slice_in_dim(glue_sheet_reciprocal_operators, 2 * tier_index, 2, 1)
        updated = select_solve(own_rows, gathered, glue_zone_label)
        heating_snapshot = heating_snapshot.at[0, 0].set(updated[0]).at[0, -1].set(updated[1])
    return heating_snapshot


def solution(mesh):
    in_specs = (
        P("tier", None, "tile", None),
        P("tier", None, "tile", None),
        P("tile", None),
        P("tier", "tile", None),
        P(),
        P("tier", None),
        P(),
    )
    out_specs = P("tier", None, "tile", None)
    return jax.shard_map(local, mesh=mesh, in_specs=in_specs, out_specs=out_specs, check_vma=False)
```

profile of v0, /device:TPU:0, one launch (start us, length us, event | category | flops | bytes accessed | tf_op | source)
XLA Modules:
  0.0 424.2 jit_solution(13224484290999744595)
XLA Ops:
  6.5 1.9 fusion.86
  8.5 5.0 %stack.22 = f32[1,1,16,32,2048]{4,0,3,2,1:T(1,128)S(1)} reshape(f32[1,16,32,2048]{3,2,1,0:T(8,128)} %param.19) | data formatting | bytes 8388608 | tf_op jit(solution)/shard_map/stack | solution.py:86
  13.5 44.8 %fusion.8 = f32[1,1,16,32,2048]{4,0,3,2,1:T(1,128)S(1)} fusion(s32[1,16,32,2048]{3,2,1,0:T(8,128)S(1)} %copy-done.16, f32[]{:T(128)} %bitcast.15, f32[]{:T(128)} %bitcast.14, f32[]{:T(128)} %bitcast.13, f32[]{:T(128)} %bitcast.12, f32[]{:T(128)} %bitcast.11, f32[]{:T(128)} %bitcast.10, f32[]{:T(128)} %bitcast.9, f32[]{:T(128)} %bitcast.8, f32[]{:T(128)} %bitcast.7, ...), kind=kLoop, calls=%fused_computation.33 | loop fusion | flops 33554432 | bytes 8388672 | tf_op jit(solution)/shard_map/stack | solution.py:86
  58.3 0.0 copy-start.20
  58.3 0.5 fusion.54
  58.9 2.4 collective-permute-start
  61.3 1.5 collective-permute-start.1
  62.8 23.6 %fusion.1 = f32[1,32,2048]{2,0,1:T(1,128)S(1)} fusion(s32[32,2048]{1,0:T(8,128)S(1)} %bitcast.110, f32[1,128]{1,0:T(1,128)S(1)} %copy-done.20), kind=kOutput, calls=%fused_computation.2 | convolution fusion | flops 109051904 | bytes 524800 | tf_op jit(solution)/shard_map/dot_general | solution.py:79
  86.4 0.1 bitcast_multiply_fusion
  86.5 8.0 %fusion.5 = f32[2,1,16,34,2048]{4,0,3,2,1:T(2,128)S(1)} fusion(f32[1,1,16,32,2048]{4,0,3,2,1:T(1,128)S(1)} %fusion.8, f32[2,1,16,1,2048]{4,0,3,2,1:T(2,128)S(1)} %collective-permute-done.1, f32[1,1,16,32,2048]{4,0,3,2,1:T(1,128)S(1)} %stack.22, f32[2,1,16,1,2048]{4,0,3,2,1:T(2,128)S(1)} %collective-permute-done), kind=kLoop, calls=%fused_computation.23 | loop fusion | flops 6684672 | bytes 17825792 | tf_op jit(solution)/shard_map/concatenate | solution.py:21
  94.5 7.9 %slice_bitcast_fusion.3 = (f32[1,16,34,2048]{3,0,2,1:T(1,128)S(1)}, f32[1,16,34,2048]{3,0,2,1:T(1,128)}) fusion(f32[2,1,16,34,2048]{4,0,3,2,1:T(2,128)S(1)} %fusion.5), kind=kLoop, calls=%fused_computation.32 | loop fusion | bytes 17825792 | tf_op jit(solution)/shard_map/squeeze | solution.py:88
  102.4 5.2 %slice.452 = f32[1,16,32,2048]{3,0,2,1:T(1,128)} slice(f32[1,16,34,2048]{3,0,2,1:T(1,128)S(1)} %get-tuple-element.83), slice={[0:1], [0:16], [1:33], [0:2048]} | slice | bytes 8388608 | tf_op jit(solution)/shard_map/slice | solution.py:40
  107.5 7.9 %slice.456 = f32[1,16,32,2048]{3,0,2,1:T(1,128)} slice(f32[1,16,34,2048]{3,0,2,1:T(1,128)} %get-tuple-element.84), slice={[0:1], [0:16], [1:33], [0:2048]} | slice | bytes 8388608 | tf_op jit(solution)/shard_map/slice | solution.py:39
  115.4 11.4 %fusion.21 = f32[1,15,32,2048]{3,0,2,1:T(1,128)S(1)} fusion(f32[1,16,34,2048]{3,0,2,1:T(1,128)} %get-tuple-element.84, f32[1,16,34,2048]{3,0,2,1:T(1,128)S(1)} %get-tuple-element.83), kind=kLoop, calls=%fused_computation.59 | loop fusion | flops 3932160 | bytes 19660800 | tf_op jit(solution)/shard_map/mul | solution.py:48
  126.9 46.0 %copy_add_fusion = f32[1,16,32,2048]{3,0,2,1:T(1,128)S(1)} fusion(f32[1,16,32,2048]{3,2,1,0:T(8,128)S(1)} %copy-done.11, f32[1,15,32,2048]{3,0,2,1:T(1,128)S(1)} %fusion.21, f32[1,16,32,2048]{3,0,2,1:T(1,128)S(1)} %copy-done.15, f32[1,16,32,2048]{3,0,2,1:T(1,128)S(1)} %copy-done.13, f32[1,16,34,2048]{3,0,2,1:T(1,128)} %get-tuple-element.84, ...), kind=kLoop, calls=%fused_computation.52 | loop fusion | flops 24117248 | bytes 37486592 | tf_op jit(solution)/shard_map/add | solution.py:89
  172.9 0.0 copy-start.18
  172.9 0.4 fusion.84
  173.3 0.0 copy-start.3
  173.3 2.0 copy-done.3
  175.3 0.5 pad_maximum_fusion.2
  175.8 1.1 copy.61
  176.9 0.0 all-gather.3.cloned.1.call-update
  177.0 0.4 all-gather.5.cloned.1.call-start
  177.4 0.6 slice.426
  178.1 0.7 and_reduce_fusion
  178.8 0.4 broadcast_compare_fusion
  179.2 37.9 %all-gather.3.cloned.1.call-done = f32[8,32,2048]{2,1,0:T(8,128)} async-done(((f32[2,32,2048]{2,1,0:T(8,128)}), f32[8,32,2048]{2,1,0:T(8,128)}) %all-gather.3.cloned.1.call-update) | async-done | bytes 2097168 | tf_op jit(solution)/shard_map/all_gather | solution.py:92
  217.0 4.8 %convolution_select_fusion.15 = f32[2,32,2048]{2,0,1:T(2,128)S(1)} fusion(f32[8,32,2048]{2,1,0:T(8,128)} %all-gather.3.cloned.1.call-done, pred[32,2048]{1,0:T(8,128)(4,1)S(1)} %get-tuple-element.99, f32[8,8,8]{2,1,0:T(8,128)S(1)} %copy-done, s32[]{:T(128)S(6)} %select_n.118), kind=kOutput, calls=%fused_computation.91 | convolution fusion | flops 12713984 | bytes 2688004 | tf_op jit(solution)/shard_map/ij,jxc->ixc/dot_general | solution.py:59
  221.8 4.8 %fusion.36 = f32[2,32,2048]{2,0,1:T(2,128)S(1)} fusion(f32[2,32,2048]{2,0,1:T(2,128)S(1)} %convolution_select_fusion.15, f32[8,32,2048]{2,1,0:T(8,128)} %all-gather.3.cloned.1.call-done, pred[32,2048]{1,0:T(8,128)(4,1)S(1)} %get-tuple-element.98, f32[8,8,8]{2,1,0:T(8,128)S(1)} %copy-done, s32[]{:T(128)S(6)} %add.183, s32[]{:T(128)S(6)} %select_n.118), kind=kOutput, calls=%fused_computation.90 | convolution fusion | flops 12845056 | bytes 3212296 | tf_op jit(solution)/shard_map/ij,jxc->ixc/dot_general | solution.py:59
  226.7 3.2 fusion.35
  229.9 3.4 fusion.34
  233.4 3.2 fusion.33
  236.6 3.2 fusion.32
  239.9 3.2 fusion.31
  243.1 3.6 fusion.30
  246.8 0.2 fusion.58
  247.0 1.7 fusion.55
  248.7 0.4 fusion.53
  249.1 1.8 collective-permute-start.2
  250.9 1.3 collective-permute-start.3
  252.2 3.4 collective-permute-done.3
  255.6 7.9 %fusion.7 = f32[2,1,16,34,2048]{4,0,3,2,1:T(2,128)S(1)} fusion(f32[1,1,16,32,2048]{4,0,3,2,1:T(1,128)S(1)} %copy-done.8, f32[2,1,16,1,2048]{4,0,3,2,1:T(2,128)S(1)} %collective-permute-done.3, f32[1,1,16,32,2048]{4,0,3,2,1:T(1,128)S(1)} %bitcast.109, f32[2,1,16,1,2048]{4,0,3,2,1:T(2,128)S(1)} %collective-permute-done.2), kind=kLoop, calls=%fused_computation.25 | loop fusion | flops 6684672 | bytes 17825792 | tf_op jit(solution)/shard_map/concatenate | solution.py:21
  263.5 7.9 %slice_bitcast_fusion.1 = (f32[1,16,34,2048]{3,0,2,1:T(1,128)S(1)}, f32[1,16,34,2048]{3,0,2,1:T(1,128)}) fusion(f32[2,1,16,34,2048]{4,0,3,2,1:T(2,128)S(1)} %fusion.7), kind=kLoop, calls=%fused_computation.30 | loop fusion | bytes 17825792 | tf_op jit(solution)/shard_map/squeeze | solution.py:88
  271.4 5.2 %slice.470 = f32[1,16,32,2048]{3,0,2,1:T(1,128)} slice(f32[1,16,34,2048]{3,0,2,1:T(1,128)S(1)} %get-tuple-element.81), slice={[0:1], [0:16], [1:33], [0:2048]} | slice | bytes 8388608 | tf_op jit(solution)/shard_map/slice | solution.py:40
  276.6 7.9 %slice.474 = f32[1,16,32,2048]{3,0,2,1:T(1,128)} slice(f32[1,16,34,2048]{3,0,2,1:T(1,128)} %get-tuple-element.82), slice={[0:1], [0:16], [1:33], [0:2048]} | slice | bytes 8388608 | tf_op jit(solution)/shard_map/slice | solution.py:39
  284.5 11.4 %fusion.19 = f32[1,15,32,2048]{3,0,2,1:T(1,128)S(1)} fusion(f32[1,16,34,2048]{3,0,2,1:T(1,128)} %get-tuple-element.82, f32[1,16,34,2048]{3,0,2,1:T(1,128)S(1)} %get-tuple-element.81), kind=kLoop, calls=%fused_computation.55 | loop fusion | flops 3932160 | bytes 19660800 | tf_op jit(solution)/shard_map/mul | solution.py:48
  295.9 42.6 %multiply_add_fusion = f32[1,16,32,2048]{3,0,2,1:T(1,128)S(1)} fusion(f32[1,16,32,2048]{3,0,2,1:T(1,128)S(1)} %copy-done.6, f32[1,15,32,2048]{3,0,2,1:T(1,128)S(1)} %fusion.19, f32[1,16,32,2048]{3,0,2,1:T(1,128)S(1)} %copy-done.14, f32[1,16,32,2048]{3,0,2,1:T(1,128)S(1)} %copy-done.12, f32[1,16,34,2048]{3,0,2,1:T(1,128)} %get-tuple-element.82, ...), kind=kLoop, calls=%fused_computation.53 | loop fusion | flops 24117248 | bytes 37486592 | tf_op jit(solution)/shard_map/add | solution.py:89
  338.5 0.4 fusion.85
  338.9 2.0 copy-done.9
  341.0 0.5 pad_maximum_fusion.3
  341.5 1.1 copy.70
  342.6 0.0 all-gather.5.cloned.1.call-update
  342.6 39.0 %all-gather.5.cloned.1.call-done = f32[8,32,2048]{2,1,0:T(8,128)} async-done(((f32[2,32,2048]{2,1,0:T(8,128)}), f32[8,32,2048]{2,1,0:T(8,128)}) %all-gather.5.cloned.1.call-update) | async-done | bytes 2097168 | tf_op jit(solution)/shard_map/all_gather | solution.py:92
  381.5 4.8 %convolution_select_fusion.7 = f32[2,32,2048]{2,0,1:T(2,128)S(1)} fusion(f32[8,32,2048]{2,1,0:T(8,128)} %all-gather.5.cloned.1.call-done, pred[32,2048]{1,0:T(8,128)(4,1)S(1)} %get-tuple-element.99, f32[8,8,8]{2,1,0:T(8,128)S(1)} %copy-done, s32[]{:T(128)S(6)} %select_n.118), kind=kOutput, calls=%fused_computation.76 | convolution fusion | flops 12713984 | bytes 2688004 | tf_op jit(solution)/shard_map/ij,jxc->ixc/dot_general | solution.py:59
  386.3 4.8 %fusion.29 = f32[2,32,2048]{2,0,1:T(2,128)S(1)} fusion(f32[2,32,2048]{2,0,1:T(2,128)S(1)} %convolution_select_fusion.7, f32[8,32,2048]{2,1,0:T(8,128)} %all-gather.5.cloned.1.call-done, pred[32,2048]{1,0:T(8,128)(4,1)S(1)} %get-tuple-element.98, f32[8,8,8]{2,1,0:T(8,128)S(1)} %copy-done, s32[]{:T(128)S(6)} %add.183, s32[]{:T(128)S(6)} %select_n.118), kind=kOutput, calls=%fused_computation.75 | convolution fusion | flops 12845056 | bytes 3212296 | tf_op jit(solution)/shard_map/ij,jxc->ixc/dot_general | solution.py:59
  391.2 3.2 fusion.28
  394.4 3.5 fusion.27
  397.9 3.2 fusion.26
  401.2 3.2 fusion.25
  404.4 3.5 fusion.24
  407.9 3.2 fusion.23
  411.2 0.2 fusion.57
  411.4 1.7 fusion.56
  413.1 4.0 copy.79
  (44 shorter events, 0.1 us)
Async XLA Ops:
  6.5 210.5 %copy-start = (f32[8,8,8]{2,1,0:T(8,128)S(1)}, f32[8,8,8]{2,1,0:T(8,128)}, u32[]{:S(2)}) copy-start(f32[8,8,8]{2,1,0:T(8,128)} %param.25) | copy-start | bytes 6148
  6.5 210.5 %all-gather.3.cloned.1.call-start = ((), (), s32[]{:S(2)}) async-start(), calls=%async_computation | async-start | bytes 2621440 | tf_op jit(solution)/shard_map/all_gather | solution.py:92
  8.5 5.0 %copy-start.16 = (s32[1,16,32,2048]{3,2,1,0:T(8,128)S(1)}, s32[1,16,32,2048]{3,2,1,0:T(8,128)}, u32[]{:S(2)}) copy-start(s32[1,16,32,2048]{3,2,1,0:T(8,128)} %param.20) | copy-start | bytes 12582916
  58.3 28.2 %copy-start.7 = (f32[1,1,16,32,2048]{4,0,3,2,1:T(1,128)}, f32[1,1,16,32,2048]{4,0,3,2,1:T(1,128)S(1)}, u32[]{:S(2)}) copy-start(f32[1,1,16,32,2048]{4,0,3,2,1:T(1,128)S(1)} %fusion.8) | copy-start | bytes 12582916
  58.3 4.4 %copy-start.19 = (s32[1,32,2048]{2,1,0:T(8,128)S(1)}, s32[1,32,2048]{2,1,0:T(8,128)}, u32[]{:S(2)}) copy-start(s32[1,32,2048]{2,1,0:T(8,128)} %param.22) | copy-start | bytes 786436
  58.3 4.4 %copy-start.20 = (f32[1,128]{1,0:T(1,128)S(1)}, f32[1,128]{1,0:T(1,128)}, u32[]{:S(2)}) copy-start(f32[1,128]{1,0:T(1,128)} %param.24) | copy-start | bytes 1540
  58.9 27.6 %collective-permute-start = (f32[2,1,16,1,2048]{4,0,3,2,1:T(2,128)S(1)}, f32[2,1,16,1,2048]{4,0,3,2,1:T(2,128)S(1)}, u32[]{:S(2)}, u32[]{:S(2)}) collective-permute-start(f32[2,1,16,1,2048]{4,0,3,2,1:T(2,128)S(1)} %get-tuple-element.77), channel_id=1, source_target_pairs={{0,1},{1,2},{2,3},{3,4},{4,5},{5,6},{6,7},{8,9},{9,10},{10,11},{11... | collective-permute-start | bytes 786440 | tf_op jit(solution)/shard_map/ppermute | solution.py:23
  61.3 25.2 %collective-permute-start.1 = (f32[2,1,16,1,2048]{4,0,3,2,1:T(2,128)S(1)}, f32[2,1,16,1,2048]{4,0,3,2,1:T(2,128)S(1)}, u32[]{:S(2)}, u32[]{:S(2)}) collective-permute-start(f32[2,1,16,1,2048]{4,0,3,2,1:T(2,128)S(1)} %get-tuple-element.91), channel_id=1, source_target_pairs={{1,0},{2,1},{3,2},{4,3},{5,4},{6,5},{7,6},{9,8},{10,9},{11,10},{12... | collective-permute-start | bytes 786440 | tf_op jit(solution)/shard_map/ppermute | solution.py:25
  115.4 11.4 %copy-start.11 = (f32[1,16,32,2048]{3,2,1,0:T(8,128)S(1)}, f32[1,16,32,2048]{3,2,1,0:T(8,128)}, u32[]{:S(2)}) copy-start(f32[1,16,32,2048]{3,2,1,0:T(8,128)} %param.19) | copy-start | bytes 12582916
  115.4 11.4 %copy-start.13 = (f32[1,16,32,2048]{3,0,2,1:T(1,128)S(1)}, f32[1,16,32,2048]{3,0,2,1:T(1,128)}, u32[]{:S(2)}) copy-start(f32[1,16,32,2048]{3,0,2,1:T(1,128)} %slice.452) | copy-start | bytes 12582916
  115.4 11.4 %copy-start.15 = (f32[1,16,32,2048]{3,0,2,1:T(1,128)S(1)}, f32[1,16,32,2048]{3,0,2,1:T(1,128)}, u32[]{:S(2)}) copy-start(f32[1,16,32,2048]{3,0,2,1:T(1,128)} %slice.456) | copy-start | bytes 12582916
  172.9 5.2 %copy-start.18 = (s32[4]{0:T(128)S(1)}, s32[4]{0:T(128)}, u32[]{:S(2)}) copy-start(s32[4]{0:T(128)} %constant.199.clone.1) | copy-start | bytes 52
  172.9 5.9 %copy-start.17 = (s32[32,2048]{1,0:T(8,128)S(1)}, s32[32,2048]{1,0:T(8,128)}, u32[]{:S(2)}) copy-start(s32[32,2048]{1,0:T(8,128)} %param.21) | copy-start | bytes 786436
  173.3 2.0 copy-start.3
  177.0 204.6 %all-gather.5.cloned.1.call-start = ((), (), s32[]{:S(2)}) async-start(), calls=%async_computation.1 | async-start | bytes 2621440 | tf_op jit(solution)/shard_map/all_gather | solution.py:92
  217.0 9.7 %copy-start.1 = (f32[8,32,2048]{2,1,0:T(8,128)S(1)}, f32[8,32,2048]{2,1,0:T(8,128)}, u32[]{:S(2)}) copy-start(f32[8,32,2048]{2,1,0:T(8,128)} %all-gather.3.cloned.1.call-done) | copy-start | bytes 6291460
  236.6 10.2 %copy-start.4 = (f32[1,16,32,2048]{3,0,2,1:T(1,128)S(1)}, f32[1,16,32,2048]{3,0,2,1:T(1,128)}, u32[]{:S(2)}) copy-start(f32[1,16,32,2048]{3,0,2,1:T(1,128)} %copy-done.3) | copy-start | bytes 12582916
  243.1 12.4 %copy-start.8 = (f32[1,1,16,32,2048]{4,0,3,2,1:T(1,128)S(1)}, f32[1,1,16,32,2048]{4,0,3,2,1:T(1,128)}, u32[]{:S(2)}) copy-start(f32[1,1,16,32,2048]{4,0,3,2,1:T(1,128)} %copy-done.7) | copy-start | bytes 12582916
  248.7 6.8 %copy-start.5 = (f32[1,16,32,2048]{3,0,2,1:T(1,128)}, f32[1,16,32,2048]{3,0,2,1:T(1,128)S(1)}, u32[]{:S(2)}) copy-start(f32[1,16,32,2048]{3,0,2,1:T(1,128)S(1)} %fusion.55) | copy-start | bytes 12582916
  249.1 3.1 collective-permute-start.2
  250.9 4.7 %collective-permute-start.3 = (f32[2,1,16,1,2048]{4,0,3,2,1:T(2,128)S(1)}, f32[2,1,16,1,2048]{4,0,3,2,1:T(2,128)S(1)}, u32[]{:S(2)}, u32[]{:S(2)}) collective-permute-start(f32[2,1,16,1,2048]{4,0,3,2,1:T(2,128)S(1)} %get-tuple-element.90), channel_id=1, source_target_pairs={{1,0},{2,1},{3,2},{4,3},{5,4},{6,5},{7,6},{9,8},{10,9},{11,10},{12... | collective-permute-start | bytes 786440 | tf_op jit(solution)/shard_map/ppermute | solution.py:25
  284.5 11.4 %copy-start.6 = (f32[1,16,32,2048]{3,0,2,1:T(1,128)S(1)}, f32[1,16,32,2048]{3,0,2,1:T(1,128)}, u32[]{:S(2)}) copy-start(f32[1,16,32,2048]{3,0,2,1:T(1,128)} %copy-done.5) | copy-start | bytes 12582916
  284.5 11.4 %copy-start.12 = (f32[1,16,32,2048]{3,0,2,1:T(1,128)S(1)}, f32[1,16,32,2048]{3,0,2,1:T(1,128)}, u32[]{:S(2)}) copy-start(f32[1,16,32,2048]{3,0,2,1:T(1,128)} %slice.470) | copy-start | bytes 12582916
  284.5 11.4 %copy-start.14 = (f32[1,16,32,2048]{3,0,2,1:T(1,128)S(1)}, f32[1,16,32,2048]{3,0,2,1:T(1,128)}, u32[]{:S(2)}) copy-start(f32[1,16,32,2048]{3,0,2,1:T(1,128)} %slice.474) | copy-start | bytes 12582916
  338.9 2.0 copy-start.9
  381.5 9.7 %copy-start.2 = (f32[8,32,2048]{2,1,0:T(8,128)S(1)}, f32[8,32,2048]{2,1,0:T(8,128)}, u32[]{:S(2)}) copy-start(f32[8,32,2048]{2,1,0:T(8,128)} %all-gather.5.cloned.1.call-done) | copy-start | bytes 6291460
  401.2 10.0 %copy-start.10 = (f32[1,16,32,2048]{3,0,2,1:T(1,128)S(1)}, f32[1,16,32,2048]{3,0,2,1:T(1,128)}, u32[]{:S(2)}) copy-start(f32[1,16,32,2048]{3,0,2,1:T(1,128)} %copy-done.9) | copy-start | bytes 12582916
Sparse Core Ops, SparseCore 0:
  177.1 39.8 all-gather.2
  342.7 38.7 all-gather.4
where the time goes:
time: 428 us; the launch traced here: 424 us
  other arithmetic  179 us (42%)
  matrix products  82.8 us (19%)
  waiting for transfers between devices  80.2 us (19%)
  local copies, waits for them, and re-layouts  60.2 us (14%)
  between operations  14.2 us (3%)
  starting transfers between devices  7.34 us (2%)
    add x2, other arithmetic, local(): heating_snapshot = heating_snapshot + step_dt * conduct(padded_t, padded_k)  88.6 us
    all_gather x2, waiting for transfers between devices, local(): gathered = lax.all_gather(planes, 'tier', axis=0, tiled=True)  76.8 us
    dot_general x16, matrix products, select_solve(): jnp.einsum('ij,jxc->ixc', matrices[which], planes, precision=lax.Precisio...  59.2 us
    another operation x3, other arithmetic, local(): joined = padded(jnp.stack([heating_snapshot, kappa]), (('tile', 3),), 1)  45.7 us
    dot_general x1, matrix products, local(): jnp.dot(onehot.reshape(-1, POWER_TILES), dissipation_per_patch[0], precis...  23.6 us
    mul x2, other arithmetic, conduct(): 0.5 * (kcell[..., 1:, :, :] + kcell[..., :-1, :, :])  22.8 us
    concatenate x2, other arithmetic, padded(): jnp.concatenate([lax.ppermute(tail, axis, [(i, (i + 1) % count) for i in...  15.9 us
    slice x2, local copies, waits for them, and re-layouts, conduct(): centre = padded_t[..., 1:-1, :]  15.8 us
  transfers between devices with their start and end apart: 6, of which 3 were waited for; matrix products, arithmetic and copies ran while one was open for 6% of the time, Pallas kernels for 0%

commit v1 on v0

v1 whole, which is shorter than its diff:
```python
import functools

import jax
import jax.numpy as jnp
from jax import lax
from jax.experimental import pallas as pl
from jax.experimental.pallas import tpu as pltpu
from jax.sharding import PartitionSpec as P

STEPS = 2
step_dt = 0.04
half_dt = 0.5 * step_dt
LANES = 128
ROWS = 8
MIB = 1 << 20

VMEM = pl.BlockSpec(memory_space=pltpu.VMEM)
SMEM = pl.BlockSpec(memory_space=pltpu.SMEM)
ANY = pl.BlockSpec(memory_space=pl.ANY)


def tile(r, c):
    return pl.ds(ROWS * r, ROWS), pl.ds(LANES * c, LANES)


def lane_ids():
    return lax.broadcasted_iota(jnp.int32, (ROWS, LANES), 1)


def row_ids():
    return lax.broadcasted_iota(jnp.int32, (ROWS, LANES), 0)


def choose(values, labels):
    values, bit = list(values), 1
    while len(values) > 1:
        odd = (labels & bit) != 0
        paired = [
            jnp.where(odd, values[i + 1], values[i]) if i + 1 < len(values) else values[i]
            for i in range(0, len(values), 2)
        ]
        values, bit = paired, 2 * bit
    return values[0]


def lookup(row, labels):
    table = jnp.broadcast_to(row, labels.shape)
    return jnp.take_along_axis(table, labels, axis=1, mode="promise_in_bounds")


def conductance(kap, labels):
    table = [kap[i] for i in range(kap.shape[0])]
    return half_dt * choose(table, labels)


def stencil(R, W, get_s, get_h, get_z, halo, put):
    C, S = W // LANES, R // ROWS
    lane, row = lane_ids(), row_ids()
    first, last = lane == 0, lane == LANES - 1
    top, bottom = row == 0, row == ROWS - 1
    before = None
    for c in range(C):
        s = [get_s(r, c) for r in range(S)]
        h = [get_h(r, c) for r in range(S)]
        rs = [pltpu.roll(v, 1, 1) for v in s]
        rh = [pltpu.roll(v, 1, 1) for v in h]
        us = [pltpu.roll(v, 1, 0) for v in s]
        uh = [pltpu.roll(v, 1, 0) for v in h]
        if halo is not None:
            sa, ha, sb, hb = halo(c)
        acc, back, down = [], [], []
        for r in range(S):
            if c == 0:
                sl, hl = jnp.where(first, 0.0, rs[r]), jnp.where(first, 0.0, rh[r])
            else:
                sl = jnp.where(first, before[0][r], rs[r])
                hl = jnp.where(first, before[1][r], rh[r])
            face = (h[r] + hl) * (sl - s[r])
            back.append(pltpu.roll(face, LANES - 1, 1))
            if r == 0:
                if halo is None:
                    su, hu = us[0], uh[0]
                else:
                    su, hu = jnp.where(top, sa, us[0]), jnp.where(top, ha, uh[0])
            else:
                su, hu = jnp.where(top, us[r - 1], us[r]), jnp.where(top, uh[r - 1], uh[r])
            upper = (h[r] + hu) * (su - s[r])
            down.append(pltpu.roll(upper, ROWS - 1, 0))
            acc.append((s[r] + get_z(r, c, s[r], h[r])) + (face + upper))
        for r in range(S):
            if r + 1 < S:
                lower = jnp.where(bottom, down[r + 1], down[r])
            elif halo is None:
                lower = down[r]
            else:
                lower = jnp.where(bottom, (h[r] + hb) * (s[r] - sb), down[r])
            acc[r] = acc[r] - lower
        if before is not None:
            for r in range(S):
                put(r, c - 1, before[3][r] - jnp.where(last, back[r], before[2][r]))
        before = (rs, rh, back, acc, s, h)
    for r in range(S):
        out = before[5][r] * before[4][r]
        put(r, C - 1, before[3][r] - jnp.where(last, out, before[2][r]))


def vertical(s, h, s_up, h_up, s_down, h_down):
    return (h + h_up) * (s_up - s) + (h + h_down) * (s_down - s)


def first_planes_kernel(s_any, lab_any, patch, kap, power, left, right, h_out, src, s_v, lab_v, sem):
    L, R, W = s_any.shape
    C = W // LANES
    starts = (0, L - 2)
    copies = []
    for p, a in enumerate(starts):
        copies.append(
            [
                pltpu.make_async_copy(s_any.at[pl.ds(a, 2)], s_v.at[p], sem.at[0, p]),
                pltpu.make_async_copy(lab_any.at[pl.ds(a, 2)], lab_v.at[p], sem.at[1, p]),
            ]
        )
    for group in copies:
        for copy in group:
            copy.start()
    for p, a in enumerate(starts):
        for copy in copies[p]:
            copy.wait()
        own, near = (0, 1) if p == 0 else (1, 0)

        def get_s(r, c):
            return s_v[(p, own) + tile(r, c)]

        def get_h(r, c):
            value = conductance(kap, lab_v[(p, own) + tile(r, c)])
            h_out[(a + own,) + tile(r, c)] = value
            return value

        def get_z(r, c, s, h):
            h_near = conductance(kap, lab_v[(p, near) + tile(r, c)])
            h_out[(a + near,) + tile(r, c)] = h_near
            flow = (h + h_near) * (s_v[(p, near) + tile(r, c)] - s)
            if p == 0:
                heat = step_dt * lookup(power[...], patch[tile(r, c)])
                src[tile(r, c)] = heat
                flow = flow + heat
            return flow

        def put(r, c, value):
            half = C // 2
            if c < half:
                left[(p,) + tile(r, c)] = value
            else:
                right[(p,) + tile(r, c - half)] = value

        stencil(R, W, get_s, get_h, get_z, None, put)


def first_planes(s, lab, patch, kap, power):
    L, R, W = s.shape
    f32 = jnp.float32
    return pl.pallas_call(
        first_planes_kernel,
        out_shape=(
            jax.ShapeDtypeStruct((2, R, W // 2), f32),
            jax.ShapeDtypeStruct((2, R, W // 2), f32),
            jax.ShapeDtypeStruct((L, R, W), f32),
            jax.ShapeDtypeStruct((R, W), f32),
        ),
        in_specs=[ANY, ANY, VMEM, SMEM, VMEM],
        out_specs=[VMEM] * 4,
        scratch_shapes=[
            pltpu.VMEM((2, 2, R, W), f32),
            pltpu.VMEM((2, 2, R, W), jnp.int32),
            pltpu.SemaphoreType.DMA((2, 2)),
        ],
        compiler_params=pltpu.CompilerParams(vmem_limit_bytes=16 * MIB),
        name="first_planes",
    )(s, lab, patch, kap, power)


def pack_kernel(s_lo, s_hi, l_lo, l_hi, p_lo, p_hi, g_lo, g_hi, kap, power, up, down):
    L, _, W = s_lo.shape

    def body(c, _):
        lanes = pl.ds(pl.multiple_of(c * LANES, LANES), LANES)
        for out, s, lab, patch, glue, rows in (
            (up, s_lo, l_lo, p_lo, g_lo, (0, 1)),
            (down, s_hi, l_hi, p_hi, g_hi, (ROWS - 2, ROWS - 1)),
        ):
            for k, row in enumerate(rows):
                out[pl.ds(k * L, L), lanes] = s[:, row, lanes]
                out[pl.ds((2 + k) * L, L), lanes] = conductance(kap, lab[:, row, lanes])
            edge = 0 if out is up else ROWS - 1
            heat = step_dt * lookup(power[...], patch[:, lanes])
            glued = glue[:, lanes].astype(jnp.float32)
            row = row_ids()
            pair = jnp.where(row == 0, heat[edge : edge + 1], glued[edge : edge + 1])
            out[pl.ds(4 * L, ROWS), lanes] = pair
        return 0

    lax.fori_loop(0, W // LANES, body, 0)


def pack(s, lab, patch, glue, kap, power):
    L, R, W = s.shape
    n = R // ROWS - 1
    lo3, hi3 = (pl.BlockSpec((L, ROWS, W), lambda i, k=k: (0, k, 0)) for k in (0, n))
    lo2, hi2 = (pl.BlockSpec((ROWS, W), lambda i, k=k: (k, 0)) for k in (0, n))
    rows = 4 * L + ROWS
    whole = pl.BlockSpec((rows, W), lambda i: (0, 0))
    return pl.pallas_call(
        pack_kernel,
        grid=(1,),
        out_shape=(jax.ShapeDtypeStruct((rows, W), jnp.float32),) * 2,
        in_specs=[lo3, hi3, lo3, hi3, lo2, hi2, lo2, hi2, SMEM, pl.BlockSpec(power.shape, lambda i: (0, 0))],
        out_specs=[whole, whole],
        compiler_params=pltpu.CompilerParams(vmem_limit_bytes=24 * MIB),
        name="pack",
    )(s, s, lab, lab, patch, patch, glue, glue, kap, power)


def edge_kernel(place, own_up, own_down, lo, hi, edges, beyond, aux):
    rows, W = own_up.shape
    L = (rows - ROWS) // 4
    col = lax.broadcasted_iota(jnp.int32, (L, W), 1)
    layer = lax.broadcasted_iota(jnp.int32, (L, W), 0)

    def part(ref, k):
        return ref[pl.ds(k * L, L), :]

    def step(s_a, h_a, s, h, s_b, h_b):
        def toward(s_n, h_n):
            return (h + h_n) * (s_n - s)

        def moved(shift, axis, gone):
            return jnp.where(gone, 0.0, pltpu.roll(s, shift, axis)), jnp.where(
                gone, 0.0, pltpu.roll(h, shift, axis)
            )

        total = s + toward(s_a, h_a) + toward(s_b, h_b)
        total = total + toward(*moved(1, 1, col == 0)) + toward(*moved(W - 1, 1, col == W - 1))
        under = jnp.where(layer == 0, 0.0, toward(pltpu.roll(s, 1, 0), pltpu.roll(h, 1, 0)))
        over = jnp.where(layer == L - 1, 0.0, toward(pltpu.roll(s, L - 1, 0), pltpu.roll(h, L - 1, 0)))
        return total + under + over

    for side, (other, own, there) in enumerate(((lo, own_up, place[0]), (hi, own_down, place[1]))):
        far, near = (0, 1) if side == 0 else (1, 0)
        exists = there != 0
        sf, sn = (jnp.where(exists, part(other, k), 0.0) for k in (far, near))
        hf, hn = (jnp.where(exists, part(other, 2 + k), 0.0) for k in (far, near))
        first, second = (0, 1) if side == 0 else (1, 0)
        s0, s1, h0, h1 = part(own, first), part(own, second), part(own, 2 + first), part(own, 2 + second)
        out = step(sf, hf, sn, hn, s0, h0)
        out = jnp.where(exists, out, 0.0)
        inner = step(sn, hn, s0, h0, s1, h1)
        beyond[side] = out
        heat_out = jnp.where(exists, other[pl.ds(4 * L, 1), :], 0.0)
        heat_in = own[pl.ds(4 * L, 1), :]
        k_out, k_in = (0, 1) if side == 0 else (3, 2)
        edges[pl.ds(k_out, 1), :] = out[0:1] + heat_out
        edges[pl.ds(k_in, 1), :] = inner[0:1] + heat_in
        edges[pl.ds(4 + k_out, 1), :] = out[L - 1 : L]
        edges[pl.ds(4 + k_in, 1), :] = inner[L - 1 : L]
        aux[pl.ds(2 * side, 1), :] = hn[0:1]
        aux[pl.ds(2 * side + 1, 1), :] = hn[L - 1 : L]
        zone_out = jnp.where(exists, other[pl.ds(4 * L + 1, 1), :], 0.0)
        aux[pl.ds(4 + k_out, 1), :] = zone_out
        aux[pl.ds(4 + k_in, 1), :] = own[pl.ds(4 * L + 1, 1), :]


def edge_rows(place, own_up, own_down, lo, hi):
    rows, W = own_up.shape
    L = (rows - ROWS) // 4
    f32 = jnp.float32
    return pl.pallas_call(
        edge_kernel,
        out_shape=(
            jax.ShapeDtypeStruct((ROWS, W), f32),
            jax.ShapeDtypeStruct((2, L, W), f32),
            jax.ShapeDtypeStruct((ROWS, W), f32),
        ),
        in_specs=[SMEM] + [VMEM] * 4,
        out_specs=[VMEM] * 3,
        compiler_params=pltpu.CompilerParams(vmem_limit_bytes=16 * MIB),
        name="edge_rows",
    )(place, own_up, own_down, lo, hi)


def pick(ref, base, l, lanes, row):
    at = base + (l // ROWS) * ROWS
    if not isinstance(l, int):
        at = pl.multiple_of(at, ROWS)
    return pltpu.roll(ref[pl.ds(at, ROWS), lanes], (row - l) % ROWS, 0)


def halo_rows(lo, hi, place, lanes, l, L):
    above, below = place[0] != 0, place[1] != 0
    end = ROWS - 1
    sa = jnp.where(above, pick(lo, L, l, lanes, 0), 0.0)
    ha = jnp.where(above, pick(lo, 3 * L, l, lanes, 0), 0.0)
    sb = jnp.where(below, pick(hi, 0, l, lanes, end), 0.0)
    hb = jnp.where(below, pick(hi, 2 * L, l, lanes, end), 0.0)
    return sa, ha, sb, hb


def first_layer(l, L, R, W, place, s_ref, lab, kap, lo, hi, h_ref, out, ready):
    def get_h(r, c):
        return h_ref[(l,) + tile(r, c)]

    def get_s(r, c):
        return s_ref[(l,) + tile(r, c)]

    def near(k, r, c):
        at = (l + k,) + tile(r, c)
        if k in ready:
            return h_ref[at]
        value = conductance(kap, lab[at])
        h_ref[at] = value
        return value

    def get_z(r, c, s, h):
        return vertical(
            s, h, s_ref[(l - 1,) + tile(r, c)], near(-1, r, c), s_ref[(l + 1,) + tile(r, c)], near(1, r, c)
        )

    def put(r, c, value):
        out[(l,) + tile(r, c)] = value

    def halo(c):
        return halo_rows(lo, hi, place, pl.ds(LANES * c, LANES), l, L)

    stencil(R, W, get_s, get_h, get_z, halo, put)


def outer_kernel(place, s_ref, lab, kap, lo, hi, h_in, h_ref, out):
    L, R, W = s_ref.shape
    first_layer(1, L, R, W, place, s_ref, lab, kap, lo, hi, h_ref, out, (-1, 0))
    first_layer(L - 2, L, R, W, place, s_ref, lab, kap, lo, hi, h_ref, out, (0, 1))


def outer_layers(place, s, lab, kap, lo, hi, h):
    return pl.pallas_call(
        outer_kernel,
        out_shape=(jax.ShapeDtypeStruct(s.shape, jnp.float32),) * 2,
        in_specs=[SMEM, VMEM, VMEM, SMEM, VMEM, VMEM, VMEM],
        out_specs=[VMEM, VMEM],
        input_output_aliases={6: 0},
        compiler_params=pltpu.CompilerParams(vmem_limit_bytes=24 * MIB),
        name="outer_layers",
    )(place, s, lab, kap, lo, hi, h)


def inner_kernel(place, s_ref, lab, kap, lo, hi, h_in, t_in, h_ref, out):
    L, R, W = s_ref.shape

    def body(l, _):
        first_layer(l, L, R, W, place, s_ref, lab, kap, lo, hi, h_ref, out, (-1, 0))
        return 0

    lax.fori_loop(2, L - 2, body, 0)


def inner_layers(place, s, lab, kap, lo, hi, h, t):
    return pl.pallas_call(
        inner_kernel,
        out_shape=(jax.ShapeDtypeStruct(s.shape, jnp.float32),) * 2,
        in_specs=[SMEM, VMEM, VMEM, SMEM, VMEM, VMEM, VMEM, VMEM],
        out_specs=[VMEM, VMEM],
        input_output_aliases={6: 0, 7: 1},
        compiler_params=pltpu.CompilerParams(vmem_limit_bytes=24 * MIB),
        name="inner_layers",
    )(place, s, lab, kap, lo, hi, h, t)


def last_kernel(place, t_ref, h_ref, lo, hi, beyond, out, buf, sem):
    L, R, W = t_ref.shape

    def send(l):
        return pltpu.make_async_copy(buf.at[l], out.at[l], sem.at[l])

    def body(l, _):
        def get_s(r, c):
            return t_ref[(l,) + tile(r, c)]

        def get_h(r, c):
            return h_ref[(l,) + tile(r, c)]

        def get_z(r, c, s, h):
            a, b = (l - 1,) + tile(r, c), (l + 1,) + tile(r, c)
            return vertical(s, h, t_ref[a], h_ref[a], t_ref[b], h_ref[b])

        def put(r, c, value):
            buf[(l,) + tile(r, c)] = value

        def halo(c):
            lanes = pl.ds(LANES * c, LANES)
            _, ha, _, hb = halo_rows(lo, hi, place, lanes, l, L)
            sa, sb = pick(beyond.at[0], 0, l, lanes, 0), pick(beyond.at[1], 0, l, lanes, ROWS - 1)
            return sa, ha, sb, hb

        stencil(R, W, get_s, get_h, get_z, halo, put)
        send(l).start()
        return 0

    lax.fori_loop(1, L - 1, body, 0)

    def drain(l, _):
        send(l).wait()
        return 0

    lax.fori_loop(1, L - 1, drain, 0)


def last_layers(place, t, h, lo, hi, beyond):
    L = t.shape[0]
    return pl.pallas_call(
        last_kernel,
        out_shape=jax.ShapeDtypeStruct(t.shape, jnp.float32),
        in_specs=[SMEM] + [VMEM] * 5,
        out_specs=ANY,
        scratch_shapes=[pltpu.VMEM(t.shape, jnp.float32), pltpu.SemaphoreType.DMA((L,))],
        compiler_params=pltpu.CompilerParams(vmem_limit_bytes=24 * MIB),
        name="last_layers",
    )(place, t, h, lo, hi, beyond)


def coefficient(ops, tiers, regions, region, i, j):
    return ops[(region * 2 * tiers + i) * 2 * tiers + j]


def mixed(ops, tiers, regions, zone, row, planes):
    total = None
    for index, value in planes:
        table = [coefficient(ops, tiers, regions, g, row, index) for g in range(regions)]
        term = choose(table, zone) * value
        total = term if total is None else total + term
    return total


def combine_kernel(tiers, regions, tier, ops, zone, left, left_x, right, right_y, to_y, to_x):
    _, R, half = left.shape
    me = tier[0]
    for out, own, other, near, target, base in (
        (to_y, left, left_x, tier[1], tier[2], 0),
        (to_x, right, right_y, tier[2], tier[1], half),
    ):

        def body(c, _, out=out, own=own, other=other, near=near, target=target, base=base):
            lanes = pl.ds(pl.multiple_of(c * LANES, LANES), LANES)
            zone_lanes = pl.ds(pl.multiple_of(base + c * LANES, LANES), LANES)
            for r in range(R // ROWS):
                rows = pl.ds(ROWS * r, ROWS)
                planes = [(2 * me + j, own[j, rows, lanes]) for j in range(2)]
                planes += [(2 * near + j, other[j, rows, lanes]) for j in range(2)]
                for i in range(2):
                    out[i, rows, lanes] = mixed(
                        ops, tiers, regions, zone[rows, zone_lanes], 2 * target + i, planes
                    )
            return 0

        lax.fori_loop(0, half // LANES, body, 0)


def combine(tiers, regions, tier, ops, zone, left, left_x, right, right_y):
    return pl.pallas_call(
        functools.partial(combine_kernel, tiers, regions),
        out_shape=(jax.ShapeDtypeStruct(left.shape, jnp.float32),) * 2,
        in_specs=[SMEM, SMEM] + [VMEM] * 5,
        out_specs=[VMEM, VMEM],
        compiler_params=pltpu.CompilerParams(vmem_limit_bytes=16 * MIB),
        name="combine",
    )(tier, ops, zone, left, left_x, right, right_y)


def solve_half(tiers, regions, me, ops, zone, R, half, base, raw, partial, put):
    def body(c, _):
        lanes = pl.ds(pl.multiple_of(c * LANES, LANES), LANES)
        whole = pl.ds(pl.multiple_of(base + c * LANES, LANES), LANES)
        for r in range(R // ROWS):
            rows = pl.ds(ROWS * r, ROWS)
            planes = [(2 * q + j, ref[k + j, rows, lanes]) for q, ref, k in raw for j in range(2)]
            for i in range(2):
                value = mixed(ops, tiers, regions, zone[rows, whole], 2 * me + i, planes)
                for ref in partial:
                    value = value + ref[i, rows, lanes]
                put(i, rows, whole, value)
        return 0

    lax.fori_loop(0, half // LANES, body, 0)


def sources(tiers, tier, refs, paired):
    if paired is not None:
        own, other, part = refs
        return [(tier[0], own, 0), (tier[paired], other, 0)], [part]
    (every,) = refs
    return [(q, every, 2 * q) for q in range(tiers)], []


def bond_kernel(tiers, regions, count, place, tier, ops, zone, aux, heat, h_ref, *refs):
    pairs = tiers == 4
    per = 3 if pairs else 1
    left, right, refs = refs[:per], refs[per : 2 * per], refs[2 * per :]
    edge_refs, refs = refs[: 4 if pairs else 1], refs[4 if pairs else 1 :]
    t_in, t_ref, out_left, out_right, rim = refs
    L, R, W = t_ref.shape
    half, C = W // 2, W // LANES
    me = tier[0]
    row = row_ids()

    def put(i, rows, lanes, value):
        t_ref[i * (L - 1), rows, lanes] = value

    for side, group in enumerate((left, right)):
        raw, partial = sources(tiers, tier, group, 1 + side if pairs else None)
        solve_half(tiers, regions, me, ops, zone, R, half, side * half, raw, partial, put)

    def edge_body(c, _):
        lanes = pl.ds(pl.multiple_of(c * LANES, LANES), LANES)
        if pairs:
            tiles = [(tier[q], ref[:, lanes]) for q, ref in enumerate(edge_refs)]
        else:
            tiles = [(q, edge_refs[0][q, :, lanes]) for q in range(tiers)]
        zones = aux[pl.ds(4, 4), lanes].astype(jnp.int32)
        zones = jnp.concatenate([zones, zones], axis=0)
        total = []
        for i in range(2):
            planes = []
            for q, value in tiles:
                swapped = pltpu.roll(value, 4, 0)
                planes += [(2 * q + i, value), (2 * q + 1 - i, swapped)]
            total.append(mixed(ops, tiers, regions, zones, 2 * me + i, planes))
        value = jnp.where(row < 4, total[0], total[1])
        gone = ((row % 4 == 0) & (place[0] == 0)) | ((row % 4 == 3) & (place[1] == 0))
        value = jnp.where(gone, 0.0, value)
        rim[:, lanes] = value
        for i in range(2):
            t_ref[i * (L - 1), pl.ds(0, 1), lanes] = value[4 * i + 1 : 4 * i + 2]
            t_ref[i * (L - 1), pl.ds(R - 1, 1), lanes] = value[4 * i + 2 : 4 * i + 3]
        return 0

    lax.fori_loop(0, C, edge_body, 0)

    for p in range(2):
        own, near = (0, 1) if p == 0 else (L - 1, L - 2)

        def get_s(r, c):
            return t_ref[(own,) + tile(r, c)]

        def get_h(r, c):
            return h_ref[(own,) + tile(r, c)]

        def get_z(r, c, s, h):
            at = (near,) + tile(r, c)
            flow = (h + h_ref[at]) * (t_ref[at] - s)
            return flow + heat[tile(r, c)] if p == 0 else flow

        def halo(c):
            lanes = pl.ds(LANES * c, LANES)
            return (
                rim[pl.ds(4 * p, 1), lanes],
                aux[pl.ds(p, 1), lanes],
                rim[pl.ds(4 * p + 3, 1), lanes],
                aux[pl.ds(2 + p, 1), lanes],
            )

        def put_out(r, c, value):
            if c < C // 2:
                out_left[(p,) + tile(r, c)] = value
            else:
                out_right[(p,) + tile(r, c - C // 2)] = value

        stencil(R, W, get_s, get_h, get_z, halo, put_out)


def bond(tiers, regions, place, tier, ops, zone, aux, heat, h, left, right, edges, t):
    L, R, W = t.shape
    args = (place, tier, ops, zone, aux, heat, h, *left, *right, *edges, t)
    f32 = jnp.float32
    return pl.pallas_call(
        functools.partial(bond_kernel, tiers, regions, len(left)),
        out_shape=(
            jax.ShapeDtypeStruct(t.shape, f32),
            jax.ShapeDtypeStruct((2, R, W // 2), f32),
            jax.ShapeDtypeStruct((2, R, W // 2), f32),
        ),
        in_specs=[SMEM] * 3 + [VMEM] * (len(args) - 3),
        out_specs=[VMEM] * 3,
        scratch_shapes=[pltpu.VMEM((ROWS, W), f32)],
        input_output_aliases={len(args) - 1: 0},
        compiler_params=pltpu.CompilerParams(vmem_limit_bytes=24 * MIB),
        name="bond",
    )(*args)


def final_kernel(tiers, regions, tier, ops, zone, *refs):
    per = 3 if tiers == 4 else 1
    left, right = refs[:per], refs[per : 2 * per]
    _, out, buf, sem = refs[2 * per :]
    L, R, W = out.shape
    half = W // 2
    copies = []
    for side, group in enumerate((left, right)):
        raw, partial = sources(tiers, tier, group, 1 + side if tiers == 4 else None)

        def put(i, rows, lanes, value):
            buf[i, rows, lanes] = value

        solve_half(tiers, regions, tier[0], ops, zone, R, half, side * half, raw, partial, put)
        lanes = pl.ds(side * half, half)
        for i in range(2):
            copies.append(
                pltpu.make_async_copy(
                    buf.at[i, :, lanes], out.at[i * (L - 1), :, lanes], sem.at[2 * side + i]
                )
            )
            copies[-1].start()
    for copy in copies:
        copy.wait()


def final_planes(tiers, regions, tier, ops, zone, left, right, out):
    args = (tier, ops, zone, *left, *right, out)
    _, R, W = out.shape
    return pl.pallas_call(
        functools.partial(final_kernel, tiers, regions),
        out_shape=jax.ShapeDtypeStruct(out.shape, jnp.float32),
        in_specs=[SMEM, SMEM] + [VMEM] * (len(args) - 3) + [ANY],
        out_specs=ANY,
        scratch_shapes=[pltpu.VMEM((2, R, W), jnp.float32), pltpu.SemaphoreType.DMA((4,))],
        input_output_aliases={len(args) - 1: 0},
        compiler_params=pltpu.CompilerParams(vmem_limit_bytes=16 * MIB),
        name="final_planes",
    )(*args)


def across(value, bits, tiers):
    return lax.ppermute(value, "tier", [(i, i ^ bits) for i in range(tiers)])


def every(value, tiers):
    gathered = lax.all_gather(value, "tier", axis=0, tiled=False)
    return gathered.reshape((tiers * value.shape[0],) + value.shape[1:]) if value.ndim == 3 else gathered


def exchange(tiers, regions, tier, ops, zone, left, right):
    if tiers != 4:
        return (every(left, tiers),), (every(right, tiers),)
    left_x, right_y = across(left, 1, tiers), across(right, 2, tiers)
    to_y, to_x = combine(tiers, regions, tier, ops, zone, left, left_x, right, right_y)
    return (left, left_x, across(to_y, 2, tiers)), (right, right_y, across(to_x, 1, tiers))


def local(warming, substance, zone, patch, kap, power, ops):
    tiers, tiles = lax.axis_size("tier"), lax.axis_size("tile")
    regions = ops.shape[0]
    ops = ops.reshape(-1)
    s, lab, patch = warming[0], substance[0], patch[0]
    me, at = lax.axis_index("tier"), lax.axis_index("tile")
    tier = jnp.stack([me, me ^ 1, me ^ 2, me ^ 3]).astype(jnp.int32)
    place = jnp.stack([at > 0, at < tiles - 1]).astype(jnp.int32)

    left, right, h, heat = first_planes(s, lab, patch, kap, power)
    up, down = pack(s, lab, patch, zone, kap, power)
    lo = lax.ppermute(down, "tile", [(i, (i + 1) % tiles) for i in range(tiles)])
    hi = lax.ppermute(up, "tile", [((i + 1) % tiles, i) for i in range(tiles)])
    left, right = exchange(tiers, regions, tier, ops, zone, left, right)
    edges, beyond, aux = edge_rows(place, up, down, lo, hi)
    if tiers == 4:
        edges = (edges, across(edges, 1, tiers), across(edges, 2, tiers), across(edges, 3, tiers))
    else:
        edges = (every(edges, tiers),)
    h, t = outer_layers(place, s, lab, kap, lo, hi, h)
    t, left, right = bond(tiers, regions, place, tier, ops, zone, aux, heat, h, left, right, edges, t)
    left, right = exchange(tiers, regions, tier, ops, zone, left, right)
    h, t = inner_layers(place, s, lab, kap, lo, hi, h, t)
    out = last_layers(place, t, h, lo, hi, beyond)
    out = final_planes(tiers, regions, tier, ops, zone, left, right, out)
    return out[None]


def solution(mesh):
    in_specs = (
        P("tier", None, "tile", None),
        P("tier", None, "tile", None),
        P("tile", None),
        P("tier", "tile", None),
        P(),
        P("tier", None),
        P(),
    )
    out_specs = P("tier", None, "tile", None)
    return jax.shard_map(local, mesh=mesh, in_specs=in_specs, out_specs=out_specs, check_vma=False)
```

time: 428 us -> 110 us (0.26)
  other arithmetic: 179 us -> 0.15 us
  matrix products: 82.8 us -> 0 us
  waiting for transfers between devices: 80.2 us -> 10.8 us
  Pallas kernels: 0 us -> 57.3 us
  local copies, waits for them, and re-layouts: 60.2 us -> 24.7 us
  between operations: 14.2 us -> 0.17 us
  starting transfers between devices: 7.34 us -> 16.3 us
    add x2 -> x0, other arithmetic: 88.6 us -> none  [local(): heating_snapshot = heating_snapshot + step_dt * conduct(padded_t, padded_k)]
    dot_general x17 -> x0, matrix products: 82.8 us -> none  [the longest x16 59.2 us: select_solve(): jnp.einsum('ij,jxc->ixc', matrices[which], planes, precision=lax.Precisio...]
    all_gather x2 -> x0, waiting for transfers between devices: 76.8 us -> none  [local(): gathered = lax.all_gather(planes, 'tier', axis=0, tiled=True)]
    pallas_call x0 -> x10, Pallas kernels: none -> 57.3 us  [the longest x1 10.6 us: last_layers(): pl.pallas_call(last_kernel, out_shape=jax.ShapeDtypeStruct(t.shape, jnp.f...]
    another operation x9 -> x1, other arithmetic: 48.2 us -> 0.08 us  [local(): tier = jnp.stack([me, me ^ 1, me ^ 2, me ^ 3]).astype(jnp.int32)]
    slice x5 -> x0, local copies, waits for them, and re-layouts: 28.1 us -> none  [the longest x2 15.8 us: conduct(): centre = padded_t[..., 1:-1, :]]
    mul x3 -> x0, other arithmetic: 22.9 us -> none  [the longest x2 22.8 us: conduct(): 0.5 * (kcell[..., 1:, :, :] + kcell[..., :-1, :, :])]
    unnamed x42, local copies, waits for them, and re-layouts: 4.11 us -> 24.6 us
  transfers between devices with their start and end apart: 6 -> 13, of which waited for: 3 -> 4; matrix products, arithmetic and copies ran while one was open for 6% -> 0% of each run, Pallas kernels for 0% -> 29%
where the time goes in v1:
time: 110 us; the launch traced here: 109 us
  Pallas kernels  57.3 us (52%)
  local copies, waits for them, and re-layouts  24.7 us (22%)
  starting transfers between devices  16.3 us (15%)
  waiting for transfers between devices  10.8 us (10%)
    unnamed x42, local copies, waits for them, and re-layouts  24.6 us
    ppermute x11, starting transfers between devices, across(): return lax.ppermute(value, 'tier', [(i, i ^ bits) for i in range(tiers)])  11.8 us
    ppermute x11, waiting for transfers between devices, across(): return lax.ppermute(value, 'tier', [(i, i ^ bits) for i in range(tiers)])  10.8 us
    pallas_call x1, Pallas kernels, last_layers(): pl.pallas_call(last_kernel, out_shape=jax.ShapeDtypeStruct(t.shape, jnp.f...  10.6 us
    pallas_call x2, Pallas kernels, combine(): pl.pallas_call(functools.partial(combine_kernel, tiers, regions), out_sha...  9.37 us
    pallas_call x1, Pallas kernels, bond(): pl.pallas_call(functools.partial(bond_kernel, tiers, regions, len(left)),...  9.31 us
    pallas_call x1, Pallas kernels, inner_layers(): pl.pallas_call(inner_kernel, out_shape=(jax.ShapeDtypeStruct(s.shape, jnp...  9.17 us
    pallas_call x1, Pallas kernels, pack(): pl.pallas_call(pack_kernel, grid=(1,), out_shape=(jax.ShapeDtypeStruct((r...  6.85 us
  transfers between devices with their start and end apart: 13, of which 4 were waited for; matrix products, arithmetic and copies ran while one was open for 0% of the time, Pallas kernels for 29%

profile of v1, /device:TPU:0, one launch (start us, length us, event | category | flops | bytes accessed | tf_op | source)
XLA Modules:
  0.0 109.4 jit_solution(13685590919732558114)
XLA Ops:
  0.0 2.2 %copy-done = f32[1,16,32,2048]{3,2,1,0:T(8,128)S(1)} copy-done((f32[1,16,32,2048]{3,2,1,0:T(8,128)S(1)}, f32[1,16,32,2048]{3,2,1,0:T(8,128)}, u32[]{:S(2)}) %copy-start) | copy-done | bytes 4194328
  2.2 2.2 %copy-done.4 = s32[1,16,32,2048]{3,2,1,0:T(8,128)S(1)} copy-done((s32[1,16,32,2048]{3,2,1,0:T(8,128)S(1)}, s32[1,16,32,2048]{3,2,1,0:T(8,128)}, u32[]{:S(2)}) %copy-start.4) | copy-done | bytes 4194328
  4.4 0.9 copy-done.14
  5.3 0.9 copy-done.16
  6.3 0.7 copy-done.17
  6.9 0.7 copy-done.19
  7.6 6.8 %pack.1 = (f32[72,2048]{1,0:T(8,128)S(1)}, f32[72,2048]{1,0:T(8,128)}) custom-call(f32[16,32,2048]{2,1,0:T(8,128)S(1)} %bitcast.10, f32[16,32,2048]{2,1,0:T(8,128)S(1)} %bitcast.11, s32[16,32,2048]{2,1,0:T(8,128)S(1)} %bitcast.15, s32[16,32,2048]{2,1,0:T(8,128)S(1)} %bitcast.16, s32[32,2048]{1,0:T(8,128)S(1)} %bitcast.20, s32[32,2048]{1,0:T(8,128)S(1)} %bitcast.21, ...), custom_call_target="tpu_custom_call" | custom-call | tf_op jit(solution)/shard_map/pack/pallas_call | solution.py:212
  14.4 4.5 %collective-permute-start.1 = (f32[72,2048]{1,0:T(8,128)S(1)}, f32[72,2048]{1,0:T(8,128)S(1)}, u32[]{:S(2)}, u32[]{:S(2)}) collective-permute-start(f32[72,2048]{1,0:T(8,128)S(1)} %get-tuple-element.25.own_up), channel_id=1, source_target_pairs={{1,0},{2,1},{3,2},{4,3},{5,4},{6,5},{7,6},{0,7},{9,8},{10,9},{11,1... | collective-permute-start | bytes 1769480 | tf_op jit(solution)/shard_map/ppermute | solution.py:667
  18.9 0.0 collective-permute-start
  18.9 0.0 copy-done.1
  19.0 0.0 copy-done.5
  19.0 2.6 %first_planes.1 = (f32[2,32,1024]{2,1,0:T(8,128)S(1)}, f32[2,32,1024]{2,1,0:T(8,128)S(1)}, f32[16,32,2048]{2,1,0:T(8,128)S(1)}, f32[32,2048]{1,0:T(8,128)S(1)}) custom-call(f32[16,32,2048]{2,1,0:T(8,128)S(1)} %bitcast.12, s32[16,32,2048]{2,1,0:T(8,128)S(1)} %bitcast.17, s32[32,2048]{1,0:T(8,128)S(1)} %bitcast.22, f32[16]{0:T(128)S(1)} %copy-done.17, ...), custom_call_target="tpu_custom_call" | custom-call | tf_op jit(solution)/shard_map/first_planes/pallas_call | solution.py:162
  21.5 0.0 copy-start.8
  21.5 2.0 %copy-done.8 = f32[16,32,2048]{2,1,0:T(8,128)} copy-done((f32[16,32,2048]{2,1,0:T(8,128)}, f32[16,32,2048]{2,1,0:T(8,128)S(1)}, u32[]{:S(2)}) %copy-start.8) | copy-done | bytes 4194328
  23.5 1.5 %collective-permute-start.2 = (f32[2,32,1024]{2,1,0:T(8,128)S(1)}, f32[2,32,1024]{2,1,0:T(8,128)S(1)}, u32[]{:S(2)}, u32[]{:S(2)}) collective-permute-start(f32[2,32,1024]{2,1,0:T(8,128)S(1)} %get-tuple-element.31.left.refs_0_), channel_id=1, source_target_pairs={{0,8},{8,0},{16,24},{24,16},{1,9},{9,1},{17,25},{25,17},{2,10},{10... | collective-permute-start | bytes 786440 | tf_op jit(solution)/shard_map/ppermute | solution.py:639
  25.0 1.5 %collective-permute-start.3 = (f32[2,32,1024]{2,1,0:T(8,128)S(1)}, f32[2,32,1024]{2,1,0:T(8,128)S(1)}, u32[]{:S(2)}, u32[]{:S(2)}) collective-permute-start(f32[2,32,1024]{2,1,0:T(8,128)S(1)} %get-tuple-element.32.right.refs_3_), channel_id=1, source_target_pairs={{0,16},{8,24},{16,0},{24,8},{1,17},{9,25},{17,1},{25,9},{2,18},{10... | collective-permute-start | bytes 786440 | tf_op jit(solution)/shard_map/ppermute | solution.py:639
  26.6 0.0 copy-done.20
  26.6 0.1 reshape.3.ops
  26.6 0.1 pad_add_fusion.tier
  26.7 3.7 %collective-permute-done.2.left_x.refs_1_ = f32[2,32,1024]{2,1,0:T(8,128)S(1)} collective-permute-done((f32[2,32,1024]{2,1,0:T(8,128)S(1)}, f32[2,32,1024]{2,1,0:T(8,128)S(1)}, u32[]{:S(2)}, u32[]{:S(2)}) %collective-permute-start.2) | collective-permute-done | bytes 262176 | tf_op jit(solution)/shard_map/ppermute | solution.py:639
  30.4 1.2 %collective-permute-done.3.right_y.refs_4_ = f32[2,32,1024]{2,1,0:T(8,128)S(1)} collective-permute-done((f32[2,32,1024]{2,1,0:T(8,128)S(1)}, f32[2,32,1024]{2,1,0:T(8,128)S(1)}, u32[]{:S(2)}, u32[]{:S(2)}) %collective-permute-start.3) | collective-permute-done | bytes 262176 | tf_op jit(solution)/shard_map/ppermute | solution.py:639
  31.7 0.0 copy-done.15
  31.7 5.1 %combine.2 = (f32[2,32,1024]{2,1,0:T(8,128)}, f32[2,32,1024]{2,1,0:T(8,128)}) custom-call(s32[4]{0:T(128)S(1)} %pad_add_fusion.tier, f32[512]{0:T(512)S(1)} %reshape.3.ops, s32[32,2048]{1,0:T(8,128)S(1)} %copy-done.15, f32[2,32,1024]{2,1,0:T(8,128)S(1)} %get-tuple-element.31.left.refs_0_, f32[2,32,1024]{2,1,0:T(8,128)S(1)} %collective-permute-done.2.left_x.refs_1_, ...), custom_call_target="tpu_custom_call" | custom-call | tf_op jit(solution)/shard_map/combine/pallas_call | solution.py:466
  36.8 1.5 %collective-permute-start.4 = (f32[2,32,1024]{2,1,0:T(8,128)}, f32[2,32,1024]{2,1,0:T(8,128)}, u32[]{:S(2)}, u32[]{:S(2)}) collective-permute-start(f32[2,32,1024]{2,1,0:T(8,128)} %get-tuple-element.33), channel_id=1, source_target_pairs={{0,16},{8,24},{16,0},{24,8},{1,17},{9,25},{17,1},{25,9},{2,18},{10... | collective-permute-start | bytes 786440 | tf_op jit(solution)/shard_map/ppermute | solution.py:639
  38.3 0.5 collective-permute-start.5
  38.8 0.1 add_convert_fusion.place
  38.9 0.0 collective-permute-done.1.hi
  38.9 0.0 collective-permute-done.lo
  38.9 1.9 %edge_rows.1 = (f32[8,2048]{1,0:T(8,128)S(1)}, f32[2,16,2048]{2,1,0:T(8,128)S(1)}, f32[8,2048]{1,0:T(8,128)S(1)}) custom-call(s32[2]{0:T(128)S(1)} %add_convert_fusion.place, f32[72,2048]{1,0:T(8,128)S(1)} %get-tuple-element.25.own_up, f32[72,2048]{1,0:T(8,128)} %get-tuple-element.26.own_down, f32[72,2048]{1,0:T(8,128)S(1)} %collective-permute-done.lo, ...), custom_call_target="tpu_custom_call" | custom-call | tf_op jit(solution)/shard_map/edge_rows/pallas_call | solution.py:276
  40.8 1.5 %collective-permute-start.8 = (f32[8,2048]{1,0:T(8,128)S(1)}, f32[8,2048]{1,0:T(8,128)S(1)}, u32[]{:S(2)}, u32[]{:S(2)}) collective-permute-start(f32[8,2048]{1,0:T(8,128)S(1)} %get-tuple-element.35.refs_6_), channel_id=1, source_target_pairs={{0,24},{8,16},{16,8},{24,0},{1,25},{9,17},{17,9},{25,1},{2,26},{10... | collective-permute-start | bytes 196616 | tf_op jit(solution)/shard_map/ppermute | solution.py:639
  42.3 1.5 %collective-permute-start.7 = (f32[8,2048]{1,0:T(8,128)S(1)}, f32[8,2048]{1,0:T(8,128)S(1)}, u32[]{:S(2)}, u32[]{:S(2)}) collective-permute-start(f32[8,2048]{1,0:T(8,128)S(1)} %get-tuple-element.35.refs_6_), channel_id=1, source_target_pairs={{0,16},{8,24},{16,0},{24,8},{1,17},{9,25},{17,1},{25,9},{2,18},{10... | collective-permute-start | bytes 196616 | tf_op jit(solution)/shard_map/ppermute | solution.py:639
  43.8 0.5 collective-permute-start.6
  44.4 0.0 copy-done.18
  44.4 2.2 %copy-done.2 = f32[1,16,32,2048]{3,2,1,0:T(8,128)S(1)} copy-done((f32[1,16,32,2048]{3,2,1,0:T(8,128)S(1)}, f32[1,16,32,2048]{3,2,1,0:T(8,128)}, u32[]{:S(2)}) %copy-start.2) | copy-done | bytes 4194328
  46.6 2.2 %copy-done.6 = s32[1,16,32,2048]{3,2,1,0:T(8,128)S(1)} copy-done((s32[1,16,32,2048]{3,2,1,0:T(8,128)S(1)}, s32[1,16,32,2048]{3,2,1,0:T(8,128)}, u32[]{:S(2)}) %copy-start.6) | copy-done | bytes 4194328
  48.8 2.2 %copy-done.9 = f32[16,32,2048]{2,1,0:T(8,128)S(1)} copy-done((f32[16,32,2048]{2,1,0:T(8,128)S(1)}, f32[16,32,2048]{2,1,0:T(8,128)}, u32[]{:S(2)}) %copy-start.9) | copy-done | bytes 4194328
  50.9 2.5 %outer_layers.1 = (f32[16,32,2048]{2,1,0:T(8,128)S(1)}, f32[16,32,2048]{2,1,0:T(8,128)S(1)}) custom-call(s32[2]{0:T(128)S(1)} %add_convert_fusion.place, f32[16,32,2048]{2,1,0:T(8,128)S(1)} %bitcast.13, s32[16,32,2048]{2,1,0:T(8,128)S(1)} %bitcast.18, f32[16]{0:T(128)S(1)} %copy-done.18, ...), custom_call_target="tpu_custom_call", output_to_operand_aliasing={{0}: (6, {})} | custom-call | tf_op jit(solution)/shard_map/outer_layers/pallas_call | solution.py:343
  53.5 0.0 copy-start.10
  53.5 2.0 %copy-done.10 = f32[16,32,2048]{2,1,0:T(8,128)} copy-done((f32[16,32,2048]{2,1,0:T(8,128)}, f32[16,32,2048]{2,1,0:T(8,128)S(1)}, u32[]{:S(2)}) %copy-start.10) | copy-done | bytes 4194328
  55.5 0.0 collective-permute-done.4.refs_2_
  55.5 0.0 collective-permute-done.5.refs_5_
  55.5 0.0 collective-permute-done.8.refs_9_
  55.5 0.0 collective-permute-done.7.refs_8_
  55.5 0.0 collective-permute-done.6.refs_7_
  55.5 0.0 copy-start.11
  55.5 2.2 %copy-done.11 = f32[16,32,2048]{2,1,0:T(8,128)S(1)} copy-done((f32[16,32,2048]{2,1,0:T(8,128)S(1)}, f32[16,32,2048]{2,1,0:T(8,128)}, u32[]{:S(2)}) %copy-start.11) | copy-done | bytes 4194328
  57.7 9.3 %bond.1 = (f32[16,32,2048]{2,1,0:T(8,128)S(1)}, f32[2,32,1024]{2,1,0:T(8,128)S(1)}, f32[2,32,1024]{2,1,0:T(8,128)S(1)}) custom-call(s32[2]{0:T(128)S(1)} %add_convert_fusion.place, s32[4]{0:T(128)S(1)} %pad_add_fusion.tier, f32[512]{0:T(512)S(1)} %reshape.3.ops, s32[32,2048]{1,0:T(8,128)S(1)} %copy-done.15, ...), custom_call_target="tpu_custom_call", output_to_operand_aliasing={{0}: (17, {})} | custom-call | tf_op jit(solution)/shard_map/bond/pallas_call | solution.py:581
  67.0 1.6 %collective-permute-start.9 = (f32[2,32,1024]{2,1,0:T(8,128)S(1)}, f32[2,32,1024]{2,1,0:T(8,128)S(1)}, u32[]{:S(2)}, u32[]{:S(2)}) collective-permute-start(f32[2,32,1024]{2,1,0:T(8,128)S(1)} %get-tuple-element.37.left.refs_0_), channel_id=1, source_target_pairs={{0,8},{8,0},{16,24},{24,16},{1,9},{9,1},{17,25},{25,17},{2,10},{10... | collective-permute-start | bytes 786440 | tf_op jit(solution)/shard_map/ppermute | solution.py:639
  68.6 0.5 collective-permute-start.10
  69.1 4.4 %collective-permute-done.9.left_x.refs_1_ = f32[2,32,1024]{2,1,0:T(8,128)S(1)} collective-permute-done((f32[2,32,1024]{2,1,0:T(8,128)S(1)}, f32[2,32,1024]{2,1,0:T(8,128)S(1)}, u32[]{:S(2)}, u32[]{:S(2)}) %collective-permute-start.9) | collective-permute-done | bytes 262176 | tf_op jit(solution)/shard_map/ppermute | solution.py:639
  73.5 1.5 %collective-permute-done.10.right_y.refs_4_ = f32[2,32,1024]{2,1,0:T(8,128)S(1)} collective-permute-done((f32[2,32,1024]{2,1,0:T(8,128)S(1)}, f32[2,32,1024]{2,1,0:T(8,128)S(1)}, u32[]{:S(2)}, u32[]{:S(2)}) %collective-permute-start.10) | collective-permute-done | bytes 262176 | tf_op jit(solution)/shard_map/ppermute | solution.py:639
  75.0 4.3 %combine.3 = (f32[2,32,1024]{2,1,0:T(8,128)S(1)}, f32[2,32,1024]{2,1,0:T(8,128)S(1)}) custom-call(s32[4]{0:T(128)S(1)} %pad_add_fusion.tier, f32[512]{0:T(512)S(1)} %reshape.3.ops, s32[32,2048]{1,0:T(8,128)S(1)} %copy-done.15, f32[2,32,1024]{2,1,0:T(8,128)S(1)} %get-tuple-element.37.left.refs_0_, f32[2,32,1024]{2,1,0:T(8,128)S(1)} %collective-permute-done.9.left_x.refs_1_, ...), custom_call_target="tpu_custom_call" | custom-call | tf_op jit(solution)/shard_map/combine/pallas_call | solution.py:466
  79.2 0.6 collective-permute-start.11
  79.8 0.5 collective-permute-start.12
  80.3 0.0 copy-done.3
  80.3 0.0 copy-done.7
  80.3 9.2 %inner_layers.1 = (f32[16,32,2048]{2,1,0:T(8,128)S(1)}, f32[16,32,2048]{2,1,0:T(8,128)S(1)}) custom-call(s32[2]{0:T(128)S(1)} %add_convert_fusion.place, f32[16,32,2048]{2,1,0:T(8,128)S(1)} %bitcast.14, s32[16,32,2048]{2,1,0:T(8,128)S(1)} %bitcast.19, f32[16]{0:T(128)S(1)} %copy-done.18, ...), custom_call_target="tpu_custom_call", output_to_operand_aliasing={{0}: (6, {}), {1}: (7, {})} | custom-call | tf_op jit(solution)/shard_map/inner_layers/pallas_call | solution.py:365
  89.5 0.0 copy-start.12
  89.5 2.0 %copy-done.12 = f32[16,32,2048]{2,1,0:T(8,128)} copy-done((f32[16,32,2048]{2,1,0:T(8,128)}, f32[16,32,2048]{2,1,0:T(8,128)S(1)}, u32[]{:S(2)}) %copy-start.12) | copy-done | bytes 4194328
  91.5 2.2 %copy-done.13 = f32[16,32,2048]{2,1,0:T(8,128)S(1)} copy-done((f32[16,32,2048]{2,1,0:T(8,128)S(1)}, f32[16,32,2048]{2,1,0:T(8,128)}, u32[]{:S(2)}) %copy-start.13) | copy-done | bytes 4194328
  93.7 10.6 %last_layers.1.refs_6_ = f32[16,32,2048]{2,1,0:T(8,128)} custom-call(s32[2]{0:T(128)S(1)} %add_convert_fusion.place, f32[16,32,2048]{2,1,0:T(8,128)S(1)} %get-tuple-element.42.t_ref, f32[16,32,2048]{2,1,0:T(8,128)S(1)} %copy-done.13, f32[72,2048]{1,0:T(8,128)S(1)} %collective-permute-done.lo, f32[72,2048]{1,0:T(8,128)S(1)} %collective-permute-done.1.hi, ...), custom_call_target="tpu_custom_call" | custom-call | tf_op jit(solution)/shard_map/last_layers/pallas_call | solution.py:417
  104.3 0.0 collective-permute-done.11.refs_2_
  104.3 0.0 collective-permute-done.12.refs_5_
  104.3 5.1 %final_planes.1 = f32[16,32,2048]{2,1,0:T(8,128)} custom-call(s32[4]{0:T(128)S(1)} %pad_add_fusion.tier, f32[512]{0:T(512)S(1)} %reshape.3.ops, s32[32,2048]{1,0:T(8,128)S(1)} %copy-done.15, f32[2,32,1024]{2,1,0:T(8,128)S(1)} %get-tuple-element.37.left.refs_0_, ...), custom_call_target="tpu_custom_call", output_to_operand_aliasing={{}: (9, {})} | custom-call | tf_op jit(solution)/shard_map/final_planes/pallas_call | solution.py:626
  (17 shorter events, 0.0 us)
Async XLA Ops:
  0.0 2.2 %copy-start = (f32[1,16,32,2048]{3,2,1,0:T(8,128)S(1)}, f32[1,16,32,2048]{3,2,1,0:T(8,128)}, u32[]{:S(2)}) copy-start(f32[1,16,32,2048]{3,2,1,0:T(8,128)} %param.7) | copy-start | bytes 12582916
  2.2 2.2 %copy-start.4 = (s32[1,16,32,2048]{3,2,1,0:T(8,128)S(1)}, s32[1,16,32,2048]{3,2,1,0:T(8,128)}, u32[]{:S(2)}) copy-start(s32[1,16,32,2048]{3,2,1,0:T(8,128)} %param.8) | copy-start | bytes 12582916
  4.4 0.9 copy-start.14
  5.3 0.9 copy-start.16
  6.3 0.7 copy-start.17
  6.9 0.7 copy-start.19
  7.6 11.4 %copy-start.1 = (f32[1,16,32,2048]{3,2,1,0:T(8,128)S(1)}, f32[1,16,32,2048]{3,2,1,0:T(8,128)}, u32[]{:S(2)}) copy-start(f32[1,16,32,2048]{3,2,1,0:T(8,128)} %param.7) | copy-start | bytes 12582916
  7.6 11.4 %copy-start.5 = (s32[1,16,32,2048]{3,2,1,0:T(8,128)S(1)}, s32[1,16,32,2048]{3,2,1,0:T(8,128)}, u32[]{:S(2)}) copy-start(s32[1,16,32,2048]{3,2,1,0:T(8,128)} %param.8) | copy-start | bytes 12582916
  14.4 24.4 %collective-permute-start.1 = (f32[72,2048]{1,0:T(8,128)S(1)}, f32[72,2048]{1,0:T(8,128)S(1)}, u32[]{:S(2)}, u32[]{:S(2)}) collective-permute-start(f32[72,2048]{1,0:T(8,128)S(1)} %get-tuple-element.25.own_up), channel_id=1, source_target_pairs={{1,0},{2,1},{3,2},{4,3},{5,4},{6,5},{7,6},{0,7},{9,8},{10,9},{11,1... | collective-permute-start | bytes 1769480 | tf_op jit(solution)/shard_map/ppermute | solution.py:667
  18.9 7.6 %copy-start.20 = (f32[8,8,8]{2,1,0:T(8,128)S(1)}, f32[8,8,8]{2,1,0:T(8,128)}, u32[]{:S(2)}) copy-start(f32[8,8,8]{2,1,0:T(8,128)} %param.13) | copy-start | bytes 6148
  18.9 12.7 %copy-start.15 = (s32[32,2048]{1,0:T(8,128)S(1)}, s32[32,2048]{1,0:T(8,128)}, u32[]{:S(2)}) copy-start(s32[32,2048]{1,0:T(8,128)} %zone.7) | copy-start | bytes 786436
  18.9 25.4 %copy-start.18 = (f32[16]{0:T(128)S(1)}, f32[16]{0:T(128)}, u32[]{:S(2)}) copy-start(f32[16]{0:T(128)} %kap.7) | copy-start | bytes 196
  18.9 20.0 %collective-permute-start = (f32[72,2048]{1,0:T(8,128)}, f32[72,2048]{1,0:T(8,128)S(1)}, u32[]{:S(2)}, u32[]{:S(2)}) collective-permute-start(f32[72,2048]{1,0:T(8,128)} %get-tuple-element.26.own_down), channel_id=1, source_target_pairs={{0,1},{1,2},{2,3},{3,4},{4,5},{5,6},{6,7},{7,0},{8,9},{9,10},{10,1... | collective-permute-start | bytes 1769480 | tf_op jit(solution)/shard_map/ppermute | solution.py:666
  21.5 2.0 %copy-start.8 = (f32[16,32,2048]{2,1,0:T(8,128)}, f32[16,32,2048]{2,1,0:T(8,128)S(1)}, u32[]{:S(2)}) copy-start(f32[16,32,2048]{2,1,0:T(8,128)S(1)} %get-tuple-element.29.h_in) | copy-start | bytes 12582916
  23.5 6.9 %collective-permute-start.2 = (f32[2,32,1024]{2,1,0:T(8,128)S(1)}, f32[2,32,1024]{2,1,0:T(8,128)S(1)}, u32[]{:S(2)}, u32[]{:S(2)}) collective-permute-start(f32[2,32,1024]{2,1,0:T(8,128)S(1)} %get-tuple-element.31.left.refs_0_), channel_id=1, source_target_pairs={{0,8},{8,0},{16,24},{24,16},{1,9},{9,1},{17,25},{25,17},{2,10},{10... | collective-permute-start | bytes 786440 | tf_op jit(solution)/shard_map/ppermute | solution.py:639
  25.0 6.6 %collective-permute-start.3 = (f32[2,32,1024]{2,1,0:T(8,128)S(1)}, f32[2,32,1024]{2,1,0:T(8,128)S(1)}, u32[]{:S(2)}, u32[]{:S(2)}) collective-permute-start(f32[2,32,1024]{2,1,0:T(8,128)S(1)} %get-tuple-element.32.right.refs_3_), channel_id=1, source_target_pairs={{0,16},{8,24},{16,0},{24,8},{1,17},{9,25},{17,1},{25,9},{2,18},{10... | collective-permute-start | bytes 786440 | tf_op jit(solution)/shard_map/ppermute | solution.py:639
  36.8 18.7 %collective-permute-start.4 = (f32[2,32,1024]{2,1,0:T(8,128)}, f32[2,32,1024]{2,1,0:T(8,128)}, u32[]{:S(2)}, u32[]{:S(2)}) collective-permute-start(f32[2,32,1024]{2,1,0:T(8,128)} %get-tuple-element.33), channel_id=1, source_target_pairs={{0,16},{8,24},{16,0},{24,8},{1,17},{9,25},{17,1},{25,9},{2,18},{10... | collective-permute-start | bytes 786440 | tf_op jit(solution)/shard_map/ppermute | solution.py:639
  38.3 17.2 %collective-permute-start.5 = (f32[2,32,1024]{2,1,0:T(8,128)}, f32[2,32,1024]{2,1,0:T(8,128)}, u32[]{:S(2)}, u32[]{:S(2)}) collective-permute-start(f32[2,32,1024]{2,1,0:T(8,128)} %get-tuple-element.34), channel_id=1, source_target_pairs={{0,8},{8,0},{16,24},{24,16},{1,9},{9,1},{17,25},{25,17},{2,10},{10... | collective-permute-start | bytes 786440 | tf_op jit(solution)/shard_map/ppermute | solution.py:639
  40.8 14.7 %collective-permute-start.8 = (f32[8,2048]{1,0:T(8,128)S(1)}, f32[8,2048]{1,0:T(8,128)S(1)}, u32[]{:S(2)}, u32[]{:S(2)}) collective-permute-start(f32[8,2048]{1,0:T(8,128)S(1)} %get-tuple-element.35.refs_6_), channel_id=1, source_target_pairs={{0,24},{8,16},{16,8},{24,0},{1,25},{9,17},{17,9},{25,1},{2,26},{10... | collective-permute-start | bytes 196616 | tf_op jit(solution)/shard_map/ppermute | solution.py:639
  42.3 13.2 %collective-permute-start.7 = (f32[8,2048]{1,0:T(8,128)S(1)}, f32[8,2048]{1,0:T(8,128)S(1)}, u32[]{:S(2)}, u32[]{:S(2)}) collective-permute-start(f32[8,2048]{1,0:T(8,128)S(1)} %get-tuple-element.35.refs_6_), channel_id=1, source_target_pairs={{0,16},{8,24},{16,0},{24,8},{1,17},{9,25},{17,1},{25,9},{2,18},{10... | collective-permute-start | bytes 196616 | tf_op jit(solution)/shard_map/ppermute | solution.py:639
  43.8 11.7 %collective-permute-start.6 = (f32[8,2048]{1,0:T(8,128)S(1)}, f32[8,2048]{1,0:T(8,128)S(1)}, u32[]{:S(2)}, u32[]{:S(2)}) collective-permute-start(f32[8,2048]{1,0:T(8,128)S(1)} %get-tuple-element.35.refs_6_), channel_id=1, source_target_pairs={{0,8},{8,0},{16,24},{24,16},{1,9},{9,1},{17,25},{25,17},{2,10},{10... | collective-permute-start | bytes 196616 | tf_op jit(solution)/shard_map/ppermute | solution.py:639
  44.4 2.2 %copy-start.2 = (f32[1,16,32,2048]{3,2,1,0:T(8,128)S(1)}, f32[1,16,32,2048]{3,2,1,0:T(8,128)}, u32[]{:S(2)}) copy-start(f32[1,16,32,2048]{3,2,1,0:T(8,128)} %param.7) | copy-start | bytes 12582916
  46.6 2.2 %copy-start.6 = (s32[1,16,32,2048]{3,2,1,0:T(8,128)S(1)}, s32[1,16,32,2048]{3,2,1,0:T(8,128)}, u32[]{:S(2)}) copy-start(s32[1,16,32,2048]{3,2,1,0:T(8,128)} %param.8) | copy-start | bytes 12582916
  48.8 2.2 %copy-start.9 = (f32[16,32,2048]{2,1,0:T(8,128)S(1)}, f32[16,32,2048]{2,1,0:T(8,128)}, u32[]{:S(2)}) copy-start(f32[16,32,2048]{2,1,0:T(8,128)} %copy-done.8) | copy-start | bytes 12582916
  53.5 2.0 %copy-start.10 = (f32[16,32,2048]{2,1,0:T(8,128)}, f32[16,32,2048]{2,1,0:T(8,128)S(1)}, u32[]{:S(2)}) copy-start(f32[16,32,2048]{2,1,0:T(8,128)S(1)} %get-tuple-element.30.h_ref.h_in) | copy-start | bytes 12582916
  55.5 2.2 %copy-start.11 = (f32[16,32,2048]{2,1,0:T(8,128)S(1)}, f32[16,32,2048]{2,1,0:T(8,128)}, u32[]{:S(2)}) copy-start(f32[16,32,2048]{2,1,0:T(8,128)} %copy-done.10) | copy-start | bytes 12582916
  57.7 22.6 %copy-start.3 = (f32[1,16,32,2048]{3,2,1,0:T(8,128)S(1)}, f32[1,16,32,2048]{3,2,1,0:T(8,128)}, u32[]{:S(2)}) copy-start(f32[1,16,32,2048]{3,2,1,0:T(8,128)} %param.7) | copy-start | bytes 12582916
  57.7 22.6 %copy-start.7 = (s32[1,16,32,2048]{3,2,1,0:T(8,128)S(1)}, s32[1,16,32,2048]{3,2,1,0:T(8,128)}, u32[]{:S(2)}) copy-start(s32[1,16,32,2048]{3,2,1,0:T(8,128)} %param.8) | copy-start | bytes 12582916
  67.0 6.4 %collective-permute-start.9 = (f32[2,32,1024]{2,1,0:T(8,128)S(1)}, f32[2,32,1024]{2,1,0:T(8,128)S(1)}, u32[]{:S(2)}, u32[]{:S(2)}) collective-permute-start(f32[2,32,1024]{2,1,0:T(8,128)S(1)} %get-tuple-element.37.left.refs_0_), channel_id=1, source_target_pairs={{0,8},{8,0},{16,24},{24,16},{1,9},{9,1},{17,25},{25,17},{2,10},{10... | collective-permute-start | bytes 786440 | tf_op jit(solution)/shard_map/ppermute | solution.py:639
  68.6 6.4 %collective-permute-start.10 = (f32[2,32,1024]{2,1,0:T(8,128)S(1)}, f32[2,32,1024]{2,1,0:T(8,128)S(1)}, u32[]{:S(2)}, u32[]{:S(2)}) collective-permute-start(f32[2,32,1024]{2,1,0:T(8,128)S(1)} %get-tuple-element.38.right.refs_3_), channel_id=1, source_target_pairs={{0,16},{8,24},{16,0},{24,8},{1,17},{9,25},{17,1},{25,9},{2,18},{10... | collective-permute-start | bytes 786440 | tf_op jit(solution)/shard_map/ppermute | solution.py:639
  79.2 25.1 %collective-permute-start.11 = (f32[2,32,1024]{2,1,0:T(8,128)S(1)}, f32[2,32,1024]{2,1,0:T(8,128)S(1)}, u32[]{:S(2)}, u32[]{:S(2)}) collective-permute-start(f32[2,32,1024]{2,1,0:T(8,128)S(1)} %get-tuple-element.39), channel_id=1, source_target_pairs={{0,16},{8,24},{16,0},{24,8},{1,17},{9,25},{17,1},{25,9},{2,18},{10... | collective-permute-start | bytes 786440 | tf_op jit(solution)/shard_map/ppermute | solution.py:639
  79.8 24.5 %collective-permute-start.12 = (f32[2,32,1024]{2,1,0:T(8,128)S(1)}, f32[2,32,1024]{2,1,0:T(8,128)S(1)}, u32[]{:S(2)}, u32[]{:S(2)}) collective-permute-start(f32[2,32,1024]{2,1,0:T(8,128)S(1)} %get-tuple-element.40), channel_id=1, source_target_pairs={{0,8},{8,0},{16,24},{24,16},{1,9},{9,1},{17,25},{25,17},{2,10},{10... | collective-permute-start | bytes 786440 | tf_op jit(solution)/shard_map/ppermute | solution.py:639
  89.5 2.0 %copy-start.12 = (f32[16,32,2048]{2,1,0:T(8,128)}, f32[16,32,2048]{2,1,0:T(8,128)S(1)}, u32[]{:S(2)}) copy-start(f32[16,32,2048]{2,1,0:T(8,128)S(1)} %get-tuple-element.43.h_ref) | copy-start | bytes 12582916
  91.5 2.2 %copy-start.13 = (f32[16,32,2048]{2,1,0:T(8,128)S(1)}, f32[16,32,2048]{2,1,0:T(8,128)}, u32[]{:S(2)}) copy-start(f32[16,32,2048]{2,1,0:T(8,128)} %copy-done.12) | copy-start | bytes 12582916

commit v2 on v1

v2 whole, which is shorter than its diff:
```python
import functools
import math

import jax
import jax.numpy as jnp
from jax import lax
from jax.experimental import pallas as pl
from jax.experimental.pallas import tpu as pltpu
from jax.sharding import PartitionSpec as P

STEPS = 2
step_dt = 0.04
half_dt = 0.5 * step_dt
LANES = 128
ROWS = 8
MIB = 1 << 20

VMEM = pl.BlockSpec(memory_space=pltpu.VMEM)
SMEM = pl.BlockSpec(memory_space=pltpu.SMEM)
ANY = pl.BlockSpec(memory_space=pl.ANY)
HBM = pl.BlockSpec(memory_space=pltpu.HBM)


def tile(r, c):
    return pl.ds(ROWS * r, ROWS), pl.ds(LANES * c, LANES)


def lasts(us):
    return pl.CostEstimate(flops=0, bytes_accessed=int(us * 3.3e6), transcendentals=0)


def lane_ids():
    return lax.broadcasted_iota(jnp.int32, (ROWS, LANES), 1)


def row_ids():
    return lax.broadcasted_iota(jnp.int32, (ROWS, LANES), 0)


def choose(values, labels):
    values, bit = list(values), 1
    while len(values) > 1:
        odd = (labels & bit) != 0
        paired = [
            jnp.where(odd, values[i + 1], values[i]) if i + 1 < len(values) else values[i]
            for i in range(0, len(values), 2)
        ]
        values, bit = paired, 2 * bit
    return values[0]


def lookup(row, labels):
    return jnp.take_along_axis(row, labels, axis=1, mode="promise_in_bounds")


def splats(kap):
    return [jnp.full((ROWS, LANES), half_dt * kap[i], jnp.float32) for i in range(kap.shape[0])]


def stencil(R, W, get_s, get_h, get_z, halo, put, get_g=None, put_g=None):
    C, S = W // LANES, R // ROWS
    lane, row = lane_ids(), row_ids()
    first, last = lane == 0, lane == LANES - 1
    top, bottom = row == 0, row == ROWS - 1
    before = None
    for c in range(C):
        s = [get_s(r, c) for r in range(S)]
        h = [get_h(r, c) for r in range(S)]
        rs = [pltpu.roll(v, 1, 1) for v in s]
        rh = [pltpu.roll(v, 1, 1) for v in h] if get_g is None else None
        us = [pltpu.roll(v, 1, 0) for v in s]
        uh = [pltpu.roll(v, 1, 0) for v in h]
        if halo is not None:
            sa, ha, sb, hb = halo(c)
        acc, back, down = [], [], []
        for r in range(S):
            sl = jnp.where(first, 0.0 if c == 0 else before[0][r], rs[r])
            if get_g is None:
                g = h[r] + jnp.where(first, 0.0 if c == 0 else before[1][r], rh[r])
                if put_g is not None:
                    put_g(r, c, g)
            else:
                g = get_g(r, c)
            face = g * (sl - s[r])
            back.append(pltpu.roll(face, LANES - 1, 1))
            if r == 0:
                if halo is None:
                    su, hu = us[0], uh[0]
                else:
                    su, hu = jnp.where(top, sa, us[0]), jnp.where(top, ha, uh[0])
            else:
                su, hu = jnp.where(top, us[r - 1], us[r]), jnp.where(top, uh[r - 1], uh[r])
            upper = (h[r] + hu) * (su - s[r])
            down.append(pltpu.roll(upper, ROWS - 1, 0))
            acc.append((s[r] + get_z(r, c, s[r], h[r])) + (face + upper))
        for r in range(S):
            if r + 1 < S:
                lower = jnp.where(bottom, down[r + 1], down[r])
            elif halo is None:
                lower = down[r]
            else:
                lower = jnp.where(bottom, (h[r] + hb) * (s[r] - sb), down[r])
            acc[r] = acc[r] - lower
        if before is not None:
            for r in range(S):
                put(r, c - 1, before[3][r] - jnp.where(last, back[r], before[2][r]))
        before = (rs, rh, back, acc, s, h)
    for r in range(S):
        out = before[5][r] * before[4][r]
        put(r, C - 1, before[3][r] - jnp.where(last, out, before[2][r]))


def vertical(s, h, s_up, h_up, s_down, h_down):
    return (h + h_up) * (s_up - s) + (h + h_down) * (s_down - s)


def begin_kernel(
    s_hbm, lab_hbm, patch_hbm, zone_hbm, kap_hbm, power_hbm,
    left, right, heat, swap_a, swap_b, s_v, lab_v,
    patch, zone_v, kap, power, sem,
):
    L, R, W = s_hbm.shape
    C, half = W // LANES, W // 2
    starts = (0, R - ROWS)
    small = [
        pltpu.make_async_copy(kap_hbm, kap, sem.at[0]),
        pltpu.make_async_copy(power_hbm, power, sem.at[1]),
        pltpu.make_async_copy(patch_hbm, patch, sem.at[2]),
    ]
    groups = [(0, 2), (L - 2, 2), (2, L - 4)]
    layers = [
        [
            pltpu.make_async_copy(s_hbm.at[pl.ds(l, n)], s_v.at[pl.ds(l, n)], sem.at[3 + 2 * k]),
            pltpu.make_async_copy(lab_hbm.at[pl.ds(l, n)], lab_v.at[pl.ds(l, n)], sem.at[4 + 2 * k]),
        ]
        for k, (l, n) in enumerate(groups)
    ]
    layers[2] += [
        pltpu.make_async_copy(zone_hbm.at[pl.ds(start, ROWS)], zone_v.at[k], sem.at[9 + k])
        for k, start in enumerate(starts)
    ]
    for copy in small + layers[0] + layers[1] + layers[2]:
        copy.start()
    for copy in small:
        copy.wait()
    values = splats(kap)
    heats = step_dt * jnp.broadcast_to(power[...], (ROWS, LANES))
    for p in range(2):
        for copy in layers[p]:
            copy.wait()
        own, near = (0, 1) if p == 0 else (L - 1, L - 2)

        def get_s(r, c):
            return s_v[(own,) + tile(r, c)]

        def get_h(r, c):
            return choose(values, lab_v[(own,) + tile(r, c)])

        def get_z(r, c, s, h):
            h_near = choose(values, lab_v[(near,) + tile(r, c)])
            flow = (h + h_near) * (s_v[(near,) + tile(r, c)] - s)
            if p == 0:
                value = lookup(heats, patch[tile(r, c)])
                heat[tile(r, c)] = value
                flow = flow + value
            return flow

        def put(r, c, value):
            out = left if c < C // 2 else right
            out[(p,) + tile(r, c % (C // 2))] = value

        stencil(R, W, get_s, get_h, get_z, None, put)
    row = row_ids()
    for copy in layers[2]:
        copy.wait()

    def pack(k, out):
        rows = ((0, 1), (ROWS - 2, ROWS - 1))[k]

        def body(c, _):
            lanes = pl.ds(pl.multiple_of(c * LANES, LANES), LANES)
            edge = pl.ds(starts[k], ROWS)
            for base in range(0, L, ROWS):
                for ref, at in ((s_v, 0), (lab_v, 2 * L)):
                    tiles = [ref[base + q, edge, lanes] for q in range(ROWS)]
                    for j, source in enumerate(rows):
                        packed = tiles[source]
                        for q in range(ROWS):
                            if q != source:
                                packed = jnp.where(row == q, pltpu.roll(tiles[q], (q - source) % ROWS, 0), packed)
                        if ref is lab_v:
                            packed = choose(values, packed)
                        out[pl.ds(at + j * L + base, ROWS), lanes] = packed
            last = rows[0] if k == 0 else rows[1]
            warm = heat[edge, lanes]
            zones = zone_v[k, :, lanes].astype(jnp.float32)
            pair = jnp.where(row == 0, pltpu.roll(warm, -last % ROWS, 0), pltpu.roll(zones, (1 - last) % ROWS, 0))
            out[pl.ds(4 * L, ROWS), lanes] = pair
            return 0

        lax.fori_loop(0, W // LANES, body, 0)

    odd = lax.axis_index("tile") % 2 == 1

    @pl.when(odd)
    def _():
        pack(0, swap_a)
        pack(1, swap_b)

    @pl.when(jnp.logical_not(odd))
    def _():
        pack(1, swap_a)
        pack(0, swap_b)


def begin(s, lab, patch, zone, kap, power):
    L, R, W = s.shape
    f32, i32 = jnp.float32, jnp.int32
    packed = pltpu.VMEM((4 * L + ROWS, W), f32)
    plane = pltpu.VMEM((2, R, W // 2), f32)
    args = [pltpu.with_memory_space_constraint(x, pltpu.HBM) for x in (s, lab, patch, zone, kap, power)]
    return pl.pallas_call(
        begin_kernel,
        out_shape=(
            plane, plane, pltpu.VMEM((R, W), f32), packed, packed, pltpu.VMEM(s.shape, f32), pltpu.VMEM(lab.shape, i32)
        ),
        in_specs=[HBM] * 6,
        out_specs=[VMEM] * 7,
        scratch_shapes=[
            pltpu.VMEM((R, W), i32),
            pltpu.VMEM((2, ROWS, W), i32),
            pltpu.SMEM(kap.shape, f32),
            pltpu.VMEM(power.shape, f32),
            pltpu.SemaphoreType.DMA((11,)),
        ],
        compiler_params=pltpu.CompilerParams(vmem_limit_bytes=16 * MIB),
        name="begin",
    )(*args)


def above_exists():
    return lax.axis_index("tile") > 0


def below_exists():
    return lax.axis_index("tile") < lax.axis_size("tile") - 1


def edge_kernel(own_a, own_b, got_a, got_b, edges, rims, aux):
    rows, W = own_a.shape
    L = (rows - ROWS) // 4
    col = lax.broadcasted_iota(jnp.int32, (L, W), 1)
    layer = lax.broadcasted_iota(jnp.int32, (L, W), 0)
    odd = lax.axis_index("tile") % 2 == 1

    def step(s_a, h_a, s, h, s_b, h_b):
        def toward(s_n, h_n):
            return (h + h_n) * (s_n - s)

        def moved(shift, axis, gone):
            return jnp.where(gone, 0.0, pltpu.roll(s, shift, axis)), jnp.where(
                gone, 0.0, pltpu.roll(h, shift, axis)
            )

        total = s + toward(s_a, h_a) + toward(s_b, h_b)
        total = total + toward(*moved(1, 1, col == 0)) + toward(*moved(W - 1, 1, col == W - 1))
        under = jnp.where(layer == 0, 0.0, toward(pltpu.roll(s, 1, 0), pltpu.roll(h, 1, 0)))
        over = jnp.where(layer == L - 1, 0.0, toward(pltpu.roll(s, L - 1, 0), pltpu.roll(h, L - 1, 0)))
        return total + under + over

    for side, exists in enumerate((above_exists(), below_exists())):
        first_swap = odd if side == 0 else jnp.logical_not(odd)

        def other(at, n):
            at = pl.ds(at, n)
            return jnp.where(exists, jnp.where(first_swap, got_a[at, :], got_b[at, :]), 0.0)

        def own(at, n):
            at = pl.ds(at, n)
            return jnp.where(first_swap, own_a[at, :], own_b[at, :])

        far, near = (0, 1) if side == 0 else (1, 0)
        sf, sn, hf, hn = (other(k * L, L) for k in (far, near, 2 + far, 2 + near))
        s0, s1, h0, h1 = (own(k * L, L) for k in (1 - near, near, 3 - near, 2 + near))
        out = jnp.where(exists, step(sf, hf, sn, hn, s0, h0), 0.0)
        inner = step(sn, hn, s0, h0, s1, h1)
        rims[2 * side] = sn
        rims[2 * side + 1] = hn
        rims[4 + side] = out
        k_out, k_in = (0, 1) if side == 0 else (3, 2)
        edges[pl.ds(k_out, 1), :] = out[0:1] + other(4 * L, 1)
        edges[pl.ds(k_in, 1), :] = inner[0:1] + own(4 * L, 1)
        edges[pl.ds(4 + k_out, 1), :] = out[L - 1 : L]
        edges[pl.ds(4 + k_in, 1), :] = inner[L - 1 : L]
        aux[pl.ds(2 * side, 1), :] = hn[0:1]
        aux[pl.ds(2 * side + 1, 1), :] = hn[L - 1 : L]
        aux[pl.ds(4 + k_out, 1), :] = other(4 * L + 1, 1)
        aux[pl.ds(4 + k_in, 1), :] = own(4 * L + 1, 1)


def edge_rows(own_a, own_b, got_a, got_b):
    rows, W = own_a.shape
    L = (rows - ROWS) // 4
    f32 = jnp.float32
    return pl.pallas_call(
        edge_kernel,
        out_shape=(
            jax.ShapeDtypeStruct((ROWS, W), f32),
            jax.ShapeDtypeStruct((6, L, W), f32),
            jax.ShapeDtypeStruct((ROWS, W), f32),
        ),
        in_specs=[VMEM] * 4,
        out_specs=[VMEM] * 3,
        compiler_params=pltpu.CompilerParams(vmem_limit_bytes=16 * MIB),
        cost_estimate=lasts(1.0),
        name="edge_rows",
    )(own_a, own_b, got_a, got_b)


def pick(ref, base, l, lanes, row):
    at = base + (l // ROWS) * ROWS
    if not isinstance(l, int):
        at = pl.multiple_of(at, ROWS)
    return pltpu.roll(ref[pl.ds(at, ROWS), lanes], (row - l) % ROWS, 0)


def halo_rows(rims, state, lanes, l):
    end = ROWS - 1
    where = ((state[0], 0), (1, 0), (state[1], end), (3, end))
    return tuple(pick(rims.at[k], 0, l, lanes, row) for k, row in where)


def fill_faces(first, end, lab, values, h_out, g_out):
    _, R, W = lab.shape
    edge = lane_ids() == 0

    def body(l, _):
        for r in range(R // ROWS):
            before = 0.0
            for c in range(W // LANES):
                at = (l,) + tile(r, c)
                h = choose(values, lab[at])
                moved = pltpu.roll(h, 1, 1)
                h_out[at] = h
                g_out[at] = h + jnp.where(edge, before, moved)
                before = moved
        return 0

    lax.fori_loop(first, end, body, 0)


def faces_kernel(lab, kap, _, __, h_out, g_out):
    L = lab.shape[0]
    values = splats(kap)
    fill_faces(0, 3, lab, values, h_out, g_out)
    fill_faces(L - 3, L, lab, values, h_out, g_out)


def faces(lab, kap, first, second):
    return pl.pallas_call(
        faces_kernel,
        out_shape=(jax.ShapeDtypeStruct(lab.shape, jnp.float32),) * 2,
        in_specs=[VMEM, SMEM, ANY, ANY],
        out_specs=[VMEM] * 2,
        compiler_params=pltpu.CompilerParams(vmem_limit_bytes=20 * MIB),
        name="faces",
    )(lab, kap, first, second)


def layer_step(l, s_ref, h_ref, g_ref, halo, put):
    _, R, W = s_ref.shape

    def get_s(r, c):
        return s_ref[(l,) + tile(r, c)]

    def get_h(r, c):
        return h_ref[(l,) + tile(r, c)]

    def get_g(r, c):
        return g_ref[(l,) + tile(r, c)]

    def get_z(r, c, s, h):
        a, b = (l - 1,) + tile(r, c), (l + 1,) + tile(r, c)
        return vertical(s, h, s_ref[a], h_ref[a], s_ref[b], h_ref[b])

    stencil(R, W, get_s, get_h, get_z, halo, put, get_g=get_g)


def first_step(l, s_ref, h_ref, g_ref, rims, t):
    def put(r, c, value):
        t[(l,) + tile(r, c)] = value

    def halo(c):
        return halo_rows(rims, (0, 2), pl.ds(LANES * c, LANES), l)

    layer_step(l, s_ref, h_ref, g_ref, halo, put)


def outer_kernel(s_ref, h_ref, g_ref, rims, t):
    L = s_ref.shape[0]

    def body(k, _):
        first_step(1 + k * (L - 3), s_ref, h_ref, g_ref, rims, t)
        return 0

    lax.fori_loop(0, 2, body, 0)


def outer(s, h, g, rims):
    return pl.pallas_call(
        outer_kernel,
        out_shape=jax.ShapeDtypeStruct(s.shape, jnp.float32),
        in_specs=[VMEM] * 4,
        out_specs=VMEM,
        compiler_params=pltpu.CompilerParams(vmem_limit_bytes=20 * MIB),
        cost_estimate=lasts(0.8),
        name="outer",
    )(s, h, g, rims)


def inside_kernel(s_ref, lab, kap, rims, h_in, g_in, t_in, _, h_ref, g_ref, t):
    L = s_ref.shape[0]
    fill_faces(3, L - 3, lab, splats(kap), h_ref, g_ref)

    def body(l, _):
        first_step(l, s_ref, h_ref, g_ref, rims, t)
        return 0

    lax.fori_loop(2, L - 2, body, 0)


def inside(s, lab, kap, rims, h, g, t, after):
    return pl.pallas_call(
        inside_kernel,
        out_shape=(jax.ShapeDtypeStruct(s.shape, jnp.float32),) * 3,
        in_specs=[VMEM, VMEM, SMEM] + [VMEM] * 4 + [ANY],
        out_specs=[VMEM] * 3,
        input_output_aliases={4: 0, 5: 1, 6: 2},
        compiler_params=pltpu.CompilerParams(vmem_limit_bytes=28 * MIB),
        name="inside",
    )(s, lab, kap, rims, h, g, t, after)


def last_kernel(t_ref, h_ref, g_ref, rims, out, buf, sem):
    L, R, W = t_ref.shape

    def send(l):
        return pltpu.make_async_copy(buf.at[l], out.at[l], sem.at[l])

    def body(l, _):
        def put(r, c, value):
            buf[(l,) + tile(r, c)] = value

        def halo(c):
            return halo_rows(rims, (4, 5), pl.ds(LANES * c, LANES), l)

        layer_step(l, t_ref, h_ref, g_ref, halo, put)
        send(l).start()
        return 0

    lax.fori_loop(1, L - 1, body, 0)

    def drain(l, _):
        send(l).wait()
        return 0

    lax.fori_loop(1, L - 1, drain, 0)


def last_layers(t, h, g, rims):
    L = t.shape[0]
    return pl.pallas_call(
        last_kernel,
        out_shape=jax.ShapeDtypeStruct(t.shape, jnp.float32),
        in_specs=[VMEM] * 4,
        out_specs=HBM,
        scratch_shapes=[pltpu.VMEM(t.shape, jnp.float32), pltpu.SemaphoreType.DMA((L,))],
        compiler_params=pltpu.CompilerParams(vmem_limit_bytes=24 * MIB),
        cost_estimate=lasts(5.5),
        name="last_layers",
    )(t, h, g, rims)


def near_of(side):
    me = lax.axis_index("tier")
    return (me ^ 1, me ^ 2) if side == 0 else (me ^ 2, me ^ 1)


def entries(tiers):
    me = lax.axis_index("tier")
    if tiers != 4:
        return [(2 * me + i, j) for i in range(2) for j in range(2 * tiers)]
    listed = []
    for side in range(2):
        near, target = near_of(side)
        columns = [2 * me, 2 * me + 1, 2 * near, 2 * near + 1]
        for who in (target, me):
            listed += [(2 * who + i, j) for i in range(2) for j in columns]
    return listed


def table_kernel(tiers, ops, table, rim_table):
    regions = ops.shape[0]
    me = lax.axis_index("tier")
    for k, (i, j) in enumerate(entries(tiers)):
        for g in range(regions):
            table[k, g] = jnp.full((ROWS, LANES), ops[g, i, j], jnp.float32)
    lane, upper = lane_ids(), row_ids() < 4
    for q in range(tiers):
        source = me ^ q if tiers == 4 else q
        for k in range(2):
            value = jnp.zeros((ROWS, LANES), jnp.float32)
            for g in range(regions):
                a, b = ops[g, 2 * me, 2 * source + k], ops[g, 2 * me + 1, 2 * source + 1 - k]
                value = jnp.where(lane == g, jnp.where(upper, a, b), value)
            rim_table[2 * q + k] = value


def make_tables(tiers, ops):
    regions = ops.shape[0]
    count = 32 if tiers == 4 else 4 * tiers
    return pl.pallas_call(
        functools.partial(table_kernel, tiers),
        out_shape=(
            jax.ShapeDtypeStruct((count, regions, ROWS, LANES), jnp.float32),
            jax.ShapeDtypeStruct((2 * tiers, ROWS, LANES), jnp.float32),
        ),
        in_specs=[SMEM],
        out_specs=[VMEM, VMEM],
        compiler_params=pltpu.CompilerParams(vmem_limit_bytes=16 * MIB),
        cost_estimate=lasts(1.4),
        name="make_tables",
    )(ops)


def product(table, at, zone, refs, partial, base, c, S, put):
    regions = table.shape[1]
    lanes = pl.ds(pl.multiple_of(c * LANES, LANES), LANES)
    whole = pl.ds(pl.multiple_of(base + c * LANES, LANES), LANES)
    for r0 in range(0, S, 2):
        rows = [pl.ds(ROWS * r, ROWS) for r in range(r0, min(S, r0 + 2))]
        zones = [zone[x, whole] for x in rows]
        for i in range(2):
            totals = [None] * len(rows)
            for j, (ref, index) in enumerate(refs):
                values = [table[at + i * len(refs) + j, g] for g in range(regions)]
                for k, x in enumerate(rows):
                    term = choose(values, zones[k]) * ref[index, x, lanes]
                    totals[k] = term if totals[k] is None else totals[k] + term
            for k, x in enumerate(rows):
                for ref in partial:
                    totals[k] = totals[k] + ref[i, x, lanes]
                put(i, x, lanes, whole, totals[k])


def combine_kernel(table, zone, left, left_x, right, right_y, _, to_y, to_x):
    _, R, half = left.shape

    def body(c, _):
        for side, (out, own, other) in enumerate(((to_y, left, left_x), (to_x, right, right_y))):

            def put(i, rows, lanes, whole, value, out=out):
                out[i, rows, lanes] = value

            refs = [(own, 0), (own, 1), (other, 0), (other, 1)]
            product(table, 16 * side, zone, refs, [], side * half, c, R // ROWS, put)
        return 0

    lax.fori_loop(0, half // LANES, body, 0)


def combine(table, zone, left, left_x, right, right_y, after):
    return pl.pallas_call(
        combine_kernel,
        out_shape=(jax.ShapeDtypeStruct(left.shape, jnp.float32),) * 2,
        in_specs=[VMEM] * 6 + [ANY],
        out_specs=[VMEM, VMEM],
        compiler_params=pltpu.CompilerParams(vmem_limit_bytes=16 * MIB),
        cost_estimate=lasts(0.75),
        name="combine",
    )(table, zone, left, left_x, right, right_y, after)


def solve(tiers, table, zone, groups, R, half, put, after=None):
    for side, group in enumerate(groups):
        if tiers == 4:
            own, other, part = group
            refs, partial, at = [(own, 0), (own, 1), (other, 0), (other, 1)], [part], 16 * side + 8
        else:
            refs, partial, at = [(group[0], k) for k in range(2 * tiers)], [], 0

        def body(c, _):
            product(table, at, zone, refs, partial, side * half, c, R // ROWS, put)
            return 0

        lax.fori_loop(0, half // LANES, body, 0)
        if after is not None:
            after(side)


def bond_kernel(tiers, zone, table, rim_table, aux, heat, h_ref, t_in, *refs):
    pairs = tiers == 4
    per = 3 if pairs else 1
    groups, refs = (refs[:per], refs[per : 2 * per]), refs[2 * per :]
    edge_refs, (t, out_left, out_right, rim) = refs[:-4], refs[-4:]
    L, R, W = t.shape
    half, C = W // 2, W // LANES
    row = row_ids()

    def put(i, rows, lanes, whole, value):
        t[i * (L - 1), rows, whole] = value

    solve(tiers, table, zone, groups, R, half, put)
    gone = ((row % 4 == 0) & jnp.logical_not(above_exists())) | ((row % 4 == 3) & jnp.logical_not(below_exists()))

    for c in range(C):
        lanes = pl.ds(c * LANES, LANES)
        if pairs:
            tiles = [ref[:, lanes] for ref in edge_refs]
        else:
            tiles = [edge_refs[0][q, :, lanes] for q in range(tiers)]
        zones = aux[:, lanes].astype(jnp.int32)
        zones = jnp.where(row < 4, pltpu.roll(zones, 4, 0), zones)
        value = None
        for q, mine in enumerate(tiles):
            for k, x in enumerate((mine, pltpu.roll(mine, 4, 0))):
                entry = jnp.take_along_axis(rim_table[2 * q + k], zones, axis=1, mode="promise_in_bounds")
                value = entry * x if value is None else value + entry * x
        value = jnp.where(gone, 0.0, value)
        rim[:, lanes] = value
        for i in range(2):
            t[i * (L - 1), pl.ds(0, 1), lanes] = value[4 * i + 1 : 4 * i + 2]
            t[i * (L - 1), pl.ds(R - 1, 1), lanes] = value[4 * i + 2 : 4 * i + 3]

    for p in range(2):
        own, near = (0, 1) if p == 0 else (L - 1, L - 2)

        def get_s(r, c):
            return t[(p * (L - 1),) + tile(r, c)]

        def get_h(r, c):
            return h_ref[(own,) + tile(r, c)]

        def get_z(r, c, s, h):
            at = (near,) + tile(r, c)
            flow = (h + h_ref[at]) * (t[at] - s)
            return flow + heat[tile(r, c)] if p == 0 else flow

        def halo(c):
            lanes = pl.ds(LANES * c, LANES)
            sides, walls = rim[:, lanes], aux[:, lanes]
            return (
                pltpu.roll(sides, -4 * p % ROWS, 0),
                pltpu.roll(walls, -p % ROWS, 0),
                pltpu.roll(sides, ROWS - 1 - (4 * p + 3), 0),
                pltpu.roll(walls, ROWS - 1 - (2 + p), 0),
            )

        def put_out(r, c, value):
            if c < C // 2:
                out_left[(p,) + tile(r, c)] = value
            else:
                out_right[(p,) + tile(r, c - C // 2)] = value

        stencil(R, W, get_s, get_h, get_z, halo, put_out)


def bond(tiers, zone, tables, aux, heat, h, t, left, right, edges):
    R, W = zone.shape
    args = (zone, *tables, aux, heat, h, t, *left, *right, *edges)
    f32 = jnp.float32
    return pl.pallas_call(
        functools.partial(bond_kernel, tiers),
        out_shape=(
            jax.ShapeDtypeStruct(t.shape, f32),
            jax.ShapeDtypeStruct((2, R, W // 2), f32),
            jax.ShapeDtypeStruct((2, R, W // 2), f32),
        ),
        in_specs=[VMEM] * len(args),
        out_specs=[VMEM] * 3,
        input_output_aliases={6: 0},
        scratch_shapes=[pltpu.VMEM((ROWS, W), f32)],
        compiler_params=pltpu.CompilerParams(vmem_limit_bytes=20 * MIB),
        cost_estimate=lasts(3.3),
        name="bond",
    )(*args)


def final_kernel(tiers, zone, table, *refs):
    per = 3 if tiers == 4 else 1
    groups = refs[:per], refs[per : 2 * per]
    _, out, buf, sem = refs[2 * per :]
    L, R, W = out.shape
    half = W // 2
    copies = []

    def put(i, rows, lanes, whole, value):
        buf[i, rows, whole] = value

    def after(side):
        lanes = pl.ds(side * half, half)
        for i in range(2):
            copies.append(
                pltpu.make_async_copy(
                    buf.at[i, :, lanes], out.at[i * (L - 1), :, lanes], sem.at[2 * side + i]
                )
            )
            copies[-1].start()

    solve(tiers, table, zone, groups, R, half, put, after)
    for copy in copies:
        copy.wait()


def final_planes(tiers, zone, table, left, right, out):
    args = (zone, table, *left, *right, out)
    _, R, W = out.shape
    return pl.pallas_call(
        functools.partial(final_kernel, tiers),
        out_shape=jax.ShapeDtypeStruct(out.shape, jnp.float32),
        in_specs=[VMEM] * (len(args) - 1) + [HBM],
        out_specs=HBM,
        scratch_shapes=[pltpu.VMEM((2, R, W), jnp.float32), pltpu.SemaphoreType.DMA((4,))],
        input_output_aliases={len(args) - 1: 0},
        compiler_params=pltpu.CompilerParams(vmem_limit_bytes=16 * MIB),
        cost_estimate=lasts(1.6),
        name="final_planes",
    )(*args)


def across(value, bits, tiers):
    return lax.ppermute(value, "tier", [(i, i ^ bits) for i in range(tiers)])


def every(value, tiers):
    gathered = lax.all_gather(value, "tier", axis=0, tiled=False)
    return gathered.reshape((tiers * value.shape[0],) + value.shape[1:]) if value.ndim == 3 else gathered


def exchange(tiers, table, zone, left, right, after):
    if tiers != 4:
        return (every(left, tiers),), (every(right, tiers),), left
    left_x, right_y = across(left, 1, tiers), across(right, 2, tiers)
    to_y, to_x = combine(table, zone, left, left_x, right, right_y, after)
    return (left, left_x, across(to_y, 2, tiers)), (right, right_y, across(to_x, 1, tiers)), to_y


def local(warming, substance, zone, patch, kap, power, ops):
    tiers, tiles = lax.axis_size("tier"), lax.axis_size("tile")
    s, lab, patch = warming[0], substance[0], patch[0]

    left, right, heat, swap_a, swap_b, s, lab = begin(s, lab, patch, zone, kap, power)
    pairs = [(i, i ^ 1) for i in range(tiles) if i ^ 1 < tiles]
    got_a = lax.ppermute(swap_a, "tile", pairs)
    pairs = [(i, ((i - 1) ^ 1) + 1) for i in range(1, tiles - 1 + tiles % 2)]
    got_b = lax.ppermute(swap_b, "tile", pairs)
    tables = make_tables(tiers, ops)
    left, right, sent = exchange(tiers, tables[0], zone, left, right, heat)
    edges, rims, aux = edge_rows(swap_a, swap_b, got_a, got_b)
    h, g = faces(lab, kap, edges, sent)
    if tiers == 4:
        edges = (edges, across(edges, 1, tiers), across(edges, 2, tiers), across(edges, 3, tiers))
    else:
        edges = (every(edges, tiers),)
    t = outer(s, h, g, rims)
    t, left, right = bond(tiers, zone, tables, aux, heat, h, t, left, right, edges)
    h, g, t = inside(s, lab, kap, rims, h, g, t, left)
    left, right, _ = exchange(tiers, tables[0], zone, left, right, t)
    out = last_layers(t, h, g, rims)
    out = final_planes(tiers, zone, tables[0], left, right, out)
    return out[None]


def solution(mesh):
    in_specs = (
        P("tier", None, "tile", None),
        P("tier", None, "tile", None),
        P("tile", None),
        P("tier", "tile", None),
        P(),
        P("tier", None),
        P(),
    )
    out_specs = P("tier", None, "tile", None)
    return jax.shard_map(local, mesh=mesh, in_specs=in_specs, out_specs=out_specs, check_vma=False)
```

time: 110 us -> 53.6 us (0.49)
  Pallas kernels: 57.3 us -> 29.8 us
  local copies, waits for them, and re-layouts: 24.7 us -> 0.01 us
  waiting for transfers between devices: 10.8 us -> 7.55 us
    unnamed x42 -> x6, local copies, waits for them, and re-layouts: 24.6 us -> 0.01 us
    pallas_call x8 -> x9, Pallas kernels: 44.8 us -> 23 us  [the longest x1 7.44 us: inside(): pl.pallas_call(inside_kernel, out_shape=(jax.ShapeDtypeStruct(s.shape, jn...]
    pallas_call x1, Pallas kernels: 10.6 us -> 5.81 us  [last_layers(): pl.pallas_call(last_kernel, out_shape=jax.ShapeDtypeStruct(t.shape, jnp.f...]
    ppermute x2, starting transfers between devices: 4.49 us -> 1.21 us  [the longest x1 0.69 us: local(): got_b = lax.ppermute(swap_b, 'tile', pairs)]
    ppermute x11, waiting for transfers between devices: 10.8 us -> 7.55 us  [across(): return lax.ppermute(value, 'tier', [(i, i ^ bits) for i in range(tiers)])]
    ppermute x11, starting transfers between devices: 11.8 us -> 14.7 us  [across(): return lax.ppermute(value, 'tier', [(i, i ^ bits) for i in range(tiers)])]
  transfers between devices with their start and end apart: 13 -> 13, of which waited for: 4 -> 7; matrix products, arithmetic and copies ran while one was open for 0% -> 0% of each run, Pallas kernels for 29% -> 36%
where the time goes in v2:
time: 53.6 us; the launch traced here: 53.4 us
  Pallas kernels  29.8 us (56%)
  starting transfers between devices  16 us (30%)
  waiting for transfers between devices  7.55 us (14%)
    ppermute x11, starting transfers between devices, across(): return lax.ppermute(value, 'tier', [(i, i ^ bits) for i in range(tiers)])  14.7 us
    ppermute x11, waiting for transfers between devices, across(): return lax.ppermute(value, 'tier', [(i, i ^ bits) for i in range(tiers)])  7.55 us
    pallas_call x1, Pallas kernels, inside(): pl.pallas_call(inside_kernel, out_shape=(jax.ShapeDtypeStruct(s.shape, jn...  7.44 us
    pallas_call x1, Pallas kernels, last_layers(): pl.pallas_call(last_kernel, out_shape=jax.ShapeDtypeStruct(t.shape, jnp.f...  5.81 us
    pallas_call x1, Pallas kernels, begin(): pl.pallas_call(begin_kernel, out_shape=(plane, plane, pltpu.VMEM((R, W),...  4.87 us
    pallas_call x1, Pallas kernels, bond(): pl.pallas_call(functools.partial(bond_kernel, tiers), out_shape=(jax.Shap...  3.29 us
    pallas_call x1, Pallas kernels, faces(): pl.pallas_call(faces_kernel, out_shape=(jax.ShapeDtypeStruct(lab.shape, j...  2.16 us
    pallas_call x1, Pallas kernels, final_planes(): pl.pallas_call(functools.partial(final_kernel, tiers), out_shape=jax.Shap...  1.59 us
  transfers between devices with their start and end apart: 13, of which 7 were waited for; matrix products, arithmetic and copies ran while one was open for 0% of the time, Pallas kernels for 36%

profile of v2, /device:TPU:0, one launch (start us, length us, event | category | flops | bytes accessed | tf_op | source)
XLA Modules:
  0.0 53.4 jit_solution(6074462758568201999)
XLA Ops:
  0.0 0.0 copy-start.1
  0.0 0.0 copy-start
  0.0 4.9 %begin.1 = (f32[2,32,1024]{2,1,0:T(8,128)S(1)}, f32[2,32,1024]{2,1,0:T(8,128)S(1)}, f32[32,2048]{1,0:T(8,128)S(1)}, f32[72,2048]{1,0:T(8,128)S(1)}, f32[72,2048]...) custom-call(f32[16,32,2048]{2,1,0:T(8,128)} %bitcast.4, s32[16,32,2048]{2,1,0:T(8,128)} %bitcast.5, ...), custom_call_target="tpu_custom_call" | custom-call | tf_op jit(solution)/shard_map/begin/pallas_call | solution.py:222
  4.9 0.0 copy-start.2
  4.9 0.5 collective-permute-start
  5.4 0.7 %collective-permute-start.1 = (f32[72,2048]{1,0:T(8,128)S(1)}, f32[72,2048]{1,0:T(8,128)S(1)}, u32[]{:S(2)}, u32[]{:S(2)}) collective-permute-start(f32[72,2048]{1,0:T(8,128)S(1)} %get-tuple-element.32.own_b), channel_id=1, source_target_pairs={{1,2},{2,1},{3,4},{4,3},{5,6},{6,5},{9,10},{10,9},{11,12},{12,11},... | collective-permute-start | bytes 1769480 | tf_op jit(solution)/shard_map/ppermute | solution.py:756
  6.1 2.6 %collective-permute-start.2 = (f32[2,32,1024]{2,1,0:T(8,128)S(1)}, f32[2,32,1024]{2,1,0:T(8,128)S(1)}, u32[]{:S(2)}, u32[]{:S(2)}) collective-permute-start(f32[2,32,1024]{2,1,0:T(8,128)S(1)} %get-tuple-element.37.left.refs_0_), channel_id=1, source_target_pairs={{0,8},{8,0},{16,24},{24,16},{1,9},{9,1},{17,25},{25,17},{2,10},{10... | collective-permute-start | bytes 786440 | tf_op jit(solution)/shard_map/ppermute | solution.py:732
  8.7 1.5 %collective-permute-start.3 = (f32[2,32,1024]{2,1,0:T(8,128)S(1)}, f32[2,32,1024]{2,1,0:T(8,128)S(1)}, u32[]{:S(2)}, u32[]{:S(2)}) collective-permute-start(f32[2,32,1024]{2,1,0:T(8,128)S(1)} %get-tuple-element.38.right.refs_3_), channel_id=1, source_target_pairs={{0,16},{8,24},{16,0},{24,8},{1,17},{9,25},{17,1},{25,9},{2,18},{10... | collective-permute-start | bytes 786440 | tf_op jit(solution)/shard_map/ppermute | solution.py:732
  10.2 0.0 copy-done.1
  10.2 1.4 %make_tables.1 = (f32[32,8,8,128]{3,2,1,0:T(8,128)S(1)}, f32[8,8,128]{2,1,0:T(8,128)S(1)}) custom-call(f32[8,8,8]{2,1,0:T(8,128)S(1)} %copy-done.1), custom_call_target="tpu_custom_call" | custom-call | bytes 4620000 | tf_op jit(solution)/shard_map/make_tables/pallas_call | solution.py:522
  11.6 1.7 %collective-permute-done.2.left_x.refs_1_ = f32[2,32,1024]{2,1,0:T(8,128)S(1)} collective-permute-done((f32[2,32,1024]{2,1,0:T(8,128)S(1)}, f32[2,32,1024]{2,1,0:T(8,128)S(1)}, u32[]{:S(2)}, u32[]{:S(2)}) %collective-permute-start.2) | collective-permute-done | bytes 262176 | tf_op jit(solution)/shard_map/ppermute | solution.py:732
  13.4 2.8 %collective-permute-done.3.right_y.refs_4_ = f32[2,32,1024]{2,1,0:T(8,128)S(1)} collective-permute-done((f32[2,32,1024]{2,1,0:T(8,128)S(1)}, f32[2,32,1024]{2,1,0:T(8,128)S(1)}, u32[]{:S(2)}, u32[]{:S(2)}) %collective-permute-start.3) | collective-permute-done | bytes 262176 | tf_op jit(solution)/shard_map/ppermute | solution.py:732
  16.1 0.0 copy-done
  16.1 0.8 %combine.2 = (f32[2,32,1024]{2,1,0:T(8,128)S(1)}, f32[2,32,1024]{2,1,0:T(8,128)S(1)}) custom-call(f32[32,8,8,128]{3,2,1,0:T(8,128)S(1)} %get-tuple-element.29.table, s32[32,2048]{1,0:T(8,128)S(1)} %copy-done, f32[2,32,1024]{2,1,0:T(8,128)S(1)} %get-tuple-element.37.left.refs_0_, f32[2,32,1024]{2,1,0:T(8,128)S(1)} %collective-permute-done.2.left_x.refs_1_, ...), custom_call_target="tpu_custom_call" | custom-call | bytes 2475000 | tf_op jit(solution)/shard_map/combine/pallas_call | solution.py:573
  16.9 0.1 collective-permute-start.5
  17.0 2.0 %collective-permute-start.4 = (f32[2,32,1024]{2,1,0:T(8,128)S(1)}, f32[2,32,1024]{2,1,0:T(8,128)S(1)}, u32[]{:S(2)}, u32[]{:S(2)}) collective-permute-start(f32[2,32,1024]{2,1,0:T(8,128)S(1)} %get-tuple-element.39.__), channel_id=1, source_target_pairs={{0,16},{8,24},{16,0},{24,8},{1,17},{9,25},{17,1},{25,9},{2,18},{10... | collective-permute-start | bytes 786440 | tf_op jit(solution)/shard_map/ppermute | solution.py:732
  19.0 0.0 collective-permute-done.got_a
  19.0 0.0 collective-permute-done.1.got_b
  19.0 1.0 %edge_rows.1 = (f32[8,2048]{1,0:T(8,128)S(1)}, f32[6,16,2048]{2,1,0:T(8,128)S(1)}, f32[8,2048]{1,0:T(8,128)S(1)}) custom-call(f32[72,2048]{1,0:T(8,128)S(1)} %get-tuple-element.31.own_a, f32[72,2048]{1,0:T(8,128)S(1)} %get-tuple-element.32.own_b, f32[72,2048]{1,0:T(8,128)S(1)} %collective-permute-done.got_a, f32[72,2048]{1,0:T(8,128)S(1)} %collective-permute-done.1.got_b), custom_call_target="tpu_custom_call" | custom-call | bytes 3300000 | tf_op jit(solution)/shard_map/edge_rows/pallas_call | solution.py:305
  20.0 1.5 %collective-permute-start.8 = (f32[8,2048]{1,0:T(8,128)S(1)}, f32[8,2048]{1,0:T(8,128)S(1)}, u32[]{:S(2)}, u32[]{:S(2)}) collective-permute-start(f32[8,2048]{1,0:T(8,128)S(1)} %get-tuple-element.36._.refs_6_), channel_id=1, source_target_pairs={{0,24},{8,16},{16,8},{24,0},{1,25},{9,17},{17,9},{25,1},{2,26},{10... | collective-permute-start | bytes 196616 | tf_op jit(solution)/shard_map/ppermute | solution.py:732
  21.5 1.5 %collective-permute-start.7 = (f32[8,2048]{1,0:T(8,128)S(1)}, f32[8,2048]{1,0:T(8,128)S(1)}, u32[]{:S(2)}, u32[]{:S(2)}) collective-permute-start(f32[8,2048]{1,0:T(8,128)S(1)} %get-tuple-element.36._.refs_6_), channel_id=1, source_target_pairs={{0,16},{8,24},{16,0},{24,8},{1,17},{9,25},{17,1},{25,9},{2,18},{10... | collective-permute-start | bytes 196616 | tf_op jit(solution)/shard_map/ppermute | solution.py:732
  23.1 0.5 %collective-permute-start.6 = (f32[8,2048]{1,0:T(8,128)S(1)}, f32[8,2048]{1,0:T(8,128)S(1)}, u32[]{:S(2)}, u32[]{:S(2)}) collective-permute-start(f32[8,2048]{1,0:T(8,128)S(1)} %get-tuple-element.36._.refs_6_), channel_id=1, source_target_pairs={{0,8},{8,0},{16,24},{24,16},{1,9},{9,1},{17,25},{25,17},{2,10},{10... | collective-permute-start | bytes 196616 | tf_op jit(solution)/shard_map/ppermute | solution.py:732
  23.6 0.0 copy-done.2
  23.6 2.2 %faces.1 = (f32[16,32,2048]{2,1,0:T(8,128)S(1)}, f32[16,32,2048]{2,1,0:T(8,128)S(1)}) custom-call(s32[16,32,2048]{2,1,0:T(8,128)S(1)} %get-tuple-element.35.lab, f32[16]{0:T(128)S(1)} %copy-done.2, f32[8,2048]{1,0:T(8,128)S(1)} %get-tuple-element.36._.refs_6_, f32[2,32,1024]{2,1,0:T(8,128)S(1)} %get-tuple-element.39.__), custom_call_target="tpu_custom_call" | custom-call | tf_op jit(solution)/shard_map/faces/pallas_call | solution.py:360
  25.8 0.7 %outer.1.t_in = f32[16,32,2048]{2,1,0:T(8,128)S(1)} custom-call(f32[16,32,2048]{2,1,0:T(8,128)S(1)} %get-tuple-element.41.s_ref, f32[16,32,2048]{2,1,0:T(8,128)S(1)} %get-tuple-element.40.h_ref.h_in, f32[16,32,2048]{2,1,0:T(8,128)S(1)} %get-tuple-element.42.g_ref.g_in, f32[6,16,2048]{2,1,0:T(8,128)S(1)} %get-tuple-element.43.rims), custom_call_target="tpu_custom_call" | custom-call | bytes 2640000 | tf_op jit(solution)/shard_map/outer/pallas_call | solution.py:410
  26.5 0.0 collective-permute-done.5.refs_5_
  26.5 0.0 collective-permute-done.4.refs_2_
  26.5 1.6 %collective-permute-done.8.refs_9_ = f32[8,2048]{1,0:T(8,128)S(1)} collective-permute-done((f32[8,2048]{1,0:T(8,128)S(1)}, f32[8,2048]{1,0:T(8,128)S(1)}, u32[]{:S(2)}, u32[]{:S(2)}) %collective-permute-start.8) | collective-permute-done | bytes 65568 | tf_op jit(solution)/shard_map/ppermute | solution.py:732
  28.1 0.1 collective-permute-done.7.refs_8_
  28.2 0.2 collective-permute-done.6.refs_7_
  28.4 3.3 %bond.1 = (f32[16,32,2048]{2,1,0:T(8,128)S(1)}, f32[2,32,1024]{2,1,0:T(8,128)S(1)}, f32[2,32,1024]{2,1,0:T(8,128)S(1)}) custom-call(s32[32,2048]{1,0:T(8,128)S(1)} %copy-done, f32[32,8,8,128]{3,2,1,0:T(8,128)S(1)} %get-tuple-element.29.table, f32[8,8,128]{2,1,0:T(8,128)S(1)} %get-tuple-element.30.rim_table, ...), custom_call_target="tpu_custom_call", output_to_operand_aliasing={{0}: (6, {})} | custom-call | bytes 10890000 | tf_op jit(solution)/shard_map/bond/pallas_call | solution.py:672
  31.7 2.3 %collective-permute-start.10 = (f32[2,32,1024]{2,1,0:T(8,128)S(1)}, f32[2,32,1024]{2,1,0:T(8,128)S(1)}, u32[]{:S(2)}, u32[]{:S(2)}) collective-permute-start(f32[2,32,1024]{2,1,0:T(8,128)S(1)} %get-tuple-element.46.right.refs_3_), channel_id=1, source_target_pairs={{0,16},{8,24},{16,0},{24,8},{1,17},{9,25},{17,1},{25,9},{2,18},{10... | collective-permute-start | bytes 786440 | tf_op jit(solution)/shard_map/ppermute | solution.py:732
  34.1 1.5 %collective-permute-start.9 = (f32[2,32,1024]{2,1,0:T(8,128)S(1)}, f32[2,32,1024]{2,1,0:T(8,128)S(1)}, u32[]{:S(2)}, u32[]{:S(2)}) collective-permute-start(f32[2,32,1024]{2,1,0:T(8,128)S(1)} %get-tuple-element.45._.left.refs_0_), channel_id=1, source_target_pairs={{0,8},{8,0},{16,24},{24,16},{1,9},{9,1},{17,25},{25,17},{2,10},{10... | collective-permute-start | bytes 786440 | tf_op jit(solution)/shard_map/ppermute | solution.py:732
  35.6 7.4 %inside.1 = (f32[16,32,2048]{2,1,0:T(8,128)S(1)}, f32[16,32,2048]{2,1,0:T(8,128)S(1)}, f32[16,32,2048]{2,1,0:T(8,128)S(1)}) custom-call(f32[16,32,2048]{2,1,0:T(8,128)S(1)} %get-tuple-element.41.s_ref, s32[16,32,2048]{2,1,0:T(8,128)S(1)} %get-tuple-element.35.lab, f32[16]{0:T(128)S(1)} %copy-done.2, ...), custom_call_target="tpu_custom_call", output_to_operand_aliasing={{0}: (4, {}), {1}: (5, {}), {2}: (6, {})} | custom-call | tf_op jit(solution)/shard_map/inside/pallas_call | solution.py:433
  43.0 0.0 collective-permute-done.10.right_y.refs_4_
  43.0 0.0 collective-permute-done.9.left_x.refs_1_
  43.0 0.8 %combine.3 = (f32[2,32,1024]{2,1,0:T(8,128)S(1)}, f32[2,32,1024]{2,1,0:T(8,128)S(1)}) custom-call(f32[32,8,8,128]{3,2,1,0:T(8,128)S(1)} %get-tuple-element.29.table, s32[32,2048]{1,0:T(8,128)S(1)} %copy-done, f32[2,32,1024]{2,1,0:T(8,128)S(1)} %get-tuple-element.45._.left.refs_0_, f32[2,32,1024]{2,1,0:T(8,128)S(1)} %collective-permute-done.9.left_x.refs_1_, ...), custom_call_target="tpu_custom_call" | custom-call | bytes 2475000 | tf_op jit(solution)/shard_map/combine/pallas_call | solution.py:573
  43.8 0.6 %collective-permute-start.11 = (f32[2,32,1024]{2,1,0:T(8,128)S(1)}, f32[2,32,1024]{2,1,0:T(8,128)S(1)}, u32[]{:S(2)}, u32[]{:S(2)}) collective-permute-start(f32[2,32,1024]{2,1,0:T(8,128)S(1)} %get-tuple-element.49), channel_id=1, source_target_pairs={{0,16},{8,24},{16,0},{24,8},{1,17},{9,25},{17,1},{25,9},{2,18},{10... | collective-permute-start | bytes 786440 | tf_op jit(solution)/shard_map/ppermute | solution.py:732
  44.4 0.6 %collective-permute-start.12 = (f32[2,32,1024]{2,1,0:T(8,128)S(1)}, f32[2,32,1024]{2,1,0:T(8,128)S(1)}, u32[]{:S(2)}, u32[]{:S(2)}) collective-permute-start(f32[2,32,1024]{2,1,0:T(8,128)S(1)} %get-tuple-element.50), channel_id=1, source_target_pairs={{0,8},{8,0},{16,24},{24,16},{1,9},{9,1},{17,25},{25,17},{2,10},{10... | collective-permute-start | bytes 786440 | tf_op jit(solution)/shard_map/ppermute | solution.py:732
  44.9 5.8 %last_layers.1.refs_6_ = f32[16,32,2048]{2,1,0:T(8,128)} custom-call(f32[16,32,2048]{2,1,0:T(8,128)S(1)} %get-tuple-element.48._.t_ref, f32[16,32,2048]{2,1,0:T(8,128)S(1)} %get-tuple-element.51.h_ref, f32[16,32,2048]{2,1,0:T(8,128)S(1)} %get-tuple-element.52.g_ref, f32[6,16,2048]{2,1,0:T(8,128)S(1)} %get-tuple-element.43.rims), custom_call_target="tpu_custom_call" | custom-call | bytes 18150000 | tf_op jit(solution)/shard_map/last_layers/pallas_call | solution.py:472
  50.8 0.9 %collective-permute-done.11.refs_2_ = f32[2,32,1024]{2,1,0:T(8,128)S(1)} collective-permute-done((f32[2,32,1024]{2,1,0:T(8,128)S(1)}, f32[2,32,1024]{2,1,0:T(8,128)S(1)}, u32[]{:S(2)}, u32[]{:S(2)}) %collective-permute-start.11) | collective-permute-done | bytes 262176 | tf_op jit(solution)/shard_map/ppermute | solution.py:732
  51.6 0.2 collective-permute-done.12.refs_5_
  51.9 1.6 %final_planes.1 = f32[16,32,2048]{2,1,0:T(8,128)} custom-call(s32[32,2048]{1,0:T(8,128)S(1)} %copy-done, f32[32,8,8,128]{3,2,1,0:T(8,128)S(1)} %get-tuple-element.29.table, f32[2,32,1024]{2,1,0:T(8,128)S(1)} %get-tuple-element.45._.left.refs_0_, f32[2,32,1024]{2,1,0:T(8,128)S(1)} %collective-permute-done.9.left_x.refs_1_, ...), custom_call_target="tpu_custom_call", output_to_operand_aliasing={{}: (8, {})} | custom-call | bytes 5280000 | tf_op jit(solution)/shard_map/final_planes/pallas_call | solution.py:718
Async XLA Ops:
  0.0 10.2 %copy-start.1 = (f32[8,8,8]{2,1,0:T(8,128)S(1)}, f32[8,8,8]{2,1,0:T(8,128)}, u32[]{:S(2)}) copy-start(f32[8,8,8]{2,1,0:T(8,128)} %ops.1) | copy-start | bytes 6148
  0.0 16.1 %copy-start = (s32[32,2048]{1,0:T(8,128)S(1)}, s32[32,2048]{1,0:T(8,128)}, u32[]{:S(2)}) copy-start(s32[32,2048]{1,0:T(8,128)} %zone.7) | copy-start | bytes 786436
  4.9 18.7 %copy-start.2 = (f32[16]{0:T(128)S(1)}, f32[16]{0:T(128)}, u32[]{:S(2)}) copy-start(f32[16]{0:T(128)} %kap.3) | copy-start | bytes 196
  4.9 14.1 %collective-permute-start = (f32[72,2048]{1,0:T(8,128)S(1)}, f32[72,2048]{1,0:T(8,128)S(1)}, u32[]{:S(2)}, u32[]{:S(2)}) collective-permute-start(f32[72,2048]{1,0:T(8,128)S(1)} %get-tuple-element.31.own_a), channel_id=1, source_target_pairs={{0,1},{1,0},{2,3},{3,2},{4,5},{5,4},{6,7},{7,6},{8,9},{9,8},{10,11... | collective-permute-start | bytes 1769480 | tf_op jit(solution)/shard_map/ppermute | solution.py:754
  5.4 13.6 %collective-permute-start.1 = (f32[72,2048]{1,0:T(8,128)S(1)}, f32[72,2048]{1,0:T(8,128)S(1)}, u32[]{:S(2)}, u32[]{:S(2)}) collective-permute-start(f32[72,2048]{1,0:T(8,128)S(1)} %get-tuple-element.32.own_b), channel_id=1, source_target_pairs={{1,2},{2,1},{3,4},{4,3},{5,6},{6,5},{9,10},{10,9},{11,12},{12,11},... | collective-permute-start | bytes 1769480 | tf_op jit(solution)/shard_map/ppermute | solution.py:756
  6.1 7.3 %collective-permute-start.2 = (f32[2,32,1024]{2,1,0:T(8,128)S(1)}, f32[2,32,1024]{2,1,0:T(8,128)S(1)}, u32[]{:S(2)}, u32[]{:S(2)}) collective-permute-start(f32[2,32,1024]{2,1,0:T(8,128)S(1)} %get-tuple-element.37.left.refs_0_), channel_id=1, source_target_pairs={{0,8},{8,0},{16,24},{24,16},{1,9},{9,1},{17,25},{25,17},{2,10},{10... | collective-permute-start | bytes 786440 | tf_op jit(solution)/shard_map/ppermute | solution.py:732
  8.7 7.5 %collective-permute-start.3 = (f32[2,32,1024]{2,1,0:T(8,128)S(1)}, f32[2,32,1024]{2,1,0:T(8,128)S(1)}, u32[]{:S(2)}, u32[]{:S(2)}) collective-permute-start(f32[2,32,1024]{2,1,0:T(8,128)S(1)} %get-tuple-element.38.right.refs_3_), channel_id=1, source_target_pairs={{0,16},{8,24},{16,0},{24,8},{1,17},{9,25},{17,1},{25,9},{2,18},{10... | collective-permute-start | bytes 786440 | tf_op jit(solution)/shard_map/ppermute | solution.py:732
  16.9 9.6 %collective-permute-start.5 = (f32[2,32,1024]{2,1,0:T(8,128)S(1)}, f32[2,32,1024]{2,1,0:T(8,128)S(1)}, u32[]{:S(2)}, u32[]{:S(2)}) collective-permute-start(f32[2,32,1024]{2,1,0:T(8,128)S(1)} %get-tuple-element.44), channel_id=1, source_target_pairs={{0,8},{8,0},{16,24},{24,16},{1,9},{9,1},{17,25},{25,17},{2,10},{10... | collective-permute-start | bytes 786440 | tf_op jit(solution)/shard_map/ppermute | solution.py:732
  17.0 9.5 %collective-permute-start.4 = (f32[2,32,1024]{2,1,0:T(8,128)S(1)}, f32[2,32,1024]{2,1,0:T(8,128)S(1)}, u32[]{:S(2)}, u32[]{:S(2)}) collective-permute-start(f32[2,32,1024]{2,1,0:T(8,128)S(1)} %get-tuple-element.39.__), channel_id=1, source_target_pairs={{0,16},{8,24},{16,0},{24,8},{1,17},{9,25},{17,1},{25,9},{2,18},{10... | collective-permute-start | bytes 786440 | tf_op jit(solution)/shard_map/ppermute | solution.py:732
  20.0 8.1 %collective-permute-start.8 = (f32[8,2048]{1,0:T(8,128)S(1)}, f32[8,2048]{1,0:T(8,128)S(1)}, u32[]{:S(2)}, u32[]{:S(2)}) collective-permute-start(f32[8,2048]{1,0:T(8,128)S(1)} %get-tuple-element.36._.refs_6_), channel_id=1, source_target_pairs={{0,24},{8,16},{16,8},{24,0},{1,25},{9,17},{17,9},{25,1},{2,26},{10... | collective-permute-start | bytes 196616 | tf_op jit(solution)/shard_map/ppermute | solution.py:732
  21.5 6.7 %collective-permute-start.7 = (f32[8,2048]{1,0:T(8,128)S(1)}, f32[8,2048]{1,0:T(8,128)S(1)}, u32[]{:S(2)}, u32[]{:S(2)}) collective-permute-start(f32[8,2048]{1,0:T(8,128)S(1)} %get-tuple-element.36._.refs_6_), channel_id=1, source_target_pairs={{0,16},{8,24},{16,0},{24,8},{1,17},{9,25},{17,1},{25,9},{2,18},{10... | collective-permute-start | bytes 196616 | tf_op jit(solution)/shard_map/ppermute | solution.py:732
  23.1 5.4 %collective-permute-start.6 = (f32[8,2048]{1,0:T(8,128)S(1)}, f32[8,2048]{1,0:T(8,128)S(1)}, u32[]{:S(2)}, u32[]{:S(2)}) collective-permute-start(f32[8,2048]{1,0:T(8,128)S(1)} %get-tuple-element.36._.refs_6_), channel_id=1, source_target_pairs={{0,8},{8,0},{16,24},{24,16},{1,9},{9,1},{17,25},{25,17},{2,10},{10... | collective-permute-start | bytes 196616 | tf_op jit(solution)/shard_map/ppermute | solution.py:732
  31.7 11.3 %collective-permute-start.10 = (f32[2,32,1024]{2,1,0:T(8,128)S(1)}, f32[2,32,1024]{2,1,0:T(8,128)S(1)}, u32[]{:S(2)}, u32[]{:S(2)}) collective-permute-start(f32[2,32,1024]{2,1,0:T(8,128)S(1)} %get-tuple-element.46.right.refs_3_), channel_id=1, source_target_pairs={{0,16},{8,24},{16,0},{24,8},{1,17},{9,25},{17,1},{25,9},{2,18},{10... | collective-permute-start | bytes 786440 | tf_op jit(solution)/shard_map/ppermute | solution.py:732
  34.1 8.9 %collective-permute-start.9 = (f32[2,32,1024]{2,1,0:T(8,128)S(1)}, f32[2,32,1024]{2,1,0:T(8,128)S(1)}, u32[]{:S(2)}, u32[]{:S(2)}) collective-permute-start(f32[2,32,1024]{2,1,0:T(8,128)S(1)} %get-tuple-element.45._.left.refs_0_), channel_id=1, source_target_pairs={{0,8},{8,0},{16,24},{24,16},{1,9},{9,1},{17,25},{25,17},{2,10},{10... | collective-permute-start | bytes 786440 | tf_op jit(solution)/shard_map/ppermute | solution.py:732
  43.8 7.8 %collective-permute-start.11 = (f32[2,32,1024]{2,1,0:T(8,128)S(1)}, f32[2,32,1024]{2,1,0:T(8,128)S(1)}, u32[]{:S(2)}, u32[]{:S(2)}) collective-permute-start(f32[2,32,1024]{2,1,0:T(8,128)S(1)} %get-tuple-element.49), channel_id=1, source_target_pairs={{0,16},{8,24},{16,0},{24,8},{1,17},{9,25},{17,1},{25,9},{2,18},{10... | collective-permute-start | bytes 786440 | tf_op jit(solution)/shard_map/ppermute | solution.py:732
  44.4 7.5 %collective-permute-start.12 = (f32[2,32,1024]{2,1,0:T(8,128)S(1)}, f32[2,32,1024]{2,1,0:T(8,128)S(1)}, u32[]{:S(2)}, u32[]{:S(2)}) collective-permute-start(f32[2,32,1024]{2,1,0:T(8,128)S(1)} %get-tuple-element.50), channel_id=1, source_target_pairs={{0,8},{8,0},{16,24},{24,16},{1,9},{9,1},{17,25},{25,17},{2,10},{10... | collective-permute-start | bytes 786440 | tf_op jit(solution)/shard_map/ppermute | solution.py:732

commit v3 on v2

--- a/solution.py
+++ b/solution.py
@@ -23,10 +23,6 @@
 
 def tile(r, c):
     return pl.ds(ROWS * r, ROWS), pl.ds(LANES * c, LANES)
-
-
-def lasts(us):
-    return pl.CostEstimate(flops=0, bytes_accessed=int(us * 3.3e6), transcendentals=0)
 
 
 def lane_ids():
@@ -116,11 +112,11 @@
 
 def begin_kernel(
     s_hbm, lab_hbm, patch_hbm, zone_hbm, kap_hbm, power_hbm,
-    left, right, heat, swap_a, swap_b, s_v, lab_v,
+    planes, heat, swap_a, swap_b, s_v, lab_v,
     patch, zone_v, kap, power, sem,
 ):
     L, R, W = s_hbm.shape
-    C, half = W // LANES, W // 2
+    C = W // LANES
     starts = (0, R - ROWS)
     small = [
         pltpu.make_async_copy(kap_hbm, kap, sem.at[0]),
@@ -166,8 +162,7 @@
             return flow
 
         def put(r, c, value):
-            out = left if c < C // 2 else right
-            out[(p,) + tile(r, c % (C // 2))] = value
+            planes[(p,) + tile(r, c)] = value
 
         stencil(R, W, get_s, get_h, get_z, None, put)
     row = row_ids()
@@ -217,15 +212,14 @@
     L, R, W = s.shape
     f32, i32 = jnp.float32, jnp.int32
     packed = pltpu.VMEM((4 * L + ROWS, W), f32)
-    plane = pltpu.VMEM((2, R, W // 2), f32)
     args = [pltpu.with_memory_space_constraint(x, pltpu.HBM) for x in (s, lab, patch, zone, kap, power)]
     return pl.pallas_call(
         begin_kernel,
         out_shape=(
-            plane, plane, pltpu.VMEM((R, W), f32), packed, packed, pltpu.VMEM(s.shape, f32), pltpu.VMEM(lab.shape, i32)
+            pltpu.VMEM((2, R, W), f32), pltpu.VMEM((R, W), f32), packed, packed, pltpu.VMEM(s.shape, f32), pltpu.VMEM(lab.shape, i32)
         ),
         in_specs=[HBM] * 6,
-        out_specs=[VMEM] * 7,
+        out_specs=[VMEM] * 6,
         scratch_shapes=[
             pltpu.VMEM((R, W), i32),
             pltpu.VMEM((2, ROWS, W), i32),
@@ -312,7 +306,6 @@
         in_specs=[VMEM] * 4,
         out_specs=[VMEM] * 3,
         compiler_params=pltpu.CompilerParams(vmem_limit_bytes=16 * MIB),
-        cost_estimate=lasts(1.0),
         name="edge_rows",
     )(own_a, own_b, got_a, got_b)
 
@@ -349,22 +342,19 @@
     lax.fori_loop(first, end, body, 0)
 
 
-def faces_kernel(lab, kap, _, __, h_out, g_out):
-    L = lab.shape[0]
-    values = splats(kap)
-    fill_faces(0, 3, lab, values, h_out, g_out)
-    fill_faces(L - 3, L, lab, values, h_out, g_out)
-
-
-def faces(lab, kap, first, second):
+def faces_kernel(lab, kap, h_out, g_out):
+    fill_faces(0, lab.shape[0], lab, splats(kap), h_out, g_out)
+
+
+def faces(lab, kap):
     return pl.pallas_call(
         faces_kernel,
         out_shape=(jax.ShapeDtypeStruct(lab.shape, jnp.float32),) * 2,
-        in_specs=[VMEM, SMEM, ANY, ANY],
+        in_specs=[VMEM, SMEM],
         out_specs=[VMEM] * 2,
         compiler_params=pltpu.CompilerParams(vmem_limit_bytes=20 * MIB),
         name="faces",
-    )(lab, kap, first, second)
+    )(lab, kap)
 
 
 def layer_step(l, s_ref, h_ref, g_ref, halo, put):
@@ -413,14 +403,12 @@
         in_specs=[VMEM] * 4,
         out_specs=VMEM,
         compiler_params=pltpu.CompilerParams(vmem_limit_bytes=20 * MIB),
-        cost_estimate=lasts(0.8),
         name="outer",
     )(s, h, g, rims)
 
 
-def inside_kernel(s_ref, lab, kap, rims, h_in, g_in, t_in, _, h_ref, g_ref, t):
+def inside_kernel(s_ref, h_ref, g_ref, rims, t_in, _, t):
     L = s_ref.shape[0]
-    fill_faces(3, L - 3, lab, splats(kap), h_ref, g_ref)
 
     def body(l, _):
         first_step(l, s_ref, h_ref, g_ref, rims, t)
@@ -429,16 +417,16 @@
     lax.fori_loop(2, L - 2, body, 0)
 
 
-def inside(s, lab, kap, rims, h, g, t, after):
+def inside(s, h, g, rims, t, after):
     return pl.pallas_call(
         inside_kernel,
-        out_shape=(jax.ShapeDtypeStruct(s.shape, jnp.float32),) * 3,
-        in_specs=[VMEM, VMEM, SMEM] + [VMEM] * 4 + [ANY],
-        out_specs=[VMEM] * 3,
-        input_output_aliases={4: 0, 5: 1, 6: 2},
-        compiler_params=pltpu.CompilerParams(vmem_limit_bytes=28 * MIB),
+        out_shape=jax.ShapeDtypeStruct(s.shape, jnp.float32),
+        in_specs=[VMEM] * 5 + [ANY],
+        out_specs=VMEM,
+        input_output_aliases={4: 0},
+        compiler_params=pltpu.CompilerParams(vmem_limit_bytes=24 * MIB),
         name="inside",
-    )(s, lab, kap, rims, h, g, t, after)
+    )(s, h, g, rims, t, after)
 
 
 def last_kernel(t_ref, h_ref, g_ref, rims, out, buf, sem):
@@ -476,7 +464,6 @@
         out_specs=HBM,
         scratch_shapes=[pltpu.VMEM(t.shape, jnp.float32), pltpu.SemaphoreType.DMA((L,))],
         compiler_params=pltpu.CompilerParams(vmem_limit_bytes=24 * MIB),
-        cost_estimate=lasts(5.5),
         name="last_layers",
     )(t, h, g, rims)
 
@@ -484,6 +471,11 @@
 def near_of(side):
     me = lax.axis_index("tier")
     return (me ^ 1, me ^ 2) if side == 0 else (me ^ 2, me ^ 1)
+
+
+def routes(tier, tile):
+    odd = tile % 2
+    return tier ^ (1 + odd), tier ^ (2 - odd)
 
 
 def entries(tiers):
@@ -499,133 +491,169 @@
     return listed
 
 
+def rim_entries(tiers):
+    me = lax.axis_index("tier")
+    if tiers != 4:
+        return [(me, q) for q in range(tiers)]
+    near, target = routes(me, lax.axis_index("tile"))
+    return [(who, source) for who in (target, me) for source in (me, near)]
+
+
 def table_kernel(tiers, ops, table, rim_table):
     regions = ops.shape[0]
-    me = lax.axis_index("tier")
     for k, (i, j) in enumerate(entries(tiers)):
         for g in range(regions):
             table[k, g] = jnp.full((ROWS, LANES), ops[g, i, j], jnp.float32)
     lane, upper = lane_ids(), row_ids() < 4
-    for q in range(tiers):
-        source = me ^ q if tiers == 4 else q
+    for q, (who, source) in enumerate(rim_entries(tiers)):
         for k in range(2):
             value = jnp.zeros((ROWS, LANES), jnp.float32)
             for g in range(regions):
-                a, b = ops[g, 2 * me, 2 * source + k], ops[g, 2 * me + 1, 2 * source + 1 - k]
+                a, b = ops[g, 2 * who, 2 * source + k], ops[g, 2 * who + 1, 2 * source + 1 - k]
                 value = jnp.where(lane == g, jnp.where(upper, a, b), value)
             rim_table[2 * q + k] = value
 
 
 def make_tables(tiers, ops):
     regions = ops.shape[0]
-    count = 32 if tiers == 4 else 4 * tiers
+    f32 = jnp.float32
+    count, rims = (32, 8) if tiers == 4 else (4 * tiers, 2 * tiers)
     return pl.pallas_call(
         functools.partial(table_kernel, tiers),
-        out_shape=(
-            jax.ShapeDtypeStruct((count, regions, ROWS, LANES), jnp.float32),
-            jax.ShapeDtypeStruct((2 * tiers, ROWS, LANES), jnp.float32),
-        ),
+        out_shape=(pltpu.VMEM((count, regions, ROWS, LANES), f32), pltpu.VMEM((rims, ROWS, LANES), f32)),
         in_specs=[SMEM],
         out_specs=[VMEM, VMEM],
         compiler_params=pltpu.CompilerParams(vmem_limit_bytes=16 * MIB),
-        cost_estimate=lasts(1.4),
         name="make_tables",
     )(ops)
 
 
-def product(table, at, zone, refs, partial, base, c, S, put):
+def product(table, at, zone, refs, partial, base, put):
     regions = table.shape[1]
-    lanes = pl.ds(pl.multiple_of(c * LANES, LANES), LANES)
-    whole = pl.ds(pl.multiple_of(base + c * LANES, LANES), LANES)
-    for r0 in range(0, S, 2):
-        rows = [pl.ds(ROWS * r, ROWS) for r in range(r0, min(S, r0 + 2))]
-        zones = [zone[x, whole] for x in rows]
-        for i in range(2):
-            totals = [None] * len(rows)
-            for j, (ref, index) in enumerate(refs):
-                values = [table[at + i * len(refs) + j, g] for g in range(regions)]
+    R, W = refs[0][0].shape[1:]
+    S = R // ROWS
+
+    def body(c, _):
+        lanes = pl.ds(pl.multiple_of(c * LANES, LANES), LANES)
+        whole = pl.ds(pl.multiple_of(base + c * LANES, LANES), LANES)
+        for r0 in range(0, S, 2):
+            rows = [pl.ds(ROWS * r, ROWS) for r in range(r0, min(S, r0 + 2))]
+            zones = [zone[x, whole] for x in rows]
+            for i in range(2):
+                totals = [None] * len(rows)
+                for j, (ref, index) in enumerate(refs):
+                    values = [table[at + i * len(refs) + j, g] for g in range(regions)]
+                    for k, x in enumerate(rows):
+                        term = choose(values, zones[k]) * ref[index, x, lanes]
+                        totals[k] = term if totals[k] is None else totals[k] + term
                 for k, x in enumerate(rows):
-                    term = choose(values, zones[k]) * ref[index, x, lanes]
-                    totals[k] = term if totals[k] is None else totals[k] + term
-            for k, x in enumerate(rows):
-                for ref in partial:
-                    totals[k] = totals[k] + ref[i, x, lanes]
-                put(i, x, lanes, whole, totals[k])
-
-
-def combine_kernel(table, zone, left, left_x, right, right_y, _, to_y, to_x):
-    _, R, half = left.shape
-
-    def body(c, _):
-        for side, (out, own, other) in enumerate(((to_y, left, left_x), (to_x, right, right_y))):
-
-            def put(i, rows, lanes, whole, value, out=out):
-                out[i, rows, lanes] = value
-
-            refs = [(own, 0), (own, 1), (other, 0), (other, 1)]
-            product(table, 16 * side, zone, refs, [], side * half, c, R // ROWS, put)
+                    for ref in partial:
+                        totals[k] = totals[k] + ref[i, x, lanes]
+                    put(i, x, lanes, whole, totals[k])
         return 0
 
-    lax.fori_loop(0, half // LANES, body, 0)
-
-
-def combine(table, zone, left, left_x, right, right_y, after):
+    lax.fori_loop(0, W // LANES, body, 0)
+
+
+def both(own, near):
+    return [(own, 0), (own, 1), (near, 0), (near, 1)]
+
+
+def put_in(out):
+    def put(i, rows, lanes, whole, value):
+        out[i, rows, lanes] = value
+
+    return put
+
+
+def way_of_tile():
+    return lax.axis_index("tile") % 2
+
+
+def combine_kernel(table, zone, own, near, _, out):
+    product(table, 16 * way_of_tile(), zone, both(own, near), [], 0, put_in(out))
+
+
+def combine(table, zone, own, near, after):
     return pl.pallas_call(
         combine_kernel,
-        out_shape=(jax.ShapeDtypeStruct(left.shape, jnp.float32),) * 2,
+        out_shape=pltpu.VMEM(own.shape, jnp.float32),
+        in_specs=[VMEM] * 4 + [ANY],
+        out_specs=VMEM,
+        compiler_params=pltpu.CompilerParams(vmem_limit_bytes=16 * MIB),
+        name="combine",
+    )(table, zone, own, near, after)
+
+
+def combine_halves_kernel(table, zone, left, left_x, right, right_y, _, to_y, to_x):
+    product(table, 0, zone, both(left, left_x), [], 0, put_in(to_y))
+    product(table, 16, zone, both(right, right_y), [], left.shape[2], put_in(to_x))
+
+
+def combine_halves(table, zone, left, left_x, right, right_y, after):
+    return pl.pallas_call(
+        combine_halves_kernel,
+        out_shape=(pltpu.VMEM(left.shape, jnp.float32),) * 2,
         in_specs=[VMEM] * 6 + [ANY],
         out_specs=[VMEM, VMEM],
         compiler_params=pltpu.CompilerParams(vmem_limit_bytes=16 * MIB),
-        cost_estimate=lasts(0.75),
-        name="combine",
+        name="combine_halves",
     )(table, zone, left, left_x, right, right_y, after)
 
 
-def solve(tiers, table, zone, groups, R, half, put, after=None):
-    for side, group in enumerate(groups):
-        if tiers == 4:
-            own, other, part = group
-            refs, partial, at = [(own, 0), (own, 1), (other, 0), (other, 1)], [part], 16 * side + 8
-        else:
-            refs, partial, at = [(group[0], k) for k in range(2 * tiers)], [], 0
-
-        def body(c, _):
-            product(table, at, zone, refs, partial, side * half, c, R // ROWS, put)
-            return 0
-
-        lax.fori_loop(0, half // LANES, body, 0)
-        if after is not None:
-            after(side)
-
-
-def bond_kernel(tiers, zone, table, rim_table, aux, heat, h_ref, t_in, *refs):
+def rim_product(rim_table, pairs, aux, lanes):
+    zones = aux[:, lanes].astype(jnp.int32)
+    zones = jnp.where(row_ids() < 4, pltpu.roll(zones, 4, 0), zones)
+    value = None
+    for at, planes in pairs:
+        for k, x in enumerate((planes, pltpu.roll(planes, 4, 0))):
+            term = lookup(rim_table[at + k], zones) * x
+            value = term if value is None else value + term
+    return value
+
+
+def combine_rim_kernel(rim_table, aux, own, near, out):
+    for c in range(own.shape[1] // LANES):
+        lanes = pl.ds(c * LANES, LANES)
+        out[:, lanes] = rim_product(rim_table, [(0, own[:, lanes]), (2, near[:, lanes])], aux, lanes)
+
+
+def combine_rim(rim_table, aux, own, near):
+    return pl.pallas_call(
+        combine_rim_kernel,
+        out_shape=pltpu.VMEM(own.shape, jnp.float32),
+        in_specs=[VMEM] * 4,
+        out_specs=VMEM,
+        compiler_params=pltpu.CompilerParams(vmem_limit_bytes=16 * MIB),
+        name="combine_rim",
+    )(rim_table, aux, own, near)
+
+
+def bond_kernel(tiers, zone, table, rim_table, aux, heat, h_ref, g_ref, t_in, *refs):
     pairs = tiers == 4
     per = 3 if pairs else 1
-    groups, refs = (refs[:per], refs[per : 2 * per]), refs[2 * per :]
-    edge_refs, (t, out_left, out_right, rim) = refs[:-4], refs[-4:]
+    arrays, edges, (t, left, right, rim) = refs[:per], refs[per : 2 * per], refs[2 * per :]
     L, R, W = t.shape
-    half, C = W // 2, W // LANES
+    C = W // LANES
     row = row_ids()
 
     def put(i, rows, lanes, whole, value):
-        t[i * (L - 1), rows, whole] = value
-
-    solve(tiers, table, zone, groups, R, half, put)
+        t[i * (L - 1), rows, lanes] = value
+
+    if pairs:
+        own, near, part = arrays
+        product(table, 16 * way_of_tile() + 8, zone, both(own, near), [part], 0, put)
+    else:
+        product(table, 0, zone, [(arrays[0], k) for k in range(2 * tiers)], [], 0, put)
     gone = ((row % 4 == 0) & jnp.logical_not(above_exists())) | ((row % 4 == 3) & jnp.logical_not(below_exists()))
 
     for c in range(C):
         lanes = pl.ds(c * LANES, LANES)
         if pairs:
-            tiles = [ref[:, lanes] for ref in edge_refs]
+            tiles = [(4, edges[0][:, lanes]), (6, edges[1][:, lanes])]
+            value = rim_product(rim_table, tiles, aux, lanes) + edges[2][:, lanes]
         else:
-            tiles = [edge_refs[0][q, :, lanes] for q in range(tiers)]
-        zones = aux[:, lanes].astype(jnp.int32)
-        zones = jnp.where(row < 4, pltpu.roll(zones, 4, 0), zones)
-        value = None
-        for q, mine in enumerate(tiles):
-            for k, x in enumerate((mine, pltpu.roll(mine, 4, 0))):
-                entry = jnp.take_along_axis(rim_table[2 * q + k], zones, axis=1, mode="promise_in_bounds")
-                value = entry * x if value is None else value + entry * x
+            value = rim_product(rim_table, [(2 * q, edges[0][q, :, lanes]) for q in range(tiers)], aux, lanes)
         value = jnp.where(gone, 0.0, value)
         rim[:, lanes] = value
         for i in range(2):
@@ -640,6 +668,9 @@
 
         def get_h(r, c):
             return h_ref[(own,) + tile(r, c)]
+
+        def get_g(r, c):
+            return g_ref[(own,) + tile(r, c)]
 
         def get_z(r, c, s, h):
             at = (near,) + tile(r, c)
@@ -657,17 +688,15 @@
             )
 
         def put_out(r, c, value):
-            if c < C // 2:
-                out_left[(p,) + tile(r, c)] = value
-            else:
-                out_right[(p,) + tile(r, c - C // 2)] = value
-
-        stencil(R, W, get_s, get_h, get_z, halo, put_out)
-
-
-def bond(tiers, zone, tables, aux, heat, h, t, left, right, edges):
-    R, W = zone.shape
-    args = (zone, *tables, aux, heat, h, t, *left, *right, *edges)
+            out, c = (left, c) if c < C // 2 else (right, c - C // 2)
+            out[(p,) + tile(r, c)] = value
+
+        stencil(R, W, get_s, get_h, get_z, halo, put_out, get_g=get_g)
+
+
+def bond(tiers, zone, tables, aux, heat, h, g, t, arrays, edges):
+    _, R, W = t.shape
+    args = (zone, *tables, aux, heat, h, g, t, *arrays, *edges)
     f32 = jnp.float32
     return pl.pallas_call(
         functools.partial(bond_kernel, tiers),
@@ -678,10 +707,9 @@
         ),
         in_specs=[VMEM] * len(args),
         out_specs=[VMEM] * 3,
-        input_output_aliases={6: 0},
         scratch_shapes=[pltpu.VMEM((ROWS, W), f32)],
-        compiler_params=pltpu.CompilerParams(vmem_limit_bytes=20 * MIB),
-        cost_estimate=lasts(3.3),
+        input_output_aliases={7: 0},
+        compiler_params=pltpu.CompilerParams(vmem_limit_bytes=24 * MIB),
         name="bond",
     )(*args)
 
@@ -692,22 +720,23 @@
     _, out, buf, sem = refs[2 * per :]
     L, R, W = out.shape
     half = W // 2
-    copies = []
 
     def put(i, rows, lanes, whole, value):
         buf[i, rows, whole] = value
 
-    def after(side):
+    copies = []
+    for side, group in enumerate(groups):
+        if tiers == 4:
+            product(table, 16 * side + 8, zone, both(group[0], group[1]), [group[2]], side * half, put)
+        else:
+            product(table, 0, zone, [(group[0], k) for k in range(2 * tiers)], [], side * half, put)
         lanes = pl.ds(side * half, half)
         for i in range(2):
-            copies.append(
-                pltpu.make_async_copy(
-                    buf.at[i, :, lanes], out.at[i * (L - 1), :, lanes], sem.at[2 * side + i]
-                )
+            copy = pltpu.make_async_copy(
+                buf.at[i, :, lanes], out.at[i * (L - 1), :, lanes], sem.at[2 * side + i]
             )
-            copies[-1].start()
-
-    solve(tiers, table, zone, groups, R, half, put, after)
+            copy.start()
+            copies.append(copy)
     for copy in copies:
         copy.wait()
 
@@ -723,7 +752,6 @@
         scratch_shapes=[pltpu.VMEM((2, R, W), jnp.float32), pltpu.SemaphoreType.DMA((4,))],
         input_output_aliases={len(args) - 1: 0},
         compiler_params=pltpu.CompilerParams(vmem_limit_bytes=16 * MIB),
-        cost_estimate=lasts(1.6),
         name="final_planes",
     )(*args)
 
@@ -737,35 +765,52 @@
     return gathered.reshape((tiers * value.shape[0],) + value.shape[1:]) if value.ndim == 3 else gathered
 
 
-def exchange(tiers, table, zone, left, right, after):
+def along(value, way, tiers, tiles):
+    places = [(tier, tile) for tier in range(tiers) for tile in range(tiles)]
+    pairs = [(tier * tiles + tile, routes(tier, tile)[way] * tiles + tile) for tier, tile in places]
+    return lax.ppermute(value, ("tier", "tile"), pairs)
+
+
+def exchange(tiers, tiles, table, zone, planes, after):
     if tiers != 4:
-        return (every(left, tiers),), (every(right, tiers),), left
+        return (every(planes, tiers),)
+    near = along(planes, 0, tiers, tiles)
+    return planes, near, along(combine(table, zone, planes, near, after), 1, tiers, tiles)
+
+
+def exchange_rim(tiers, tiles, rim_table, aux, edges):
+    if tiers != 4:
+        return (every(edges, tiers),)
+    near = along(edges, 0, tiers, tiles)
+    return edges, near, along(combine_rim(rim_table, aux, edges, near), 1, tiers, tiles)
+
+
+def exchange_halves(tiers, table, zone, left, right, after):
+    if tiers != 4:
+        return (every(left, tiers),), (every(right, tiers),)
     left_x, right_y = across(left, 1, tiers), across(right, 2, tiers)
-    to_y, to_x = combine(table, zone, left, left_x, right, right_y, after)
-    return (left, left_x, across(to_y, 2, tiers)), (right, right_y, across(to_x, 1, tiers)), to_y
+    to_y, to_x = combine_halves(table, zone, left, left_x, right, right_y, after)
+    return (left, left_x, across(to_y, 2, tiers)), (right, right_y, across(to_x, 1, tiers))
 
 
 def local(warming, substance, zone, patch, kap, power, ops):
     tiers, tiles = lax.axis_size("tier"), lax.axis_size("tile")
     s, lab, patch = warming[0], substance[0], patch[0]
 
-    left, right, heat, swap_a, swap_b, s, lab = begin(s, lab, patch, zone, kap, power)
+    planes, heat, swap_a, swap_b, s, lab = begin(s, lab, patch, zone, kap, power)
     pairs = [(i, i ^ 1) for i in range(tiles) if i ^ 1 < tiles]
     got_a = lax.ppermute(swap_a, "tile", pairs)
     pairs = [(i, ((i - 1) ^ 1) + 1) for i in range(1, tiles - 1 + tiles % 2)]
     got_b = lax.ppermute(swap_b, "tile", pairs)
     tables = make_tables(tiers, ops)
-    left, right, sent = exchange(tiers, tables[0], zone, left, right, heat)
+    h, g = faces(lab, kap)
+    arrays = exchange(tiers, tiles, tables[0], zone, planes, h)
     edges, rims, aux = edge_rows(swap_a, swap_b, got_a, got_b)
-    h, g = faces(lab, kap, edges, sent)
-    if tiers == 4:
-        edges = (edges, across(edges, 1, tiers), across(edges, 2, tiers), across(edges, 3, tiers))
-    else:
-        edges = (every(edges, tiers),)
+    edges = exchange_rim(tiers, tiles, tables[1], aux, edges)
     t = outer(s, h, g, rims)
-    t, left, right = bond(tiers, zone, tables, aux, heat, h, t, left, right, edges)
-    h, g, t = inside(s, lab, kap, rims, h, g, t, left)
-    left, right, _ = exchange(tiers, tables[0], zone, left, right, t)
+    t, left, right = bond(tiers, zone, tables, aux, heat, h, g, t, arrays, edges)
+    t = inside(s, h, g, rims, t, left)
+    left, right = exchange_halves(tiers, tables[0], zone, left, right, t)
     out = last_layers(t, h, g, rims)
     out = final_planes(tiers, zone, tables[0], left, right, out)
     return out[None]

time: 53.6 us -> 51.5 us (0.961)
  starting transfers between devices: 16 us -> 11.1 us
  waiting for transfers between devices: 7.55 us -> 12 us
  Pallas kernels: 29.8 us -> 28.1 us
    ppermute x11 -> x4, starting transfers between devices: 14.7 us -> 3.62 us  [across(): return lax.ppermute(value, 'tier', [(i, i ^ bits) for i in range(tiers)])]
    ppermute x0 -> x4, waiting for transfers between devices: none -> 7.3 us  [along(): return lax.ppermute(value, ('tier', 'tile'), pairs)]
    ppermute x0 -> x4, starting transfers between devices: none -> 6.74 us  [along(): return lax.ppermute(value, ('tier', 'tile'), pairs)]
    pallas_call x5 -> x6, Pallas kernels: 15.2 us -> 11.9 us  [the longest x1 4.84 us: begin(): pl.pallas_call(begin_kernel, out_shape=(pltpu.VMEM((2, R, W), f32), pltpu...]
    ppermute x11 -> x4, waiting for transfers between devices: 7.55 us -> 4.71 us  [across(): return lax.ppermute(value, 'tier', [(i, i ^ bits) for i in range(tiers)])]
    pallas_call x1, Pallas kernels: 2.16 us -> 4.83 us  [faces(): pl.pallas_call(faces_kernel, out_shape=(jax.ShapeDtypeStruct(lab.shape, j...]
    pallas_call x1, Pallas kernels: 5.81 us -> 5.27 us  [last_layers(): pl.pallas_call(last_kernel, out_shape=jax.ShapeDtypeStruct(t.shape, jnp.f...]
  transfers between devices with their start and end apart: 13 -> 10, of which waited for: 7 -> 7; matrix products, arithmetic and copies ran while one was open for 0% -> 0% of each run, Pallas kernels for 36% -> 35%
where the time goes in v3:
time: 51.5 us; the launch traced here: 51.3 us
  Pallas kernels  28.1 us (55%)
  waiting for transfers between devices  12 us (23%)
  starting transfers between devices  11.1 us (22%)
    ppermute x4, waiting for transfers between devices, along(): return lax.ppermute(value, ('tier', 'tile'), pairs)  7.3 us
    ppermute x4, starting transfers between devices, along(): return lax.ppermute(value, ('tier', 'tile'), pairs)  6.74 us
    pallas_call x1, Pallas kernels, last_layers(): pl.pallas_call(last_kernel, out_shape=jax.ShapeDtypeStruct(t.shape, jnp.f...  5.27 us
    pallas_call x1, Pallas kernels, begin(): pl.pallas_call(begin_kernel, out_shape=(pltpu.VMEM((2, R, W), f32), pltpu...  4.84 us
    pallas_call x1, Pallas kernels, faces(): pl.pallas_call(faces_kernel, out_shape=(jax.ShapeDtypeStruct(lab.shape, j...  4.83 us
    ppermute x4, waiting for transfers between devices, across(): return lax.ppermute(value, 'tier', [(i, i ^ bits) for i in range(tiers)])  4.71 us
    pallas_call x1, Pallas kernels, inside(): pl.pallas_call(inside_kernel, out_shape=jax.ShapeDtypeStruct(s.shape, jnp...  3.78 us
    ppermute x4, starting transfers between devices, across(): return lax.ppermute(value, 'tier', [(i, i ^ bits) for i in range(tiers)])  3.62 us
  transfers between devices with their start and end apart: 10, of which 7 were waited for; matrix products, arithmetic and copies ran while one was open for 0% of the time, Pallas kernels for 35%

profile of v3, /device:TPU:0, one launch (start us, length us, event | category | flops | bytes accessed | tf_op | source)
XLA Modules:
  0.0 51.3 jit_solution(16154167026824419883)
XLA Ops:
  0.0 0.0 copy-start.1
  0.0 0.0 copy-start.2
  0.0 4.8 %begin.1 = (f32[2,32,2048]{2,1,0:T(8,128)S(1)}, f32[32,2048]{1,0:T(8,128)S(1)}, f32[72,2048]{1,0:T(8,128)S(1)}, f32[72,2048]{1,0:T(8,128)S(1)}, f32[16,32,2048]{...) custom-call(f32[16,32,2048]{2,1,0:T(8,128)} %bitcast.4, s32[16,32,2048]{2,1,0:T(8,128)} %bitcast.5, s32[32,2048]{1,0:T(8,128)} %bitcast.6, ...), custom_call_target="tpu_custom_call" | custom-call | tf_op jit(solution)/shard_map/begin/pallas_call | solution.py:216
  4.8 0.0 copy-start
  4.9 3.0 %collective-permute-start.2 = (f32[2,32,2048]{2,1,0:T(8,128)S(1)}, f32[2,32,2048]{2,1,0:T(8,128)S(1)}, u32[]{:S(2)}, u32[]{:S(2)}) collective-permute-start(f32[2,32,2048]{2,1,0:T(8,128)S(1)} %get-tuple-element.34.own.refs_0_), channel_id=1, source_target_pairs={{0,8},{1,17},{2,10},{3,19},{4,12},{5,21},{6,14},{7,23},{8,0},{9,25... | collective-permute-start | bytes 1572872 | tf_op jit(solution)/shard_map/ppermute | solution.py:771
  7.9 0.0 collective-permute-start
  7.9 0.7 %collective-permute-start.1 = (f32[72,2048]{1,0:T(8,128)S(1)}, f32[72,2048]{1,0:T(8,128)S(1)}, u32[]{:S(2)}, u32[]{:S(2)}) collective-permute-start(f32[72,2048]{1,0:T(8,128)S(1)} %get-tuple-element.26.own_b), channel_id=1, source_target_pairs={{1,2},{2,1},{3,4},{4,3},{5,6},{6,5},{9,10},{10,9},{11,12},{12,11},... | collective-permute-start | bytes 1769480 | tf_op jit(solution)/shard_map/ppermute | solution.py:804
  8.6 0.0 copy-done.1
  8.6 1.4 %make_tables.1 = (f32[32,8,8,128]{3,2,1,0:T(8,128)S(1)}, f32[8,8,128]{2,1,0:T(8,128)S(1)}) custom-call(f32[8,8,8]{2,1,0:T(8,128)S(1)} %copy-done.1), custom_call_target="tpu_custom_call" | custom-call | tf_op jit(solution)/shard_map/make_tables/pallas_call | solution.py:521
  10.0 0.0 copy-done.2
  10.0 4.8 %faces.1 = (f32[16,32,2048]{2,1,0:T(8,128)S(1)}, f32[16,32,2048]{2,1,0:T(8,128)S(1)}) custom-call(s32[16,32,2048]{2,1,0:T(8,128)S(1)} %get-tuple-element.29.lab, f32[16]{0:T(128)S(1)} %copy-done.2), custom_call_target="tpu_custom_call" | custom-call | tf_op jit(solution)/shard_map/faces/pallas_call | solution.py:350
  14.9 0.2 collective-permute-done.2.near.refs_1_
  15.0 0.0 copy-done
  15.0 0.8 %combine.1 = f32[2,32,2048]{2,1,0:T(8,128)S(1)} custom-call(f32[32,8,8,128]{3,2,1,0:T(8,128)S(1)} %get-tuple-element.23.table, s32[32,2048]{1,0:T(8,128)S(1)} %copy-done, f32[2,32,2048]{2,1,0:T(8,128)S(1)} %get-tuple-element.34.own.refs_0_, f32[2,32,2048]{2,1,0:T(8,128)S(1)} %collective-permute-done.2.near.refs_1_, f32[16,32,2048]{2,1,0:T(8,128)S(1)} %get-tuple-element.30.h_ref._), custom_call_target="tpu_custom_call" | custom-call | tf_op jit(solution)/shard_map/combine/pallas_call | solution.py:578
  15.9 2.1 %collective-permute-start.3 = (f32[2,32,2048]{2,1,0:T(8,128)S(1)}, f32[2,32,2048]{2,1,0:T(8,128)S(1)}, u32[]{:S(2)}, u32[]{:S(2)}) collective-permute-start(f32[2,32,2048]{2,1,0:T(8,128)S(1)} %combine.1), channel_id=1, source_target_pairs={{0,16},{1,9},{2,18},{3,11},{4,20},{5,13},{6,22},{7,15},{8,24},{9,1... | collective-permute-start | bytes 1572872 | tf_op jit(solution)/shard_map/ppermute | solution.py:771
  18.0 0.0 collective-permute-done.got_a
  18.0 0.0 collective-permute-done.1.got_b
  18.0 1.0 %edge_rows.1 = (f32[8,2048]{1,0:T(8,128)S(1)}, f32[6,16,2048]{2,1,0:T(8,128)S(1)}, f32[8,2048]{1,0:T(8,128)S(1)}) custom-call(f32[72,2048]{1,0:T(8,128)S(1)} %get-tuple-element.25.own_a, f32[72,2048]{1,0:T(8,128)S(1)} %get-tuple-element.26.own_b, f32[72,2048]{1,0:T(8,128)S(1)} %collective-permute-done.got_a, f32[72,2048]{1,0:T(8,128)S(1)} %collective-permute-done.1.got_b), custom_call_target="tpu_custom_call" | custom-call | tf_op jit(solution)/shard_map/edge_rows/pallas_call | solution.py:299
  19.0 1.6 %collective-permute-start.4 = (f32[8,2048]{1,0:T(8,128)S(1)}, f32[8,2048]{1,0:T(8,128)S(1)}, u32[]{:S(2)}, u32[]{:S(2)}) collective-permute-start(f32[8,2048]{1,0:T(8,128)S(1)} %get-tuple-element.35.own.refs_3_), channel_id=1, source_target_pairs={{0,8},{1,17},{2,10},{3,19},{4,12},{5,21},{6,14},{7,23},{8,0},{9,25... | collective-permute-start | bytes 196616 | tf_op jit(solution)/shard_map/ppermute | solution.py:771
  20.5 3.5 %collective-permute-done.4.near.refs_4_ = f32[8,2048]{1,0:T(8,128)S(1)} collective-permute-done((f32[8,2048]{1,0:T(8,128)S(1)}, f32[8,2048]{1,0:T(8,128)S(1)}, u32[]{:S(2)}, u32[]{:S(2)}) %collective-permute-start.4) | collective-permute-done | bytes 65568 | tf_op jit(solution)/shard_map/ppermute | solution.py:771
  24.1 0.2 combine_rim.1
  24.3 0.1 collective-permute-start.5
  24.3 0.6 %outer.1.t_in = f32[16,32,2048]{2,1,0:T(8,128)S(1)} custom-call(f32[16,32,2048]{2,1,0:T(8,128)S(1)} %get-tuple-element.32.s_ref, f32[16,32,2048]{2,1,0:T(8,128)S(1)} %get-tuple-element.30.h_ref._, f32[16,32,2048]{2,1,0:T(8,128)S(1)} %get-tuple-element.31.g_ref, f32[6,16,2048]{2,1,0:T(8,128)S(1)} %get-tuple-element.33.rims), custom_call_target="tpu_custom_call" | custom-call | tf_op jit(solution)/shard_map/outer/pallas_call | solution.py:400
  25.0 3.6 %collective-permute-done.5.refs_5_ = f32[8,2048]{1,0:T(8,128)S(1)} collective-permute-done((f32[8,2048]{1,0:T(8,128)S(1)}, f32[8,2048]{1,0:T(8,128)S(1)}, u32[]{:S(2)}, u32[]{:S(2)}) %collective-permute-start.5) | collective-permute-done | bytes 65568 | tf_op jit(solution)/shard_map/ppermute | solution.py:771
  28.6 0.0 collective-permute-done.3.refs_2_
  28.6 2.9 %bond.1 = (f32[16,32,2048]{2,1,0:T(8,128)S(1)}, f32[2,32,1024]{2,1,0:T(8,128)S(1)}, f32[2,32,1024]{2,1,0:T(8,128)S(1)}) custom-call(s32[32,2048]{1,0:T(8,128)S(1)} %copy-done, f32[32,8,8,128]{3,2,1,0:T(8,128)S(1)} %get-tuple-element.23.table, f32[8,8,128]{2,1,0:T(8,128)S(1)} %get-tuple-element.24.rim_table, ...), custom_call_target="tpu_custom_call", output_to_operand_aliasing={{0}: (7, {})} | custom-call | tf_op jit(solution)/shard_map/bond/pallas_call | solution.py:701
  31.5 0.1 collective-permute-start.7
  31.6 2.0 %collective-permute-start.6 = (f32[2,32,1024]{2,1,0:T(8,128)S(1)}, f32[2,32,1024]{2,1,0:T(8,128)S(1)}, u32[]{:S(2)}, u32[]{:S(2)}) collective-permute-start(f32[2,32,1024]{2,1,0:T(8,128)S(1)} %get-tuple-element.36._.left.refs_0_), channel_id=1, source_target_pairs={{0,8},{8,0},{16,24},{24,16},{1,9},{9,1},{17,25},{25,17},{2,10},{10... | collective-permute-start | bytes 786440 | tf_op jit(solution)/shard_map/ppermute | solution.py:760
  33.6 3.8 %inside.1._.t_ref = f32[16,32,2048]{2,1,0:T(8,128)S(1)} custom-call(f32[16,32,2048]{2,1,0:T(8,128)S(1)} %get-tuple-element.32.s_ref, f32[16,32,2048]{2,1,0:T(8,128)S(1)} %get-tuple-element.30.h_ref._, f32[16,32,2048]{2,1,0:T(8,128)S(1)} %get-tuple-element.31.g_ref, f32[6,16,2048]{2,1,0:T(8,128)S(1)} %get-tuple-element.33.rims, ...), custom_call_target="tpu_custom_call", output_to_operand_aliasing={{}: (4, {})} | custom-call | tf_op jit(solution)/shard_map/inside/pallas_call | solution.py:421
  37.4 2.5 %collective-permute-done.7.right_y.refs_4_ = f32[2,32,1024]{2,1,0:T(8,128)S(1)} collective-permute-done((f32[2,32,1024]{2,1,0:T(8,128)S(1)}, f32[2,32,1024]{2,1,0:T(8,128)S(1)}, u32[]{:S(2)}, u32[]{:S(2)}) %collective-permute-start.7) | collective-permute-done | bytes 262176 | tf_op jit(solution)/shard_map/ppermute | solution.py:760
  39.9 0.7 %collective-permute-done.6.left_x.refs_1_ = f32[2,32,1024]{2,1,0:T(8,128)S(1)} collective-permute-done((f32[2,32,1024]{2,1,0:T(8,128)S(1)}, f32[2,32,1024]{2,1,0:T(8,128)S(1)}, u32[]{:S(2)}, u32[]{:S(2)}) %collective-permute-start.6) | collective-permute-done | bytes 262176 | tf_op jit(solution)/shard_map/ppermute | solution.py:760
  40.7 0.8 %combine_halves.1 = (f32[2,32,1024]{2,1,0:T(8,128)S(1)}, f32[2,32,1024]{2,1,0:T(8,128)S(1)}) custom-call(f32[32,8,8,128]{3,2,1,0:T(8,128)S(1)} %get-tuple-element.23.table, s32[32,2048]{1,0:T(8,128)S(1)} %copy-done, f32[2,32,1024]{2,1,0:T(8,128)S(1)} %get-tuple-element.36._.left.refs_0_, f32[2,32,1024]{2,1,0:T(8,128)S(1)} %collective-permute-done.6.left_x.refs_1_, ...), custom_call_target="tpu_custom_call" | custom-call | tf_op jit(solution)/shard_map/combine_halves/pallas_call | solution.py:594
  41.5 1.1 %collective-permute-start.8 = (f32[2,32,1024]{2,1,0:T(8,128)S(1)}, f32[2,32,1024]{2,1,0:T(8,128)S(1)}, u32[]{:S(2)}, u32[]{:S(2)}) collective-permute-start(f32[2,32,1024]{2,1,0:T(8,128)S(1)} %get-tuple-element.39), channel_id=1, source_target_pairs={{0,16},{8,24},{16,0},{24,8},{1,17},{9,25},{17,1},{25,9},{2,18},{10... | collective-permute-start | bytes 786440 | tf_op jit(solution)/shard_map/ppermute | solution.py:760
  42.5 0.5 collective-permute-start.9
  43.0 5.3 %last_layers.1.refs_6_ = f32[16,32,2048]{2,1,0:T(8,128)} custom-call(f32[16,32,2048]{2,1,0:T(8,128)S(1)} %inside.1._.t_ref, f32[16,32,2048]{2,1,0:T(8,128)S(1)} %get-tuple-element.30.h_ref._, f32[16,32,2048]{2,1,0:T(8,128)S(1)} %get-tuple-element.31.g_ref, f32[6,16,2048]{2,1,0:T(8,128)S(1)} %get-tuple-element.33.rims), custom_call_target="tpu_custom_call" | custom-call | tf_op jit(solution)/shard_map/last_layers/pallas_call | solution.py:460
  48.3 1.3 %collective-permute-done.8.refs_2_ = f32[2,32,1024]{2,1,0:T(8,128)S(1)} collective-permute-done((f32[2,32,1024]{2,1,0:T(8,128)S(1)}, f32[2,32,1024]{2,1,0:T(8,128)S(1)}, u32[]{:S(2)}, u32[]{:S(2)}) %collective-permute-start.8) | collective-permute-done | bytes 262176 | tf_op jit(solution)/shard_map/ppermute | solution.py:760
  49.7 0.1 collective-permute-done.9.refs_5_
  49.7 1.6 %final_planes.1 = f32[16,32,2048]{2,1,0:T(8,128)} custom-call(s32[32,2048]{1,0:T(8,128)S(1)} %copy-done, f32[32,8,8,128]{3,2,1,0:T(8,128)S(1)} %get-tuple-element.23.table, f32[2,32,1024]{2,1,0:T(8,128)S(1)} %get-tuple-element.36._.left.refs_0_, f32[2,32,1024]{2,1,0:T(8,128)S(1)} %collective-permute-done.6.left_x.refs_1_, ...), custom_call_target="tpu_custom_call", output_to_operand_aliasing={{}: (8, {})} | custom-call | tf_op jit(solution)/shard_map/final_planes/pallas_call | solution.py:747
Async XLA Ops:
  0.0 8.6 %copy-start.1 = (f32[8,8,8]{2,1,0:T(8,128)S(1)}, f32[8,8,8]{2,1,0:T(8,128)}, u32[]{:S(2)}) copy-start(f32[8,8,8]{2,1,0:T(8,128)} %ops.1) | copy-start | bytes 6148
  0.0 10.0 %copy-start.2 = (f32[16]{0:T(128)S(1)}, f32[16]{0:T(128)}, u32[]{:S(2)}) copy-start(f32[16]{0:T(128)} %kap.1) | copy-start | bytes 196
  4.8 10.2 %copy-start = (s32[32,2048]{1,0:T(8,128)S(1)}, s32[32,2048]{1,0:T(8,128)}, u32[]{:S(2)}) copy-start(s32[32,2048]{1,0:T(8,128)} %zone.7) | copy-start | bytes 786436
  4.9 10.2 %collective-permute-start.2 = (f32[2,32,2048]{2,1,0:T(8,128)S(1)}, f32[2,32,2048]{2,1,0:T(8,128)S(1)}, u32[]{:S(2)}, u32[]{:S(2)}) collective-permute-start(f32[2,32,2048]{2,1,0:T(8,128)S(1)} %get-tuple-element.34.own.refs_0_), channel_id=1, source_target_pairs={{0,8},{1,17},{2,10},{3,19},{4,12},{5,21},{6,14},{7,23},{8,0},{9,25... | collective-permute-start | bytes 1572872 | tf_op jit(solution)/shard_map/ppermute | solution.py:771
  7.9 10.1 %collective-permute-start = (f32[72,2048]{1,0:T(8,128)S(1)}, f32[72,2048]{1,0:T(8,128)S(1)}, u32[]{:S(2)}, u32[]{:S(2)}) collective-permute-start(f32[72,2048]{1,0:T(8,128)S(1)} %get-tuple-element.25.own_a), channel_id=1, source_target_pairs={{0,1},{1,0},{2,3},{3,2},{4,5},{5,4},{6,7},{7,6},{8,9},{9,8},{10,11... | collective-permute-start | bytes 1769480 | tf_op jit(solution)/shard_map/ppermute | solution.py:802
  7.9 10.1 %collective-permute-start.1 = (f32[72,2048]{1,0:T(8,128)S(1)}, f32[72,2048]{1,0:T(8,128)S(1)}, u32[]{:S(2)}, u32[]{:S(2)}) collective-permute-start(f32[72,2048]{1,0:T(8,128)S(1)} %get-tuple-element.26.own_b), channel_id=1, source_target_pairs={{1,2},{2,1},{3,4},{4,3},{5,6},{6,5},{9,10},{10,9},{11,12},{12,11},... | collective-permute-start | bytes 1769480 | tf_op jit(solution)/shard_map/ppermute | solution.py:804
  15.9 12.7 %collective-permute-start.3 = (f32[2,32,2048]{2,1,0:T(8,128)S(1)}, f32[2,32,2048]{2,1,0:T(8,128)S(1)}, u32[]{:S(2)}, u32[]{:S(2)}) collective-permute-start(f32[2,32,2048]{2,1,0:T(8,128)S(1)} %combine.1), channel_id=1, source_target_pairs={{0,16},{1,9},{2,18},{3,11},{4,20},{5,13},{6,22},{7,15},{8,24},{9,1... | collective-permute-start | bytes 1572872 | tf_op jit(solution)/shard_map/ppermute | solution.py:771
  19.0 5.1 %collective-permute-start.4 = (f32[8,2048]{1,0:T(8,128)S(1)}, f32[8,2048]{1,0:T(8,128)S(1)}, u32[]{:S(2)}, u32[]{:S(2)}) collective-permute-start(f32[8,2048]{1,0:T(8,128)S(1)} %get-tuple-element.35.own.refs_3_), channel_id=1, source_target_pairs={{0,8},{1,17},{2,10},{3,19},{4,12},{5,21},{6,14},{7,23},{8,0},{9,25... | collective-permute-start | bytes 196616 | tf_op jit(solution)/shard_map/ppermute | solution.py:771
  24.3 4.3 %collective-permute-start.5 = (f32[8,2048]{1,0:T(8,128)S(1)}, f32[8,2048]{1,0:T(8,128)S(1)}, u32[]{:S(2)}, u32[]{:S(2)}) collective-permute-start(f32[8,2048]{1,0:T(8,128)S(1)} %combine_rim.1), channel_id=1, source_target_pairs={{0,16},{1,9},{2,18},{3,11},{4,20},{5,13},{6,22},{7,15},{8,24},{9,1... | collective-permute-start | bytes 196616 | tf_op jit(solution)/shard_map/ppermute | solution.py:771
  31.5 8.4 %collective-permute-start.7 = (f32[2,32,1024]{2,1,0:T(8,128)S(1)}, f32[2,32,1024]{2,1,0:T(8,128)S(1)}, u32[]{:S(2)}, u32[]{:S(2)}) collective-permute-start(f32[2,32,1024]{2,1,0:T(8,128)S(1)} %get-tuple-element.37.right.refs_3_), channel_id=1, source_target_pairs={{0,16},{8,24},{16,0},{24,8},{1,17},{9,25},{17,1},{25,9},{2,18},{10... | collective-permute-start | bytes 786440 | tf_op jit(solution)/shard_map/ppermute | solution.py:760
  31.6 9.0 %collective-permute-start.6 = (f32[2,32,1024]{2,1,0:T(8,128)S(1)}, f32[2,32,1024]{2,1,0:T(8,128)S(1)}, u32[]{:S(2)}, u32[]{:S(2)}) collective-permute-start(f32[2,32,1024]{2,1,0:T(8,128)S(1)} %get-tuple-element.36._.left.refs_0_), channel_id=1, source_target_pairs={{0,8},{8,0},{16,24},{24,16},{1,9},{9,1},{17,25},{25,17},{2,10},{10... | collective-permute-start | bytes 786440 | tf_op jit(solution)/shard_map/ppermute | solution.py:760
  41.5 8.2 %collective-permute-start.8 = (f32[2,32,1024]{2,1,0:T(8,128)S(1)}, f32[2,32,1024]{2,1,0:T(8,128)S(1)}, u32[]{:S(2)}, u32[]{:S(2)}) collective-permute-start(f32[2,32,1024]{2,1,0:T(8,128)S(1)} %get-tuple-element.39), channel_id=1, source_target_pairs={{0,16},{8,24},{16,0},{24,8},{1,17},{9,25},{17,1},{25,9},{2,18},{10... | collective-permute-start | bytes 786440 | tf_op jit(solution)/shard_map/ppermute | solution.py:760
  42.5 7.2 %collective-permute-start.9 = (f32[2,32,1024]{2,1,0:T(8,128)S(1)}, f32[2,32,1024]{2,1,0:T(8,128)S(1)}, u32[]{:S(2)}, u32[]{:S(2)}) collective-permute-start(f32[2,32,1024]{2,1,0:T(8,128)S(1)} %get-tuple-element.40), channel_id=1, source_target_pairs={{0,8},{8,0},{16,24},{24,16},{1,9},{9,1},{17,25},{25,17},{2,10},{10... | collective-permute-start | bytes 786440 | tf_op jit(solution)/shard_map/ppermute | solution.py:760

commit v4 on v3

--- a/solution.py
+++ b/solution.py
@@ -110,6 +110,14 @@
     return (h + h_up) * (s_up - s) + (h + h_down) * (s_down - s)
 
 
+def collect(row, pieces):
+    value = None
+    for q, (source_tile, source) in enumerate(pieces):
+        moved = source_tile if q == source else pltpu.roll(source_tile, (q - source) % ROWS, 0)
+        value = moved if value is None else jnp.where(row == q, moved, value)
+    return value
+
+
 def begin_kernel(
     s_hbm, lab_hbm, patch_hbm, zone_hbm, kap_hbm, power_hbm,
     planes, heat, swap_a, swap_b, s_v, lab_v,
@@ -141,10 +149,21 @@
         copy.wait()
     values = splats(kap)
     heats = step_dt * jnp.broadcast_to(power[...], (ROWS, LANES))
-    for p in range(2):
-        for copy in layers[p]:
-            copy.wait()
-        own, near = (0, 1) if p == 0 else (L - 1, L - 2)
+
+    def warm(c, _):
+        lanes = pl.ds(pl.multiple_of(c * LANES, LANES), LANES)
+        for r in range(R // ROWS):
+            at = (pl.ds(ROWS * r, ROWS), lanes)
+            heat[at] = lookup(heats, patch[at])
+        return 0
+
+    lax.fori_loop(0, C, warm, 0)
+    for copy in layers[0] + layers[1]:
+        copy.wait()
+
+    def plane(p, _):
+        own, near = p * (L - 1), 1 + p * (L - 3)
+        heated = jnp.where(p == 0, 1.0, 0.0)
 
         def get_s(r, c):
             return s_v[(own,) + tile(r, c)]
@@ -154,17 +173,15 @@
 
         def get_z(r, c, s, h):
             h_near = choose(values, lab_v[(near,) + tile(r, c)])
-            flow = (h + h_near) * (s_v[(near,) + tile(r, c)] - s)
-            if p == 0:
-                value = lookup(heats, patch[tile(r, c)])
-                heat[tile(r, c)] = value
-                flow = flow + value
-            return flow
+            return (h + h_near) * (s_v[(near,) + tile(r, c)] - s) + heated * heat[tile(r, c)]
 
         def put(r, c, value):
             planes[(p,) + tile(r, c)] = value
 
         stencil(R, W, get_s, get_h, get_z, None, put)
+        return 0
+
+    lax.fori_loop(0, 2, plane, 0)
     row = row_ids()
     for copy in layers[2]:
         copy.wait()
@@ -179,18 +196,12 @@
                 for ref, at in ((s_v, 0), (lab_v, 2 * L)):
                     tiles = [ref[base + q, edge, lanes] for q in range(ROWS)]
                     for j, source in enumerate(rows):
-                        packed = tiles[source]
-                        for q in range(ROWS):
-                            if q != source:
-                                packed = jnp.where(row == q, pltpu.roll(tiles[q], (q - source) % ROWS, 0), packed)
+                        packed = collect(row, [(x, source) for x in tiles])
                         if ref is lab_v:
                             packed = choose(values, packed)
                         out[pl.ds(at + j * L + base, ROWS), lanes] = packed
-            last = rows[0] if k == 0 else rows[1]
-            warm = heat[edge, lanes]
             zones = zone_v[k, :, lanes].astype(jnp.float32)
-            pair = jnp.where(row == 0, pltpu.roll(warm, -last % ROWS, 0), pltpu.roll(zones, (1 - last) % ROWS, 0))
-            out[pl.ds(4 * L, ROWS), lanes] = pair
+            out[pl.ds(4 * L, ROWS), lanes] = collect(row, [(heat[edge, lanes], rows[k]), (zones, rows[k])])
             return 0
 
         lax.fori_loop(0, W // LANES, body, 0)
@@ -240,7 +251,85 @@
     return lax.axis_index("tile") < lax.axis_size("tile") - 1
 
 
-def edge_kernel(own_a, own_b, got_a, got_b, edges, rims, aux):
+def near_edge_kernel(own_a, own_b, got_a, got_b, edges, aux):
+    rows, W = own_a.shape
+    L = (rows - ROWS) // 4
+    col = lax.broadcasted_iota(jnp.int32, (ROWS, W), 1)
+    row = lax.broadcasted_iota(jnp.int32, (ROWS, W), 0)
+    odd = lax.axis_index("tile") % 2 == 1
+    above, below = above_exists(), below_exists()
+
+    def four_sides(at):
+        at = pl.ds(at, ROWS)
+        up = jnp.where(odd, own_a[at, :], own_b[at, :])
+        down = jnp.where(odd, own_b[at, :], own_a[at, :])
+        lo = jnp.where(above, jnp.where(odd, got_a[at, :], got_b[at, :]), 0.0)
+        hi = jnp.where(below, jnp.where(odd, got_b[at, :], got_a[at, :]), 0.0)
+        return lo, up, down, hi
+
+    def part(k):
+        first, second = 2 * k * L, 2 * k * L + L
+        a0, a1, b0, b1 = (four_sides(at) for at in (first, first + L - ROWS, second, second + L - ROWS))
+        end = ROWS - 1
+        return [
+            collect(
+                row,
+                [(a0[x], 0), (b0[x], 0), (a0[x], 1), (b0[x], 1)]
+                + [(a1[x], end), (b1[x], end), (a1[x], end - 1), (b1[x], end - 1)],
+            )
+            for x in range(4)
+        ]
+
+    def four(*pieces):
+        value = None
+        for k, (x, source) in enumerate(pieces):
+            moved = x if k == source else pltpu.roll(x, (k - source) % ROWS, 0)
+            value = moved if value is None else jnp.where(row % 4 == k, moved, value)
+        return value
+
+    def arrange(lo, up, down, hi):
+        centre = four((lo, 1), (up, 0), (down, 1), (hi, 0))
+        upper = four((lo, 0), (lo, 1), (down, 0), (down, 1))
+        lower = four((up, 0), (up, 1), (hi, 0), (hi, 1))
+        inward = four((lo, 3), (up, 2), (down, 3), (hi, 2))
+        return centre, upper, lower, inward
+
+    s, s_up, s_down, s_in = arrange(*part(0))
+    h, h_up, h_down, h_in = arrange(*part(1))
+
+    def toward(s_n, h_n):
+        return (h + h_n) * (s_n - s)
+
+    def moved(shift, gone):
+        return jnp.where(gone, 0.0, pltpu.roll(s, shift, 1)), jnp.where(gone, 0.0, pltpu.roll(h, shift, 1))
+
+    total = s + toward(s_up, h_up) + toward(s_down, h_down) + toward(s_in, h_in)
+    total = total + toward(*moved(1, col == 0)) + toward(*moved(W - 1, col == W - 1))
+    extra = four_sides(4 * L)
+    heat = four(*((x, 0) for x in extra))
+    total = total + jnp.where(row < 4, heat, 0.0)
+    gone = ((row % 4 == 0) & jnp.logical_not(above)) | ((row % 4 == 3) & jnp.logical_not(below))
+    edges[...] = jnp.where(gone, 0.0, total)
+    zones = four(*((x, 1) for x in extra))
+    aux[pl.ds(0, ROWS), :] = h
+    aux[pl.ds(ROWS, ROWS), :] = jnp.where(row < 4, zones, pltpu.roll(zones, 4, 0))
+    aux[pl.ds(2 * ROWS, ROWS), :] = s_in
+    aux[pl.ds(3 * ROWS, ROWS), :] = h_in
+
+
+def near_edges(own_a, own_b, got_a, got_b):
+    W = own_a.shape[1]
+    return pl.pallas_call(
+        near_edge_kernel,
+        out_shape=(pltpu.VMEM((ROWS, W), jnp.float32), pltpu.VMEM((4 * ROWS, W), jnp.float32)),
+        in_specs=[VMEM] * 4,
+        out_specs=[VMEM] * 2,
+        compiler_params=pltpu.CompilerParams(vmem_limit_bytes=16 * MIB),
+        name="near_edges",
+    )(own_a, own_b, got_a, got_b)
+
+
+def edge_kernel(own_a, own_b, got_a, got_b, _, rims):
     rows, W = own_a.shape
     L = (rows - ROWS) // 4
     col = lax.broadcasted_iota(jnp.int32, (L, W), 1)
@@ -275,39 +364,22 @@
 
         far, near = (0, 1) if side == 0 else (1, 0)
         sf, sn, hf, hn = (other(k * L, L) for k in (far, near, 2 + far, 2 + near))
-        s0, s1, h0, h1 = (own(k * L, L) for k in (1 - near, near, 3 - near, 2 + near))
-        out = jnp.where(exists, step(sf, hf, sn, hn, s0, h0), 0.0)
-        inner = step(sn, hn, s0, h0, s1, h1)
+        s0, h0 = own((1 - near) * L, L), own((3 - near) * L, L)
         rims[2 * side] = sn
         rims[2 * side + 1] = hn
-        rims[4 + side] = out
-        k_out, k_in = (0, 1) if side == 0 else (3, 2)
-        edges[pl.ds(k_out, 1), :] = out[0:1] + other(4 * L, 1)
-        edges[pl.ds(k_in, 1), :] = inner[0:1] + own(4 * L, 1)
-        edges[pl.ds(4 + k_out, 1), :] = out[L - 1 : L]
-        edges[pl.ds(4 + k_in, 1), :] = inner[L - 1 : L]
-        aux[pl.ds(2 * side, 1), :] = hn[0:1]
-        aux[pl.ds(2 * side + 1, 1), :] = hn[L - 1 : L]
-        aux[pl.ds(4 + k_out, 1), :] = other(4 * L + 1, 1)
-        aux[pl.ds(4 + k_in, 1), :] = own(4 * L + 1, 1)
-
-
-def edge_rows(own_a, own_b, got_a, got_b):
+        rims[4 + side] = jnp.where(exists, step(sf, hf, sn, hn, s0, h0), 0.0)
+
+
+def edge_rows(own_a, own_b, got_a, got_b, after):
     rows, W = own_a.shape
-    L = (rows - ROWS) // 4
-    f32 = jnp.float32
     return pl.pallas_call(
         edge_kernel,
-        out_shape=(
-            jax.ShapeDtypeStruct((ROWS, W), f32),
-            jax.ShapeDtypeStruct((6, L, W), f32),
-            jax.ShapeDtypeStruct((ROWS, W), f32),
-        ),
-        in_specs=[VMEM] * 4,
-        out_specs=[VMEM] * 3,
+        out_shape=pltpu.VMEM((6, (rows - ROWS) // 4, W), jnp.float32),
+        in_specs=[VMEM] * 4 + [ANY],
+        out_specs=VMEM,
         compiler_params=pltpu.CompilerParams(vmem_limit_bytes=16 * MIB),
         name="edge_rows",
-    )(own_a, own_b, got_a, got_b)
+    )(own_a, own_b, got_a, got_b, after)
 
 
 def pick(ref, base, l, lanes, row):
@@ -343,7 +415,10 @@
 
 
 def faces_kernel(lab, kap, h_out, g_out):
-    fill_faces(0, lab.shape[0], lab, splats(kap), h_out, g_out)
+    L = lab.shape[0]
+    values = splats(kap)
+    fill_faces(0, 3, lab, values, h_out, g_out)
+    fill_faces(L - 3, L, lab, values, h_out, g_out)
 
 
 def faces(lab, kap):
@@ -357,6 +432,22 @@
     )(lab, kap)
 
 
+def more_faces_kernel(lab, kap, h_in, g_in, _, h_out, g_out):
+    fill_faces(3, lab.shape[0] - 3, lab, splats(kap), h_out, g_out)
+
+
+def more_faces(lab, kap, h, g, after):
+    return pl.pallas_call(
+        more_faces_kernel,
+        out_shape=(jax.ShapeDtypeStruct(lab.shape, jnp.float32),) * 2,
+        in_specs=[VMEM, SMEM, VMEM, VMEM, ANY],
+        out_specs=[VMEM] * 2,
+        input_output_aliases={2: 0, 3: 1},
+        compiler_params=pltpu.CompilerParams(vmem_limit_bytes=24 * MIB),
+        name="more_faces",
+    )(lab, kap, h, g, after)
+
+
 def layer_step(l, s_ref, h_ref, g_ref, halo, put):
     _, R, W = s_ref.shape
 
@@ -376,42 +467,52 @@
     stencil(R, W, get_s, get_h, get_z, halo, put, get_g=get_g)
 
 
-def first_step(l, s_ref, h_ref, g_ref, rims, t):
+def first_step(l, s_ref, h_ref, g_ref, halo, t):
     def put(r, c, value):
         t[(l,) + tile(r, c)] = value
 
-    def halo(c):
-        return halo_rows(rims, (0, 2), pl.ds(LANES * c, LANES), l)
-
     layer_step(l, s_ref, h_ref, g_ref, halo, put)
 
 
-def outer_kernel(s_ref, h_ref, g_ref, rims, t):
+def wall(aux, k, p, lanes):
+    rows = aux[pl.ds(k * ROWS, ROWS), lanes]
+    return pltpu.roll(rows, (2 - p) * 4 % ROWS, 0), pltpu.roll(rows, 4 - 4 * p, 0)
+
+
+def outer_kernel(s_ref, h_ref, g_ref, aux, t):
     L = s_ref.shape[0]
 
-    def body(k, _):
-        first_step(1 + k * (L - 3), s_ref, h_ref, g_ref, rims, t)
+    def body(p, _):
+        def halo(c):
+            lanes = pl.ds(LANES * c, LANES)
+            (sa, sb), (ha, hb) = wall(aux, 2, p, lanes), wall(aux, 3, p, lanes)
+            return sa, ha, sb, hb
+
+        first_step(1 + p * (L - 3), s_ref, h_ref, g_ref, halo, t)
         return 0
 
     lax.fori_loop(0, 2, body, 0)
 
 
-def outer(s, h, g, rims):
+def outer(s, h, g, aux):
     return pl.pallas_call(
         outer_kernel,
-        out_shape=jax.ShapeDtypeStruct(s.shape, jnp.float32),
+        out_shape=pltpu.VMEM(s.shape, jnp.float32),
         in_specs=[VMEM] * 4,
         out_specs=VMEM,
         compiler_params=pltpu.CompilerParams(vmem_limit_bytes=20 * MIB),
         name="outer",
-    )(s, h, g, rims)
+    )(s, h, g, aux)
 
 
 def inside_kernel(s_ref, h_ref, g_ref, rims, t_in, _, t):
     L = s_ref.shape[0]
 
     def body(l, _):
-        first_step(l, s_ref, h_ref, g_ref, rims, t)
+        def halo(c):
+            return halo_rows(rims, (0, 2), pl.ds(LANES * c, LANES), l)
+
+        first_step(l, s_ref, h_ref, g_ref, halo, t)
         return 0
 
     lax.fori_loop(2, L - 2, body, 0)
@@ -602,8 +703,7 @@
 
 
 def rim_product(rim_table, pairs, aux, lanes):
-    zones = aux[:, lanes].astype(jnp.int32)
-    zones = jnp.where(row_ids() < 4, pltpu.roll(zones, 4, 0), zones)
+    zones = aux[pl.ds(ROWS, ROWS), lanes].astype(jnp.int32)
     value = None
     for at, planes in pairs:
         for k, x in enumerate((planes, pltpu.roll(planes, 4, 0))):
@@ -612,59 +712,107 @@
     return value
 
 
-def combine_rim_kernel(rim_table, aux, own, near, out):
+def combine_rim_kernel(rim_table, aux, own, near, _, out):
     for c in range(own.shape[1] // LANES):
         lanes = pl.ds(c * LANES, LANES)
         out[:, lanes] = rim_product(rim_table, [(0, own[:, lanes]), (2, near[:, lanes])], aux, lanes)
 
 
-def combine_rim(rim_table, aux, own, near):
+def combine_rim(rim_table, aux, own, near, after):
     return pl.pallas_call(
         combine_rim_kernel,
         out_shape=pltpu.VMEM(own.shape, jnp.float32),
-        in_specs=[VMEM] * 4,
+        in_specs=[VMEM] * 4 + [ANY],
         out_specs=VMEM,
         compiler_params=pltpu.CompilerParams(vmem_limit_bytes=16 * MIB),
         name="combine_rim",
-    )(rim_table, aux, own, near)
+    )(rim_table, aux, own, near, after)
+
+
+def own_kernel(table, rim_table, aux, zone, own, near, edges, edges_near, _, base, rim_base):
+    for c in range(edges.shape[1] // LANES):
+        lanes = pl.ds(c * LANES, LANES)
+        rim_base[:, lanes] = rim_product(rim_table, [(4, edges[:, lanes]), (6, edges_near[:, lanes])], aux, lanes)
+    product(table, 16 * way_of_tile() + 8, zone, both(own, near), [], 0, put_in(base))
+
+
+def own_part(tables, aux, zone, own, near, edges, edges_near, after):
+    return pl.pallas_call(
+        own_kernel,
+        out_shape=(pltpu.VMEM(own.shape, jnp.float32), pltpu.VMEM(edges.shape, jnp.float32)),
+        in_specs=[VMEM] * 8 + [ANY],
+        out_specs=[VMEM] * 2,
+        compiler_params=pltpu.CompilerParams(vmem_limit_bytes=16 * MIB),
+        name="own_part",
+    )(*tables, aux, zone, own, near, edges, edges_near, after)
+
+
+def own_halves_kernel(table, zone, left, left_x, right, right_y, _, base):
+    half = left.shape[2]
+
+    def put(i, rows, lanes, whole, value):
+        base[i, rows, whole] = value
+
+    product(table, 8, zone, both(left, left_x), [], 0, put)
+    product(table, 24, zone, both(right, right_y), [], half, put)
+
+
+def own_halves(table, zone, left, left_x, right, right_y, after):
+    return pl.pallas_call(
+        own_halves_kernel,
+        out_shape=pltpu.VMEM((2,) + zone.shape, jnp.float32),
+        in_specs=[VMEM] * 6 + [ANY],
+        out_specs=VMEM,
+        compiler_params=pltpu.CompilerParams(vmem_limit_bytes=16 * MIB),
+        name="own_halves",
+    )(table, zone, left, left_x, right, right_y, after)
 
 
 def bond_kernel(tiers, zone, table, rim_table, aux, heat, h_ref, g_ref, t_in, *refs):
     pairs = tiers == 4
-    per = 3 if pairs else 1
-    arrays, edges, (t, left, right, rim) = refs[:per], refs[per : 2 * per], refs[2 * per :]
+    arrays, (t, left, right, rim) = refs[:-4], refs[-4:]
     L, R, W = t.shape
     C = W // LANES
     row = row_ids()
-
-    def put(i, rows, lanes, whole, value):
-        t[i * (L - 1), rows, lanes] = value
-
     if pairs:
-        own, near, part = arrays
-        product(table, 16 * way_of_tile() + 8, zone, both(own, near), [part], 0, put)
+        base, part, rim_base, rim_part = arrays
+
+        def add(c, _):
+            lanes = pl.ds(pl.multiple_of(c * LANES, LANES), LANES)
+            for r in range(R // ROWS):
+                rows = pl.ds(ROWS * r, ROWS)
+                for i in range(2):
+                    t[i * (L - 1), rows, lanes] = base[i, rows, lanes] + part[i, rows, lanes]
+            return 0
+
+        lax.fori_loop(0, C, add, 0)
     else:
-        product(table, 0, zone, [(arrays[0], k) for k in range(2 * tiers)], [], 0, put)
+        planes, edges = arrays
+
+        def put(i, rows, lanes, whole, value):
+            t[i * (L - 1), rows, lanes] = value
+
+        product(table, 0, zone, [(planes, k) for k in range(2 * tiers)], [], 0, put)
     gone = ((row % 4 == 0) & jnp.logical_not(above_exists())) | ((row % 4 == 3) & jnp.logical_not(below_exists()))
 
     for c in range(C):
         lanes = pl.ds(c * LANES, LANES)
         if pairs:
-            tiles = [(4, edges[0][:, lanes]), (6, edges[1][:, lanes])]
-            value = rim_product(rim_table, tiles, aux, lanes) + edges[2][:, lanes]
+            value = rim_base[:, lanes] + rim_part[:, lanes]
         else:
-            value = rim_product(rim_table, [(2 * q, edges[0][q, :, lanes]) for q in range(tiers)], aux, lanes)
+            value = rim_product(rim_table, [(2 * q, edges[q, :, lanes]) for q in range(tiers)], aux, lanes)
         value = jnp.where(gone, 0.0, value)
         rim[:, lanes] = value
         for i in range(2):
             t[i * (L - 1), pl.ds(0, 1), lanes] = value[4 * i + 1 : 4 * i + 2]
             t[i * (L - 1), pl.ds(R - 1, 1), lanes] = value[4 * i + 2 : 4 * i + 3]
 
-    for p in range(2):
-        own, near = (0, 1) if p == 0 else (L - 1, L - 2)
+    def plane(p, _):
+        own, near = p * (L - 1), 1 + p * (L - 3)
+        heated = jnp.where(p == 0, 1.0, 0.0)
 
         def get_s(r, c):
-            return t[(p * (L - 1),) + tile(r, c)]
+            return t[(own,) + tile(r, c)]
 
         def get_h(r, c):
             return h_ref[(own,) + tile(r, c)]
@@ -674,29 +822,26 @@
 
         def get_z(r, c, s, h):
             at = (near,) + tile(r, c)
-            flow = (h + h_ref[at]) * (t[at] - s)
-            return flow + heat[tile(r, c)] if p == 0 else flow
+            return (h + h_ref[at]) * (t[at] - s) + heated * heat[tile(r, c)]
 
         def halo(c):
             lanes = pl.ds(LANES * c, LANES)
-            sides, walls = rim[:, lanes], aux[:, lanes]
-            return (
-                pltpu.roll(sides, -4 * p % ROWS, 0),
-                pltpu.roll(walls, -p % ROWS, 0),
-                pltpu.roll(sides, ROWS - 1 - (4 * p + 3), 0),
-                pltpu.roll(walls, ROWS - 1 - (2 + p), 0),
-            )
+            (sa, sb), (ha, hb) = wall(rim, 0, p, lanes), wall(aux, 0, p, lanes)
+            return sa, ha, sb, hb
 
         def put_out(r, c, value):
             out, c = (left, c) if c < C // 2 else (right, c - C // 2)
             out[(p,) + tile(r, c)] = value
 
         stencil(R, W, get_s, get_h, get_z, halo, put_out, get_g=get_g)
-
-
-def bond(tiers, zone, tables, aux, heat, h, g, t, arrays, edges):
+        return 0
+
+    lax.fori_loop(0, 2, plane, 0)
+
+
+def bond(tiers, zone, tables, aux, heat, h, g, t, arrays):
     _, R, W = t.shape
-    args = (zone, *tables, aux, heat, h, g, t, *arrays, *edges)
+    args = (zone, *tables, aux, heat, h, g, t, *arrays)
     f32 = jnp.float32
     return pl.pallas_call(
         functools.partial(bond_kernel, tiers),
@@ -715,22 +860,32 @@
 
 
 def final_kernel(tiers, zone, table, *refs):
-    per = 3 if tiers == 4 else 1
-    groups = refs[:per], refs[per : 2 * per]
-    _, out, buf, sem = refs[2 * per :]
+    arrays, (_, out, buf, sem) = refs[:-4], refs[-4:]
     L, R, W = out.shape
     half = W // 2
-
-    def put(i, rows, lanes, whole, value):
-        buf[i, rows, whole] = value
-
     copies = []
-    for side, group in enumerate(groups):
+    for side in range(2):
+        first = side * half
+
+        def put(i, rows, lanes, whole, value):
+            buf[i, rows, whole] = value
+
         if tiers == 4:
-            product(table, 16 * side + 8, zone, both(group[0], group[1]), [group[2]], side * half, put)
+            base, part = arrays[0], arrays[1 + side]
+
+            def add(c, _):
+                lanes = pl.ds(pl.multiple_of(c * LANES, LANES), LANES)
+                whole = pl.ds(pl.multiple_of(first + c * LANES, LANES), LANES)
+                for r in range(R // ROWS):
+                    rows = pl.ds(ROWS * r, ROWS)
+                    for i in range(2):
+                        buf[i, rows, whole] = base[i, rows, whole] + part[i, rows, lanes]
+                return 0
+
+            lax.fori_loop(0, half // LANES, add, 0)
         else:
-            product(table, 0, zone, [(group[0], k) for k in range(2 * tiers)], [], side * half, put)
-        lanes = pl.ds(side * half, half)
+            product(table, 0, zone, [(arrays[side], k) for k in range(2 * tiers)], [], first, put)
+        lanes = pl.ds(first, half)
         for i in range(2):
             copy = pltpu.make_async_copy(
                 buf.at[i, :, lanes], out.at[i * (L - 1), :, lanes], sem.at[2 * side + i]
@@ -741,8 +896,8 @@
         copy.wait()
 
 
-def final_planes(tiers, zone, table, left, right, out):
-    args = (zone, table, *left, *right, out)
+def final_planes(tiers, zone, table, arrays, out):
+    args = (zone, table, *arrays, out)
     _, R, W = out.shape
     return pl.pallas_call(
         functools.partial(final_kernel, tiers),
@@ -771,26 +926,25 @@
     return lax.ppermute(value, ("tier", "tile"), pairs)
 
 
-def exchange(tiers, tiles, table, zone, planes, after):
-    if tiers != 4:
-        return (every(planes, tiers),)
+def exchange(tiers, tiles, tables, zone, planes, after):
     near = along(planes, 0, tiers, tiles)
-    return planes, near, along(combine(table, zone, planes, near, after), 1, tiers, tiles)
-
-
-def exchange_rim(tiers, tiles, rim_table, aux, edges):
-    if tiers != 4:
-        return (every(edges, tiers),)
+    total = combine(tables[0], zone, planes, near, after)
+    return near, along(total, 1, tiers, tiles)
+
+
+def exchange_rim(tiers, tiles, tables, aux, edges, after):
     near = along(edges, 0, tiers, tiles)
-    return edges, near, along(combine_rim(rim_table, aux, edges, near), 1, tiers, tiles)
+    total = combine_rim(tables[1], aux, edges, near, after)
+    return near, total, along(total, 1, tiers, tiles)
 
 
 def exchange_halves(tiers, table, zone, left, right, after):
     if tiers != 4:
-        return (every(left, tiers),), (every(right, tiers),)
+        return every(left, tiers), every(right, tiers)
     left_x, right_y = across(left, 1, tiers), across(right, 2, tiers)
     to_y, to_x = combine_halves(table, zone, left, left_x, right, right_y, after)
-    return (left, left_x, across(to_y, 2, tiers)), (right, right_y, across(to_x, 1, tiers))
+    parts = across(to_y, 2, tiers), across(to_x, 1, tiers)
+    return own_halves(table, zone, left, left_x, right, right_y, to_y), *parts
 
 
 def local(warming, substance, zone, patch, kap, power, ops):
@@ -804,15 +958,23 @@
     got_b = lax.ppermute(swap_b, "tile", pairs)
     tables = make_tables(tiers, ops)
     h, g = faces(lab, kap)
-    arrays = exchange(tiers, tiles, tables[0], zone, planes, h)
-    edges, rims, aux = edge_rows(swap_a, swap_b, got_a, got_b)
-    edges = exchange_rim(tiers, tiles, tables[1], aux, edges)
-    t = outer(s, h, g, rims)
-    t, left, right = bond(tiers, zone, tables, aux, heat, h, g, t, arrays, edges)
+    if tiers == 4:
+        near, part = exchange(tiers, tiles, tables, zone, planes, h)
+    edges, aux = near_edges(swap_a, swap_b, got_a, got_b)
+    h, g = more_faces(lab, kap, h, g, aux)
+    if tiers == 4:
+        edges_near, sent, rim_part = exchange_rim(tiers, tiles, tables, aux, edges, h)
+        base, rim_base = own_part(tables, aux, zone, planes, near, edges, edges_near, sent)
+        arrays = base, part, rim_base, rim_part
+    else:
+        arrays = every(planes, tiers), every(edges, tiers)
+    t = outer(s, h, g, aux)
+    t, left, right = bond(tiers, zone, tables, aux, heat, h, g, t, arrays)
+    rims = edge_rows(swap_a, swap_b, got_a, got_b, left)
     t = inside(s, h, g, rims, t, left)
-    left, right = exchange_halves(tiers, tables[0], zone, left, right, t)
+    arrays = exchange_halves(tiers, tables[0], zone, left, right, t)
     out = last_layers(t, h, g, rims)
-    out = final_planes(tiers, zone, tables[0], left, right, out)
+    out = final_planes(tiers, zone, tables[0], arrays, out)
     return out[None]
 
 

time: 51.5 us -> 48.7 us (0.946)
  waiting for transfers between devices: 12 us -> 7.07 us
  starting transfers between devices: 11.1 us -> 12.4 us
    pallas_call x2 -> x6, Pallas kernels: 1.63 us -> 6.8 us  [the longest x1 3.23 us: more_faces(): pl.pallas_call(more_faces_kernel, out_shape=(jax.ShapeDtypeStruct(lab.sha...]
    ppermute x4, waiting for transfers between devices: 4.71 us -> 1.59 us  [across(): return lax.ppermute(value, 'tier', [(i, i ^ bits) for i in range(tiers)])]
    pallas_call x1, Pallas kernels: 4.83 us -> 2.16 us  [faces(): pl.pallas_call(faces_kernel, out_shape=(jax.ShapeDtypeStruct(lab.shape, j...]
    pallas_call x1, Pallas kernels: 2.93 us -> 0.81 us  [bond(): pl.pallas_call(functools.partial(bond_kernel, tiers), out_shape=(jax.Shap...]
    ppermute x4, waiting for transfers between devices: 7.3 us -> 5.48 us  [along(): return lax.ppermute(value, ('tier', 'tile'), pairs)]
    ppermute x4, starting transfers between devices: 3.62 us -> 4.81 us  [across(): return lax.ppermute(value, 'tier', [(i, i ^ bits) for i in range(tiers)])]
    pallas_call x1, Pallas kernels: 1.59 us -> 0.94 us  [final_planes(): pl.pallas_call(functools.partial(final_kernel, tiers), out_shape=jax.Shap...]
  transfers between devices with their start and end apart: 10 -> 10, of which waited for: 7 -> 5; matrix products, arithmetic and copies ran while one was open for 0% -> 0% of each run, Pallas kernels for 35% -> 44%
where the time goes in v4:
time: 48.7 us; the launch traced here: 48.2 us
  Pallas kernels  28.5 us (59%)
  starting transfers between devices  12.4 us (25%)
  waiting for transfers between devices  7.07 us (15%)
    ppermute x4, starting transfers between devices, along(): return lax.ppermute(value, ('tier', 'tile'), pairs)  6.94 us
    ppermute x4, waiting for transfers between devices, along(): return lax.ppermute(value, ('tier', 'tile'), pairs)  5.48 us
    pallas_call x1, Pallas kernels, last_layers(): pl.pallas_call(last_kernel, out_shape=jax.ShapeDtypeStruct(t.shape, jnp.f...  5.28 us
    pallas_call x1, Pallas kernels, begin(): pl.pallas_call(begin_kernel, out_shape=(pltpu.VMEM((2, R, W), f32), pltpu...  4.95 us
    ppermute x4, starting transfers between devices, across(): return lax.ppermute(value, 'tier', [(i, i ^ bits) for i in range(tiers)])  4.81 us
    pallas_call x1, Pallas kernels, inside(): pl.pallas_call(inside_kernel, out_shape=jax.ShapeDtypeStruct(s.shape, jnp...  4.29 us
    pallas_call x1, Pallas kernels, more_faces(): pl.pallas_call(more_faces_kernel, out_shape=(jax.ShapeDtypeStruct(lab.sha...  3.23 us
    pallas_call x1, Pallas kernels, faces(): pl.pallas_call(faces_kernel, out_shape=(jax.ShapeDtypeStruct(lab.shape, j...  2.16 us
  transfers between devices with their start and end apart: 10, of which 5 were waited for; matrix products, arithmetic and copies ran while one was open for 0% of the time, Pallas kernels for 44%

profile of v4, /device:TPU:0, one launch (start us, length us, event | category | flops | bytes accessed | tf_op | source)
XLA Modules:
  0.0 48.2 jit_solution(16972435592398104985)
XLA Ops:
  0.0 0.0 copy-start.1
  0.0 0.0 copy-start.2
  0.0 4.9 %begin.1 = (f32[2,32,2048]{2,1,0:T(8,128)S(1)}, f32[32,2048]{1,0:T(8,128)S(1)}, f32[72,2048]{1,0:T(8,128)S(1)}, f32[72,2048]{1,0:T(8,128)S(1)}, f32[16,32,2048]{...) custom-call(f32[16,32,2048]{2,1,0:T(8,128)} %bitcast.4, s32[16,32,2048]{2,1,0:T(8,128)} %bitcast.5, s32[32,2048]{1,0:T(8,128)} %bitcast.6, ...), custom_call_target="tpu_custom_call" | custom-call | tf_op jit(solution)/shard_map/begin/pallas_call | solution.py:227
  5.0 0.0 copy-start
  5.0 3.0 %collective-permute-start.2 = (f32[2,32,2048]{2,1,0:T(8,128)S(1)}, f32[2,32,2048]{2,1,0:T(8,128)S(1)}, u32[]{:S(2)}, u32[]{:S(2)}) collective-permute-start(f32[2,32,2048]{2,1,0:T(8,128)S(1)} %get-tuple-element.38.own), channel_id=1, source_target_pairs={{0,8},{1,17},{2,10},{3,19},{4,12},{5,21},{6,14},{7,23},{8,0},{9,25... | collective-permute-start | bytes 1572872 | tf_op jit(solution)/shard_map/ppermute | solution.py:926
  8.0 0.0 collective-permute-start
  8.0 0.7 %collective-permute-start.1 = (f32[72,2048]{1,0:T(8,128)S(1)}, f32[72,2048]{1,0:T(8,128)S(1)}, u32[]{:S(2)}, u32[]{:S(2)}) collective-permute-start(f32[72,2048]{1,0:T(8,128)S(1)} %get-tuple-element.29.own_b), channel_id=1, source_target_pairs={{1,2},{2,1},{3,4},{4,3},{5,6},{6,5},{9,10},{10,9},{11,12},{12,11},... | collective-permute-start | bytes 1769480 | tf_op jit(solution)/shard_map/ppermute | solution.py:958
  8.7 0.0 copy-done.1
  8.7 1.4 %make_tables.1 = (f32[32,8,8,128]{3,2,1,0:T(8,128)S(1)}, f32[8,8,128]{2,1,0:T(8,128)S(1)}) custom-call(f32[8,8,8]{2,1,0:T(8,128)S(1)} %copy-done.1), custom_call_target="tpu_custom_call" | custom-call | tf_op jit(solution)/shard_map/make_tables/pallas_call | solution.py:622
  10.1 0.0 copy-done.2
  10.1 2.2 %faces.1 = (f32[16,32,2048]{2,1,0:T(8,128)S(1)}, f32[16,32,2048]{2,1,0:T(8,128)S(1)}) custom-call(s32[16,32,2048]{2,1,0:T(8,128)S(1)} %get-tuple-element.32.lab, f32[16]{0:T(128)S(1)} %copy-done.2), custom_call_target="tpu_custom_call" | custom-call | tf_op jit(solution)/shard_map/faces/pallas_call | solution.py:425
  12.3 2.8 %collective-permute-done.2.near = f32[2,32,2048]{2,1,0:T(8,128)S(1)} collective-permute-done((f32[2,32,2048]{2,1,0:T(8,128)S(1)}, f32[2,32,2048]{2,1,0:T(8,128)S(1)}, u32[]{:S(2)}, u32[]{:S(2)}) %collective-permute-start.2) | collective-permute-done | bytes 524320 | tf_op jit(solution)/shard_map/ppermute | solution.py:926
  15.1 0.0 copy-done
  15.1 0.8 %combine.1 = f32[2,32,2048]{2,1,0:T(8,128)S(1)} custom-call(f32[32,8,8,128]{3,2,1,0:T(8,128)S(1)} %get-tuple-element.26.table, s32[32,2048]{1,0:T(8,128)S(1)} %copy-done, f32[2,32,2048]{2,1,0:T(8,128)S(1)} %get-tuple-element.38.own, f32[2,32,2048]{2,1,0:T(8,128)S(1)} %collective-permute-done.2.near, f32[16,32,2048]{2,1,0:T(8,128)S(1)} %get-tuple-element.33.h_in._), custom_call_target="tpu_custom_call" | custom-call | tf_op jit(solution)/shard_map/combine/pallas_call | solution.py:679
  16.0 2.1 %collective-permute-start.4 = (f32[2,32,2048]{2,1,0:T(8,128)S(1)}, f32[2,32,2048]{2,1,0:T(8,128)S(1)}, u32[]{:S(2)}, u32[]{:S(2)}) collective-permute-start(f32[2,32,2048]{2,1,0:T(8,128)S(1)} %combine.1), channel_id=1, source_target_pairs={{0,16},{1,9},{2,18},{3,11},{4,20},{5,13},{6,22},{7,15},{8,24},{9,1... | collective-permute-start | bytes 1572872 | tf_op jit(solution)/shard_map/ppermute | solution.py:926
  18.1 0.0 collective-permute-done.got_a
  18.1 0.0 collective-permute-done.1.got_b
  18.1 0.5 %near_edges.1 = (f32[8,2048]{1,0:T(8,128)S(1)}, f32[32,2048]{1,0:T(8,128)S(1)}) custom-call(f32[72,2048]{1,0:T(8,128)S(1)} %get-tuple-element.28.own_a, f32[72,2048]{1,0:T(8,128)S(1)} %get-tuple-element.29.own_b, f32[72,2048]{1,0:T(8,128)S(1)} %collective-permute-done.got_a, f32[72,2048]{1,0:T(8,128)S(1)} %collective-permute-done.1.got_b), custom_call_target="tpu_custom_call" | custom-call | tf_op jit(solution)/shard_map/near_edges/pallas_call | solution.py:322
  18.6 1.6 %collective-permute-start.3 = (f32[8,2048]{1,0:T(8,128)S(1)}, f32[8,2048]{1,0:T(8,128)S(1)}, u32[]{:S(2)}, u32[]{:S(2)}) collective-permute-start(f32[8,2048]{1,0:T(8,128)S(1)} %get-tuple-element.39.own.edges), channel_id=1, source_target_pairs={{0,8},{1,17},{2,10},{3,19},{4,12},{5,21},{6,14},{7,23},{8,0},{9,25... | collective-permute-start | bytes 196616 | tf_op jit(solution)/shard_map/ppermute | solution.py:926
  20.2 3.2 %more_faces.1 = (f32[16,32,2048]{2,1,0:T(8,128)S(1)}, f32[16,32,2048]{2,1,0:T(8,128)S(1)}) custom-call(s32[16,32,2048]{2,1,0:T(8,128)S(1)} %get-tuple-element.32.lab, f32[16]{0:T(128)S(1)} %copy-done.2, f32[16,32,2048]{2,1,0:T(8,128)S(1)} %get-tuple-element.33.h_in._, ...), custom_call_target="tpu_custom_call", output_to_operand_aliasing={{0}: (2, {}), {1}: (3, {})} | custom-call | tf_op jit(solution)/shard_map/more_faces/pallas_call | solution.py:440
  23.4 0.3 collective-permute-done.3.near.edges_near
  23.7 0.2 combine_rim.1._
  23.9 0.3 collective-permute-start.5
  24.2 0.7 %outer.1.t_in = f32[16,32,2048]{2,1,0:T(8,128)S(1)} custom-call(f32[16,32,2048]{2,1,0:T(8,128)S(1)} %get-tuple-element.37.s_ref, f32[16,32,2048]{2,1,0:T(8,128)S(1)} %get-tuple-element.35.h_ref._, f32[16,32,2048]{2,1,0:T(8,128)S(1)} %get-tuple-element.36.g_ref, f32[32,2048]{1,0:T(8,128)S(1)} %get-tuple-element.30._.aux), custom_call_target="tpu_custom_call" | custom-call | tf_op jit(solution)/shard_map/outer/pallas_call | solution.py:498
  24.9 1.0 %own_part.1 = (f32[2,32,2048]{2,1,0:T(8,128)S(1)}, f32[8,2048]{1,0:T(8,128)S(1)}) custom-call(f32[32,8,8,128]{3,2,1,0:T(8,128)S(1)} %get-tuple-element.26.table, f32[8,8,128]{2,1,0:T(8,128)S(1)} %get-tuple-element.27.rim_table, f32[32,2048]{1,0:T(8,128)S(1)} %get-tuple-element.30._.aux, s32[32,2048]{1,0:T(8,128)S(1)} %copy-done, ...), custom_call_target="tpu_custom_call" | custom-call | tf_op jit(solution)/shard_map/own_part/pallas_call | solution.py:740
  25.9 2.3 %collective-permute-done.5.refs_3_ = f32[8,2048]{1,0:T(8,128)S(1)} collective-permute-done((f32[8,2048]{1,0:T(8,128)S(1)}, f32[8,2048]{1,0:T(8,128)S(1)}, u32[]{:S(2)}, u32[]{:S(2)}) %collective-permute-start.5) | collective-permute-done | bytes 65568 | tf_op jit(solution)/shard_map/ppermute | solution.py:926
  28.3 0.0 collective-permute-done.4.refs_1_
  28.3 0.8 %bond.1 = (f32[16,32,2048]{2,1,0:T(8,128)S(1)}, f32[2,32,1024]{2,1,0:T(8,128)S(1)}, f32[2,32,1024]{2,1,0:T(8,128)S(1)}) custom-call(s32[32,2048]{1,0:T(8,128)S(1)} %copy-done, f32[32,8,8,128]{3,2,1,0:T(8,128)S(1)} %get-tuple-element.26.table, f32[8,8,128]{2,1,0:T(8,128)S(1)} %get-tuple-element.27.rim_table, ...), custom_call_target="tpu_custom_call", output_to_operand_aliasing={{0}: (7, {})} | custom-call | tf_op jit(solution)/shard_map/bond/pallas_call | solution.py:846
  29.1 1.6 %collective-permute-start.6 = (f32[2,32,1024]{2,1,0:T(8,128)S(1)}, f32[2,32,1024]{2,1,0:T(8,128)S(1)}, u32[]{:S(2)}, u32[]{:S(2)}) collective-permute-start(f32[2,32,1024]{2,1,0:T(8,128)S(1)} %get-tuple-element.42._.left), channel_id=1, source_target_pairs={{0,8},{8,0},{16,24},{24,16},{1,9},{9,1},{17,25},{25,17},{2,10},{10... | collective-permute-start | bytes 786440 | tf_op jit(solution)/shard_map/ppermute | solution.py:915
  30.6 0.5 %collective-permute-start.7 = (f32[2,32,1024]{2,1,0:T(8,128)S(1)}, f32[2,32,1024]{2,1,0:T(8,128)S(1)}, u32[]{:S(2)}, u32[]{:S(2)}) collective-permute-start(f32[2,32,1024]{2,1,0:T(8,128)S(1)} %get-tuple-element.43.right), channel_id=1, source_target_pairs={{0,16},{8,24},{16,0},{24,8},{1,17},{9,25},{17,1},{25,9},{2,18},{10... | collective-permute-start | bytes 786440 | tf_op jit(solution)/shard_map/ppermute | solution.py:915
  31.1 0.5 %edge_rows.1.rims = f32[6,16,2048]{2,1,0:T(8,128)S(1)} custom-call(f32[72,2048]{1,0:T(8,128)S(1)} %get-tuple-element.28.own_a, f32[72,2048]{1,0:T(8,128)S(1)} %get-tuple-element.29.own_b, f32[72,2048]{1,0:T(8,128)S(1)} %collective-permute-done.got_a, f32[72,2048]{1,0:T(8,128)S(1)} %collective-permute-done.1.got_b, f32[2,32,1024]{2,1,0:T(8,128)S(1)} %get-tuple-element.42._.left), custom_call_target="tpu_custom_call" | custom-call | tf_op jit(solution)/shard_map/edge_rows/pallas_call | solution.py:375
  31.7 4.3 %inside.1._.t_ref = f32[16,32,2048]{2,1,0:T(8,128)S(1)} custom-call(f32[16,32,2048]{2,1,0:T(8,128)S(1)} %get-tuple-element.37.s_ref, f32[16,32,2048]{2,1,0:T(8,128)S(1)} %get-tuple-element.35.h_ref._, f32[16,32,2048]{2,1,0:T(8,128)S(1)} %get-tuple-element.36.g_ref, f32[6,16,2048]{2,1,0:T(8,128)S(1)} %edge_rows.1.rims, ...), custom_call_target="tpu_custom_call", output_to_operand_aliasing={{}: (4, {})} | custom-call | tf_op jit(solution)/shard_map/inside/pallas_call | solution.py:522
  36.0 1.5 %collective-permute-done.6.left_x = f32[2,32,1024]{2,1,0:T(8,128)S(1)} collective-permute-done((f32[2,32,1024]{2,1,0:T(8,128)S(1)}, f32[2,32,1024]{2,1,0:T(8,128)S(1)}, u32[]{:S(2)}, u32[]{:S(2)}) %collective-permute-start.6) | collective-permute-done | bytes 262176 | tf_op jit(solution)/shard_map/ppermute | solution.py:915
  37.5 0.1 collective-permute-done.7.right_y
  37.5 0.8 %combine_halves.1 = (f32[2,32,1024]{2,1,0:T(8,128)S(1)}, f32[2,32,1024]{2,1,0:T(8,128)S(1)}) custom-call(f32[32,8,8,128]{3,2,1,0:T(8,128)S(1)} %get-tuple-element.26.table, s32[32,2048]{1,0:T(8,128)S(1)} %copy-done, f32[2,32,1024]{2,1,0:T(8,128)S(1)} %get-tuple-element.42._.left, f32[2,32,1024]{2,1,0:T(8,128)S(1)} %collective-permute-done.6.left_x, ...), custom_call_target="tpu_custom_call" | custom-call | tf_op jit(solution)/shard_map/combine_halves/pallas_call | solution.py:695
  38.4 1.5 %collective-permute-start.8 = (f32[2,32,1024]{2,1,0:T(8,128)S(1)}, f32[2,32,1024]{2,1,0:T(8,128)S(1)}, u32[]{:S(2)}, u32[]{:S(2)}) collective-permute-start(f32[2,32,1024]{2,1,0:T(8,128)S(1)} %get-tuple-element.45._), channel_id=1, source_target_pairs={{0,16},{8,24},{16,0},{24,8},{1,17},{9,25},{17,1},{25,9},{2,18},{10... | collective-permute-start | bytes 786440 | tf_op jit(solution)/shard_map/ppermute | solution.py:915
  39.9 1.2 %collective-permute-start.9 = (f32[2,32,1024]{2,1,0:T(8,128)S(1)}, f32[2,32,1024]{2,1,0:T(8,128)S(1)}, u32[]{:S(2)}, u32[]{:S(2)}) collective-permute-start(f32[2,32,1024]{2,1,0:T(8,128)S(1)} %get-tuple-element.46), channel_id=1, source_target_pairs={{0,8},{8,0},{16,24},{24,16},{1,9},{9,1},{17,25},{25,17},{2,10},{10... | collective-permute-start | bytes 786440 | tf_op jit(solution)/shard_map/ppermute | solution.py:915
  41.1 5.3 %last_layers.1.refs_3_ = f32[16,32,2048]{2,1,0:T(8,128)} custom-call(f32[16,32,2048]{2,1,0:T(8,128)S(1)} %inside.1._.t_ref, f32[16,32,2048]{2,1,0:T(8,128)S(1)} %get-tuple-element.35.h_ref._, f32[16,32,2048]{2,1,0:T(8,128)S(1)} %get-tuple-element.36.g_ref, f32[6,16,2048]{2,1,0:T(8,128)S(1)} %edge_rows.1.rims), custom_call_target="tpu_custom_call" | custom-call | tf_op jit(solution)/shard_map/last_layers/pallas_call | solution.py:561
  46.4 0.8 %own_halves.1.refs_0_ = f32[2,32,2048]{2,1,0:T(8,128)S(1)} custom-call(f32[32,8,8,128]{3,2,1,0:T(8,128)S(1)} %get-tuple-element.26.table, s32[32,2048]{1,0:T(8,128)S(1)} %copy-done, f32[2,32,1024]{2,1,0:T(8,128)S(1)} %get-tuple-element.42._.left, f32[2,32,1024]{2,1,0:T(8,128)S(1)} %collective-permute-done.6.left_x, ...), custom_call_target="tpu_custom_call" | custom-call | tf_op jit(solution)/shard_map/own_halves/pallas_call | solution.py:761
  47.2 0.0 collective-permute-done.8.refs_1_
  47.2 0.0 collective-permute-done.9.refs_2_
  47.2 0.9 %final_planes.1 = f32[16,32,2048]{2,1,0:T(8,128)} custom-call(s32[32,2048]{1,0:T(8,128)S(1)} %copy-done, f32[32,8,8,128]{3,2,1,0:T(8,128)S(1)} %get-tuple-element.26.table, f32[2,32,2048]{2,1,0:T(8,128)S(1)} %own_halves.1.refs_0_, f32[2,32,1024]{2,1,0:T(8,128)S(1)} %collective-permute-done.8.refs_1_, ...), custom_call_target="tpu_custom_call", output_to_operand_aliasing={{}: (5, {})} | custom-call | tf_op jit(solution)/shard_map/final_planes/pallas_call | solution.py:902
Async XLA Ops:
  0.0 8.7 %copy-start.1 = (f32[8,8,8]{2,1,0:T(8,128)S(1)}, f32[8,8,8]{2,1,0:T(8,128)}, u32[]{:S(2)}) copy-start(f32[8,8,8]{2,1,0:T(8,128)} %ops.1) | copy-start | bytes 6148
  0.0 10.1 %copy-start.2 = (f32[16]{0:T(128)S(1)}, f32[16]{0:T(128)}, u32[]{:S(2)}) copy-start(f32[16]{0:T(128)} %kap.3) | copy-start | bytes 196
  5.0 10.2 %copy-start = (s32[32,2048]{1,0:T(8,128)S(1)}, s32[32,2048]{1,0:T(8,128)}, u32[]{:S(2)}) copy-start(s32[32,2048]{1,0:T(8,128)} %zone.11) | copy-start | bytes 786436
  5.0 10.2 %collective-permute-start.2 = (f32[2,32,2048]{2,1,0:T(8,128)S(1)}, f32[2,32,2048]{2,1,0:T(8,128)S(1)}, u32[]{:S(2)}, u32[]{:S(2)}) collective-permute-start(f32[2,32,2048]{2,1,0:T(8,128)S(1)} %get-tuple-element.38.own), channel_id=1, source_target_pairs={{0,8},{1,17},{2,10},{3,19},{4,12},{5,21},{6,14},{7,23},{8,0},{9,25... | collective-permute-start | bytes 1572872 | tf_op jit(solution)/shard_map/ppermute | solution.py:926
  8.0 10.1 %collective-permute-start = (f32[72,2048]{1,0:T(8,128)S(1)}, f32[72,2048]{1,0:T(8,128)S(1)}, u32[]{:S(2)}, u32[]{:S(2)}) collective-permute-start(f32[72,2048]{1,0:T(8,128)S(1)} %get-tuple-element.28.own_a), channel_id=1, source_target_pairs={{0,1},{1,0},{2,3},{3,2},{4,5},{5,4},{6,7},{7,6},{8,9},{9,8},{10,11... | collective-permute-start | bytes 1769480 | tf_op jit(solution)/shard_map/ppermute | solution.py:956
  8.0 10.1 %collective-permute-start.1 = (f32[72,2048]{1,0:T(8,128)S(1)}, f32[72,2048]{1,0:T(8,128)S(1)}, u32[]{:S(2)}, u32[]{:S(2)}) collective-permute-start(f32[72,2048]{1,0:T(8,128)S(1)} %get-tuple-element.29.own_b), channel_id=1, source_target_pairs={{1,2},{2,1},{3,4},{4,3},{5,6},{6,5},{9,10},{10,9},{11,12},{12,11},... | collective-permute-start | bytes 1769480 | tf_op jit(solution)/shard_map/ppermute | solution.py:958
  16.0 12.3 %collective-permute-start.4 = (f32[2,32,2048]{2,1,0:T(8,128)S(1)}, f32[2,32,2048]{2,1,0:T(8,128)S(1)}, u32[]{:S(2)}, u32[]{:S(2)}) collective-permute-start(f32[2,32,2048]{2,1,0:T(8,128)S(1)} %combine.1), channel_id=1, source_target_pairs={{0,16},{1,9},{2,18},{3,11},{4,20},{5,13},{6,22},{7,15},{8,24},{9,1... | collective-permute-start | bytes 1572872 | tf_op jit(solution)/shard_map/ppermute | solution.py:926
  18.6 5.1 %collective-permute-start.3 = (f32[8,2048]{1,0:T(8,128)S(1)}, f32[8,2048]{1,0:T(8,128)S(1)}, u32[]{:S(2)}, u32[]{:S(2)}) collective-permute-start(f32[8,2048]{1,0:T(8,128)S(1)} %get-tuple-element.39.own.edges), channel_id=1, source_target_pairs={{0,8},{1,17},{2,10},{3,19},{4,12},{5,21},{6,14},{7,23},{8,0},{9,25... | collective-permute-start | bytes 196616 | tf_op jit(solution)/shard_map/ppermute | solution.py:926
  23.9 4.3 %collective-permute-start.5 = (f32[8,2048]{1,0:T(8,128)S(1)}, f32[8,2048]{1,0:T(8,128)S(1)}, u32[]{:S(2)}, u32[]{:S(2)}) collective-permute-start(f32[8,2048]{1,0:T(8,128)S(1)} %combine_rim.1._), channel_id=1, source_target_pairs={{0,16},{1,9},{2,18},{3,11},{4,20},{5,13},{6,22},{7,15},{8,24},{9,1... | collective-permute-start | bytes 196616 | tf_op jit(solution)/shard_map/ppermute | solution.py:926
  29.1 8.4 %collective-permute-start.6 = (f32[2,32,1024]{2,1,0:T(8,128)S(1)}, f32[2,32,1024]{2,1,0:T(8,128)S(1)}, u32[]{:S(2)}, u32[]{:S(2)}) collective-permute-start(f32[2,32,1024]{2,1,0:T(8,128)S(1)} %get-tuple-element.42._.left), channel_id=1, source_target_pairs={{0,8},{8,0},{16,24},{24,16},{1,9},{9,1},{17,25},{25,17},{2,10},{10... | collective-permute-start | bytes 786440 | tf_op jit(solution)/shard_map/ppermute | solution.py:915
  30.6 6.9 %collective-permute-start.7 = (f32[2,32,1024]{2,1,0:T(8,128)S(1)}, f32[2,32,1024]{2,1,0:T(8,128)S(1)}, u32[]{:S(2)}, u32[]{:S(2)}) collective-permute-start(f32[2,32,1024]{2,1,0:T(8,128)S(1)} %get-tuple-element.43.right), channel_id=1, source_target_pairs={{0,16},{8,24},{16,0},{24,8},{1,17},{9,25},{17,1},{25,9},{2,18},{10... | collective-permute-start | bytes 786440 | tf_op jit(solution)/shard_map/ppermute | solution.py:915
  38.4 8.8 %collective-permute-start.8 = (f32[2,32,1024]{2,1,0:T(8,128)S(1)}, f32[2,32,1024]{2,1,0:T(8,128)S(1)}, u32[]{:S(2)}, u32[]{:S(2)}) collective-permute-start(f32[2,32,1024]{2,1,0:T(8,128)S(1)} %get-tuple-element.45._), channel_id=1, source_target_pairs={{0,16},{8,24},{16,0},{24,8},{1,17},{9,25},{17,1},{25,9},{2,18},{10... | collective-permute-start | bytes 786440 | tf_op jit(solution)/shard_map/ppermute | solution.py:915
  39.9 7.3 %collective-permute-start.9 = (f32[2,32,1024]{2,1,0:T(8,128)S(1)}, f32[2,32,1024]{2,1,0:T(8,128)S(1)}, u32[]{:S(2)}, u32[]{:S(2)}) collective-permute-start(f32[2,32,1024]{2,1,0:T(8,128)S(1)} %get-tuple-element.46), channel_id=1, source_target_pairs={{0,8},{8,0},{16,24},{24,16},{1,9},{9,1},{17,25},{25,17},{2,10},{10... | collective-permute-start | bytes 786440 | tf_op jit(solution)/shard_map/ppermute | solution.py:915

commit v5 on v3

v5 whole, which is shorter than its diff:
```python
import functools
import math

import jax
import jax.numpy as jnp
from jax import lax
from jax.experimental import pallas as pl
from jax.experimental.pallas import tpu as pltpu
from jax.sharding import PartitionSpec as P

STEPS = 2
step_dt = 0.04
half_dt = 0.5 * step_dt
LANES = 128
ROWS = 8
MIB = 1 << 20

VMEM = pl.BlockSpec(memory_space=pltpu.VMEM)
SMEM = pl.BlockSpec(memory_space=pltpu.SMEM)
ANY = pl.BlockSpec(memory_space=pl.ANY)
HBM = pl.BlockSpec(memory_space=pltpu.HBM)


def tile(r, c):
    return pl.ds(ROWS * r, ROWS), pl.ds(LANES * c, LANES)


def lane_ids():
    return lax.broadcasted_iota(jnp.int32, (ROWS, LANES), 1)


def row_ids():
    return lax.broadcasted_iota(jnp.int32, (ROWS, LANES), 0)


def choose(values, labels):
    values, bit = list(values), 1
    while len(values) > 1:
        odd = (labels & bit) != 0
        paired = [
            jnp.where(odd, values[i + 1], values[i]) if i + 1 < len(values) else values[i]
            for i in range(0, len(values), 2)
        ]
        values, bit = paired, 2 * bit
    return values[0]


def lookup(row, labels):
    return jnp.take_along_axis(row, labels, axis=1, mode="promise_in_bounds")


def splats(kap):
    return [jnp.full((ROWS, LANES), half_dt * kap[i], jnp.float32) for i in range(kap.shape[0])]


def stencil(R, W, get_s, get_h, get_z, halo, put, get_g=None, put_g=None):
    C, S = W // LANES, R // ROWS
    lane, row = lane_ids(), row_ids()
    first, last = lane == 0, lane == LANES - 1
    top, bottom = row == 0, row == ROWS - 1
    before = None
    for c in range(C):
        s = [get_s(r, c) for r in range(S)]
        h = [get_h(r, c) for r in range(S)]
        rs = [pltpu.roll(v, 1, 1) for v in s]
        rh = [pltpu.roll(v, 1, 1) for v in h] if get_g is None else None
        us = [pltpu.roll(v, 1, 0) for v in s]
        uh = [pltpu.roll(v, 1, 0) for v in h]
        if halo is not None:
            sa, ha, sb, hb = halo(c)
        acc, back, down = [], [], []
        for r in range(S):
            sl = jnp.where(first, 0.0 if c == 0 else before[0][r], rs[r])
            if get_g is None:
                g = h[r] + jnp.where(first, 0.0 if c == 0 else before[1][r], rh[r])
                if put_g is not None:
                    put_g(r, c, g)
            else:
                g = get_g(r, c)
            face = g * (sl - s[r])
            back.append(pltpu.roll(face, LANES - 1, 1))
            if r == 0:
                if halo is None:
                    su, hu = us[0], uh[0]
                else:
                    su, hu = jnp.where(top, sa, us[0]), jnp.where(top, ha, uh[0])
            else:
                su, hu = jnp.where(top, us[r - 1], us[r]), jnp.where(top, uh[r - 1], uh[r])
            upper = (h[r] + hu) * (su - s[r])
            down.append(pltpu.roll(upper, ROWS - 1, 0))
            acc.append((s[r] + get_z(r, c, s[r], h[r])) + (face + upper))
        for r in range(S):
            if r + 1 < S:
                lower = jnp.where(bottom, down[r + 1], down[r])
            elif halo is None:
                lower = down[r]
            else:
                lower = jnp.where(bottom, (h[r] + hb) * (s[r] - sb), down[r])
            acc[r] = acc[r] - lower
        if before is not None:
            for r in range(S):
                put(r, c - 1, before[3][r] - jnp.where(last, back[r], before[2][r]))
        before = (rs, rh, back, acc, s, h)
    for r in range(S):
        out = before[5][r] * before[4][r]
        put(r, C - 1, before[3][r] - jnp.where(last, out, before[2][r]))


def vertical(s, h, s_up, h_up, s_down, h_down):
    return (h + h_up) * (s_up - s) + (h + h_down) * (s_down - s)


def collect(row, pieces):
    value = None
    for q, (source_tile, source) in enumerate(pieces):
        moved = source_tile if q == source else pltpu.roll(source_tile, (q - source) % ROWS, 0)
        value = moved if value is None else jnp.where(row == q, moved, value)
    return value


def begin_kernel(
    s_hbm, lab_hbm, patch_hbm, kap_hbm, power_hbm,
    planes, heat, s_v, lab_v, h_out,
    patch, kap, power, sem,
):
    L, R, W = s_hbm.shape
    C = W // LANES
    small = [
        pltpu.make_async_copy(kap_hbm, kap, sem.at[0]),
        pltpu.make_async_copy(power_hbm, power, sem.at[1]),
        pltpu.make_async_copy(patch_hbm, patch, sem.at[2]),
    ]
    groups = [(0, 2), (L - 2, 2), (2, L - 4)]
    layers = [
        [
            pltpu.make_async_copy(s_hbm.at[pl.ds(l, n)], s_v.at[pl.ds(l, n)], sem.at[3 + 2 * k]),
            pltpu.make_async_copy(lab_hbm.at[pl.ds(l, n)], lab_v.at[pl.ds(l, n)], sem.at[4 + 2 * k]),
        ]
        for k, (l, n) in enumerate(groups)
    ]
    for copy in small + layers[0] + layers[1] + layers[2]:
        copy.start()
    for copy in small:
        copy.wait()
    values = splats(kap)
    heats = step_dt * jnp.broadcast_to(power[...], (ROWS, LANES))

    for c in range(C):
        for r in range(R // ROWS):
            heat[tile(r, c)] = lookup(heats, patch[tile(r, c)])
    for copy in layers[0] + layers[1]:
        copy.wait()

    def plane(p, _):
        own, near = p * (L - 1), 1 + p * (L - 3)
        heated = jnp.where(p == 0, 1.0, 0.0)

        def get_s(r, c):
            return s_v[(own,) + tile(r, c)]

        def get_h(r, c):
            value = choose(values, lab_v[(own,) + tile(r, c)])
            h_out[(own,) + tile(r, c)] = value
            return value

        def get_z(r, c, s, h):
            h_near = choose(values, lab_v[(near,) + tile(r, c)])
            h_out[(near,) + tile(r, c)] = h_near
            return (h + h_near) * (s_v[(near,) + tile(r, c)] - s) + heated * heat[tile(r, c)]

        def put(r, c, value):
            planes[(p,) + tile(r, c)] = value

        stencil(R, W, get_s, get_h, get_z, None, put)
        return 0

    lax.fori_loop(0, 2, plane, 0)
    for copy in layers[2]:
        copy.wait()


def begin(s, lab, patch, kap, power):
    _, R, W = s.shape
    f32, i32 = jnp.float32, jnp.int32
    args = [pltpu.with_memory_space_constraint(x, pltpu.HBM) for x in (s, lab, patch, kap, power)]
    return pl.pallas_call(
        begin_kernel,
        out_shape=(
            pltpu.VMEM((2, R, W), f32), pltpu.VMEM((R, W), f32), pltpu.VMEM(s.shape, f32), pltpu.VMEM(lab.shape, i32),
            pltpu.VMEM(s.shape, f32),
        ),
        in_specs=[HBM] * 5,
        out_specs=[VMEM] * 5,
        scratch_shapes=[
            pltpu.VMEM((R, W), i32),
            pltpu.SMEM(kap.shape, f32),
            pltpu.VMEM(power.shape, f32),
            pltpu.SemaphoreType.DMA((9,)),
        ],
        compiler_params=pltpu.CompilerParams(vmem_limit_bytes=16 * MIB),
        name="begin",
    )(*args)


def above_exists():
    return lax.axis_index("tile") > 0


def below_exists():
    return lax.axis_index("tile") < lax.axis_size("tile") - 1


def pack_kernel(s, lab, heat, zone, kap, swap_a, swap_b, rows_v, next_v):
    L, R, W = s.shape
    C = W // LANES
    row = row_ids()
    values = splats(kap)
    group = math.gcd(C, 4)

    def body(first, _):
        for c in (group * first + n for n in range(group)):
            lanes = pl.ds(pl.multiple_of(c * LANES, LANES), LANES)
            for k, (start, at_edge, inwards) in enumerate(((0, 0, 1), (R - ROWS, ROWS - 1, ROWS - 2))):
                edge = pl.ds(start, ROWS)
                for base in range(0, L, ROWS):
                    for ref, at in ((s, 0), (lab, L)):
                        tiles = [ref[base + q, edge, lanes] for q in range(ROWS)]
                        for out, source in ((rows_v, at_edge), (next_v, inwards)):
                            packed = collect(row, [(x, source) for x in tiles])
                            if ref is lab:
                                packed = choose(values, packed)
                            out[k, pl.ds(at + base, ROWS), lanes] = packed
                zones = zone[edge, lanes].astype(jnp.float32)
                rows_v[k, pl.ds(3 * L, ROWS), lanes] = collect(row, [(zones, at_edge), (heat[edge, lanes], at_edge)])
        return 0

    lax.fori_loop(0, C // group, body, 0)

    def side(k, _):
        def at(base, r, c):
            return k, pl.ds(base + ROWS * r, ROWS), pl.ds(LANES * c, LANES)

        def get_s(r, c):
            return rows_v[at(0, r, c)]

        def get_h(r, c):
            return rows_v[at(L, r, c)]

        def get_z(r, c, s, h):
            flow = (h + next_v[at(L, r, c)]) * (next_v[at(0, r, c)] - s)
            if r == 0:
                flow = flow + jnp.where(row == 0, pltpu.roll(rows_v[at(3 * L, 0, c)], ROWS - 1, 0), 0.0)
            return flow

        def ends(c):
            last = L // ROWS - 1
            return get_s(0, c), get_h(0, c), get_s(last, c), get_h(last, c)

        def put(r, c, value):
            rows_v[at(2 * L, r, c)] = value

        stencil(L, W, get_s, get_h, get_z, ends, put)
        return 0

    lax.fori_loop(0, 2, side, 0)
    odd = lax.axis_index("tile") % 2

    for r in range(swap_a.shape[0] // ROWS):
        for c in range(C):
            swap_a[tile(r, c)] = rows_v[(1 - odd,) + tile(r, c)]
            swap_b[tile(r, c)] = rows_v[(odd,) + tile(r, c)]


def pack_rows(s, lab, heat, zone, kap):
    L, _, W = s.shape
    f32 = jnp.float32
    rows = 3 * L + ROWS
    return pl.pallas_call(
        pack_kernel,
        out_shape=(pltpu.VMEM((rows, W), f32),) * 2,
        in_specs=[VMEM] * 4 + [SMEM],
        out_specs=[VMEM] * 2,
        scratch_shapes=[pltpu.VMEM((2, rows, W), f32), pltpu.VMEM((2, 2 * L, W), f32)],
        compiler_params=pltpu.CompilerParams(vmem_limit_bytes=20 * MIB),
        name="pack_rows",
    )(s, lab, heat, zone, kap)


def edge_kernel(own_a, own_b, got_a, got_b, edges, zones, rims):
    rows, W = own_a.shape
    L = (rows - ROWS) // 3
    odd = lax.axis_index("tile") % 2 == 1
    for side, exists in enumerate((above_exists(), below_exists())):
        first_swap = odd if side == 0 else jnp.logical_not(odd)
        k_out, k_in = (0, 1) if side == 0 else (3, 2)

        def both_sides(at, n):
            at = pl.ds(at, n)
            other = jnp.where(exists, jnp.where(first_swap, got_a[at, :], got_b[at, :]), 0.0)
            return other, jnp.where(first_swap, own_a[at, :], own_b[at, :])

        for base in range(0, L, ROWS):
            part = pl.ds(base, ROWS)
            s_out, s_in = both_sides(base, ROWS)
            h_out, h_in = both_sides(L + base, ROWS)
            u_out, u_in = both_sides(2 * L + base, ROWS)
            face = (h_in + h_out) * (s_out - s_in)
            t_out, t_in = jnp.where(exists, u_out - face, 0.0), u_in + face
            rims[2 * side, part, :] = s_out
            rims[2 * side + 1, part, :] = h_out
            rims[4 + side, part, :] = t_out
            for i, l in ((0, 0), (1, L - 1)):
                if base <= l < base + ROWS:
                    edges[pl.ds(4 * i + k_out, 1), :] = t_out[l - base : l - base + 1]
                    edges[pl.ds(4 * i + k_in, 1), :] = t_in[l - base : l - base + 1]
        z_out, z_in = both_sides(3 * L, 1)
        for i in range(2):
            zones[pl.ds(4 * i + k_out, 1), :] = z_out
            zones[pl.ds(4 * i + k_in, 1), :] = z_in


def edge_rows(own_a, own_b, got_a, got_b):
    rows, W = own_a.shape
    f32 = jnp.float32
    return pl.pallas_call(
        edge_kernel,
        out_shape=(pltpu.VMEM((ROWS, W), f32), pltpu.VMEM((ROWS, W), f32), pltpu.VMEM((6, (rows - ROWS) // 3, W), f32)),
        in_specs=[VMEM] * 4,
        out_specs=[VMEM] * 3,
        compiler_params=pltpu.CompilerParams(vmem_limit_bytes=16 * MIB),
        name="edge_rows",
    )(own_a, own_b, got_a, got_b)


def pick(ref, base, l, lanes, row):
    at = base + (l // ROWS) * ROWS
    if not isinstance(l, int):
        at = pl.multiple_of(at, ROWS)
    return pltpu.roll(ref[pl.ds(at, ROWS), lanes], (row - l) % ROWS, 0)


def halo_rows(rims, state, lanes, l):
    end = ROWS - 1
    where = ((state[0], 0), (1, 0), (state[1], end), (3, end))
    return tuple(pick(rims.at[k], 0, l, lanes, row) for k, row in where)


def fill_faces(first, end, h_at, h_out, g_out):
    _, R, W = h_out.shape
    edge = lane_ids() == 0

    def body(l, _):
        before = [0.0] * (R // ROWS)
        for c in range(W // LANES):
            for r in range(R // ROWS):
                at = (l,) + tile(r, c)
                h = h_at(at, c)
                moved = pltpu.roll(h, 1, 1)
                h_out[at] = h
                g_out[at] = h + jnp.where(edge, before[r], moved)
                before[r] = moved
        return 0

    lax.fori_loop(first, end, body, 0)


def from_labels(lab, kap):
    values = splats(kap)
    table, lane = jnp.zeros((ROWS, LANES), jnp.float32), lane_ids()
    for k, value in enumerate(values):
        table = jnp.where(lane == k, value, table)
    return lambda at, c: lookup(table, lab[at]) if c % 4 == 0 else choose(values, lab[at])


def faces_kernel(lab, kap, h_in, h_out, g_out):
    L = lab.shape[0]

    def held(at, c):
        return h_out[at]

    getter = from_labels(lab, kap)
    for first, end in ((0, 2), (L - 2, L)):
        fill_faces(first, end, held, h_out, g_out)
    for l in (2, L - 3):
        fill_faces(l, l + 1, getter, h_out, g_out)


def faces(lab, kap, h):
    return pl.pallas_call(
        faces_kernel,
        out_shape=(jax.ShapeDtypeStruct(lab.shape, jnp.float32),) * 2,
        in_specs=[VMEM, SMEM, VMEM],
        out_specs=[VMEM] * 2,
        input_output_aliases={2: 0},
        compiler_params=pltpu.CompilerParams(vmem_limit_bytes=20 * MIB),
        name="faces",
    )(lab, kap, h)


def more_faces_kernel(lab, kap, h_in, g_in, _, h_out, g_out):
    fill_faces(3, lab.shape[0] - 3, from_labels(lab, kap), h_out, g_out)


def more_faces(lab, kap, h, g, after):
    return pl.pallas_call(
        more_faces_kernel,
        out_shape=(jax.ShapeDtypeStruct(lab.shape, jnp.float32),) * 2,
        in_specs=[VMEM, SMEM, VMEM, VMEM, ANY],
        out_specs=[VMEM] * 2,
        input_output_aliases={2: 0, 3: 1},
        compiler_params=pltpu.CompilerParams(vmem_limit_bytes=24 * MIB),
        name="more_faces",
    )(lab, kap, h, g, after)


def layer_step(l, s_ref, h_ref, g_ref, halo, put):
    _, R, W = s_ref.shape

    def get_s(r, c):
        return s_ref[(l,) + tile(r, c)]

    def get_h(r, c):
        return h_ref[(l,) + tile(r, c)]

    def get_g(r, c):
        return g_ref[(l,) + tile(r, c)]

    def get_z(r, c, s, h):
        a, b = (l - 1,) + tile(r, c), (l + 1,) + tile(r, c)
        return vertical(s, h, s_ref[a], h_ref[a], s_ref[b], h_ref[b])

    stencil(R, W, get_s, get_h, get_z, halo, put, get_g=get_g)


def first_step(l, s_ref, h_ref, g_ref, halo, t):
    def put(r, c, value):
        t[(l,) + tile(r, c)] = value

    layer_step(l, s_ref, h_ref, g_ref, halo, put)


def outer_kernel(s_ref, h_ref, g_ref, rims, t):
    L = s_ref.shape[0]

    def body(p, _):
        l = 1 + p * (L - 3)

        def halo(c):
            return halo_rows(rims, (0, 2), pl.ds(LANES * c, LANES), l)

        first_step(l, s_ref, h_ref, g_ref, halo, t)
        return 0

    lax.fori_loop(0, 2, body, 0)


def outer(s, h, g, rims):
    return pl.pallas_call(
        outer_kernel,
        out_shape=pltpu.VMEM(s.shape, jnp.float32),
        in_specs=[VMEM] * 4,
        out_specs=VMEM,
        compiler_params=pltpu.CompilerParams(vmem_limit_bytes=20 * MIB),
        name="outer",
    )(s, h, g, rims)


def inside_kernel(s_ref, h_ref, g_ref, rims, t_in, _, t):
    L = s_ref.shape[0]

    def body(l, _):
        def halo(c):
            return halo_rows(rims, (0, 2), pl.ds(LANES * c, LANES), l)

        first_step(l, s_ref, h_ref, g_ref, halo, t)
        return 0

    lax.fori_loop(2, L - 2, body, 0)


def inside(s, h, g, rims, t, after):
    return pl.pallas_call(
        inside_kernel,
        out_shape=jax.ShapeDtypeStruct(s.shape, jnp.float32),
        in_specs=[VMEM] * 5 + [ANY],
        out_specs=VMEM,
        input_output_aliases={4: 0},
        compiler_params=pltpu.CompilerParams(vmem_limit_bytes=24 * MIB),
        name="inside",
    )(s, h, g, rims, t, after)


def last_kernel(t_ref, h_ref, g_ref, rims, out, buf, sem):
    L, R, W = t_ref.shape

    def send(l):
        return pltpu.make_async_copy(buf.at[l], out.at[l], sem.at[l])

    def body(l, _):
        def put(r, c, value):
            buf[(l,) + tile(r, c)] = value

        def halo(c):
            return halo_rows(rims, (4, 5), pl.ds(LANES * c, LANES), l)

        layer_step(l, t_ref, h_ref, g_ref, halo, put)
        send(l).start()
        return 0

    lax.fori_loop(1, L - 1, body, 0)

    def drain(l, _):
        send(l).wait()
        return 0

    lax.fori_loop(1, L - 1, drain, 0)


def last_layers(t, h, g, rims):
    L = t.shape[0]
    return pl.pallas_call(
        last_kernel,
        out_shape=jax.ShapeDtypeStruct(t.shape, jnp.float32),
        in_specs=[VMEM] * 4,
        out_specs=HBM,
        scratch_shapes=[pltpu.VMEM(t.shape, jnp.float32), pltpu.SemaphoreType.DMA((L,))],
        compiler_params=pltpu.CompilerParams(vmem_limit_bytes=24 * MIB),
        name="last_layers",
    )(t, h, g, rims)


def near_of(side):
    me = lax.axis_index("tier")
    return (me ^ 1, me ^ 2) if side == 0 else (me ^ 2, me ^ 1)


def routes(tier, tile):
    odd = tile % 2
    return tier ^ (1 + odd), tier ^ (2 - odd)


def entries(tiers):
    me = lax.axis_index("tier")
    if tiers != 4:
        return [(2 * me + i, j) for i in range(2) for j in range(2 * tiers)]
    listed = []
    for side in range(2):
        near, target = near_of(side)
        columns = [2 * me, 2 * me + 1, 2 * near, 2 * near + 1]
        for who in (target, me):
            listed += [(2 * who + i, j) for i in range(2) for j in columns]
    return listed


def rim_entries(tiers):
    me = lax.axis_index("tier")
    return [me ^ q if tiers == 4 else q for q in range(tiers)]


def table_kernel(tiers, ops, table, rim_table):
    regions = ops.shape[0]
    for k, (i, j) in enumerate(entries(tiers)):
        for g in range(regions):
            table[k, g] = jnp.full((ROWS, LANES), ops[g, i, j], jnp.float32)
    lane, upper = lane_ids(), row_ids() < 4
    me = lax.axis_index("tier")
    for q, source in enumerate(rim_entries(tiers)):
        for k in range(2):
            value = jnp.zeros((ROWS, LANES), jnp.float32)
            for g in range(regions):
                a, b = ops[g, 2 * me, 2 * source + k], ops[g, 2 * me + 1, 2 * source + 1 - k]
                value = jnp.where(lane == g, jnp.where(upper, a, b), value)
            rim_table[2 * q + k] = value


def make_tables(tiers, ops):
    regions = ops.shape[0]
    f32 = jnp.float32
    count, rims = 32 if tiers == 4 else 4 * tiers, 2 * tiers
    return pl.pallas_call(
        functools.partial(table_kernel, tiers),
        out_shape=(pltpu.VMEM((count, regions, ROWS, LANES), f32), pltpu.VMEM((rims, ROWS, LANES), f32)),
        in_specs=[SMEM],
        out_specs=[VMEM, VMEM],
        compiler_params=pltpu.CompilerParams(vmem_limit_bytes=16 * MIB),
        name="make_tables",
    )(ops)


def product(table, at, zone, refs, partial, base, put):
    regions = table.shape[1]
    R, W = refs[0][0].shape[1:]
    S = R // ROWS

    def body(c, _):
        lanes = pl.ds(pl.multiple_of(c * LANES, LANES), LANES)
        whole = pl.ds(pl.multiple_of(base + c * LANES, LANES), LANES)
        for r0 in range(0, S, 2):
            rows = [pl.ds(ROWS * r, ROWS) for r in range(r0, min(S, r0 + 2))]
            zones = [zone[x, whole] for x in rows]
            for i in range(2):
                totals = [None] * len(rows)
                for j, (ref, index) in enumerate(refs):
                    values = [table[at + i * len(refs) + j, g] for g in range(regions)]
                    for k, x in enumerate(rows):
                        term = choose(values, zones[k]) * ref[index, x, lanes]
                        totals[k] = term if totals[k] is None else totals[k] + term
                for k, x in enumerate(rows):
                    for ref in partial:
                        totals[k] = totals[k] + ref[i, x, lanes]
                    put(i, x, lanes, whole, totals[k])
        return 0

    lax.fori_loop(0, W // LANES, body, 0)


def both(own, near):
    return [(own, 0), (own, 1), (near, 0), (near, 1)]


def put_in(out):
    def put(i, rows, lanes, whole, value):
        out[i, rows, lanes] = value

    return put


def way_of_tile():
    return lax.axis_index("tile") % 2


def combine_kernel(table, zone, own, near, _, out):
    product(table, 16 * way_of_tile(), zone, both(own, near), [], 0, put_in(out))


def combine(table, zone, own, near, after):
    return pl.pallas_call(
        combine_kernel,
        out_shape=pltpu.VMEM(own.shape, jnp.float32),
        in_specs=[VMEM] * 4 + [ANY],
        out_specs=VMEM,
        compiler_params=pltpu.CompilerParams(vmem_limit_bytes=16 * MIB),
        name="combine",
    )(table, zone, own, near, after)


def rim_product(rim_table, pairs, zones, lanes):
    zones = zones[:, lanes].astype(jnp.int32)
    value = None
    for at, planes in pairs:
        for k, x in enumerate((planes, pltpu.roll(planes, 4, 0))):
            term = lookup(rim_table[at + k], zones) * x
            value = term if value is None else value + term
    return value


def own_kernel(table, zone, own, near, _, base):
    product(table, 16 * way_of_tile() + 8, zone, both(own, near), [], 0, put_in(base))


def own_part(table, zone, own, near, after):
    return pl.pallas_call(
        own_kernel,
        out_shape=pltpu.VMEM(own.shape, jnp.float32),
        in_specs=[VMEM] * 4 + [ANY],
        out_specs=VMEM,
        compiler_params=pltpu.CompilerParams(vmem_limit_bytes=16 * MIB),
        name="own_part",
    )(table, zone, own, near, after)


def bond_kernel(tiers, zone, table, rim_table, rims, heat, h_ref, g_ref, t_in, *refs):
    pairs = tiers == 4
    (edge_zones, *arrays), (t, out, rim) = refs[:-3], refs[-3:]
    L, R, W = t.shape
    C = W // LANES
    row = row_ids()
    if pairs:
        base, part, *edges = arrays

        for i in range(2):
            for r in range(R // ROWS):
                for c in range(C):
                    t[(i * (L - 1),) + tile(r, c)] = base[(i,) + tile(r, c)] + part[(i,) + tile(r, c)]
    else:
        planes, edges = arrays

        def put(i, rows, lanes, whole, value):
            t[i * (L - 1), rows, lanes] = value

        product(table, 0, zone, [(planes, k) for k in range(2 * tiers)], [], 0, put)
    gone = ((row % 4 == 0) & jnp.logical_not(above_exists())) | ((row % 4 == 3) & jnp.logical_not(below_exists()))

    for c in range(C):
        lanes = pl.ds(c * LANES, LANES)
        tiles = [edges[q][:, lanes] if pairs else edges[q, :, lanes] for q in range(tiers)]
        value = rim_product(rim_table, [(2 * q, x) for q, x in enumerate(tiles)], edge_zones, lanes)
        value = jnp.where(gone, 0.0, value)
        rim[:, lanes] = value
        for i in range(2):
            t[i * (L - 1), pl.ds(0, 1), lanes] = value[4 * i + 1 : 4 * i + 2]
            t[i * (L - 1), pl.ds(R - 1, 1), lanes] = value[4 * i + 2 : 4 * i + 3]

    def plane(p, _):
        own, near = p * (L - 1), 1 + p * (L - 3)
        heated = jnp.where(p == 0, 1.0, 0.0)

        def get_s(r, c):
            return t[(own,) + tile(r, c)]

        def get_h(r, c):
            return h_ref[(own,) + tile(r, c)]

        def get_g(r, c):
            return g_ref[(own,) + tile(r, c)]

        def get_z(r, c, s, h):
            at = (near,) + tile(r, c)
            return (h + h_ref[at]) * (t[at] - s) + heated * heat[tile(r, c)]

        def halo(c):
            lanes = pl.ds(LANES * c, LANES)
            ha, hb = pick(rims.at[1], 0, own, lanes, 0), pick(rims.at[3], 0, own, lanes, ROWS - 1)
            return pltpu.roll(rim[:, lanes], (2 - p) * 4 % ROWS, 0), ha, pltpu.roll(rim[:, lanes], 4 - 4 * p, 0), hb

        def put_out(r, c, value):
            out[(p,) + tile(r, c)] = value

        stencil(R, W, get_s, get_h, get_z, halo, put_out, get_g=get_g)
        return 0

    lax.fori_loop(0, 2, plane, 0)


def bond(tiers, zone, tables, rims, heat, h, g, t, edge_zones, arrays):
    _, R, W = t.shape
    args = (zone, *tables, rims, heat, h, g, t, edge_zones, *arrays)
    f32 = jnp.float32
    return pl.pallas_call(
        functools.partial(bond_kernel, tiers),
        out_shape=(
            jax.ShapeDtypeStruct(t.shape, f32),
            jax.ShapeDtypeStruct((2, R, W), f32),
        ),
        in_specs=[VMEM] * len(args),
        out_specs=[VMEM] * 2,
        scratch_shapes=[pltpu.VMEM((ROWS, W), f32)],
        input_output_aliases={7: 0},
        compiler_params=pltpu.CompilerParams(vmem_limit_bytes=24 * MIB),
        name="bond",
    )(*args)


def final_kernel(tiers, zone, table, *refs):
    arrays, (_, out, buf, sem) = refs[:-4], refs[-4:]
    L, R, W = out.shape

    def put(i, rows, lanes, whole, value):
        buf[i, rows, lanes] = value

    if tiers != 4:
        product(table, 0, zone, [(arrays[0], k) for k in range(2 * tiers)], [], 0, put)
    copies = []
    for i in range(2):
        if tiers == 4:
            base, part = arrays
            for r in range(R // ROWS):
                for c in range(W // LANES):
                    buf[(i,) + tile(r, c)] = base[(i,) + tile(r, c)] + part[(i,) + tile(r, c)]
        copies.append(pltpu.make_async_copy(buf.at[i], out.at[i * (L - 1)], sem.at[i]))
        copies[i].start()
    for copy in copies:
        copy.wait()


def final_planes(tiers, zone, table, arrays, out):
    args = (zone, table, *arrays, out)
    _, R, W = out.shape
    return pl.pallas_call(
        functools.partial(final_kernel, tiers),
        out_shape=jax.ShapeDtypeStruct(out.shape, jnp.float32),
        in_specs=[VMEM] * (len(args) - 1) + [HBM],
        out_specs=HBM,
        scratch_shapes=[pltpu.VMEM((2, R, W), jnp.float32), pltpu.SemaphoreType.DMA((2,))],
        input_output_aliases={len(args) - 1: 0},
        compiler_params=pltpu.CompilerParams(vmem_limit_bytes=16 * MIB),
        name="final_planes",
    )(*args)


def across(value, bits, tiers):
    return lax.ppermute(value, "tier", [(i, i ^ bits) for i in range(tiers)])


def every(value, tiers):
    gathered = lax.all_gather(value, "tier", axis=0, tiled=False)
    return gathered.reshape((tiers * value.shape[0],) + value.shape[1:]) if value.ndim == 3 else gathered


def along(value, way, tiers, tiles):
    places = [(tier, tile) for tier in range(tiers) for tile in range(tiles)]
    pairs = [(tier * tiles + tile, routes(tier, tile)[way] * tiles + tile) for tier, tile in places]
    return lax.ppermute(value, ("tier", "tile"), pairs)


def exchange(tiers, tiles, table, zone, planes, after):
    if tiers != 4:
        return (every(planes, tiers),)
    near = along(planes, 0, tiers, tiles)
    total = combine(table, zone, planes, near, after)
    return own_part(table, zone, planes, near, total), along(total, 1, tiers, tiles)


def local(warming, substance, zone, patch, kap, power, ops):
    tiers, tiles = lax.axis_size("tier"), lax.axis_size("tile")
    s, lab, patch = warming[0], substance[0], patch[0]

    planes, heat, s, lab, h = begin(s, lab, patch, kap, power)
    swap_a, swap_b = pack_rows(s, lab, heat, zone, kap)
    pairs = [(i, i ^ 1) for i in range(tiles) if i ^ 1 < tiles]
    got_a = lax.ppermute(swap_a, "tile", pairs)
    pairs = [(i, ((i - 1) ^ 1) + 1) for i in range(1, tiles - 1 + tiles % 2)]
    got_b = lax.ppermute(swap_b, "tile", pairs)
    tables = make_tables(tiers, ops)
    h, g = faces(lab, kap, h)
    arrays = exchange(tiers, tiles, tables[0], zone, planes, h)
    edges, edge_zones, rims = edge_rows(swap_a, swap_b, got_a, got_b)
    h, g = more_faces(lab, kap, h, g, edges)
    if tiers == 4:
        edges = (edges, *(across(edges, bits, tiers) for bits in (1, 2, 3)))
    else:
        edges = (every(edges, tiers),)
    t = outer(s, h, g, rims)
    t, planes = bond(tiers, zone, tables, rims, heat, h, g, t, edge_zones, (*arrays, *edges))
    t = inside(s, h, g, rims, t, planes)
    arrays = exchange(tiers, tiles, tables[0], zone, planes, t)
    out = last_layers(t, h, g, rims)
    out = final_planes(tiers, zone, tables[0], arrays, out)
    return out[None]


def solution(mesh):
    in_specs = (
        P("tier", None, "tile", None),
        P("tier", None, "tile", None),
        P("tile", None),
        P("tier", "tile", None),
        P(),
        P("tier", None),
        P(),
    )
    out_specs = P("tier", None, "tile", None)
    return jax.shard_map(local, mesh=mesh, in_specs=in_specs, out_specs=out_specs, check_vma=False)
```

time: 51.5 us -> 47.4 us (0.920)
  waiting for transfers between devices: 12 us -> 6.98 us
  starting transfers between devices: 11.1 us -> 13.7 us
  Pallas kernels: 28.1 us -> 26.4 us
    pallas_call x4 -> x6, Pallas kernels: 2.65 us -> 7.34 us  [the longest x1 2.85 us: more_faces(): pl.pallas_call(more_faces_kernel, out_shape=(jax.ShapeDtypeStruct(lab.sha...]
    ppermute x4 -> x3, waiting for transfers between devices: 4.71 us -> 1.15 us  [across(): return lax.ppermute(value, 'tier', [(i, i ^ bits) for i in range(tiers)])]
    pallas_call x1, Pallas kernels: 4.83 us -> 1.54 us  [faces(): pl.pallas_call(faces_kernel, out_shape=(jax.ShapeDtypeStruct(lab.shape, j...]
    ppermute x4, starting transfers between devices: 6.74 us -> 9.43 us  [along(): return lax.ppermute(value, ('tier', 'tile'), pairs)]
    pallas_call x1, Pallas kernels: 2.93 us -> 0.88 us  [bond(): pl.pallas_call(functools.partial(bond_kernel, tiers), out_shape=(jax.Shap...]
    ppermute x4, waiting for transfers between devices: 7.3 us -> 5.82 us  [along(): return lax.ppermute(value, ('tier', 'tile'), pairs)]
    pallas_call x1, Pallas kernels: 4.84 us -> 3.68 us  [begin(): pl.pallas_call(begin_kernel, out_shape=(pltpu.VMEM((2, R, W), f32), pltpu...]
    pallas_call x1 -> x2, Pallas kernels: 0.82 us -> 1.63 us  [combine(): pl.pallas_call(combine_kernel, out_shape=pltpu.VMEM(own.shape, jnp.float3...]
  transfers between devices with their start and end apart: 10 -> 9, of which waited for: 7 -> 4; matrix products, arithmetic and copies ran while one was open for 0% -> 0% of each run, Pallas kernels for 35% -> 43%
where the time goes in v5:
time: 47.4 us; the launch traced here: 47.3 us
  Pallas kernels  26.4 us (56%)
  starting transfers between devices  13.7 us (29%)
  waiting for transfers between devices  6.98 us (15%)
    ppermute x4, starting transfers between devices, along(): return lax.ppermute(value, ('tier', 'tile'), pairs)  9.43 us
    ppermute x4, waiting for transfers between devices, along(): return lax.ppermute(value, ('tier', 'tile'), pairs)  5.82 us
    pallas_call x1, Pallas kernels, last_layers(): pl.pallas_call(last_kernel, out_shape=jax.ShapeDtypeStruct(t.shape, jnp.f...  5.3 us
    pallas_call x1, Pallas kernels, inside(): pl.pallas_call(inside_kernel, out_shape=jax.ShapeDtypeStruct(s.shape, jnp...  3.78 us
    pallas_call x1, Pallas kernels, begin(): pl.pallas_call(begin_kernel, out_shape=(pltpu.VMEM((2, R, W), f32), pltpu...  3.68 us
    ppermute x3, starting transfers between devices, across(): return lax.ppermute(value, 'tier', [(i, i ^ bits) for i in range(tiers)])  3.55 us
    pallas_call x1, Pallas kernels, more_faces(): pl.pallas_call(more_faces_kernel, out_shape=(jax.ShapeDtypeStruct(lab.sha...  2.85 us
    pallas_call x1, Pallas kernels, pack_rows(): pl.pallas_call(pack_kernel, out_shape=(pltpu.VMEM((rows, W), f32),) * 2,...  1.98 us
  transfers between devices with their start and end apart: 9, of which 4 were waited for; matrix products, arithmetic and copies ran while one was open for 0% of the time, Pallas kernels for 43%

profile of v5, /device:TPU:0, one launch (start us, length us, event | category | flops | bytes accessed | tf_op | source)
XLA Modules:
  0.0 47.3 jit_solution(8994886849540690658)
XLA Ops:
  0.0 0.0 copy-start
  0.0 0.0 copy-start.2
  0.0 3.7 %begin.1 = (f32[2,32,2048]{2,1,0:T(8,128)S(1)}, f32[32,2048]{1,0:T(8,128)S(1)}, f32[16,32,2048]{2,1,0:T(8,128)S(1)}, s32[16,32,2048]{2,1,0:T(8,128)S(1)}, f32[16,32,2048]{2,1,0:T(8,128)S(1)}) custom-call(f32[16,32,2048]{2,1,0:T(8,128)} %bitcast.4, s32[16,32,2048]{2,1,0:T(8,128)} %bitcast.5, s32[32,2048]{1,0:T(8,128)} %bitcast.6, f32[16]{0:T(128)} %kap.5, ...), custom_call_target="tpu_custom_call" | custom-call | tf_op jit(solution)/shard_map/begin/pallas_call | solution.py:186
  3.7 3.0 %collective-permute-start.2 = (f32[2,32,2048]{2,1,0:T(8,128)S(1)}, f32[2,32,2048]{2,1,0:T(8,128)S(1)}, u32[]{:S(2)}, u32[]{:S(2)}) collective-permute-start(f32[2,32,2048]{2,1,0:T(8,128)S(1)} %get-tuple-element.38.own), channel_id=1, source_target_pairs={{0,8},{1,17},{2,10},{3,19},{4,12},{5,21},{6,14},{7,23},{8,0},{9,25... | collective-permute-start | bytes 1572872 | tf_op jit(solution)/shard_map/ppermute | solution.py:803
  6.7 0.0 copy-done
  6.7 0.0 copy-done.2
  6.7 0.0 copy-start.1
  6.7 2.0 %pack_rows.1 = (f32[56,2048]{1,0:T(8,128)S(1)}, f32[56,2048]{1,0:T(8,128)S(1)}) custom-call(f32[16,32,2048]{2,1,0:T(8,128)S(1)} %get-tuple-element.25.s.s_ref, s32[16,32,2048]{2,1,0:T(8,128)S(1)} %get-tuple-element.26.lab, f32[32,2048]{1,0:T(8,128)S(1)} %get-tuple-element.27.heat, s32[32,2048]{1,0:T(8,128)S(1)} %copy-done, f32[16]{0:T(128)S(1)} %copy-done.2), custom_call_target="tpu_custom_call" | custom-call | tf_op jit(solution)/shard_map/pack_rows/pallas_call | solution.py:278
  8.7 0.1 collective-permute-start
  8.8 0.7 %collective-permute-start.1 = (f32[56,2048]{1,0:T(8,128)S(1)}, f32[56,2048]{1,0:T(8,128)S(1)}, u32[]{:S(2)}, u32[]{:S(2)}) collective-permute-start(f32[56,2048]{1,0:T(8,128)S(1)} %get-tuple-element.29.own_b), channel_id=1, source_target_pairs={{1,2},{2,1},{3,4},{4,3},{5,6},{6,5},{9,10},{10,9},{11,12},{12,11},... | collective-permute-start | bytes 1376264 | tf_op jit(solution)/shard_map/ppermute | solution.py:823
  9.5 0.0 copy-done.1
  9.5 1.4 %make_tables.1 = (f32[32,8,8,128]{3,2,1,0:T(8,128)S(1)}, f32[8,8,128]{2,1,0:T(8,128)S(1)}) custom-call(f32[8,8,8]{2,1,0:T(8,128)S(1)} %copy-done.1), custom_call_target="tpu_custom_call" | custom-call | tf_op jit(solution)/shard_map/make_tables/pallas_call | solution.py:580
  10.9 1.5 %faces.1 = (f32[16,32,2048]{2,1,0:T(8,128)S(1)}, f32[16,32,2048]{2,1,0:T(8,128)S(1)}) custom-call(s32[16,32,2048]{2,1,0:T(8,128)S(1)} %get-tuple-element.26.lab, f32[16]{0:T(128)S(1)} %copy-done.2, f32[16,32,2048]{2,1,0:T(8,128)S(1)} %get-tuple-element.31.h_in), custom_call_target="tpu_custom_call", output_to_operand_aliasing={{0}: (2, {})} | custom-call | tf_op jit(solution)/shard_map/faces/pallas_call | solution.py:389
  12.5 1.4 %collective-permute-done.2.near = f32[2,32,2048]{2,1,0:T(8,128)S(1)} collective-permute-done((f32[2,32,2048]{2,1,0:T(8,128)S(1)}, f32[2,32,2048]{2,1,0:T(8,128)S(1)}, u32[]{:S(2)}, u32[]{:S(2)}) %collective-permute-start.2) | collective-permute-done | bytes 524320 | tf_op jit(solution)/shard_map/ppermute | solution.py:803
  13.9 0.8 %combine.2._ = f32[2,32,2048]{2,1,0:T(8,128)S(1)} custom-call(f32[32,8,8,128]{3,2,1,0:T(8,128)S(1)} %get-tuple-element.23.table, s32[32,2048]{1,0:T(8,128)S(1)} %copy-done, f32[2,32,2048]{2,1,0:T(8,128)S(1)} %get-tuple-element.38.own, f32[2,32,2048]{2,1,0:T(8,128)S(1)} %collective-permute-done.2.near, f32[16,32,2048]{2,1,0:T(8,128)S(1)} %get-tuple-element.32.h_in._), custom_call_target="tpu_custom_call" | custom-call | tf_op jit(solution)/shard_map/combine/pallas_call | solution.py:637
  14.7 2.1 %collective-permute-start.3 = (f32[2,32,2048]{2,1,0:T(8,128)S(1)}, f32[2,32,2048]{2,1,0:T(8,128)S(1)}, u32[]{:S(2)}, u32[]{:S(2)}) collective-permute-start(f32[2,32,2048]{2,1,0:T(8,128)S(1)} %combine.2._), channel_id=1, source_target_pairs={{0,16},{1,9},{2,18},{3,11},{4,20},{5,13},{6,22},{7,15},{8,24},{9,1... | collective-permute-start | bytes 1572872 | tf_op jit(solution)/shard_map/ppermute | solution.py:803
  16.8 0.0 collective-permute-done.got_a
  16.8 0.0 collective-permute-done.1.got_b
  16.8 0.2 edge_rows.1
  17.0 1.6 %collective-permute-start.4 = (f32[8,2048]{1,0:T(8,128)S(1)}, f32[8,2048]{1,0:T(8,128)S(1)}, u32[]{:S(2)}, u32[]{:S(2)}) collective-permute-start(f32[8,2048]{1,0:T(8,128)S(1)} %get-tuple-element.34._.refs_3_), channel_id=1, source_target_pairs={{0,8},{8,0},{16,24},{24,16},{1,9},{9,1},{17,25},{25,17},{2,10},{10... | collective-permute-start | bytes 196616 | tf_op jit(solution)/shard_map/ppermute | solution.py:792
  18.6 0.5 %collective-permute-start.5 = (f32[8,2048]{1,0:T(8,128)S(1)}, f32[8,2048]{1,0:T(8,128)S(1)}, u32[]{:S(2)}, u32[]{:S(2)}) collective-permute-start(f32[8,2048]{1,0:T(8,128)S(1)} %get-tuple-element.34._.refs_3_), channel_id=1, source_target_pairs={{0,16},{8,24},{16,0},{24,8},{1,17},{9,25},{17,1},{25,9},{2,18},{10... | collective-permute-start | bytes 196616 | tf_op jit(solution)/shard_map/ppermute | solution.py:792
  19.1 1.5 %collective-permute-start.6 = (f32[8,2048]{1,0:T(8,128)S(1)}, f32[8,2048]{1,0:T(8,128)S(1)}, u32[]{:S(2)}, u32[]{:S(2)}) collective-permute-start(f32[8,2048]{1,0:T(8,128)S(1)} %get-tuple-element.34._.refs_3_), channel_id=1, source_target_pairs={{0,24},{8,16},{16,8},{24,0},{1,25},{9,17},{17,9},{25,1},{2,26},{10... | collective-permute-start | bytes 196616 | tf_op jit(solution)/shard_map/ppermute | solution.py:792
  20.6 2.9 %more_faces.1 = (f32[16,32,2048]{2,1,0:T(8,128)S(1)}, f32[16,32,2048]{2,1,0:T(8,128)S(1)}) custom-call(s32[16,32,2048]{2,1,0:T(8,128)S(1)} %get-tuple-element.26.lab, f32[16]{0:T(128)S(1)} %copy-done.2, f32[16,32,2048]{2,1,0:T(8,128)S(1)} %get-tuple-element.32.h_in._, ...), custom_call_target="tpu_custom_call", output_to_operand_aliasing={{0}: (2, {}), {1}: (3, {})} | custom-call | tf_op jit(solution)/shard_map/more_faces/pallas_call | solution.py:405
  23.4 0.6 %outer.1.t_in = f32[16,32,2048]{2,1,0:T(8,128)S(1)} custom-call(f32[16,32,2048]{2,1,0:T(8,128)S(1)} %get-tuple-element.25.s.s_ref, f32[16,32,2048]{2,1,0:T(8,128)S(1)} %get-tuple-element.35.h_ref, f32[16,32,2048]{2,1,0:T(8,128)S(1)} %get-tuple-element.36.g_ref, f32[6,16,2048]{2,1,0:T(8,128)S(1)} %get-tuple-element.30.rims), custom_call_target="tpu_custom_call" | custom-call | tf_op jit(solution)/shard_map/outer/pallas_call | solution.py:458
  24.1 0.8 %own_part.2.refs_1_ = f32[2,32,2048]{2,1,0:T(8,128)S(1)} custom-call(f32[32,8,8,128]{3,2,1,0:T(8,128)S(1)} %get-tuple-element.23.table, s32[32,2048]{1,0:T(8,128)S(1)} %copy-done, f32[2,32,2048]{2,1,0:T(8,128)S(1)} %get-tuple-element.38.own, f32[2,32,2048]{2,1,0:T(8,128)S(1)} %collective-permute-done.2.near, f32[2,32,2048]{2,1,0:T(8,128)S(1)} %combine.2._), custom_call_target="tpu_custom_call" | custom-call | tf_op jit(solution)/shard_map/own_part/pallas_call | solution.py:662
  24.9 0.0 collective-permute-done.4.refs_4_
  24.9 1.1 %collective-permute-done.5.refs_5_ = f32[8,2048]{1,0:T(8,128)S(1)} collective-permute-done((f32[8,2048]{1,0:T(8,128)S(1)}, f32[8,2048]{1,0:T(8,128)S(1)}, u32[]{:S(2)}, u32[]{:S(2)}) %collective-permute-start.5) | collective-permute-done | bytes 65568 | tf_op jit(solution)/shard_map/ppermute | solution.py:792
  26.1 0.0 collective-permute-done.6.refs_6_
  26.1 0.0 collective-permute-done.3.refs_2_
  26.1 0.9 %bond.1 = (f32[16,32,2048]{2,1,0:T(8,128)S(1)}, f32[2,32,2048]{2,1,0:T(8,128)S(1)}) custom-call(s32[32,2048]{1,0:T(8,128)S(1)} %copy-done, f32[32,8,8,128]{3,2,1,0:T(8,128)S(1)} %get-tuple-element.23.table, f32[8,8,128]{2,1,0:T(8,128)S(1)} %get-tuple-element.24.rim_table, ...), custom_call_target="tpu_custom_call", output_to_operand_aliasing={{0}: (7, {})} | custom-call | tf_op jit(solution)/shard_map/bond/pallas_call | solution.py:739
  27.0 2.1 %collective-permute-start.7 = (f32[2,32,2048]{2,1,0:T(8,128)S(1)}, f32[2,32,2048]{2,1,0:T(8,128)S(1)}, u32[]{:S(2)}, u32[]{:S(2)}) collective-permute-start(f32[2,32,2048]{2,1,0:T(8,128)S(1)} %get-tuple-element.39._.own), channel_id=1, source_target_pairs={{0,8},{1,17},{2,10},{3,19},{4,12},{5,21},{6,14},{7,23},{8,0},{9,25... | collective-permute-start | bytes 1572872 | tf_op jit(solution)/shard_map/ppermute | solution.py:803
  29.0 3.8 %inside.1._.t_ref = f32[16,32,2048]{2,1,0:T(8,128)S(1)} custom-call(f32[16,32,2048]{2,1,0:T(8,128)S(1)} %get-tuple-element.25.s.s_ref, f32[16,32,2048]{2,1,0:T(8,128)S(1)} %get-tuple-element.35.h_ref, f32[16,32,2048]{2,1,0:T(8,128)S(1)} %get-tuple-element.36.g_ref, f32[6,16,2048]{2,1,0:T(8,128)S(1)} %get-tuple-element.30.rims, ...), custom_call_target="tpu_custom_call", output_to_operand_aliasing={{}: (4, {})} | custom-call | tf_op jit(solution)/shard_map/inside/pallas_call | solution.py:482
  32.8 3.4 %collective-permute-done.7.near = f32[2,32,2048]{2,1,0:T(8,128)S(1)} collective-permute-done((f32[2,32,2048]{2,1,0:T(8,128)S(1)}, f32[2,32,2048]{2,1,0:T(8,128)S(1)}, u32[]{:S(2)}, u32[]{:S(2)}) %collective-permute-start.7) | collective-permute-done | bytes 524320 | tf_op jit(solution)/shard_map/ppermute | solution.py:803
  36.2 0.8 %combine.3._ = f32[2,32,2048]{2,1,0:T(8,128)S(1)} custom-call(f32[32,8,8,128]{3,2,1,0:T(8,128)S(1)} %get-tuple-element.23.table, s32[32,2048]{1,0:T(8,128)S(1)} %copy-done, f32[2,32,2048]{2,1,0:T(8,128)S(1)} %get-tuple-element.39._.own, f32[2,32,2048]{2,1,0:T(8,128)S(1)} %collective-permute-done.7.near, f32[16,32,2048]{2,1,0:T(8,128)S(1)} %inside.1._.t_ref), custom_call_target="tpu_custom_call" | custom-call | tf_op jit(solution)/shard_map/combine/pallas_call | solution.py:637
  37.0 2.3 %collective-permute-start.8 = (f32[2,32,2048]{2,1,0:T(8,128)S(1)}, f32[2,32,2048]{2,1,0:T(8,128)S(1)}, u32[]{:S(2)}, u32[]{:S(2)}) collective-permute-start(f32[2,32,2048]{2,1,0:T(8,128)S(1)} %combine.3._), channel_id=1, source_target_pairs={{0,16},{1,9},{2,18},{3,11},{4,20},{5,13},{6,22},{7,15},{8,24},{9,1... | collective-permute-start | bytes 1572872 | tf_op jit(solution)/shard_map/ppermute | solution.py:803
  39.3 5.3 %last_layers.1.refs_2_ = f32[16,32,2048]{2,1,0:T(8,128)} custom-call(f32[16,32,2048]{2,1,0:T(8,128)S(1)} %inside.1._.t_ref, f32[16,32,2048]{2,1,0:T(8,128)S(1)} %get-tuple-element.35.h_ref, f32[16,32,2048]{2,1,0:T(8,128)S(1)} %get-tuple-element.36.g_ref, f32[6,16,2048]{2,1,0:T(8,128)S(1)} %get-tuple-element.30.rims), custom_call_target="tpu_custom_call" | custom-call | tf_op jit(solution)/shard_map/last_layers/pallas_call | solution.py:521
  44.6 0.8 %own_part.3.refs_0_ = f32[2,32,2048]{2,1,0:T(8,128)S(1)} custom-call(f32[32,8,8,128]{3,2,1,0:T(8,128)S(1)} %get-tuple-element.23.table, s32[32,2048]{1,0:T(8,128)S(1)} %copy-done, f32[2,32,2048]{2,1,0:T(8,128)S(1)} %get-tuple-element.39._.own, f32[2,32,2048]{2,1,0:T(8,128)S(1)} %collective-permute-done.7.near, f32[2,32,2048]{2,1,0:T(8,128)S(1)} %combine.3._), custom_call_target="tpu_custom_call" | custom-call | tf_op jit(solution)/shard_map/own_part/pallas_call | solution.py:662
  45.4 1.0 %collective-permute-done.8.refs_1_ = f32[2,32,2048]{2,1,0:T(8,128)S(1)} collective-permute-done((f32[2,32,2048]{2,1,0:T(8,128)S(1)}, f32[2,32,2048]{2,1,0:T(8,128)S(1)}, u32[]{:S(2)}, u32[]{:S(2)}) %collective-permute-start.8) | collective-permute-done | bytes 524320 | tf_op jit(solution)/shard_map/ppermute | solution.py:803
  46.4 0.8 %final_planes.1 = f32[16,32,2048]{2,1,0:T(8,128)} custom-call(s32[32,2048]{1,0:T(8,128)S(1)} %copy-done, f32[32,8,8,128]{3,2,1,0:T(8,128)S(1)} %get-tuple-element.23.table, f32[2,32,2048]{2,1,0:T(8,128)S(1)} %own_part.3.refs_0_, f32[2,32,2048]{2,1,0:T(8,128)S(1)} %collective-permute-done.8.refs_1_, ...), custom_call_target="tpu_custom_call", output_to_operand_aliasing={{}: (4, {})} | custom-call | tf_op jit(solution)/shard_map/final_planes/pallas_call | solution.py:779
Async XLA Ops:
  0.0 6.7 %copy-start = (s32[32,2048]{1,0:T(8,128)S(1)}, s32[32,2048]{1,0:T(8,128)}, u32[]{:S(2)}) copy-start(s32[32,2048]{1,0:T(8,128)} %zone.13) | copy-start | bytes 786436
  0.0 6.7 %copy-start.2 = (f32[16]{0:T(128)S(1)}, f32[16]{0:T(128)}, u32[]{:S(2)}) copy-start(f32[16]{0:T(128)} %kap.5) | copy-start | bytes 196
  3.7 10.2 %collective-permute-start.2 = (f32[2,32,2048]{2,1,0:T(8,128)S(1)}, f32[2,32,2048]{2,1,0:T(8,128)S(1)}, u32[]{:S(2)}, u32[]{:S(2)}) collective-permute-start(f32[2,32,2048]{2,1,0:T(8,128)S(1)} %get-tuple-element.38.own), channel_id=1, source_target_pairs={{0,8},{1,17},{2,10},{3,19},{4,12},{5,21},{6,14},{7,23},{8,0},{9,25... | collective-permute-start | bytes 1572872 | tf_op jit(solution)/shard_map/ppermute | solution.py:803
  6.7 2.8 %copy-start.1 = (f32[8,8,8]{2,1,0:T(8,128)S(1)}, f32[8,8,8]{2,1,0:T(8,128)}, u32[]{:S(2)}) copy-start(f32[8,8,8]{2,1,0:T(8,128)} %ops.1) | copy-start | bytes 6148
  8.7 8.1 %collective-permute-start = (f32[56,2048]{1,0:T(8,128)S(1)}, f32[56,2048]{1,0:T(8,128)S(1)}, u32[]{:S(2)}, u32[]{:S(2)}) collective-permute-start(f32[56,2048]{1,0:T(8,128)S(1)} %get-tuple-element.28.own_a), channel_id=1, source_target_pairs={{0,1},{1,0},{2,3},{3,2},{4,5},{5,4},{6,7},{7,6},{8,9},{9,8},{10,11... | collective-permute-start | bytes 1376264 | tf_op jit(solution)/shard_map/ppermute | solution.py:821
  8.8 8.0 %collective-permute-start.1 = (f32[56,2048]{1,0:T(8,128)S(1)}, f32[56,2048]{1,0:T(8,128)S(1)}, u32[]{:S(2)}, u32[]{:S(2)}) collective-permute-start(f32[56,2048]{1,0:T(8,128)S(1)} %get-tuple-element.29.own_b), channel_id=1, source_target_pairs={{1,2},{2,1},{3,4},{4,3},{5,6},{6,5},{9,10},{10,9},{11,12},{12,11},... | collective-permute-start | bytes 1376264 | tf_op jit(solution)/shard_map/ppermute | solution.py:823
  14.7 11.4 %collective-permute-start.3 = (f32[2,32,2048]{2,1,0:T(8,128)S(1)}, f32[2,32,2048]{2,1,0:T(8,128)S(1)}, u32[]{:S(2)}, u32[]{:S(2)}) collective-permute-start(f32[2,32,2048]{2,1,0:T(8,128)S(1)} %combine.2._), channel_id=1, source_target_pairs={{0,16},{1,9},{2,18},{3,11},{4,20},{5,13},{6,22},{7,15},{8,24},{9,1... | collective-permute-start | bytes 1572872 | tf_op jit(solution)/shard_map/ppermute | solution.py:803
  17.0 7.9 %collective-permute-start.4 = (f32[8,2048]{1,0:T(8,128)S(1)}, f32[8,2048]{1,0:T(8,128)S(1)}, u32[]{:S(2)}, u32[]{:S(2)}) collective-permute-start(f32[8,2048]{1,0:T(8,128)S(1)} %get-tuple-element.34._.refs_3_), channel_id=1, source_target_pairs={{0,8},{8,0},{16,24},{24,16},{1,9},{9,1},{17,25},{25,17},{2,10},{10... | collective-permute-start | bytes 196616 | tf_op jit(solution)/shard_map/ppermute | solution.py:792
  18.6 7.5 %collective-permute-start.5 = (f32[8,2048]{1,0:T(8,128)S(1)}, f32[8,2048]{1,0:T(8,128)S(1)}, u32[]{:S(2)}, u32[]{:S(2)}) collective-permute-start(f32[8,2048]{1,0:T(8,128)S(1)} %get-tuple-element.34._.refs_3_), channel_id=1, source_target_pairs={{0,16},{8,24},{16,0},{24,8},{1,17},{9,25},{17,1},{25,9},{2,18},{10... | collective-permute-start | bytes 196616 | tf_op jit(solution)/shard_map/ppermute | solution.py:792
  19.1 7.0 %collective-permute-start.6 = (f32[8,2048]{1,0:T(8,128)S(1)}, f32[8,2048]{1,0:T(8,128)S(1)}, u32[]{:S(2)}, u32[]{:S(2)}) collective-permute-start(f32[8,2048]{1,0:T(8,128)S(1)} %get-tuple-element.34._.refs_3_), channel_id=1, source_target_pairs={{0,24},{8,16},{16,8},{24,0},{1,25},{9,17},{17,9},{25,1},{2,26},{10... | collective-permute-start | bytes 196616 | tf_op jit(solution)/shard_map/ppermute | solution.py:792
  27.0 9.2 %collective-permute-start.7 = (f32[2,32,2048]{2,1,0:T(8,128)S(1)}, f32[2,32,2048]{2,1,0:T(8,128)S(1)}, u32[]{:S(2)}, u32[]{:S(2)}) collective-permute-start(f32[2,32,2048]{2,1,0:T(8,128)S(1)} %get-tuple-element.39._.own), channel_id=1, source_target_pairs={{0,8},{1,17},{2,10},{3,19},{4,12},{5,21},{6,14},{7,23},{8,0},{9,25... | collective-permute-start | bytes 1572872 | tf_op jit(solution)/shard_map/ppermute | solution.py:803
  37.0 9.4 %collective-permute-start.8 = (f32[2,32,2048]{2,1,0:T(8,128)S(1)}, f32[2,32,2048]{2,1,0:T(8,128)S(1)}, u32[]{:S(2)}, u32[]{:S(2)}) collective-permute-start(f32[2,32,2048]{2,1,0:T(8,128)S(1)} %combine.3._), channel_id=1, source_target_pairs={{0,16},{1,9},{2,18},{3,11},{4,20},{5,13},{6,22},{7,15},{8,24},{9,1... | collective-permute-start | bytes 1572872 | tf_op jit(solution)/shard_map/ppermute | solution.py:803

commit v6 on v5

--- a/solution.py
+++ b/solution.py
@@ -130,14 +130,16 @@
         pltpu.make_async_copy(power_hbm, power, sem.at[1]),
         pltpu.make_async_copy(patch_hbm, patch, sem.at[2]),
     ]
-    groups = [(0, 2), (L - 2, 2), (2, L - 4)]
+    places = [pl.ds(0, 2), pl.ds(L - 2, 2), pl.ds(2, 1), pl.ds(L - 3, 1)]
+    places += [(pl.ds(3, L - 6), pl.ds(row, ROWS)) for row in sorted({0, R - ROWS})]
     layers = [
         [
-            pltpu.make_async_copy(s_hbm.at[pl.ds(l, n)], s_v.at[pl.ds(l, n)], sem.at[3 + 2 * k]),
-            pltpu.make_async_copy(lab_hbm.at[pl.ds(l, n)], lab_v.at[pl.ds(l, n)], sem.at[4 + 2 * k]),
+            pltpu.make_async_copy(s_hbm.at[at], s_v.at[at], sem.at[3 + 2 * k]),
+            pltpu.make_async_copy(lab_hbm.at[at], lab_v.at[at], sem.at[4 + 2 * k]),
         ]
-        for k, (l, n) in enumerate(groups)
+        for k, at in enumerate(places)
     ]
+    layers = layers[:2] + [sum(layers[2:], [])]
     for copy in small + layers[0] + layers[1] + layers[2]:
         copy.start()
     for copy in small:
@@ -148,12 +150,17 @@
     for c in range(C):
         for r in range(R // ROWS):
             heat[tile(r, c)] = lookup(heats, patch[tile(r, c)])
-    for copy in layers[0] + layers[1]:
+    for copy in layers[0]:
         copy.wait()
 
     def plane(p, _):
         own, near = p * (L - 1), 1 + p * (L - 3)
         heated = jnp.where(p == 0, 1.0, 0.0)
+
+        @pl.when(p == 1)
+        def _():
+            for copy in layers[1]:
+                copy.wait()
 
         def get_s(r, c):
             return s_v[(own,) + tile(r, c)]
@@ -195,7 +202,7 @@
             pltpu.VMEM((R, W), i32),
             pltpu.SMEM(kap.shape, f32),
             pltpu.VMEM(power.shape, f32),
-            pltpu.SemaphoreType.DMA((9,)),
+            pltpu.SemaphoreType.DMA((15,)),
         ],
         compiler_params=pltpu.CompilerParams(vmem_limit_bytes=16 * MIB),
         name="begin",
@@ -210,9 +217,20 @@
     return lax.axis_index("tile") < lax.axis_size("tile") - 1
 
 
-def pack_kernel(s, lab, heat, zone, kap, swap_a, swap_b, rows_v, next_v):
+def pack_kernel(
+    s_hbm, lab_hbm, s_in, lab_in, heat, zone, kap, swap_a, swap_b, s, lab, rows_v, next_v, sem
+):
     L, R, W = s.shape
     C = W // LANES
+    copies = []
+    if R > 2 * ROWS:
+        at = pl.ds(3, L - 6), pl.ds(ROWS, R - 2 * ROWS)
+        copies = [
+            pltpu.make_async_copy(s_hbm.at[at], s.at[at], sem.at[0]),
+            pltpu.make_async_copy(lab_hbm.at[at], lab.at[at], sem.at[1]),
+        ]
+    for copy in copies:
+        copy.start()
     row = row_ids()
     values = splats(kap)
     group = math.gcd(C, 4)
@@ -269,24 +287,37 @@
         for c in range(C):
             swap_a[tile(r, c)] = rows_v[(1 - odd,) + tile(r, c)]
             swap_b[tile(r, c)] = rows_v[(odd,) + tile(r, c)]
-
-
-def pack_rows(s, lab, heat, zone, kap):
+    for copy in copies:
+        copy.wait()
+
+
+def pack_rows(s, lab, s_v, lab_v, heat, zone, kap):
     L, _, W = s.shape
     f32 = jnp.float32
     rows = 3 * L + ROWS
+    s, lab = (pltpu.with_memory_space_constraint(x, pltpu.HBM) for x in (s, lab))
     return pl.pallas_call(
         pack_kernel,
-        out_shape=(pltpu.VMEM((rows, W), f32),) * 2,
-        in_specs=[VMEM] * 4 + [SMEM],
-        out_specs=[VMEM] * 2,
-        scratch_shapes=[pltpu.VMEM((2, rows, W), f32), pltpu.VMEM((2, 2 * L, W), f32)],
-        compiler_params=pltpu.CompilerParams(vmem_limit_bytes=20 * MIB),
+        out_shape=(
+            pltpu.VMEM((rows, W), f32),
+            pltpu.VMEM((rows, W), f32),
+            jax.ShapeDtypeStruct(s.shape, f32),
+            jax.ShapeDtypeStruct(lab.shape, jnp.int32),
+        ),
+        in_specs=[HBM] * 2 + [VMEM] * 4 + [SMEM],
+        out_specs=[VMEM] * 4,
+        scratch_shapes=[
+            pltpu.VMEM((2, rows, W), f32),
+            pltpu.VMEM((2, 2 * L, W), f32),
+            pltpu.SemaphoreType.DMA((2,)),
+        ],
+        input_output_aliases={2: 2, 3: 3},
+        compiler_params=pltpu.CompilerParams(vmem_limit_bytes=24 * MIB),
         name="pack_rows",
-    )(s, lab, heat, zone, kap)
-
-
-def edge_kernel(own_a, own_b, got_a, got_b, edges, zones, rims):
+    )(s, lab, s_v, lab_v, heat, zone, kap)
+
+
+def edge_kernel(own_a, own_b, got_a, got_b, _, edges, zones, rims):
     rows, W = own_a.shape
     L = (rows - ROWS) // 3
     odd = lax.axis_index("tile") % 2 == 1
@@ -319,17 +350,17 @@
             zones[pl.ds(4 * i + k_in, 1), :] = z_in
 
 
-def edge_rows(own_a, own_b, got_a, got_b):
+def edge_rows(own_a, own_b, got_a, got_b, after):
     rows, W = own_a.shape
     f32 = jnp.float32
     return pl.pallas_call(
         edge_kernel,
         out_shape=(pltpu.VMEM((ROWS, W), f32), pltpu.VMEM((ROWS, W), f32), pltpu.VMEM((6, (rows - ROWS) // 3, W), f32)),
-        in_specs=[VMEM] * 4,
+        in_specs=[VMEM] * 4 + [ANY],
         out_specs=[VMEM] * 3,
         compiler_params=pltpu.CompilerParams(vmem_limit_bytes=16 * MIB),
         name="edge_rows",
-    )(own_a, own_b, got_a, got_b)
+    )(own_a, own_b, got_a, got_b, after)
 
 
 def pick(ref, base, l, lanes, row):
@@ -805,26 +836,26 @@
 
 def exchange(tiers, tiles, table, zone, planes, after):
     if tiers != 4:
-        return (every(planes, tiers),)
+        return (every(planes, tiers),), planes
     near = along(planes, 0, tiers, tiles)
     total = combine(table, zone, planes, near, after)
-    return own_part(table, zone, planes, near, total), along(total, 1, tiers, tiles)
+    return (own_part(table, zone, planes, near, total), along(total, 1, tiers, tiles)), total
 
 
 def local(warming, substance, zone, patch, kap, power, ops):
     tiers, tiles = lax.axis_size("tier"), lax.axis_size("tile")
     s, lab, patch = warming[0], substance[0], patch[0]
 
-    planes, heat, s, lab, h = begin(s, lab, patch, kap, power)
-    swap_a, swap_b = pack_rows(s, lab, heat, zone, kap)
+    planes, heat, s_v, lab_v, h = begin(s, lab, patch, kap, power)
+    swap_a, swap_b, s, lab = pack_rows(s, lab, s_v, lab_v, heat, zone, kap)
     pairs = [(i, i ^ 1) for i in range(tiles) if i ^ 1 < tiles]
     got_a = lax.ppermute(swap_a, "tile", pairs)
     pairs = [(i, ((i - 1) ^ 1) + 1) for i in range(1, tiles - 1 + tiles % 2)]
     got_b = lax.ppermute(swap_b, "tile", pairs)
     tables = make_tables(tiers, ops)
     h, g = faces(lab, kap, h)
-    arrays = exchange(tiers, tiles, tables[0], zone, planes, h)
-    edges, edge_zones, rims = edge_rows(swap_a, swap_b, got_a, got_b)
+    arrays, _ = exchange(tiers, tiles, tables[0], zone, planes, h)
+    edges, edge_zones, rims = edge_rows(swap_a, swap_b, got_a, got_b, h)
     h, g = more_faces(lab, kap, h, g, edges)
     if tiers == 4:
         edges = (edges, *(across(edges, bits, tiers) for bits in (1, 2, 3)))
@@ -833,7 +864,7 @@
     t = outer(s, h, g, rims)
     t, planes = bond(tiers, zone, tables, rims, heat, h, g, t, edge_zones, (*arrays, *edges))
     t = inside(s, h, g, rims, t, planes)
-    arrays = exchange(tiers, tiles, tables[0], zone, planes, t)
+    arrays, _ = exchange(tiers, tiles, tables[0], zone, planes, t)
     out = last_layers(t, h, g, rims)
     out = final_planes(tiers, zone, tables[0], arrays, out)
     return out[None]

time: 47.4 us -> 46.8 us (0.987)
    pallas_call x1, Pallas kernels: 3.68 us -> 3.03 us  [begin(): pl.pallas_call(begin_kernel, out_shape=(pltpu.VMEM((2, R, W), f32), pltpu...]
  transfers between devices with their start and end apart: 9 -> 9, of which waited for: 4 -> 4; matrix products, arithmetic and copies ran while one was open for 0% -> 0% of each run, Pallas kernels for 43% -> 44%
where the time goes in v6:
time: 46.8 us; the launch traced here: 46.6 us
  Pallas kernels  26.1 us (56%)
  starting transfers between devices  13.7 us (29%)
  waiting for transfers between devices  6.68 us (14%)
    ppermute x4, starting transfers between devices, along(): return lax.ppermute(value, ('tier', 'tile'), pairs)  9.43 us
    ppermute x4, waiting for transfers between devices, along(): return lax.ppermute(value, ('tier', 'tile'), pairs)  5.5 us
    pallas_call x1, Pallas kernels, last_layers(): pl.pallas_call(last_kernel, out_shape=jax.ShapeDtypeStruct(t.shape, jnp.f...  5.3 us
    pallas_call x1, Pallas kernels, inside(): pl.pallas_call(inside_kernel, out_shape=jax.ShapeDtypeStruct(s.shape, jnp...  3.78 us
    ppermute x3, starting transfers between devices, across(): return lax.ppermute(value, 'tier', [(i, i ^ bits) for i in range(tiers)])  3.55 us
    pallas_call x1, Pallas kernels, begin(): pl.pallas_call(begin_kernel, out_shape=(pltpu.VMEM((2, R, W), f32), pltpu...  3.03 us
    pallas_call x1, Pallas kernels, more_faces(): pl.pallas_call(more_faces_kernel, out_shape=(jax.ShapeDtypeStruct(lab.sha...  2.85 us
    pallas_call x1, Pallas kernels, pack_rows(): pl.pallas_call(pack_kernel, out_shape=(pltpu.VMEM((rows, W), f32), pltpu....  2.3 us
  transfers between devices with their start and end apart: 9, of which 4 were waited for; matrix products, arithmetic and copies ran while one was open for 0% of the time, Pallas kernels for 44%

profile of v6, /device:TPU:0, one launch (start us, length us, event | category | flops | bytes accessed | tf_op | source)
XLA Modules:
  0.0 46.6 jit_solution(2267147345266779978)
XLA Ops:
  0.0 0.0 copy-start
  0.0 0.0 copy-start.2
  0.0 3.0 %begin.1 = (f32[2,32,2048]{2,1,0:T(8,128)S(1)}, f32[32,2048]{1,0:T(8,128)S(1)}, f32[16,32,2048]{2,1,0:T(8,128)S(1)}, s32[16,32,2048]{2,1,0:T(8,128)S(1)}, f32[16,32,2048]{2,1,0:T(8,128)S(1)}) custom-call(f32[16,32,2048]{2,1,0:T(8,128)} %bitcast.4, s32[16,32,2048]{2,1,0:T(8,128)} %bitcast.6, s32[32,2048]{1,0:T(8,128)} %bitcast.8, f32[16]{0:T(128)} %kap.5, ...), custom_call_target="tpu_custom_call" | custom-call | tf_op jit(solution)/shard_map/begin/pallas_call | solution.py:193
  3.0 3.0 %collective-permute-start.2 = (f32[2,32,2048]{2,1,0:T(8,128)S(1)}, f32[2,32,2048]{2,1,0:T(8,128)S(1)}, u32[]{:S(2)}, u32[]{:S(2)}) collective-permute-start(f32[2,32,2048]{2,1,0:T(8,128)S(1)} %get-tuple-element.42.own), channel_id=1, source_target_pairs={{0,8},{1,17},{2,10},{3,19},{4,12},{5,21},{6,14},{7,23},{8,0},{9,25... | collective-permute-start | bytes 1572872 | tf_op jit(solution)/shard_map/ppermute | solution.py:834
  6.0 0.0 copy-done
  6.0 0.0 copy-done.2
  6.1 0.0 copy-start.1
  6.1 2.3 %pack_rows.1 = (f32[56,2048]{1,0:T(8,128)S(1)}, f32[56,2048]{1,0:T(8,128)S(1)}, f32[16,32,2048]{2,1,0:T(8,128)S(1)}, s32[16,32,2048]{2,1,0:T(8,128)S(1)}) custom-call(f32[16,32,2048]{2,1,0:T(8,128)} %bitcast.5, s32[16,32,2048]{2,1,0:T(8,128)} %bitcast.7, f32[16,32,2048]{2,1,0:T(8,128)S(1)} %get-tuple-element.27.s_in, ...), custom_call_target="tpu_custom_call", output_to_operand_aliasing={{2}: (2, {}), {3}: (3, {})} | custom-call | tf_op jit(solution)/shard_map/pack_rows/pallas_call | solution.py:299
  8.4 0.1 collective-permute-start
  8.4 0.7 %collective-permute-start.1 = (f32[56,2048]{1,0:T(8,128)S(1)}, f32[56,2048]{1,0:T(8,128)S(1)}, u32[]{:S(2)}, u32[]{:S(2)}) collective-permute-start(f32[56,2048]{1,0:T(8,128)S(1)} %get-tuple-element.31.own_b), channel_id=1, source_target_pairs={{1,2},{2,1},{3,4},{4,3},{5,6},{6,5},{9,10},{10,9},{11,12},{12,11},... | collective-permute-start | bytes 1376264 | tf_op jit(solution)/shard_map/ppermute | solution.py:854
  9.1 0.0 copy-done.1
  9.1 1.4 %make_tables.1 = (f32[32,8,8,128]{3,2,1,0:T(8,128)S(1)}, f32[8,8,128]{2,1,0:T(8,128)S(1)}) custom-call(f32[8,8,8]{2,1,0:T(8,128)S(1)} %copy-done.1), custom_call_target="tpu_custom_call" | custom-call | tf_op jit(solution)/shard_map/make_tables/pallas_call | solution.py:611
  10.6 1.5 %faces.1 = (f32[16,32,2048]{2,1,0:T(8,128)S(1)}, f32[16,32,2048]{2,1,0:T(8,128)S(1)}) custom-call(s32[16,32,2048]{2,1,0:T(8,128)S(1)} %get-tuple-element.32.lab, f32[16]{0:T(128)S(1)} %copy-done.2, f32[16,32,2048]{2,1,0:T(8,128)S(1)} %get-tuple-element.33.h_in), custom_call_target="tpu_custom_call", output_to_operand_aliasing={{0}: (2, {})} | custom-call | tf_op jit(solution)/shard_map/faces/pallas_call | solution.py:420
  12.1 1.1 %collective-permute-done.2.near = f32[2,32,2048]{2,1,0:T(8,128)S(1)} collective-permute-done((f32[2,32,2048]{2,1,0:T(8,128)S(1)}, f32[2,32,2048]{2,1,0:T(8,128)S(1)}, u32[]{:S(2)}, u32[]{:S(2)}) %collective-permute-start.2) | collective-permute-done | bytes 524320 | tf_op jit(solution)/shard_map/ppermute | solution.py:834
  13.2 0.8 %combine.2._ = f32[2,32,2048]{2,1,0:T(8,128)S(1)} custom-call(f32[32,8,8,128]{3,2,1,0:T(8,128)S(1)} %get-tuple-element.25.table, s32[32,2048]{1,0:T(8,128)S(1)} %copy-done, f32[2,32,2048]{2,1,0:T(8,128)S(1)} %get-tuple-element.42.own, f32[2,32,2048]{2,1,0:T(8,128)S(1)} %collective-permute-done.2.near, f32[16,32,2048]{2,1,0:T(8,128)S(1)} %get-tuple-element.34._.h_in), custom_call_target="tpu_custom_call" | custom-call | tf_op jit(solution)/shard_map/combine/pallas_call | solution.py:668
  14.0 2.1 %collective-permute-start.3 = (f32[2,32,2048]{2,1,0:T(8,128)S(1)}, f32[2,32,2048]{2,1,0:T(8,128)S(1)}, u32[]{:S(2)}, u32[]{:S(2)}) collective-permute-start(f32[2,32,2048]{2,1,0:T(8,128)S(1)} %combine.2._), channel_id=1, source_target_pairs={{0,16},{1,9},{2,18},{3,11},{4,20},{5,13},{6,22},{7,15},{8,24},{9,1... | collective-permute-start | bytes 1572872 | tf_op jit(solution)/shard_map/ppermute | solution.py:834
  16.1 0.0 collective-permute-done.got_a
  16.1 0.0 collective-permute-done.1.got_b
  16.1 0.2 edge_rows.1
  16.4 1.6 %collective-permute-start.4 = (f32[8,2048]{1,0:T(8,128)S(1)}, f32[8,2048]{1,0:T(8,128)S(1)}, u32[]{:S(2)}, u32[]{:S(2)}) collective-permute-start(f32[8,2048]{1,0:T(8,128)S(1)} %get-tuple-element.37._.refs_3_), channel_id=1, source_target_pairs={{0,8},{8,0},{16,24},{24,16},{1,9},{9,1},{17,25},{25,17},{2,10},{10... | collective-permute-start | bytes 196616 | tf_op jit(solution)/shard_map/ppermute | solution.py:823
  17.9 0.5 %collective-permute-start.5 = (f32[8,2048]{1,0:T(8,128)S(1)}, f32[8,2048]{1,0:T(8,128)S(1)}, u32[]{:S(2)}, u32[]{:S(2)}) collective-permute-start(f32[8,2048]{1,0:T(8,128)S(1)} %get-tuple-element.37._.refs_3_), channel_id=1, source_target_pairs={{0,16},{8,24},{16,0},{24,8},{1,17},{9,25},{17,1},{25,9},{2,18},{10... | collective-permute-start | bytes 196616 | tf_op jit(solution)/shard_map/ppermute | solution.py:823
  18.4 1.5 %collective-permute-start.6 = (f32[8,2048]{1,0:T(8,128)S(1)}, f32[8,2048]{1,0:T(8,128)S(1)}, u32[]{:S(2)}, u32[]{:S(2)}) collective-permute-start(f32[8,2048]{1,0:T(8,128)S(1)} %get-tuple-element.37._.refs_3_), channel_id=1, source_target_pairs={{0,24},{8,16},{16,8},{24,0},{1,25},{9,17},{17,9},{25,1},{2,26},{10... | collective-permute-start | bytes 196616 | tf_op jit(solution)/shard_map/ppermute | solution.py:823
  19.9 2.9 %more_faces.1 = (f32[16,32,2048]{2,1,0:T(8,128)S(1)}, f32[16,32,2048]{2,1,0:T(8,128)S(1)}) custom-call(s32[16,32,2048]{2,1,0:T(8,128)S(1)} %get-tuple-element.32.lab, f32[16]{0:T(128)S(1)} %copy-done.2, f32[16,32,2048]{2,1,0:T(8,128)S(1)} %get-tuple-element.34._.h_in, ...), custom_call_target="tpu_custom_call", output_to_operand_aliasing={{0}: (2, {}), {1}: (3, {})} | custom-call | tf_op jit(solution)/shard_map/more_faces/pallas_call | solution.py:436
  22.8 0.6 %outer.1.t_in = f32[16,32,2048]{2,1,0:T(8,128)S(1)} custom-call(f32[16,32,2048]{2,1,0:T(8,128)S(1)} %get-tuple-element.40.s_ref, f32[16,32,2048]{2,1,0:T(8,128)S(1)} %get-tuple-element.38.h_ref, f32[16,32,2048]{2,1,0:T(8,128)S(1)} %get-tuple-element.39.g_ref, f32[6,16,2048]{2,1,0:T(8,128)S(1)} %get-tuple-element.35.rims), custom_call_target="tpu_custom_call" | custom-call | tf_op jit(solution)/shard_map/outer/pallas_call | solution.py:489
  23.4 0.8 %own_part.2.refs_1_ = f32[2,32,2048]{2,1,0:T(8,128)S(1)} custom-call(f32[32,8,8,128]{3,2,1,0:T(8,128)S(1)} %get-tuple-element.25.table, s32[32,2048]{1,0:T(8,128)S(1)} %copy-done, f32[2,32,2048]{2,1,0:T(8,128)S(1)} %get-tuple-element.42.own, f32[2,32,2048]{2,1,0:T(8,128)S(1)} %collective-permute-done.2.near, f32[2,32,2048]{2,1,0:T(8,128)S(1)} %combine.2._), custom_call_target="tpu_custom_call" | custom-call | tf_op jit(solution)/shard_map/own_part/pallas_call | solution.py:693
  24.2 0.0 collective-permute-done.4.refs_4_
  24.2 1.2 %collective-permute-done.5.refs_5_ = f32[8,2048]{1,0:T(8,128)S(1)} collective-permute-done((f32[8,2048]{1,0:T(8,128)S(1)}, f32[8,2048]{1,0:T(8,128)S(1)}, u32[]{:S(2)}, u32[]{:S(2)}) %collective-permute-start.5) | collective-permute-done | bytes 65568 | tf_op jit(solution)/shard_map/ppermute | solution.py:823
  25.4 0.0 collective-permute-done.6.refs_6_
  25.4 0.0 collective-permute-done.3.refs_2_
  25.4 0.9 %bond.1 = (f32[16,32,2048]{2,1,0:T(8,128)S(1)}, f32[2,32,2048]{2,1,0:T(8,128)S(1)}) custom-call(s32[32,2048]{1,0:T(8,128)S(1)} %copy-done, f32[32,8,8,128]{3,2,1,0:T(8,128)S(1)} %get-tuple-element.25.table, f32[8,8,128]{2,1,0:T(8,128)S(1)} %get-tuple-element.26.rim_table, ...), custom_call_target="tpu_custom_call", output_to_operand_aliasing={{0}: (7, {})} | custom-call | tf_op jit(solution)/shard_map/bond/pallas_call | solution.py:770
  26.3 2.1 %collective-permute-start.7 = (f32[2,32,2048]{2,1,0:T(8,128)S(1)}, f32[2,32,2048]{2,1,0:T(8,128)S(1)}, u32[]{:S(2)}, u32[]{:S(2)}) collective-permute-start(f32[2,32,2048]{2,1,0:T(8,128)S(1)} %get-tuple-element.43._.own), channel_id=1, source_target_pairs={{0,8},{1,17},{2,10},{3,19},{4,12},{5,21},{6,14},{7,23},{8,0},{9,25... | collective-permute-start | bytes 1572872 | tf_op jit(solution)/shard_map/ppermute | solution.py:834
  28.4 3.8 %inside.1._.t_ref = f32[16,32,2048]{2,1,0:T(8,128)S(1)} custom-call(f32[16,32,2048]{2,1,0:T(8,128)S(1)} %get-tuple-element.40.s_ref, f32[16,32,2048]{2,1,0:T(8,128)S(1)} %get-tuple-element.38.h_ref, f32[16,32,2048]{2,1,0:T(8,128)S(1)} %get-tuple-element.39.g_ref, f32[6,16,2048]{2,1,0:T(8,128)S(1)} %get-tuple-element.35.rims, ...), custom_call_target="tpu_custom_call", output_to_operand_aliasing={{}: (4, {})} | custom-call | tf_op jit(solution)/shard_map/inside/pallas_call | solution.py:513
  32.2 3.4 %collective-permute-done.7.near = f32[2,32,2048]{2,1,0:T(8,128)S(1)} collective-permute-done((f32[2,32,2048]{2,1,0:T(8,128)S(1)}, f32[2,32,2048]{2,1,0:T(8,128)S(1)}, u32[]{:S(2)}, u32[]{:S(2)}) %collective-permute-start.7) | collective-permute-done | bytes 524320 | tf_op jit(solution)/shard_map/ppermute | solution.py:834
  35.6 0.8 %combine.3._ = f32[2,32,2048]{2,1,0:T(8,128)S(1)} custom-call(f32[32,8,8,128]{3,2,1,0:T(8,128)S(1)} %get-tuple-element.25.table, s32[32,2048]{1,0:T(8,128)S(1)} %copy-done, f32[2,32,2048]{2,1,0:T(8,128)S(1)} %get-tuple-element.43._.own, f32[2,32,2048]{2,1,0:T(8,128)S(1)} %collective-permute-done.7.near, f32[16,32,2048]{2,1,0:T(8,128)S(1)} %inside.1._.t_ref), custom_call_target="tpu_custom_call" | custom-call | tf_op jit(solution)/shard_map/combine/pallas_call | solution.py:668
  36.4 2.3 %collective-permute-start.8 = (f32[2,32,2048]{2,1,0:T(8,128)S(1)}, f32[2,32,2048]{2,1,0:T(8,128)S(1)}, u32[]{:S(2)}, u32[]{:S(2)}) collective-permute-start(f32[2,32,2048]{2,1,0:T(8,128)S(1)} %combine.3._), channel_id=1, source_target_pairs={{0,16},{1,9},{2,18},{3,11},{4,20},{5,13},{6,22},{7,15},{8,24},{9,1... | collective-permute-start | bytes 1572872 | tf_op jit(solution)/shard_map/ppermute | solution.py:834
  38.7 5.3 %last_layers.1.refs_2_ = f32[16,32,2048]{2,1,0:T(8,128)} custom-call(f32[16,32,2048]{2,1,0:T(8,128)S(1)} %inside.1._.t_ref, f32[16,32,2048]{2,1,0:T(8,128)S(1)} %get-tuple-element.38.h_ref, f32[16,32,2048]{2,1,0:T(8,128)S(1)} %get-tuple-element.39.g_ref, f32[6,16,2048]{2,1,0:T(8,128)S(1)} %get-tuple-element.35.rims), custom_call_target="tpu_custom_call" | custom-call | tf_op jit(solution)/shard_map/last_layers/pallas_call | solution.py:552
  44.0 0.8 %own_part.3.refs_0_ = f32[2,32,2048]{2,1,0:T(8,128)S(1)} custom-call(f32[32,8,8,128]{3,2,1,0:T(8,128)S(1)} %get-tuple-element.25.table, s32[32,2048]{1,0:T(8,128)S(1)} %copy-done, f32[2,32,2048]{2,1,0:T(8,128)S(1)} %get-tuple-element.43._.own, f32[2,32,2048]{2,1,0:T(8,128)S(1)} %collective-permute-done.7.near, f32[2,32,2048]{2,1,0:T(8,128)S(1)} %combine.3._), custom_call_target="tpu_custom_call" | custom-call | tf_op jit(solution)/shard_map/own_part/pallas_call | solution.py:693
  44.8 1.0 %collective-permute-done.8.refs_1_ = f32[2,32,2048]{2,1,0:T(8,128)S(1)} collective-permute-done((f32[2,32,2048]{2,1,0:T(8,128)S(1)}, f32[2,32,2048]{2,1,0:T(8,128)S(1)}, u32[]{:S(2)}, u32[]{:S(2)}) %collective-permute-start.8) | collective-permute-done | bytes 524320 | tf_op jit(solution)/shard_map/ppermute | solution.py:834
  45.8 0.8 %final_planes.1 = f32[16,32,2048]{2,1,0:T(8,128)} custom-call(s32[32,2048]{1,0:T(8,128)S(1)} %copy-done, f32[32,8,8,128]{3,2,1,0:T(8,128)S(1)} %get-tuple-element.25.table, f32[2,32,2048]{2,1,0:T(8,128)S(1)} %own_part.3.refs_0_, f32[2,32,2048]{2,1,0:T(8,128)S(1)} %collective-permute-done.8.refs_1_, ...), custom_call_target="tpu_custom_call", output_to_operand_aliasing={{}: (4, {})} | custom-call | tf_op jit(solution)/shard_map/final_planes/pallas_call | solution.py:810
Async XLA Ops:
  0.0 6.0 %copy-start = (s32[32,2048]{1,0:T(8,128)S(1)}, s32[32,2048]{1,0:T(8,128)}, u32[]{:S(2)}) copy-start(s32[32,2048]{1,0:T(8,128)} %zone.13) | copy-start | bytes 786436
  0.0 6.0 %copy-start.2 = (f32[16]{0:T(128)S(1)}, f32[16]{0:T(128)}, u32[]{:S(2)}) copy-start(f32[16]{0:T(128)} %kap.5) | copy-start | bytes 196
  3.0 10.2 %collective-permute-start.2 = (f32[2,32,2048]{2,1,0:T(8,128)S(1)}, f32[2,32,2048]{2,1,0:T(8,128)S(1)}, u32[]{:S(2)}, u32[]{:S(2)}) collective-permute-start(f32[2,32,2048]{2,1,0:T(8,128)S(1)} %get-tuple-element.42.own), channel_id=1, source_target_pairs={{0,8},{1,17},{2,10},{3,19},{4,12},{5,21},{6,14},{7,23},{8,0},{9,25... | collective-permute-start | bytes 1572872 | tf_op jit(solution)/shard_map/ppermute | solution.py:834
  6.1 3.1 %copy-start.1 = (f32[8,8,8]{2,1,0:T(8,128)S(1)}, f32[8,8,8]{2,1,0:T(8,128)}, u32[]{:S(2)}) copy-start(f32[8,8,8]{2,1,0:T(8,128)} %ops.1) | copy-start | bytes 6148
  8.4 7.8 %collective-permute-start = (f32[56,2048]{1,0:T(8,128)S(1)}, f32[56,2048]{1,0:T(8,128)S(1)}, u32[]{:S(2)}, u32[]{:S(2)}) collective-permute-start(f32[56,2048]{1,0:T(8,128)S(1)} %get-tuple-element.30.own_a), channel_id=1, source_target_pairs={{0,1},{1,0},{2,3},{3,2},{4,5},{5,4},{6,7},{7,6},{8,9},{9,8},{10,11... | collective-permute-start | bytes 1376264 | tf_op jit(solution)/shard_map/ppermute | solution.py:852
  8.4 7.7 %collective-permute-start.1 = (f32[56,2048]{1,0:T(8,128)S(1)}, f32[56,2048]{1,0:T(8,128)S(1)}, u32[]{:S(2)}, u32[]{:S(2)}) collective-permute-start(f32[56,2048]{1,0:T(8,128)S(1)} %get-tuple-element.31.own_b), channel_id=1, source_target_pairs={{1,2},{2,1},{3,4},{4,3},{5,6},{6,5},{9,10},{10,9},{11,12},{12,11},... | collective-permute-start | bytes 1376264 | tf_op jit(solution)/shard_map/ppermute | solution.py:854
  14.0 11.4 %collective-permute-start.3 = (f32[2,32,2048]{2,1,0:T(8,128)S(1)}, f32[2,32,2048]{2,1,0:T(8,128)S(1)}, u32[]{:S(2)}, u32[]{:S(2)}) collective-permute-start(f32[2,32,2048]{2,1,0:T(8,128)S(1)} %combine.2._), channel_id=1, source_target_pairs={{0,16},{1,9},{2,18},{3,11},{4,20},{5,13},{6,22},{7,15},{8,24},{9,1... | collective-permute-start | bytes 1572872 | tf_op jit(solution)/shard_map/ppermute | solution.py:834
  16.4 7.9 %collective-permute-start.4 = (f32[8,2048]{1,0:T(8,128)S(1)}, f32[8,2048]{1,0:T(8,128)S(1)}, u32[]{:S(2)}, u32[]{:S(2)}) collective-permute-start(f32[8,2048]{1,0:T(8,128)S(1)} %get-tuple-element.37._.refs_3_), channel_id=1, source_target_pairs={{0,8},{8,0},{16,24},{24,16},{1,9},{9,1},{17,25},{25,17},{2,10},{10... | collective-permute-start | bytes 196616 | tf_op jit(solution)/shard_map/ppermute | solution.py:823
  17.9 7.5 %collective-permute-start.5 = (f32[8,2048]{1,0:T(8,128)S(1)}, f32[8,2048]{1,0:T(8,128)S(1)}, u32[]{:S(2)}, u32[]{:S(2)}) collective-permute-start(f32[8,2048]{1,0:T(8,128)S(1)} %get-tuple-element.37._.refs_3_), channel_id=1, source_target_pairs={{0,16},{8,24},{16,0},{24,8},{1,17},{9,25},{17,1},{25,9},{2,18},{10... | collective-permute-start | bytes 196616 | tf_op jit(solution)/shard_map/ppermute | solution.py:823
  18.4 7.0 %collective-permute-start.6 = (f32[8,2048]{1,0:T(8,128)S(1)}, f32[8,2048]{1,0:T(8,128)S(1)}, u32[]{:S(2)}, u32[]{:S(2)}) collective-permute-start(f32[8,2048]{1,0:T(8,128)S(1)} %get-tuple-element.37._.refs_3_), channel_id=1, source_target_pairs={{0,24},{8,16},{16,8},{24,0},{1,25},{9,17},{17,9},{25,1},{2,26},{10... | collective-permute-start | bytes 196616 | tf_op jit(solution)/shard_map/ppermute | solution.py:823
  26.3 9.2 %collective-permute-start.7 = (f32[2,32,2048]{2,1,0:T(8,128)S(1)}, f32[2,32,2048]{2,1,0:T(8,128)S(1)}, u32[]{:S(2)}, u32[]{:S(2)}) collective-permute-start(f32[2,32,2048]{2,1,0:T(8,128)S(1)} %get-tuple-element.43._.own), channel_id=1, source_target_pairs={{0,8},{1,17},{2,10},{3,19},{4,12},{5,21},{6,14},{7,23},{8,0},{9,25... | collective-permute-start | bytes 1572872 | tf_op jit(solution)/shard_map/ppermute | solution.py:834
  36.4 9.4 %collective-permute-start.8 = (f32[2,32,2048]{2,1,0:T(8,128)S(1)}, f32[2,32,2048]{2,1,0:T(8,128)S(1)}, u32[]{:S(2)}, u32[]{:S(2)}) collective-permute-start(f32[2,32,2048]{2,1,0:T(8,128)S(1)} %combine.3._), channel_id=1, source_target_pairs={{0,16},{1,9},{2,18},{3,11},{4,20},{5,13},{6,22},{7,15},{8,24},{9,1... | collective-permute-start | bytes 1572872 | tf_op jit(solution)/shard_map/ppermute | solution.py:834

commit v7 on v6

--- a/solution.py
+++ b/solution.py
@@ -218,17 +218,14 @@
 
 
 def pack_kernel(
-    s_hbm, lab_hbm, s_in, lab_in, heat, zone, kap, swap_a, swap_b, s, lab, rows_v, next_v, sem
+    s_hbm, s_in, lab, heat, zone, kap, swap_a, swap_b, s, rows_v, next_v, sem
 ):
     L, R, W = s.shape
     C = W // LANES
     copies = []
     if R > 2 * ROWS:
         at = pl.ds(3, L - 6), pl.ds(ROWS, R - 2 * ROWS)
-        copies = [
-            pltpu.make_async_copy(s_hbm.at[at], s.at[at], sem.at[0]),
-            pltpu.make_async_copy(lab_hbm.at[at], lab.at[at], sem.at[1]),
-        ]
+        copies = [pltpu.make_async_copy(s_hbm.at[at], s.at[at], sem)]
     for copy in copies:
         copy.start()
     row = row_ids()
@@ -291,30 +288,29 @@
         copy.wait()
 
 
-def pack_rows(s, lab, s_v, lab_v, heat, zone, kap):
+def pack_rows(s, s_v, lab_v, heat, zone, kap):
     L, _, W = s.shape
     f32 = jnp.float32
     rows = 3 * L + ROWS
-    s, lab = (pltpu.with_memory_space_constraint(x, pltpu.HBM) for x in (s, lab))
+    s = pltpu.with_memory_space_constraint(s, pltpu.HBM)
     return pl.pallas_call(
         pack_kernel,
         out_shape=(
             pltpu.VMEM((rows, W), f32),
             pltpu.VMEM((rows, W), f32),
             jax.ShapeDtypeStruct(s.shape, f32),
-            jax.ShapeDtypeStruct(lab.shape, jnp.int32),
         ),
-        in_specs=[HBM] * 2 + [VMEM] * 4 + [SMEM],
-        out_specs=[VMEM] * 4,
+        in_specs=[HBM] + [VMEM] * 4 + [SMEM],
+        out_specs=[VMEM] * 3,
         scratch_shapes=[
             pltpu.VMEM((2, rows, W), f32),
             pltpu.VMEM((2, 2 * L, W), f32),
-            pltpu.SemaphoreType.DMA((2,)),
+            pltpu.SemaphoreType.DMA,
         ],
-        input_output_aliases={2: 2, 3: 3},
+        input_output_aliases={1: 2},
         compiler_params=pltpu.CompilerParams(vmem_limit_bytes=24 * MIB),
         name="pack_rows",
-    )(s, lab, s_v, lab_v, heat, zone, kap)
+    )(s, s_v, lab_v, heat, zone, kap)
 
 
 def edge_kernel(own_a, own_b, got_a, got_b, _, edges, zones, rims):
@@ -403,8 +399,14 @@
     return lambda at, c: lookup(table, lab[at]) if c % 4 == 0 else choose(values, lab[at])
 
 
-def faces_kernel(lab, kap, h_in, h_out, g_out):
-    L = lab.shape[0]
+def faces_kernel(lab_hbm, kap, h_in, lab_in, _, h_out, g_out, lab, sem):
+    L, R, _ = lab.shape
+    copies = []
+    if R > 2 * ROWS:
+        at = pl.ds(3, L - 6), pl.ds(ROWS, R - 2 * ROWS)
+        copies = [pltpu.make_async_copy(lab_hbm.at[at], lab.at[at], sem)]
+    for copy in copies:
+        copy.start()
 
     def held(at, c):
         return h_out[at]
@@ -414,18 +416,23 @@
         fill_faces(first, end, held, h_out, g_out)
     for l in (2, L - 3):
         fill_faces(l, l + 1, getter, h_out, g_out)
-
-
-def faces(lab, kap, h):
+    for copy in copies:
+        copy.wait()
+
+
+def faces(lab, kap, h, lab_v, after):
+    lab = pltpu.with_memory_space_constraint(lab, pltpu.HBM)
+    f32 = jnp.float32
     return pl.pallas_call(
         faces_kernel,
-        out_shape=(jax.ShapeDtypeStruct(lab.shape, jnp.float32),) * 2,
-        in_specs=[VMEM, SMEM, VMEM],
-        out_specs=[VMEM] * 2,
-        input_output_aliases={2: 0},
-        compiler_params=pltpu.CompilerParams(vmem_limit_bytes=20 * MIB),
+        out_shape=(jax.ShapeDtypeStruct(lab.shape, f32),) * 2 + (jax.ShapeDtypeStruct(lab.shape, jnp.int32),),
+        in_specs=[HBM, SMEM, VMEM, VMEM, ANY],
+        out_specs=[VMEM] * 3,
+        scratch_shapes=[pltpu.SemaphoreType.DMA],
+        input_output_aliases={2: 0, 3: 2},
+        compiler_params=pltpu.CompilerParams(vmem_limit_bytes=24 * MIB),
         name="faces",
-    )(lab, kap, h)
+    )(lab, kap, h, lab_v, after)
 
 
 def more_faces_kernel(lab, kap, h_in, g_in, _, h_out, g_out):
@@ -847,13 +854,13 @@
     s, lab, patch = warming[0], substance[0], patch[0]
 
     planes, heat, s_v, lab_v, h = begin(s, lab, patch, kap, power)
-    swap_a, swap_b, s, lab = pack_rows(s, lab, s_v, lab_v, heat, zone, kap)
+    swap_a, swap_b, s = pack_rows(s, s_v, lab_v, heat, zone, kap)
     pairs = [(i, i ^ 1) for i in range(tiles) if i ^ 1 < tiles]
     got_a = lax.ppermute(swap_a, "tile", pairs)
     pairs = [(i, ((i - 1) ^ 1) + 1) for i in range(1, tiles - 1 + tiles % 2)]
     got_b = lax.ppermute(swap_b, "tile", pairs)
     tables = make_tables(tiers, ops)
-    h, g = faces(lab, kap, h)
+    h, g, lab = faces(lab, kap, h, lab_v, swap_a)
     arrays, _ = exchange(tiers, tiles, tables[0], zone, planes, h)
     edges, edge_zones, rims = edge_rows(swap_a, swap_b, got_a, got_b, h)
     h, g = more_faces(lab, kap, h, g, edges)

time: 46.8 us -> 46.6 us (level)
  no operation moved by 1% of the time
where the time goes in v7:
time: 46.6 us; the launch traced here: 46.4 us
  Pallas kernels  26.1 us (56%)
  starting transfers between devices  13.6 us (29%)
  waiting for transfers between devices  6.65 us (14%)
    ppermute x4, starting transfers between devices, along(): return lax.ppermute(value, ('tier', 'tile'), pairs)  9.26 us
    ppermute x4, waiting for transfers between devices, along(): return lax.ppermute(value, ('tier', 'tile'), pairs)  5.46 us
    pallas_call x1, Pallas kernels, last_layers(): pl.pallas_call(last_kernel, out_shape=jax.ShapeDtypeStruct(t.shape, jnp.f...  5.3 us
    pallas_call x1, Pallas kernels, inside(): pl.pallas_call(inside_kernel, out_shape=jax.ShapeDtypeStruct(s.shape, jnp...  3.78 us
    ppermute x3, starting transfers between devices, across(): return lax.ppermute(value, 'tier', [(i, i ^ bits) for i in range(tiers)])  3.55 us
    pallas_call x1, Pallas kernels, begin(): pl.pallas_call(begin_kernel, out_shape=(pltpu.VMEM((2, R, W), f32), pltpu...  3.02 us
    pallas_call x1, Pallas kernels, more_faces(): pl.pallas_call(more_faces_kernel, out_shape=(jax.ShapeDtypeStruct(lab.sha...  2.85 us
    pallas_call x1, Pallas kernels, pack_rows(): pl.pallas_call(pack_kernel, out_shape=(pltpu.VMEM((rows, W), f32), pltpu....  1.99 us
  transfers between devices with their start and end apart: 9, of which 4 were waited for; matrix products, arithmetic and copies ran while one was open for 0% of the time, Pallas kernels for 44%

profile of v7, /device:TPU:0, one launch (start us, length us, event | category | flops | bytes accessed | tf_op | source)
XLA Modules:
  0.0 46.4 jit_solution(13933735129501370423)
XLA Ops:
  0.0 0.0 copy-start
  0.0 0.0 copy-start.2
  0.0 3.0 %begin.1 = (f32[2,32,2048]{2,1,0:T(8,128)S(1)}, f32[32,2048]{1,0:T(8,128)S(1)}, f32[16,32,2048]{2,1,0:T(8,128)S(1)}, s32[16,32,2048]{2,1,0:T(8,128)S(1)}, f32[16,32,2048]{2,1,0:T(8,128)S(1)}) custom-call(f32[16,32,2048]{2,1,0:T(8,128)} %bitcast.4, s32[16,32,2048]{2,1,0:T(8,128)} %bitcast.6, s32[32,2048]{1,0:T(8,128)} %bitcast.8, f32[16]{0:T(128)} %kap.5, ...), custom_call_target="tpu_custom_call" | custom-call | tf_op jit(solution)/shard_map/begin/pallas_call | solution.py:193
  3.0 3.0 %collective-permute-start.2 = (f32[2,32,2048]{2,1,0:T(8,128)S(1)}, f32[2,32,2048]{2,1,0:T(8,128)S(1)}, u32[]{:S(2)}, u32[]{:S(2)}) collective-permute-start(f32[2,32,2048]{2,1,0:T(8,128)S(1)} %get-tuple-element.42.own), channel_id=1, source_target_pairs={{0,8},{1,17},{2,10},{3,19},{4,12},{5,21},{6,14},{7,23},{8,0},{9,25... | collective-permute-start | bytes 1572872 | tf_op jit(solution)/shard_map/ppermute | solution.py:841
  6.0 0.0 copy-done
  6.0 0.0 copy-done.2
  6.0 2.0 %pack_rows.1 = (f32[56,2048]{1,0:T(8,128)S(1)}, f32[56,2048]{1,0:T(8,128)S(1)}, f32[16,32,2048]{2,1,0:T(8,128)S(1)}) custom-call(f32[16,32,2048]{2,1,0:T(8,128)} %bitcast.5, f32[16,32,2048]{2,1,0:T(8,128)S(1)} %get-tuple-element.27.s_in, s32[16,32,2048]{2,1,0:T(8,128)S(1)} %get-tuple-element.28.lab.lab_in, ...), custom_call_target="tpu_custom_call", output_to_operand_aliasing={{2}: (1, {})} | custom-call | tf_op jit(solution)/shard_map/pack_rows/pallas_call | solution.py:296
  8.0 0.1 collective-permute-start
  8.1 0.7 %collective-permute-start.1 = (f32[56,2048]{1,0:T(8,128)S(1)}, f32[56,2048]{1,0:T(8,128)S(1)}, u32[]{:S(2)}, u32[]{:S(2)}) collective-permute-start(f32[56,2048]{1,0:T(8,128)S(1)} %get-tuple-element.31.own_b), channel_id=1, source_target_pairs={{1,2},{2,1},{3,4},{4,3},{5,6},{6,5},{9,10},{10,9},{11,12},{12,11},... | collective-permute-start | bytes 1376264 | tf_op jit(solution)/shard_map/ppermute | solution.py:861
  8.8 0.0 copy-start.1
  8.8 1.9 %faces.1 = (f32[16,32,2048]{2,1,0:T(8,128)S(1)}, f32[16,32,2048]{2,1,0:T(8,128)S(1)}, s32[16,32,2048]{2,1,0:T(8,128)S(1)}) custom-call(s32[16,32,2048]{2,1,0:T(8,128)} %bitcast.7, f32[16]{0:T(128)S(1)} %copy-done.2, f32[16,32,2048]{2,1,0:T(8,128)S(1)} %get-tuple-element.32.h_in, ...), custom_call_target="tpu_custom_call", output_to_operand_aliasing={{0}: (2, {}), {2}: (3, {})} | custom-call | tf_op jit(solution)/shard_map/faces/pallas_call | solution.py:426
  10.7 0.0 copy-done.1
  10.7 1.4 %make_tables.1 = (f32[32,8,8,128]{3,2,1,0:T(8,128)S(1)}, f32[8,8,128]{2,1,0:T(8,128)S(1)}) custom-call(f32[8,8,8]{2,1,0:T(8,128)S(1)} %copy-done.1), custom_call_target="tpu_custom_call" | custom-call | tf_op jit(solution)/shard_map/make_tables/pallas_call | solution.py:618
  12.2 1.0 %collective-permute-done.2.near = f32[2,32,2048]{2,1,0:T(8,128)S(1)} collective-permute-done((f32[2,32,2048]{2,1,0:T(8,128)S(1)}, f32[2,32,2048]{2,1,0:T(8,128)S(1)}, u32[]{:S(2)}, u32[]{:S(2)}) %collective-permute-start.2) | collective-permute-done | bytes 524320 | tf_op jit(solution)/shard_map/ppermute | solution.py:841
  13.2 0.8 %combine.2._ = f32[2,32,2048]{2,1,0:T(8,128)S(1)} custom-call(f32[32,8,8,128]{3,2,1,0:T(8,128)S(1)} %get-tuple-element.25.table, s32[32,2048]{1,0:T(8,128)S(1)} %copy-done, f32[2,32,2048]{2,1,0:T(8,128)S(1)} %get-tuple-element.42.own, f32[2,32,2048]{2,1,0:T(8,128)S(1)} %collective-permute-done.2.near, f32[16,32,2048]{2,1,0:T(8,128)S(1)} %get-tuple-element.33._.h_in), custom_call_target="tpu_custom_call" | custom-call | tf_op jit(solution)/shard_map/combine/pallas_call | solution.py:675
  14.0 2.1 %collective-permute-start.3 = (f32[2,32,2048]{2,1,0:T(8,128)S(1)}, f32[2,32,2048]{2,1,0:T(8,128)S(1)}, u32[]{:S(2)}, u32[]{:S(2)}) collective-permute-start(f32[2,32,2048]{2,1,0:T(8,128)S(1)} %combine.2._), channel_id=1, source_target_pairs={{0,16},{1,9},{2,18},{3,11},{4,20},{5,13},{6,22},{7,15},{8,24},{9,1... | collective-permute-start | bytes 1572872 | tf_op jit(solution)/shard_map/ppermute | solution.py:841
  16.1 0.0 collective-permute-done.got_a
  16.1 0.0 collective-permute-done.1.got_b
  16.1 0.2 edge_rows.1
  16.3 1.6 %collective-permute-start.4 = (f32[8,2048]{1,0:T(8,128)S(1)}, f32[8,2048]{1,0:T(8,128)S(1)}, u32[]{:S(2)}, u32[]{:S(2)}) collective-permute-start(f32[8,2048]{1,0:T(8,128)S(1)} %get-tuple-element.37._.refs_3_), channel_id=1, source_target_pairs={{0,8},{8,0},{16,24},{24,16},{1,9},{9,1},{17,25},{25,17},{2,10},{10... | collective-permute-start | bytes 196616 | tf_op jit(solution)/shard_map/ppermute | solution.py:830
  17.9 0.5 %collective-permute-start.5 = (f32[8,2048]{1,0:T(8,128)S(1)}, f32[8,2048]{1,0:T(8,128)S(1)}, u32[]{:S(2)}, u32[]{:S(2)}) collective-permute-start(f32[8,2048]{1,0:T(8,128)S(1)} %get-tuple-element.37._.refs_3_), channel_id=1, source_target_pairs={{0,16},{8,24},{16,0},{24,8},{1,17},{9,25},{17,1},{25,9},{2,18},{10... | collective-permute-start | bytes 196616 | tf_op jit(solution)/shard_map/ppermute | solution.py:830
  18.4 1.5 %collective-permute-start.6 = (f32[8,2048]{1,0:T(8,128)S(1)}, f32[8,2048]{1,0:T(8,128)S(1)}, u32[]{:S(2)}, u32[]{:S(2)}) collective-permute-start(f32[8,2048]{1,0:T(8,128)S(1)} %get-tuple-element.37._.refs_3_), channel_id=1, source_target_pairs={{0,24},{8,16},{16,8},{24,0},{1,25},{9,17},{17,9},{25,1},{2,26},{10... | collective-permute-start | bytes 196616 | tf_op jit(solution)/shard_map/ppermute | solution.py:830
  19.9 2.9 %more_faces.1 = (f32[16,32,2048]{2,1,0:T(8,128)S(1)}, f32[16,32,2048]{2,1,0:T(8,128)S(1)}) custom-call(s32[16,32,2048]{2,1,0:T(8,128)S(1)} %get-tuple-element.35.lab, f32[16]{0:T(128)S(1)} %copy-done.2, f32[16,32,2048]{2,1,0:T(8,128)S(1)} %get-tuple-element.33._.h_in, ...), custom_call_target="tpu_custom_call", output_to_operand_aliasing={{0}: (2, {}), {1}: (3, {})} | custom-call | tf_op jit(solution)/shard_map/more_faces/pallas_call | solution.py:443
  22.7 0.6 %outer.1.t_in = f32[16,32,2048]{2,1,0:T(8,128)S(1)} custom-call(f32[16,32,2048]{2,1,0:T(8,128)S(1)} %get-tuple-element.40.s_ref, f32[16,32,2048]{2,1,0:T(8,128)S(1)} %get-tuple-element.38.h_ref, f32[16,32,2048]{2,1,0:T(8,128)S(1)} %get-tuple-element.39.g_ref, f32[6,16,2048]{2,1,0:T(8,128)S(1)} %get-tuple-element.34.rims), custom_call_target="tpu_custom_call" | custom-call | tf_op jit(solution)/shard_map/outer/pallas_call | solution.py:496
  23.4 0.8 %own_part.2.refs_1_ = f32[2,32,2048]{2,1,0:T(8,128)S(1)} custom-call(f32[32,8,8,128]{3,2,1,0:T(8,128)S(1)} %get-tuple-element.25.table, s32[32,2048]{1,0:T(8,128)S(1)} %copy-done, f32[2,32,2048]{2,1,0:T(8,128)S(1)} %get-tuple-element.42.own, f32[2,32,2048]{2,1,0:T(8,128)S(1)} %collective-permute-done.2.near, f32[2,32,2048]{2,1,0:T(8,128)S(1)} %combine.2._), custom_call_target="tpu_custom_call" | custom-call | tf_op jit(solution)/shard_map/own_part/pallas_call | solution.py:700
  24.2 0.0 collective-permute-done.4.refs_4_
  24.2 1.2 %collective-permute-done.5.refs_5_ = f32[8,2048]{1,0:T(8,128)S(1)} collective-permute-done((f32[8,2048]{1,0:T(8,128)S(1)}, f32[8,2048]{1,0:T(8,128)S(1)}, u32[]{:S(2)}, u32[]{:S(2)}) %collective-permute-start.5) | collective-permute-done | bytes 65568 | tf_op jit(solution)/shard_map/ppermute | solution.py:830
  25.4 0.0 collective-permute-done.6.refs_6_
  25.4 0.0 collective-permute-done.3.refs_2_
  25.4 0.9 %bond.1 = (f32[16,32,2048]{2,1,0:T(8,128)S(1)}, f32[2,32,2048]{2,1,0:T(8,128)S(1)}) custom-call(s32[32,2048]{1,0:T(8,128)S(1)} %copy-done, f32[32,8,8,128]{3,2,1,0:T(8,128)S(1)} %get-tuple-element.25.table, f32[8,8,128]{2,1,0:T(8,128)S(1)} %get-tuple-element.26.rim_table, ...), custom_call_target="tpu_custom_call", output_to_operand_aliasing={{0}: (7, {})} | custom-call | tf_op jit(solution)/shard_map/bond/pallas_call | solution.py:777
  26.3 2.1 %collective-permute-start.7 = (f32[2,32,2048]{2,1,0:T(8,128)S(1)}, f32[2,32,2048]{2,1,0:T(8,128)S(1)}, u32[]{:S(2)}, u32[]{:S(2)}) collective-permute-start(f32[2,32,2048]{2,1,0:T(8,128)S(1)} %get-tuple-element.43._.own), channel_id=1, source_target_pairs={{0,8},{1,17},{2,10},{3,19},{4,12},{5,21},{6,14},{7,23},{8,0},{9,25... | collective-permute-start | bytes 1572872 | tf_op jit(solution)/shard_map/ppermute | solution.py:841
  28.4 3.8 %inside.1._.t_ref = f32[16,32,2048]{2,1,0:T(8,128)S(1)} custom-call(f32[16,32,2048]{2,1,0:T(8,128)S(1)} %get-tuple-element.40.s_ref, f32[16,32,2048]{2,1,0:T(8,128)S(1)} %get-tuple-element.38.h_ref, f32[16,32,2048]{2,1,0:T(8,128)S(1)} %get-tuple-element.39.g_ref, f32[6,16,2048]{2,1,0:T(8,128)S(1)} %get-tuple-element.34.rims, ...), custom_call_target="tpu_custom_call", output_to_operand_aliasing={{}: (4, {})} | custom-call | tf_op jit(solution)/shard_map/inside/pallas_call | solution.py:520
  32.1 3.4 %collective-permute-done.7.near = f32[2,32,2048]{2,1,0:T(8,128)S(1)} collective-permute-done((f32[2,32,2048]{2,1,0:T(8,128)S(1)}, f32[2,32,2048]{2,1,0:T(8,128)S(1)}, u32[]{:S(2)}, u32[]{:S(2)}) %collective-permute-start.7) | collective-permute-done | bytes 524320 | tf_op jit(solution)/shard_map/ppermute | solution.py:841
  35.5 0.8 %combine.3._ = f32[2,32,2048]{2,1,0:T(8,128)S(1)} custom-call(f32[32,8,8,128]{3,2,1,0:T(8,128)S(1)} %get-tuple-element.25.table, s32[32,2048]{1,0:T(8,128)S(1)} %copy-done, f32[2,32,2048]{2,1,0:T(8,128)S(1)} %get-tuple-element.43._.own, f32[2,32,2048]{2,1,0:T(8,128)S(1)} %collective-permute-done.7.near, f32[16,32,2048]{2,1,0:T(8,128)S(1)} %inside.1._.t_ref), custom_call_target="tpu_custom_call" | custom-call | tf_op jit(solution)/shard_map/combine/pallas_call | solution.py:675
  36.4 2.1 %collective-permute-start.8 = (f32[2,32,2048]{2,1,0:T(8,128)S(1)}, f32[2,32,2048]{2,1,0:T(8,128)S(1)}, u32[]{:S(2)}, u32[]{:S(2)}) collective-permute-start(f32[2,32,2048]{2,1,0:T(8,128)S(1)} %combine.3._), channel_id=1, source_target_pairs={{0,16},{1,9},{2,18},{3,11},{4,20},{5,13},{6,22},{7,15},{8,24},{9,1... | collective-permute-start | bytes 1572872 | tf_op jit(solution)/shard_map/ppermute | solution.py:841
  38.5 5.3 %last_layers.1.refs_2_ = f32[16,32,2048]{2,1,0:T(8,128)} custom-call(f32[16,32,2048]{2,1,0:T(8,128)S(1)} %inside.1._.t_ref, f32[16,32,2048]{2,1,0:T(8,128)S(1)} %get-tuple-element.38.h_ref, f32[16,32,2048]{2,1,0:T(8,128)S(1)} %get-tuple-element.39.g_ref, f32[6,16,2048]{2,1,0:T(8,128)S(1)} %get-tuple-element.34.rims), custom_call_target="tpu_custom_call" | custom-call | tf_op jit(solution)/shard_map/last_layers/pallas_call | solution.py:559
  43.8 0.8 %own_part.3.refs_0_ = f32[2,32,2048]{2,1,0:T(8,128)S(1)} custom-call(f32[32,8,8,128]{3,2,1,0:T(8,128)S(1)} %get-tuple-element.25.table, s32[32,2048]{1,0:T(8,128)S(1)} %copy-done, f32[2,32,2048]{2,1,0:T(8,128)S(1)} %get-tuple-element.43._.own, f32[2,32,2048]{2,1,0:T(8,128)S(1)} %collective-permute-done.7.near, f32[2,32,2048]{2,1,0:T(8,128)S(1)} %combine.3._), custom_call_target="tpu_custom_call" | custom-call | tf_op jit(solution)/shard_map/own_part/pallas_call | solution.py:700
  44.6 1.0 %collective-permute-done.8.refs_1_ = f32[2,32,2048]{2,1,0:T(8,128)S(1)} collective-permute-done((f32[2,32,2048]{2,1,0:T(8,128)S(1)}, f32[2,32,2048]{2,1,0:T(8,128)S(1)}, u32[]{:S(2)}, u32[]{:S(2)}) %collective-permute-start.8) | collective-permute-done | bytes 524320 | tf_op jit(solution)/shard_map/ppermute | solution.py:841
  45.6 0.8 %final_planes.1 = f32[16,32,2048]{2,1,0:T(8,128)} custom-call(s32[32,2048]{1,0:T(8,128)S(1)} %copy-done, f32[32,8,8,128]{3,2,1,0:T(8,128)S(1)} %get-tuple-element.25.table, f32[2,32,2048]{2,1,0:T(8,128)S(1)} %own_part.3.refs_0_, f32[2,32,2048]{2,1,0:T(8,128)S(1)} %collective-permute-done.8.refs_1_, ...), custom_call_target="tpu_custom_call", output_to_operand_aliasing={{}: (4, {})} | custom-call | tf_op jit(solution)/shard_map/final_planes/pallas_call | solution.py:817
Async XLA Ops:
  0.0 6.0 %copy-start = (s32[32,2048]{1,0:T(8,128)S(1)}, s32[32,2048]{1,0:T(8,128)}, u32[]{:S(2)}) copy-start(s32[32,2048]{1,0:T(8,128)} %zone.13) | copy-start | bytes 786436
  0.0 6.0 %copy-start.2 = (f32[16]{0:T(128)S(1)}, f32[16]{0:T(128)}, u32[]{:S(2)}) copy-start(f32[16]{0:T(128)} %kap.5) | copy-start | bytes 196
  3.0 10.2 %collective-permute-start.2 = (f32[2,32,2048]{2,1,0:T(8,128)S(1)}, f32[2,32,2048]{2,1,0:T(8,128)S(1)}, u32[]{:S(2)}, u32[]{:S(2)}) collective-permute-start(f32[2,32,2048]{2,1,0:T(8,128)S(1)} %get-tuple-element.42.own), channel_id=1, source_target_pairs={{0,8},{1,17},{2,10},{3,19},{4,12},{5,21},{6,14},{7,23},{8,0},{9,25... | collective-permute-start | bytes 1572872 | tf_op jit(solution)/shard_map/ppermute | solution.py:841
  8.0 8.1 %collective-permute-start = (f32[56,2048]{1,0:T(8,128)S(1)}, f32[56,2048]{1,0:T(8,128)S(1)}, u32[]{:S(2)}, u32[]{:S(2)}) collective-permute-start(f32[56,2048]{1,0:T(8,128)S(1)} %get-tuple-element.30._.own_a), channel_id=1, source_target_pairs={{0,1},{1,0},{2,3},{3,2},{4,5},{5,4},{6,7},{7,6},{8,9},{9,8},{10,11... | collective-permute-start | bytes 1376264 | tf_op jit(solution)/shard_map/ppermute | solution.py:859
  8.1 8.0 %collective-permute-start.1 = (f32[56,2048]{1,0:T(8,128)S(1)}, f32[56,2048]{1,0:T(8,128)S(1)}, u32[]{:S(2)}, u32[]{:S(2)}) collective-permute-start(f32[56,2048]{1,0:T(8,128)S(1)} %get-tuple-element.31.own_b), channel_id=1, source_target_pairs={{1,2},{2,1},{3,4},{4,3},{5,6},{6,5},{9,10},{10,9},{11,12},{12,11},... | collective-permute-start | bytes 1376264 | tf_op jit(solution)/shard_map/ppermute | solution.py:861
  8.8 1.9 %copy-start.1 = (f32[8,8,8]{2,1,0:T(8,128)S(1)}, f32[8,8,8]{2,1,0:T(8,128)}, u32[]{:S(2)}) copy-start(f32[8,8,8]{2,1,0:T(8,128)} %ops.1) | copy-start | bytes 6148
  14.0 11.4 %collective-permute-start.3 = (f32[2,32,2048]{2,1,0:T(8,128)S(1)}, f32[2,32,2048]{2,1,0:T(8,128)S(1)}, u32[]{:S(2)}, u32[]{:S(2)}) collective-permute-start(f32[2,32,2048]{2,1,0:T(8,128)S(1)} %combine.2._), channel_id=1, source_target_pairs={{0,16},{1,9},{2,18},{3,11},{4,20},{5,13},{6,22},{7,15},{8,24},{9,1... | collective-permute-start | bytes 1572872 | tf_op jit(solution)/shard_map/ppermute | solution.py:841
  16.3 7.9 %collective-permute-start.4 = (f32[8,2048]{1,0:T(8,128)S(1)}, f32[8,2048]{1,0:T(8,128)S(1)}, u32[]{:S(2)}, u32[]{:S(2)}) collective-permute-start(f32[8,2048]{1,0:T(8,128)S(1)} %get-tuple-element.37._.refs_3_), channel_id=1, source_target_pairs={{0,8},{8,0},{16,24},{24,16},{1,9},{9,1},{17,25},{25,17},{2,10},{10... | collective-permute-start | bytes 196616 | tf_op jit(solution)/shard_map/ppermute | solution.py:830
  17.9 7.5 %collective-permute-start.5 = (f32[8,2048]{1,0:T(8,128)S(1)}, f32[8,2048]{1,0:T(8,128)S(1)}, u32[]{:S(2)}, u32[]{:S(2)}) collective-permute-start(f32[8,2048]{1,0:T(8,128)S(1)} %get-tuple-element.37._.refs_3_), channel_id=1, source_target_pairs={{0,16},{8,24},{16,0},{24,8},{1,17},{9,25},{17,1},{25,9},{2,18},{10... | collective-permute-start | bytes 196616 | tf_op jit(solution)/shard_map/ppermute | solution.py:830
  18.4 7.0 %collective-permute-start.6 = (f32[8,2048]{1,0:T(8,128)S(1)}, f32[8,2048]{1,0:T(8,128)S(1)}, u32[]{:S(2)}, u32[]{:S(2)}) collective-permute-start(f32[8,2048]{1,0:T(8,128)S(1)} %get-tuple-element.37._.refs_3_), channel_id=1, source_target_pairs={{0,24},{8,16},{16,8},{24,0},{1,25},{9,17},{17,9},{25,1},{2,26},{10... | collective-permute-start | bytes 196616 | tf_op jit(solution)/shard_map/ppermute | solution.py:830
  26.3 9.2 %collective-permute-start.7 = (f32[2,32,2048]{2,1,0:T(8,128)S(1)}, f32[2,32,2048]{2,1,0:T(8,128)S(1)}, u32[]{:S(2)}, u32[]{:S(2)}) collective-permute-start(f32[2,32,2048]{2,1,0:T(8,128)S(1)} %get-tuple-element.43._.own), channel_id=1, source_target_pairs={{0,8},{1,17},{2,10},{3,19},{4,12},{5,21},{6,14},{7,23},{8,0},{9,25... | collective-permute-start | bytes 1572872 | tf_op jit(solution)/shard_map/ppermute | solution.py:841
  36.4 9.2 %collective-permute-start.8 = (f32[2,32,2048]{2,1,0:T(8,128)S(1)}, f32[2,32,2048]{2,1,0:T(8,128)S(1)}, u32[]{:S(2)}, u32[]{:S(2)}) collective-permute-start(f32[2,32,2048]{2,1,0:T(8,128)S(1)} %combine.3._), channel_id=1, source_target_pairs={{0,16},{1,9},{2,18},{3,11},{4,20},{5,13},{6,22},{7,15},{8,24},{9,1... | collective-permute-start | bytes 1572872 | tf_op jit(solution)/shard_map/ppermute | solution.py:841

commit v8 on v7

--- a/solution.py
+++ b/solution.py
@@ -630,7 +630,9 @@
     R, W = refs[0][0].shape[1:]
     S = R // ROWS
 
-    def body(c, _):
+    group = math.gcd(W // LANES, 2)
+
+    def column(c):
         lanes = pl.ds(pl.multiple_of(c * LANES, LANES), LANES)
         whole = pl.ds(pl.multiple_of(base + c * LANES, LANES), LANES)
         for r0 in range(0, S, 2):
@@ -647,9 +649,13 @@
                     for ref in partial:
                         totals[k] = totals[k] + ref[i, x, lanes]
                     put(i, x, lanes, whole, totals[k])
-        return 0
-
-    lax.fori_loop(0, W // LANES, body, 0)
+
+    def body(first, _):
+        for n in range(group):
+            column(group * first + n)
+        return 0
+
+    lax.fori_loop(0, W // LANES // group, body, 0)
 
 
 def both(own, near):

time: 46.6 us -> 46.5 us (level)
  no operation moved by 1% of the time
where the time goes in v8:
time: 46.5 us; the launch traced here: 46.3 us
  Pallas kernels  25.8 us (55%)
  starting transfers between devices  13.6 us (29%)
  waiting for transfers between devices  6.79 us (15%)
    ppermute x4, starting transfers between devices, along(): return lax.ppermute(value, ('tier', 'tile'), pairs)  9.26 us
    ppermute x4, waiting for transfers between devices, along(): return lax.ppermute(value, ('tier', 'tile'), pairs)  5.54 us
    pallas_call x1, Pallas kernels, last_layers(): pl.pallas_call(last_kernel, out_shape=jax.ShapeDtypeStruct(t.shape, jnp.f...  5.3 us
    pallas_call x1, Pallas kernels, inside(): pl.pallas_call(inside_kernel, out_shape=jax.ShapeDtypeStruct(s.shape, jnp...  3.78 us
    ppermute x3, starting transfers between devices, across(): return lax.ppermute(value, 'tier', [(i, i ^ bits) for i in range(tiers)])  3.55 us
    pallas_call x1, Pallas kernels, begin(): pl.pallas_call(begin_kernel, out_shape=(pltpu.VMEM((2, R, W), f32), pltpu...  3.02 us
    pallas_call x1, Pallas kernels, more_faces(): pl.pallas_call(more_faces_kernel, out_shape=(jax.ShapeDtypeStruct(lab.sha...  2.85 us
    pallas_call x1, Pallas kernels, pack_rows(): pl.pallas_call(pack_kernel, out_shape=(pltpu.VMEM((rows, W), f32), pltpu....  1.99 us
  transfers between devices with their start and end apart: 9, of which 4 were waited for; matrix products, arithmetic and copies ran while one was open for 0% of the time, Pallas kernels for 44%

profile of v8, /device:TPU:0, one launch (start us, length us, event | category | flops | bytes accessed | tf_op | source)
XLA Modules:
  0.0 46.3 jit_solution(13127268716906565628)
XLA Ops:
  0.0 0.0 copy-start
  0.0 0.0 copy-start.2
  0.0 3.0 %begin.1 = (f32[2,32,2048]{2,1,0:T(8,128)S(1)}, f32[32,2048]{1,0:T(8,128)S(1)}, f32[16,32,2048]{2,1,0:T(8,128)S(1)}, s32[16,32,2048]{2,1,0:T(8,128)S(1)}, f32[16,32,2048]{2,1,0:T(8,128)S(1)}) custom-call(f32[16,32,2048]{2,1,0:T(8,128)} %bitcast.4, s32[16,32,2048]{2,1,0:T(8,128)} %bitcast.6, s32[32,2048]{1,0:T(8,128)} %bitcast.8, f32[16]{0:T(128)} %kap.5, ...), custom_call_target="tpu_custom_call" | custom-call | tf_op jit(solution)/shard_map/begin/pallas_call | solution.py:193
  3.0 3.0 %collective-permute-start.2 = (f32[2,32,2048]{2,1,0:T(8,128)S(1)}, f32[2,32,2048]{2,1,0:T(8,128)S(1)}, u32[]{:S(2)}, u32[]{:S(2)}) collective-permute-start(f32[2,32,2048]{2,1,0:T(8,128)S(1)} %get-tuple-element.42.own), channel_id=1, source_target_pairs={{0,8},{1,17},{2,10},{3,19},{4,12},{5,21},{6,14},{7,23},{8,0},{9,25... | collective-permute-start | bytes 1572872 | tf_op jit(solution)/shard_map/ppermute | solution.py:847
  6.0 0.0 copy-done
  6.0 0.0 copy-done.2
  6.0 2.0 %pack_rows.1 = (f32[56,2048]{1,0:T(8,128)S(1)}, f32[56,2048]{1,0:T(8,128)S(1)}, f32[16,32,2048]{2,1,0:T(8,128)S(1)}) custom-call(f32[16,32,2048]{2,1,0:T(8,128)} %bitcast.5, f32[16,32,2048]{2,1,0:T(8,128)S(1)} %get-tuple-element.27.s_in, s32[16,32,2048]{2,1,0:T(8,128)S(1)} %get-tuple-element.28.lab.lab_in, ...), custom_call_target="tpu_custom_call", output_to_operand_aliasing={{2}: (1, {})} | custom-call | tf_op jit(solution)/shard_map/pack_rows/pallas_call | solution.py:296
  8.0 0.1 collective-permute-start
  8.1 0.7 %collective-permute-start.1 = (f32[56,2048]{1,0:T(8,128)S(1)}, f32[56,2048]{1,0:T(8,128)S(1)}, u32[]{:S(2)}, u32[]{:S(2)}) collective-permute-start(f32[56,2048]{1,0:T(8,128)S(1)} %get-tuple-element.31.own_b), channel_id=1, source_target_pairs={{1,2},{2,1},{3,4},{4,3},{5,6},{6,5},{9,10},{10,9},{11,12},{12,11},... | collective-permute-start | bytes 1376264 | tf_op jit(solution)/shard_map/ppermute | solution.py:867
  8.8 0.0 copy-start.1
  8.8 1.9 %faces.1 = (f32[16,32,2048]{2,1,0:T(8,128)S(1)}, f32[16,32,2048]{2,1,0:T(8,128)S(1)}, s32[16,32,2048]{2,1,0:T(8,128)S(1)}) custom-call(s32[16,32,2048]{2,1,0:T(8,128)} %bitcast.7, f32[16]{0:T(128)S(1)} %copy-done.2, f32[16,32,2048]{2,1,0:T(8,128)S(1)} %get-tuple-element.32.h_in, ...), custom_call_target="tpu_custom_call", output_to_operand_aliasing={{0}: (2, {}), {2}: (3, {})} | custom-call | tf_op jit(solution)/shard_map/faces/pallas_call | solution.py:426
  10.7 0.0 copy-done.1
  10.7 1.4 %make_tables.1 = (f32[32,8,8,128]{3,2,1,0:T(8,128)S(1)}, f32[8,8,128]{2,1,0:T(8,128)S(1)}) custom-call(f32[8,8,8]{2,1,0:T(8,128)S(1)} %copy-done.1), custom_call_target="tpu_custom_call" | custom-call | tf_op jit(solution)/shard_map/make_tables/pallas_call | solution.py:618
  12.2 1.0 %collective-permute-done.2.near = f32[2,32,2048]{2,1,0:T(8,128)S(1)} collective-permute-done((f32[2,32,2048]{2,1,0:T(8,128)S(1)}, f32[2,32,2048]{2,1,0:T(8,128)S(1)}, u32[]{:S(2)}, u32[]{:S(2)}) %collective-permute-start.2) | collective-permute-done | bytes 524320 | tf_op jit(solution)/shard_map/ppermute | solution.py:847
  13.2 0.8 %combine.2._ = f32[2,32,2048]{2,1,0:T(8,128)S(1)} custom-call(f32[32,8,8,128]{3,2,1,0:T(8,128)S(1)} %get-tuple-element.25.table, s32[32,2048]{1,0:T(8,128)S(1)} %copy-done, f32[2,32,2048]{2,1,0:T(8,128)S(1)} %get-tuple-element.42.own, f32[2,32,2048]{2,1,0:T(8,128)S(1)} %collective-permute-done.2.near, f32[16,32,2048]{2,1,0:T(8,128)S(1)} %get-tuple-element.33._.h_in), custom_call_target="tpu_custom_call" | custom-call | tf_op jit(solution)/shard_map/combine/pallas_call | solution.py:681
  14.0 2.1 %collective-permute-start.3 = (f32[2,32,2048]{2,1,0:T(8,128)S(1)}, f32[2,32,2048]{2,1,0:T(8,128)S(1)}, u32[]{:S(2)}, u32[]{:S(2)}) collective-permute-start(f32[2,32,2048]{2,1,0:T(8,128)S(1)} %combine.2._), channel_id=1, source_target_pairs={{0,16},{1,9},{2,18},{3,11},{4,20},{5,13},{6,22},{7,15},{8,24},{9,1... | collective-permute-start | bytes 1572872 | tf_op jit(solution)/shard_map/ppermute | solution.py:847
  16.1 0.0 collective-permute-done.got_a
  16.1 0.0 collective-permute-done.1.got_b
  16.1 0.2 edge_rows.1
  16.3 1.6 %collective-permute-start.4 = (f32[8,2048]{1,0:T(8,128)S(1)}, f32[8,2048]{1,0:T(8,128)S(1)}, u32[]{:S(2)}, u32[]{:S(2)}) collective-permute-start(f32[8,2048]{1,0:T(8,128)S(1)} %get-tuple-element.37._.refs_3_), channel_id=1, source_target_pairs={{0,8},{8,0},{16,24},{24,16},{1,9},{9,1},{17,25},{25,17},{2,10},{10... | collective-permute-start | bytes 196616 | tf_op jit(solution)/shard_map/ppermute | solution.py:836
  17.8 0.5 %collective-permute-start.5 = (f32[8,2048]{1,0:T(8,128)S(1)}, f32[8,2048]{1,0:T(8,128)S(1)}, u32[]{:S(2)}, u32[]{:S(2)}) collective-permute-start(f32[8,2048]{1,0:T(8,128)S(1)} %get-tuple-element.37._.refs_3_), channel_id=1, source_target_pairs={{0,16},{8,24},{16,0},{24,8},{1,17},{9,25},{17,1},{25,9},{2,18},{10... | collective-permute-start | bytes 196616 | tf_op jit(solution)/shard_map/ppermute | solution.py:836
  18.3 1.5 %collective-permute-start.6 = (f32[8,2048]{1,0:T(8,128)S(1)}, f32[8,2048]{1,0:T(8,128)S(1)}, u32[]{:S(2)}, u32[]{:S(2)}) collective-permute-start(f32[8,2048]{1,0:T(8,128)S(1)} %get-tuple-element.37._.refs_3_), channel_id=1, source_target_pairs={{0,24},{8,16},{16,8},{24,0},{1,25},{9,17},{17,9},{25,1},{2,26},{10... | collective-permute-start | bytes 196616 | tf_op jit(solution)/shard_map/ppermute | solution.py:836
  19.8 2.9 %more_faces.1 = (f32[16,32,2048]{2,1,0:T(8,128)S(1)}, f32[16,32,2048]{2,1,0:T(8,128)S(1)}) custom-call(s32[16,32,2048]{2,1,0:T(8,128)S(1)} %get-tuple-element.35.lab, f32[16]{0:T(128)S(1)} %copy-done.2, f32[16,32,2048]{2,1,0:T(8,128)S(1)} %get-tuple-element.33._.h_in, ...), custom_call_target="tpu_custom_call", output_to_operand_aliasing={{0}: (2, {}), {1}: (3, {})} | custom-call | tf_op jit(solution)/shard_map/more_faces/pallas_call | solution.py:443
  22.7 0.6 %outer.1.t_in = f32[16,32,2048]{2,1,0:T(8,128)S(1)} custom-call(f32[16,32,2048]{2,1,0:T(8,128)S(1)} %get-tuple-element.40.s_ref, f32[16,32,2048]{2,1,0:T(8,128)S(1)} %get-tuple-element.38.h_ref, f32[16,32,2048]{2,1,0:T(8,128)S(1)} %get-tuple-element.39.g_ref, f32[6,16,2048]{2,1,0:T(8,128)S(1)} %get-tuple-element.34.rims), custom_call_target="tpu_custom_call" | custom-call | tf_op jit(solution)/shard_map/outer/pallas_call | solution.py:496
  23.3 0.8 %own_part.2.refs_1_ = f32[2,32,2048]{2,1,0:T(8,128)S(1)} custom-call(f32[32,8,8,128]{3,2,1,0:T(8,128)S(1)} %get-tuple-element.25.table, s32[32,2048]{1,0:T(8,128)S(1)} %copy-done, f32[2,32,2048]{2,1,0:T(8,128)S(1)} %get-tuple-element.42.own, f32[2,32,2048]{2,1,0:T(8,128)S(1)} %collective-permute-done.2.near, f32[2,32,2048]{2,1,0:T(8,128)S(1)} %combine.2._), custom_call_target="tpu_custom_call" | custom-call | tf_op jit(solution)/shard_map/own_part/pallas_call | solution.py:706
  24.1 0.0 collective-permute-done.4.refs_4_
  24.1 1.2 %collective-permute-done.5.refs_5_ = f32[8,2048]{1,0:T(8,128)S(1)} collective-permute-done((f32[8,2048]{1,0:T(8,128)S(1)}, f32[8,2048]{1,0:T(8,128)S(1)}, u32[]{:S(2)}, u32[]{:S(2)}) %collective-permute-start.5) | collective-permute-done | bytes 65568 | tf_op jit(solution)/shard_map/ppermute | solution.py:836
  25.3 0.0 collective-permute-done.6.refs_6_
  25.3 0.0 collective-permute-done.3.refs_2_
  25.3 0.9 %bond.1 = (f32[16,32,2048]{2,1,0:T(8,128)S(1)}, f32[2,32,2048]{2,1,0:T(8,128)S(1)}) custom-call(s32[32,2048]{1,0:T(8,128)S(1)} %copy-done, f32[32,8,8,128]{3,2,1,0:T(8,128)S(1)} %get-tuple-element.25.table, f32[8,8,128]{2,1,0:T(8,128)S(1)} %get-tuple-element.26.rim_table, ...), custom_call_target="tpu_custom_call", output_to_operand_aliasing={{0}: (7, {})} | custom-call | tf_op jit(solution)/shard_map/bond/pallas_call | solution.py:783
  26.2 2.1 %collective-permute-start.7 = (f32[2,32,2048]{2,1,0:T(8,128)S(1)}, f32[2,32,2048]{2,1,0:T(8,128)S(1)}, u32[]{:S(2)}, u32[]{:S(2)}) collective-permute-start(f32[2,32,2048]{2,1,0:T(8,128)S(1)} %get-tuple-element.43._.own), channel_id=1, source_target_pairs={{0,8},{1,17},{2,10},{3,19},{4,12},{5,21},{6,14},{7,23},{8,0},{9,25... | collective-permute-start | bytes 1572872 | tf_op jit(solution)/shard_map/ppermute | solution.py:847
  28.3 3.8 %inside.1._.t_ref = f32[16,32,2048]{2,1,0:T(8,128)S(1)} custom-call(f32[16,32,2048]{2,1,0:T(8,128)S(1)} %get-tuple-element.40.s_ref, f32[16,32,2048]{2,1,0:T(8,128)S(1)} %get-tuple-element.38.h_ref, f32[16,32,2048]{2,1,0:T(8,128)S(1)} %get-tuple-element.39.g_ref, f32[6,16,2048]{2,1,0:T(8,128)S(1)} %get-tuple-element.34.rims, ...), custom_call_target="tpu_custom_call", output_to_operand_aliasing={{}: (4, {})} | custom-call | tf_op jit(solution)/shard_map/inside/pallas_call | solution.py:520
  32.1 3.4 %collective-permute-done.7.near = f32[2,32,2048]{2,1,0:T(8,128)S(1)} collective-permute-done((f32[2,32,2048]{2,1,0:T(8,128)S(1)}, f32[2,32,2048]{2,1,0:T(8,128)S(1)}, u32[]{:S(2)}, u32[]{:S(2)}) %collective-permute-start.7) | collective-permute-done | bytes 524320 | tf_op jit(solution)/shard_map/ppermute | solution.py:847
  35.5 0.7 %combine.3._ = f32[2,32,2048]{2,1,0:T(8,128)S(1)} custom-call(f32[32,8,8,128]{3,2,1,0:T(8,128)S(1)} %get-tuple-element.25.table, s32[32,2048]{1,0:T(8,128)S(1)} %copy-done, f32[2,32,2048]{2,1,0:T(8,128)S(1)} %get-tuple-element.43._.own, f32[2,32,2048]{2,1,0:T(8,128)S(1)} %collective-permute-done.7.near, f32[16,32,2048]{2,1,0:T(8,128)S(1)} %inside.1._.t_ref), custom_call_target="tpu_custom_call" | custom-call | tf_op jit(solution)/shard_map/combine/pallas_call | solution.py:681
  36.2 2.1 %collective-permute-start.8 = (f32[2,32,2048]{2,1,0:T(8,128)S(1)}, f32[2,32,2048]{2,1,0:T(8,128)S(1)}, u32[]{:S(2)}, u32[]{:S(2)}) collective-permute-start(f32[2,32,2048]{2,1,0:T(8,128)S(1)} %combine.3._), channel_id=1, source_target_pairs={{0,16},{1,9},{2,18},{3,11},{4,20},{5,13},{6,22},{7,15},{8,24},{9,1... | collective-permute-start | bytes 1572872 | tf_op jit(solution)/shard_map/ppermute | solution.py:847
  38.3 5.3 %last_layers.1.refs_2_ = f32[16,32,2048]{2,1,0:T(8,128)} custom-call(f32[16,32,2048]{2,1,0:T(8,128)S(1)} %inside.1._.t_ref, f32[16,32,2048]{2,1,0:T(8,128)S(1)} %get-tuple-element.38.h_ref, f32[16,32,2048]{2,1,0:T(8,128)S(1)} %get-tuple-element.39.g_ref, f32[6,16,2048]{2,1,0:T(8,128)S(1)} %get-tuple-element.34.rims), custom_call_target="tpu_custom_call" | custom-call | tf_op jit(solution)/shard_map/last_layers/pallas_call | solution.py:559
  43.6 0.8 %own_part.3.refs_0_ = f32[2,32,2048]{2,1,0:T(8,128)S(1)} custom-call(f32[32,8,8,128]{3,2,1,0:T(8,128)S(1)} %get-tuple-element.25.table, s32[32,2048]{1,0:T(8,128)S(1)} %copy-done, f32[2,32,2048]{2,1,0:T(8,128)S(1)} %get-tuple-element.43._.own, f32[2,32,2048]{2,1,0:T(8,128)S(1)} %collective-permute-done.7.near, f32[2,32,2048]{2,1,0:T(8,128)S(1)} %combine.3._), custom_call_target="tpu_custom_call" | custom-call | tf_op jit(solution)/shard_map/own_part/pallas_call | solution.py:706
  44.4 1.1 %collective-permute-done.8.refs_1_ = f32[2,32,2048]{2,1,0:T(8,128)S(1)} collective-permute-done((f32[2,32,2048]{2,1,0:T(8,128)S(1)}, f32[2,32,2048]{2,1,0:T(8,128)S(1)}, u32[]{:S(2)}, u32[]{:S(2)}) %collective-permute-start.8) | collective-permute-done | bytes 524320 | tf_op jit(solution)/shard_map/ppermute | solution.py:847
  45.5 0.8 %final_planes.1 = f32[16,32,2048]{2,1,0:T(8,128)} custom-call(s32[32,2048]{1,0:T(8,128)S(1)} %copy-done, f32[32,8,8,128]{3,2,1,0:T(8,128)S(1)} %get-tuple-element.25.table, f32[2,32,2048]{2,1,0:T(8,128)S(1)} %own_part.3.refs_0_, f32[2,32,2048]{2,1,0:T(8,128)S(1)} %collective-permute-done.8.refs_1_, ...), custom_call_target="tpu_custom_call", output_to_operand_aliasing={{}: (4, {})} | custom-call | tf_op jit(solution)/shard_map/final_planes/pallas_call | solution.py:823
Async XLA Ops:
  0.0 6.0 %copy-start = (s32[32,2048]{1,0:T(8,128)S(1)}, s32[32,2048]{1,0:T(8,128)}, u32[]{:S(2)}) copy-start(s32[32,2048]{1,0:T(8,128)} %zone.13) | copy-start | bytes 786436
  0.0 6.0 %copy-start.2 = (f32[16]{0:T(128)S(1)}, f32[16]{0:T(128)}, u32[]{:S(2)}) copy-start(f32[16]{0:T(128)} %kap.5) | copy-start | bytes 196
  3.0 10.2 %collective-permute-start.2 = (f32[2,32,2048]{2,1,0:T(8,128)S(1)}, f32[2,32,2048]{2,1,0:T(8,128)S(1)}, u32[]{:S(2)}, u32[]{:S(2)}) collective-permute-start(f32[2,32,2048]{2,1,0:T(8,128)S(1)} %get-tuple-element.42.own), channel_id=1, source_target_pairs={{0,8},{1,17},{2,10},{3,19},{4,12},{5,21},{6,14},{7,23},{8,0},{9,25... | collective-permute-start | bytes 1572872 | tf_op jit(solution)/shard_map/ppermute | solution.py:847
  8.0 8.0 %collective-permute-start = (f32[56,2048]{1,0:T(8,128)S(1)}, f32[56,2048]{1,0:T(8,128)S(1)}, u32[]{:S(2)}, u32[]{:S(2)}) collective-permute-start(f32[56,2048]{1,0:T(8,128)S(1)} %get-tuple-element.30._.own_a), channel_id=1, source_target_pairs={{0,1},{1,0},{2,3},{3,2},{4,5},{5,4},{6,7},{7,6},{8,9},{9,8},{10,11... | collective-permute-start | bytes 1376264 | tf_op jit(solution)/shard_map/ppermute | solution.py:865
  8.1 8.0 %collective-permute-start.1 = (f32[56,2048]{1,0:T(8,128)S(1)}, f32[56,2048]{1,0:T(8,128)S(1)}, u32[]{:S(2)}, u32[]{:S(2)}) collective-permute-start(f32[56,2048]{1,0:T(8,128)S(1)} %get-tuple-element.31.own_b), channel_id=1, source_target_pairs={{1,2},{2,1},{3,4},{4,3},{5,6},{6,5},{9,10},{10,9},{11,12},{12,11},... | collective-permute-start | bytes 1376264 | tf_op jit(solution)/shard_map/ppermute | solution.py:867
  8.8 1.9 %copy-start.1 = (f32[8,8,8]{2,1,0:T(8,128)S(1)}, f32[8,8,8]{2,1,0:T(8,128)}, u32[]{:S(2)}) copy-start(f32[8,8,8]{2,1,0:T(8,128)} %ops.1) | copy-start | bytes 6148
  14.0 11.4 %collective-permute-start.3 = (f32[2,32,2048]{2,1,0:T(8,128)S(1)}, f32[2,32,2048]{2,1,0:T(8,128)S(1)}, u32[]{:S(2)}, u32[]{:S(2)}) collective-permute-start(f32[2,32,2048]{2,1,0:T(8,128)S(1)} %combine.2._), channel_id=1, source_target_pairs={{0,16},{1,9},{2,18},{3,11},{4,20},{5,13},{6,22},{7,15},{8,24},{9,1... | collective-permute-start | bytes 1572872 | tf_op jit(solution)/shard_map/ppermute | solution.py:847
  16.3 7.8 %collective-permute-start.4 = (f32[8,2048]{1,0:T(8,128)S(1)}, f32[8,2048]{1,0:T(8,128)S(1)}, u32[]{:S(2)}, u32[]{:S(2)}) collective-permute-start(f32[8,2048]{1,0:T(8,128)S(1)} %get-tuple-element.37._.refs_3_), channel_id=1, source_target_pairs={{0,8},{8,0},{16,24},{24,16},{1,9},{9,1},{17,25},{25,17},{2,10},{10... | collective-permute-start | bytes 196616 | tf_op jit(solution)/shard_map/ppermute | solution.py:836
  17.8 7.5 %collective-permute-start.5 = (f32[8,2048]{1,0:T(8,128)S(1)}, f32[8,2048]{1,0:T(8,128)S(1)}, u32[]{:S(2)}, u32[]{:S(2)}) collective-permute-start(f32[8,2048]{1,0:T(8,128)S(1)} %get-tuple-element.37._.refs_3_), channel_id=1, source_target_pairs={{0,16},{8,24},{16,0},{24,8},{1,17},{9,25},{17,1},{25,9},{2,18},{10... | collective-permute-start | bytes 196616 | tf_op jit(solution)/shard_map/ppermute | solution.py:836
  18.3 7.0 %collective-permute-start.6 = (f32[8,2048]{1,0:T(8,128)S(1)}, f32[8,2048]{1,0:T(8,128)S(1)}, u32[]{:S(2)}, u32[]{:S(2)}) collective-permute-start(f32[8,2048]{1,0:T(8,128)S(1)} %get-tuple-element.37._.refs_3_), channel_id=1, source_target_pairs={{0,24},{8,16},{16,8},{24,0},{1,25},{9,17},{17,9},{25,1},{2,26},{10... | collective-permute-start | bytes 196616 | tf_op jit(solution)/shard_map/ppermute | solution.py:836
  26.2 9.2 %collective-permute-start.7 = (f32[2,32,2048]{2,1,0:T(8,128)S(1)}, f32[2,32,2048]{2,1,0:T(8,128)S(1)}, u32[]{:S(2)}, u32[]{:S(2)}) collective-permute-start(f32[2,32,2048]{2,1,0:T(8,128)S(1)} %get-tuple-element.43._.own), channel_id=1, source_target_pairs={{0,8},{1,17},{2,10},{3,19},{4,12},{5,21},{6,14},{7,23},{8,0},{9,25... | collective-permute-start | bytes 1572872 | tf_op jit(solution)/shard_map/ppermute | solution.py:847
  36.2 9.2 %collective-permute-start.8 = (f32[2,32,2048]{2,1,0:T(8,128)S(1)}, f32[2,32,2048]{2,1,0:T(8,128)S(1)}, u32[]{:S(2)}, u32[]{:S(2)}) collective-permute-start(f32[2,32,2048]{2,1,0:T(8,128)S(1)} %combine.3._), channel_id=1, source_target_pairs={{0,16},{1,9},{2,18},{3,11},{4,20},{5,13},{6,22},{7,15},{8,24},{9,1... | collective-permute-start | bytes 1572872 | tf_op jit(solution)/shard_map/ppermute | solution.py:847
